TPU v7x, 256 devices: a whole 4x4x8 slice. The times are simulated.
256 devices in a mesh: seq: 32 (over y, x, core), tensor: 8 (over z).
Axes of the slice: x: 4, y: 4, z: 8, core: 2. Of those that a mesh axis runs over, the one named last changes fastest.
Arguments:
- tokens: bfloat16 [8192, 4096], P('seq', 'tensor'), may hold values from -6 to 6
- x_gain: bfloat16 [4096], replicated, may hold values from 0.099609375 to 1.8984375
- nbr_gain: bfloat16 [4096], replicated, may hold values from 0.099609375 to 1.8984375
- database: bfloat16 [512, 128, 4096], P('seq', None, 'tensor'), may hold values from -6 to 6
- nbr_shard: int32 [128, 2], P('seq'), may hold values from 0 to 31, all different within a row; in each aligned block of 4 rows (0 to 3, 4 to 7, ...) at most 2 rows name the same one
- nbr_row: int32 [128, 2], P('seq'), may hold values from 0 to 15
- nbr_count: int32 [128], P('seq'), may hold values from 1 to 2
- wq: bfloat16 [4096, 2048], P(None, 'tensor'), may hold values from -8 to 8
- wk: bfloat16 [4096, 2048], P(None, 'tensor'), may hold values from -0.09375 to 0.09375
- wv: bfloat16 [4096, 2048], P(None, 'tensor'), may hold values from -0.09375 to 0.09375
- wo: bfloat16 [2048, 4096], P('tensor'), may hold values from -0.125 to 0.125
Outputs:
- mixed: bfloat16 [8192, 4096], P('seq', 'tensor')
Inputs may be any that keep to these rules, and one draw needn't show every extreme that they name: `nbr_shard`: among the spans of one device no shard is named more than 2 times, a bound that some block reaches; the 2 neighbours of a span name different shards.
All inputs are finite; a program needn't handle non-finite values.
Results may differ from a plain program's by a relative error of at most 0.015.
The roundings to bfloat16 on the way count: a program that leaves them out, or rounds other values in their place, can miss the bound.
Values may be sent and summed in bfloat16 or wider, within the bound.
No kernel may reach another device: no remote copies, remote signals or barrier semaphores. Data moves between devices by JAX's collectives and lax.ppermute only.
A program may use at most 192 MiB of HBM per device.

v0:
```python
import jax
import jax.numpy as jnp
from jax import lax
from jax.sharding import PartitionSpec as P

HS = 128
NB = 2
CAP = 2


def passed_along(x, axis, by):
    size = lax.axis_size(axis)
    pairs = [(i, i + by) for i in range(size) if 0 <= i + by < size]
    return lax.ppermute(x, axis, pairs)


def rms_scale(rows, gain):
    values = rows.astype(jnp.float32)
    inverse = lax.rsqrt(jnp.mean(values * values, axis=-1, keepdims=True) + 1e-06)
    return (values * inverse * gain.astype(jnp.float32)).astype(jnp.bfloat16)


def attend(queries, keys, values, count):
    scores = jnp.einsum("bqhe,bkhe->bhqk", queries, keys, preferred_element_type=jnp.float32)
    width = keys.shape[1]
    owner = jnp.arange(width, dtype=jnp.int32) // (width // NB)
    valid = (owner[None, :] < count[:, None])[:, None, None, :]
    scores = jnp.where(valid, scores, jnp.float32(-1e30))
    top = jnp.max(scores, axis=-1, keepdims=True)
    expo = jnp.exp(scores - top)
    weights = (expo / jnp.sum(expo, axis=-1, keepdims=True)).astype(jnp.bfloat16)
    return jnp.einsum(
        "bhqk,bkhe->bqhe", weights, values, preferred_element_type=jnp.float32
    ).astype(jnp.bfloat16)


def body(tokens, x_gain, nbr_gain, database, nbr_shard, nbr_row, nbr_count, wq, wk, wv, wo):
    n_seq = lax.axis_size("seq")
    n_ten = lax.axis_size("tensor")
    tok_dev = tokens.shape[0]
    span_dev = nbr_shard.shape[0]
    span_len = tok_dev // span_dev
    nbr_len = database.shape[1]
    d_part = database.shape[2]
    head_cols = wq.shape[1]
    heads_dev = head_cols // HS
    items = span_dev * NB
    owners = nbr_shard.reshape(-1)
    offsets = nbr_row.reshape(-1)
    order = jnp.arange(items, dtype=jnp.int32)
    earlier = (owners[:, None] == owners[None, :]) & (order[None, :] < order[:, None])
    rank = jnp.sum(earlier.astype(jnp.int32), axis=1)
    slots = owners * CAP + rank
    table = jnp.arange(n_seq * CAP, dtype=jnp.int32)
    hit = (slots[:, None] == table[None, :]).astype(jnp.int32)
    wanted = jnp.sum(hit * offsets[:, None], axis=0).reshape(n_seq, CAP)
    asked = lax.all_to_all(wanted, "seq", split_axis=0, concat_axis=0, tiled=True)
    outgoing = database[asked.reshape(-1)].reshape(n_seq, CAP, nbr_len, d_part)
    replies = lax.all_to_all(outgoing, "seq", split_axis=0, concat_axis=0, tiled=True)
    rows = replies.reshape(n_seq * CAP, nbr_len, d_part)[slots]
    whole = lax.all_gather(tokens, "tensor", axis=1, tiled=True)
    normed = rms_scale(whole, x_gain)
    queries = (jnp.dot(normed, wq, preferred_element_type=jnp.float32) * HS ** (-0.5)).astype(
        jnp.bfloat16
    )
    n_rows = items * nbr_len
    full_rows = lax.all_gather(rows, "tensor", axis=2, tiled=True)
    encoded = rms_scale(full_rows, nbr_gain).reshape(n_rows, d_part * n_ten)
    keys = jnp.dot(encoded, wk, preferred_element_type=jnp.float32).astype(jnp.bfloat16)
    values = jnp.dot(encoded, wv, preferred_element_type=jnp.float32).astype(jnp.bfloat16)
    key_spans = keys.reshape(span_dev, NB * nbr_len, heads_dev, HS)
    value_spans = values.reshape(span_dev, NB * nbr_len, heads_dev, HS)
    lead = jnp.zeros((1, head_cols), jnp.bfloat16)
    tail = jnp.zeros((span_len - 1, head_cols), jnp.bfloat16)
    query_blocks = jnp.concatenate([lead, queries, tail], axis=0).reshape(
        span_dev + 1, span_len, heads_dev, HS
    )
    prev_keys, prev_values, prev_count = passed_along(
        (key_spans[-1], value_spans[-1], nbr_count[-1:]), "seq", 1
    )
    all_keys = jnp.concatenate([prev_keys[None], key_spans], axis=0)
    all_values = jnp.concatenate([prev_values[None], value_spans], axis=0)
    counts = jnp.concatenate([prev_count, nbr_count], axis=0)
    result = attend(query_blocks, all_keys, all_values, counts)
    attended = result.reshape((span_dev + 1) * span_len, head_cols)[1 : 1 + tok_dev]
    part = jnp.dot(attended, wo, preferred_element_type=jnp.float32).astype(jnp.bfloat16)
    part = lax.optimization_barrier(part)
    summed = lax.psum_scatter(
        part.astype(jnp.float32).astype(jnp.bfloat16), "tensor", scatter_dimension=1, tiled=True
    ).astype(jnp.float32)
    return (tokens.astype(jnp.float32) + summed).astype(jnp.bfloat16)


def solution(mesh):
    placed = (
        P("seq", "tensor"),
        P(),
        P(),
        P("seq", None, "tensor"),
        P("seq", None),
        P("seq", None),
        P("seq"),
        P(None, "tensor"),
        P(None, "tensor"),
        P(None, "tensor"),
        P("tensor", None),
    )
    return jax.shard_map(
        body, mesh=mesh, in_specs=placed, out_specs=P("seq", "tensor"), check_vma=False
    )
```

profile of v0, /device:TPU:8, one launch (start us, length us, event | category | flops | bytes accessed | tf_op | source)
XLA Modules:
  0.0 337.9 jit_solution(14298476647795826664)
XLA Ops:
  8.8 13.5 %all_to_all.14 = s32[32,1,2]{2,1,0:T(1,128)S(1)} all-to-all(s32[32,1,2]{2,1,0:T(1,128)S(1)} %bitcast.41), channel_id=1, replica_groups=mesh['seq'=32,'tensor'=8] {'seq'}, dimensions={0} | all-to-all | bytes 512 | tf_op jit(solution)/shard_map/all_to_all | solution.py:57
  23.6 5.3 %gather_fusion = bf16[64,128,512]{2,1,0:T(8,128)(2,1)} fusion(bf16[16,128,512]{2,1,0:T(8,128)(2,1)S(1)} %copy-done, s32[1024]{0:T(1024)S(1)} %pad_clamp_fusion.1), kind=kCustom, calls=%fused_computation | custom fusion | bytes 16777472 | tf_op jit(solution)/shard_map/gather | solution.py:58
  28.9 6.1 %all-to-all-start.1 = ((bf16[32,2,128,512]{3,2,1,0:T(8,128)(2,1)}), bf16[32,2,128,512]{3,2,1,0:T(8,128)(2,1)}, u32[]{:S(2)}, u32[]{:S(2)}) async-start(bf16[32,2,128,512]{3,2,1,0:T(8,128)(2,1)} %bitcast.34), calls=%async_computation.1 | async-start | bytes 16777216 | tf_op jit(solution)/shard_map/all_to_all | solution.py:59
  36.1 99.9 %all-to-all-done.1 = bf16[32,2,128,512]{3,2,1,0:T(8,128)(2,1)} async-done(((bf16[32,2,128,512]{3,2,1,0:T(8,128)(2,1)}), bf16[32,2,128,512]{3,2,1,0:T(8,128)(2,1)}, u32[]{:S(2)}, u32[]{:S(2)}) %all-to-all-start.1) | async-done | bytes 8388640 | tf_op jit(solution)/shard_map/all_to_all | solution.py:59
  136.0 5.1 %gather_fusion.1 = bf16[8,128,512]{2,1,0:T(8,128)(2,1)} fusion(bf16[64,128,512]{2,1,0:T(8,128)(2,1)} %bitcast.3, s32[1024]{0:T(1024)S(1)} %pad_clamp_fusion), kind=kCustom, calls=%fused_computation.1 | custom fusion | bytes 2097184 | tf_op jit(solution)/shard_map/gather | solution.py:60
  141.7 1.9 collective-permute-start.1
  143.8 5.0 %collective-permute-done.1 = s32[1]{0:T(128)} collective-permute-done((s32[1]{0:T(128)}, s32[1]{0:T(128)}, u32[]{:S(2)}, u32[]{:S(2)}) %collective-permute-start.1) | collective-permute-done | bytes 36 | tf_op jit(solution)/shard_map/ppermute | solution.py:14
  149.5 2.1 fusion.4
  151.6 3.0 fusion.16
  154.8 83.5 %all-gather.6.cloned.1.call-done = bf16[8,128,4096]{2,1,0:T(8,128)(2,1)} async-done(((bf16[8,128,512]{2,1,0:T(8,128)(2,1)}), bf16[8,128,4096]{2,1,0:T(8,128)(2,1)}) %all-gather.6.cloned.1.call-update) | async-done | bytes 8388624 | tf_op jit(solution)/shard_map/all_gather | solution.py:67
  238.3 5.1 %fusion.1 = f32[8,128]{1,0:T(8,128)S(1)} fusion(bf16[8,128,4096]{2,1,0:T(8,128)(2,1)} %all-gather.6.cloned.1.call-done), kind=kLoop, calls=%fused_computation.5 | loop fusion | flops 12581888 | bytes 8392704 | tf_op jit(solution)/shard_map/reduce_sum | solution.py:19
  243.4 10.3 %fusion.3 = bf16[8,128,4096]{2,1,0:T(8,128)(2,1)} fusion(bf16[8,128,4096]{2,1,0:T(8,128)(2,1)} %all-gather.6.cloned.1.call-done, f32[4096]{0:T(1024)S(1)} %convert_element_type.57, f32[8,128]{1,0:T(8,128)S(1)} %add_rsqrt_fusion), kind=kLoop, calls=%fused_computation.7 | loop fusion | flops 16777216 | bytes 16797696 | tf_op jit(solution)/shard_map/convert_element_type | solution.py:20
  253.7 6.3 %convolution_convert_fusion.1 = bf16[1024,256]{0,1:T(8,128)(2,1)S(1)} fusion(bf16[1024,4096]{1,0:T(8,128)(2,1)} %bitcast.35, bf16[4096,256]{1,0:T(8,128)(2,1)} %param.19), kind=kOutput, calls=%fused_computation.18 | convolution fusion | flops 2147745792 | bytes 11010048 | tf_op jit(solution)/shard_map/dot_general | solution.py:69
  260.9 2.1 collective-permute-start.2
  263.0 7.2 %convolution_convert_fusion.2 = bf16[1024,256]{0,1:T(8,128)(2,1)} fusion(bf16[1024,4096]{1,0:T(8,128)(2,1)} %bitcast.36, bf16[4096,256]{1,0:T(8,128)(2,1)} %param.20), kind=kOutput, calls=%fused_computation.19 | convolution fusion | flops 2147745792 | bytes 11010048 | tf_op jit(solution)/shard_map/dot_general | solution.py:70
  270.5 2.3 reshape.161
  273.2 2.1 copy.44
  276.0 3.5 %collective-permute-start = (bf16[256,2,128]{2,0,1:T(8,128)(2,1)}, bf16[256,2,128]{2,0,1:T(8,128)(2,1)}, u32[]{:S(2)}, u32[]{:S(2)}) collective-permute-start(bf16[256,2,128]{2,0,1:T(8,128)(2,1)} %copy.43), channel_id=1, source_target_pairs={{0,8},{8,16},{16,24},{24,32},{32,40},{40,48},{48,56},{56,64},{64,7... | collective-permute-start | bytes 393224 | tf_op jit(solution)/shard_map/ppermute | solution.py:14
  280.8 1.4 fusion.56
  282.2 2.5 collective-permute-done
  284.7 2.2 fusion.19
  287.2 3.7 %convolution_convert_fusion = bf16[256,4096]{1,0:T(8,128)(2,1)} fusion(bf16[256,4096]{1,0:T(8,128)(2,1)} %param.21, bf16[320,256]{1,0:T(8,128)(2,1)S(1)} %bitcast.39), kind=kOutput, calls=%fused_computation.10 | convolution fusion | flops 537919488 | bytes 4325376 | tf_op jit(solution)/shard_map/dot_general | solution.py:86
  290.9 38.7 %reduce-scatter.2.cloned.1.call-done = bf16[256,512]{1,0:T(8,128)(2,1)} async-done(((bf16[256,4096]{1,0:T(8,128)(2,1)}), bf16[256,512]{1,0:T(8,128)(2,1)}) %reduce-scatter.2.cloned.1.call-update) | async-done | bytes 262160 | tf_op jit(solution)/shard_map/reduce_scatter | solution.py:88
  329.6 1.7 add_convert_fusion
  (61 shorter events, 10.0 us)
Async XLA Ops:
  6.5 17.1 %copy-start = (bf16[16,128,512]{2,1,0:T(8,128)(2,1)S(1)}, bf16[16,128,512]{2,1,0:T(8,128)(2,1)}, u32[]{:S(2)}) copy-start(bf16[16,128,512]{2,1,0:T(8,128)(2,1)} %param.14) | copy-start | bytes 6291460
  28.9 6.9 %copy-start.4 = (s32[4,2]{0,1:T(2,128)S(1)}, s32[4,2]{0,1:T(2,128)}, u32[]{:S(2)}) copy-start(s32[4,2]{0,1:T(2,128)} %param.15) | copy-start | bytes 100
  28.9 112.2 %copy-start.5 = (s32[4]{0:T(128)S(1)}, s32[4]{0:T(128)}, u32[]{:S(2)}) copy-start(s32[4]{0:T(128)} %param.17) | copy-start | bytes 52
  28.9 114.7 %copy-start.2 = (bf16[4096]{0:T(1024)(128)(2,1)S(1)}, bf16[4096]{0:T(1024)(128)(2,1)}, u32[]{:S(2)}) copy-start(bf16[4096]{0:T(1024)(128)(2,1)} %param.13) | copy-start | bytes 24580
  28.9 114.7 %copy-start.3 = (bf16[4096]{0:T(1024)(128)(2,1)S(1)}, bf16[4096]{0:T(1024)(128)(2,1)}, u32[]{:S(2)}) copy-start(bf16[4096]{0:T(1024)(128)(2,1)} %param.12) | copy-start | bytes 24580
  28.9 107.0 %all-to-all-start.1 = ((bf16[32,2,128,512]{3,2,1,0:T(8,128)(2,1)}), bf16[32,2,128,512]{3,2,1,0:T(8,128)(2,1)}, u32[]{:S(2)}, u32[]{:S(2)}) async-start(bf16[32,2,128,512]{3,2,1,0:T(8,128)(2,1)} %bitcast.34), calls=%async_computation.1 | async-start | bytes 16777216 | tf_op jit(solution)/shard_map/all_to_all | solution.py:59
  35.1 114.5 %all-gather.4.cloned.1.call-start = ((), (), s32[]{:S(2)}) async-start(), calls=%async_computation.3 | async-start | bytes 2359296 | tf_op jit(solution)/shard_map/all_gather | solution.py:61
  35.8 202.5 %all-gather.6.cloned.1.call-start = ((), (), s32[]{:S(2)}) async-start(), calls=%async_computation.5 | async-start | bytes 9437184 | tf_op jit(solution)/shard_map/all_gather | solution.py:67
  141.1 188.6 %reduce-scatter.2.cloned.1.call-start = ((), (), s32[]{:S(2)}) async-start(), calls=%async_computation.4 | async-start | bytes 2359296 | tf_op jit(solution)/shard_map/reduce_scatter | solution.py:88
  141.7 7.0 %collective-permute-start.1 = (s32[1]{0:T(128)}, s32[1]{0:T(128)}, u32[]{:S(2)}, u32[]{:S(2)}) collective-permute-start(s32[1]{0:T(128)} %slice.15), channel_id=1, source_target_pairs={{0,8},{8,16},{16,24},{24,32},{32,40},{40,48},{48,56},{56,64},{64,7... | collective-permute-start | bytes 20 | tf_op jit(solution)/shard_map/ppermute | solution.py:14
  260.9 18.6 %collective-permute-start.2 = (bf16[256,2,128]{2,0,1:T(8,128)(2,1)}, bf16[256,2,128]{2,0,1:T(8,128)(2,1)}, u32[]{:S(2)}, u32[]{:S(2)}) collective-permute-start(bf16[256,2,128]{2,0,1:T(8,128)(2,1)} %copy.45), channel_id=1, source_target_pairs={{0,8},{8,16},{16,24},{24,32},{32,40},{40,48},{48,56},{56,64},{64,7... | collective-permute-start | bytes 393224 | tf_op jit(solution)/shard_map/ppermute | solution.py:14
  270.1 5.1 %slice-start = ((bf16[1024,256]{0,1:T(8,128)(2,1)}), bf16[256,256]{0,1:T(8,128)(2,1)S(1)}, s32[]{:S(2)}) async-start(bf16[1024,256]{0,1:T(8,128)(2,1)} %convolution_convert_fusion.2), calls=%async_computation.6 | async-start | bytes 262144 | tf_op jit(solution)/shard_map/slice | solution.py:79
  276.0 8.7 %collective-permute-start = (bf16[256,2,128]{2,0,1:T(8,128)(2,1)}, bf16[256,2,128]{2,0,1:T(8,128)(2,1)}, u32[]{:S(2)}, u32[]{:S(2)}) collective-permute-start(bf16[256,2,128]{2,0,1:T(8,128)(2,1)} %copy.43), channel_id=1, source_target_pairs={{0,8},{8,16},{16,24},{24,32},{32,40},{40,48},{48,56},{56,64},{64,7... | collective-permute-start | bytes 393224 | tf_op jit(solution)/shard_map/ppermute | solution.py:14
  287.0 42.6 %copy-start.1 = (bf16[256,512]{1,0:T(8,128)(2,1)S(1)}, bf16[256,512]{1,0:T(8,128)(2,1)}, u32[]{:S(2)}) copy-start(bf16[256,512]{1,0:T(8,128)(2,1)} %param.11) | copy-start | bytes 786436
Sparse Core Ops, SparseCore 0:
  37.7 44.0 all-gather.3
  141.2 97.1 all-gather.5
  291.0 38.5 reduce-scatter.1
where the time goes:
time: 339 us; the launch traced here: 338 us
  waiting for transfers between devices  230 us (68%)
  matrix products  25.1 us (7%)
  other arithmetic  21.2 us (6%)
  local copies, waits for them, and re-layouts  20.7 us (6%)
  starting transfers between devices  13.7 us (4%)
  blocking collectives  13.5 us (4%)
  between operations  13.4 us (4%)
    all_to_all x1, waiting for transfers between devices, body(): lax.all_to_all(outgoing, 'seq', split_axis=0, concat_axis=0, tiled=True)  99.9 us
    all_gather x1, waiting for transfers between devices, body(): full_rows = lax.all_gather(rows, 'tensor', axis=2, tiled=True)  83.5 us
    reduce_scatter x1, waiting for transfers between devices, body(): lax.psum_scatter(part.astype(jnp.float32).astype(jnp.bfloat16), 'tensor',...  38.7 us
    all_to_all x1, blocking collectives, body(): lax.all_to_all(wanted, 'seq', split_axis=0, concat_axis=0, tiled=True)  13.5 us
    convert_element_type x3, other arithmetic, rms_scale(): return (values * inverse * gain.astype(jnp.float32)).astype(jnp.bfloat16)  10.3 us
    ppermute x3, waiting for transfers between devices, passed_along(): return lax.ppermute(x, axis, pairs)  7.51 us
    ppermute x3, starting transfers between devices, passed_along(): return lax.ppermute(x, axis, pairs)  7.47 us
    dot_general x1, matrix products, body(): jnp.dot(encoded, wv, preferred_element_type=jnp.float32)  7.16 us
  transfers between devices with their start and end apart: 7, of which 5 were waited for; matrix products, arithmetic and copies ran while one was open for 8% of the time, Pallas kernels for 0%

commit v1 on v0

--- a/solution.py
+++ b/solution.py
@@ -5,7 +5,8 @@
 
 HS = 128
 NB = 2
-CAP = 2
+PIECE_T = 16
+PIECE_F = 128
 
 
 def passed_along(x, axis, by):
@@ -45,19 +46,19 @@
     head_cols = wq.shape[1]
     heads_dev = head_cols // HS
     items = span_dev * NB
-    owners = nbr_shard.reshape(-1)
-    offsets = nbr_row.reshape(-1)
-    order = jnp.arange(items, dtype=jnp.int32)
-    earlier = (owners[:, None] == owners[None, :]) & (order[None, :] < order[:, None])
-    rank = jnp.sum(earlier.astype(jnp.int32), axis=1)
-    slots = owners * CAP + rank
-    table = jnp.arange(n_seq * CAP, dtype=jnp.int32)
-    hit = (slots[:, None] == table[None, :]).astype(jnp.int32)
-    wanted = jnp.sum(hit * offsets[:, None], axis=0).reshape(n_seq, CAP)
-    asked = lax.all_to_all(wanted, "seq", split_axis=0, concat_axis=0, tiled=True)
-    outgoing = database[asked.reshape(-1)].reshape(n_seq, CAP, nbr_len, d_part)
+    pieces_t = nbr_len // PIECE_T
+    pieces_f = d_part // PIECE_F
+    per_shard = database.shape[0]
+    index = (nbr_shard * per_shard + nbr_row).reshape(-1)
+    everyone = lax.all_gather(index, "seq", axis=0, tiled=True)
+    cut = database.reshape(per_shard, pieces_t, PIECE_T, pieces_f, PIECE_F)
+    cut = cut.transpose(1, 3, 0, 2, 4).reshape(n_seq, per_shard, PIECE_T, PIECE_F)
+    spread = lax.all_to_all(cut, "seq", split_axis=0, concat_axis=0, tiled=True)
+    spread = spread.reshape(n_seq * per_shard, PIECE_T, PIECE_F)
+    outgoing = spread[everyone].reshape(n_seq, items, PIECE_T, PIECE_F)
     replies = lax.all_to_all(outgoing, "seq", split_axis=0, concat_axis=0, tiled=True)
-    rows = replies.reshape(n_seq * CAP, nbr_len, d_part)[slots]
+    rows = replies.reshape(pieces_t, pieces_f, items, PIECE_T, PIECE_F)
+    rows = rows.transpose(2, 0, 3, 1, 4).reshape(items, nbr_len, d_part)
     whole = lax.all_gather(tokens, "tensor", axis=1, tiled=True)
     normed = rms_scale(whole, x_gain)
     queries = (jnp.dot(normed, wq, preferred_element_type=jnp.float32) * HS ** (-0.5)).astype(

time: 339 us -> 277 us (0.82)
  waiting for transfers between devices: 230 us -> 128 us
  blocking collectives: 13.5 us -> 53.7 us
    all_to_all x1, waiting for transfers between devices: 99.9 us -> 0.01 us  [body(): spread = lax.all_to_all(cut, 'seq', split_axis=0, concat_axis=0, tiled=True)]
    unnamed x0 -> x1, blocking collectives: none -> 34 us
    gather x2 -> x1, local copies, waits for them, and re-layouts: 10.3 us -> 2.44 us  [body(): outgoing = spread[everyone].reshape(n_seq, items, PIECE_T, PIECE_F)]
    all_to_all x1, blocking collectives: 13.5 us -> 19.6 us  [body(): lax.all_to_all(outgoing, 'seq', split_axis=0, concat_axis=0, tiled=True)]
    reshape x2 -> x3, local copies, waits for them, and re-layouts: 0.19 us -> 5.27 us  [the longest x1 3.95 us: body(): cut = database.reshape(per_shard, pieces_t, PIECE_T, pieces_f, PIECE_F)]
    transpose x0 -> x2, local copies, waits for them, and re-layouts: none -> 4.78 us  [the longest x1 3.43 us: body(): cut.transpose(1, 3, 0, 2, 4).reshape(n_seq, per_shard, PIECE_T, PIECE_F)]
  transfers between devices with their start and end apart: 7 -> 7, of which waited for: 5 -> 4; matrix products, arithmetic and copies ran while one was open for 8% -> 13% of each run, Pallas kernels for 0% -> 0%
where the time goes in v1:
time: 277 us; the launch traced here: 276 us
  waiting for transfers between devices  128 us (46%)
  blocking collectives  53.7 us (19%)
  matrix products  22.9 us (8%)
  local copies, waits for them, and re-layouts  21 us (8%)
  other arithmetic  20.3 us (7%)
  starting transfers between devices  16.4 us (6%)
  between operations  14 us (5%)
    all_gather x1, waiting for transfers between devices, body(): full_rows = lax.all_gather(rows, 'tensor', axis=2, tiled=True)  82.3 us
    reduce_scatter x1, waiting for transfers between devices, body(): lax.psum_scatter(part.astype(jnp.float32).astype(jnp.bfloat16), 'tensor',...  38.6 us
    unnamed x1, blocking collectives  34 us
    all_to_all x1, blocking collectives, body(): lax.all_to_all(outgoing, 'seq', split_axis=0, concat_axis=0, tiled=True)  19.6 us
    convert_element_type x3, other arithmetic, rms_scale(): return (values * inverse * gain.astype(jnp.float32)).astype(jnp.bfloat16)  10.3 us
    ppermute x3, starting transfers between devices, passed_along(): return lax.ppermute(x, axis, pairs)  8.58 us
    all_to_all x1, starting transfers between devices, body(): spread = lax.all_to_all(cut, 'seq', split_axis=0, concat_axis=0, tiled=True)  7.73 us
    reduce_sum x2, other arithmetic, rms_scale(): jnp.mean(values * values, axis=-1, keepdims=True) + 1e-06  7.3 us
  transfers between devices with their start and end apart: 7, of which 4 were waited for; matrix products, arithmetic and copies ran while one was open for 13% of the time, Pallas kernels for 0%

profile of v1, /device:TPU:8, one launch (start us, length us, event | category | flops | bytes accessed | tf_op | source)
XLA Modules:
  0.0 276.5 jit_solution(17500666188873148750)
XLA Ops:
  7.3 4.0 %reshape.96 = bf16[16,8,16,4,128]{4,3,2,1,0:T(4,128)(2,1)} reshape(bf16[16,128,512]{2,1,0:T(8,128)(2,1)} %param.14) | data formatting | bytes 4194304 | tf_op jit(solution)/shard_map/reshape | solution.py:54
  11.2 3.4 %copy.25 = bf16[8,4,16,16,128]{4,3,2,1,0:T(8,128)(2,1)} copy(bf16[8,4,16,16,128]{4,1,3,0,2:T(4,128)(2,1)} %bitcast.34) | data formatting | bytes 4194304 | tf_op jit(solution)/shard_map/transpose | solution.py:55
  14.7 7.7 %all-to-all-start = ((bf16[32,16,16,128]{3,2,1,0:T(8,128)(2,1)}), bf16[32,16,16,128]{3,2,1,0:T(8,128)(2,1)}, u32[]{:S(2)}, u32[]{:S(2)}) async-start(bf16[32,16,16,128]{3,2,1,0:T(8,128)(2,1)} %bitcast.33), calls=%async_computation | async-start | bytes 4194304 | tf_op jit(solution)/shard_map/all_to_all | solution.py:56
  24.1 34.0 %all-reduce = s32[256]{0:T(256)S(1)} all-reduce(s32[256]{0:T(256)S(1)} %dynamic-update-slice), channel_id=1, replica_groups=mesh['seq'=32,'tensor'=8] {'seq'}, use_global_device_ids=true, to_apply=%add | all-reduce | flops 256 | bytes 2048
  58.2 2.4 gather_fusion
  60.6 19.6 %all_to_all.10 = bf16[32,8,16,128]{3,2,1,0:T(8,128)(2,1)S(1)} all-to-all(bf16[32,8,16,128]{3,2,1,0:T(8,128)(2,1)S(1)} %bitcast.36), channel_id=1, replica_groups=mesh['seq'=32,'tensor'=8] {'seq'}, dimensions={0} | all-to-all | bytes 2097152 | tf_op jit(solution)/shard_map/all_to_all | solution.py:59
  83.6 3.0 %collective-permute-start.1 = (s32[1]{0:T(128)}, s32[1]{0:T(128)}, u32[]{:S(2)}, u32[]{:S(2)}) collective-permute-start(s32[1]{0:T(128)} %slice.15), channel_id=1, source_target_pairs={{0,8},{8,16},{16,24},{24,32},{32,40},{40,48},{48,56},{56,64},{64,7... | collective-permute-start | bytes 20 | tf_op jit(solution)/shard_map/ppermute | solution.py:15
  86.7 4.1 %collective-permute-done.1 = s32[1]{0:T(128)} collective-permute-done((s32[1]{0:T(128)}, s32[1]{0:T(128)}, u32[]{:S(2)}, u32[]{:S(2)}) %collective-permute-start.1) | collective-permute-done | bytes 36 | tf_op jit(solution)/shard_map/ppermute | solution.py:15
  91.5 2.2 fusion.4
  93.7 2.4 fusion.16
  96.3 82.3 %all-gather.3.cloned.1.call-done = bf16[8,128,4096]{2,1,0:T(8,128)(2,1)} async-done(((bf16[8,128,512]{2,1,0:T(8,128)(2,1)}), bf16[8,128,4096]{2,1,0:T(8,128)(2,1)}) %all-gather.3.cloned.1.call-update) | async-done | bytes 8388624 | tf_op jit(solution)/shard_map/all_gather | solution.py:68
  178.6 5.1 %fusion.1 = f32[8,128]{1,0:T(8,128)S(1)} fusion(bf16[8,128,4096]{2,1,0:T(8,128)(2,1)} %all-gather.3.cloned.1.call-done), kind=kLoop, calls=%fused_computation.4 | loop fusion | flops 12581888 | bytes 8392704 | tf_op jit(solution)/shard_map/reduce_sum | solution.py:20
  183.7 10.3 %fusion.3 = bf16[8,128,4096]{2,1,0:T(8,128)(2,1)} fusion(bf16[8,128,4096]{2,1,0:T(8,128)(2,1)} %all-gather.3.cloned.1.call-done, f32[4096]{0:T(1024)S(1)} %convert_element_type.52, f32[8,128]{1,0:T(8,128)S(1)} %add_rsqrt_fusion), kind=kLoop, calls=%fused_computation.6 | loop fusion | flops 16777216 | bytes 16797696 | tf_op jit(solution)/shard_map/convert_element_type | solution.py:21
  194.0 6.3 %convolution_convert_fusion.1 = bf16[1024,256]{0,1:T(8,128)(2,1)S(1)} fusion(bf16[1024,4096]{1,0:T(8,128)(2,1)} %bitcast.31, bf16[4096,256]{1,0:T(8,128)(2,1)} %param.19), kind=kOutput, calls=%fused_computation.17 | convolution fusion | flops 2147745792 | bytes 11010048 | tf_op jit(solution)/shard_map/dot_general | solution.py:70
  201.1 2.1 collective-permute-start.2
  203.3 7.2 %convolution_convert_fusion.2 = bf16[1024,256]{0,1:T(8,128)(2,1)} fusion(bf16[1024,4096]{1,0:T(8,128)(2,1)} %bitcast.32, bf16[4096,256]{1,0:T(8,128)(2,1)} %param.20), kind=kOutput, calls=%fused_computation.18 | convolution fusion | flops 2147745792 | bytes 11010048 | tf_op jit(solution)/shard_map/dot_general | solution.py:71
  210.8 2.2 reshape.104
  213.4 2.1 copy.29
  216.3 3.5 %collective-permute-start = (bf16[256,2,128]{2,0,1:T(8,128)(2,1)}, bf16[256,2,128]{2,0,1:T(8,128)(2,1)}, u32[]{:S(2)}, u32[]{:S(2)}) collective-permute-start(bf16[256,2,128]{2,0,1:T(8,128)(2,1)} %copy.28), channel_id=1, source_target_pairs={{0,8},{8,16},{16,24},{24,32},{32,40},{40,48},{48,56},{56,64},{64,7... | collective-permute-start | bytes 393224 | tf_op jit(solution)/shard_map/ppermute | solution.py:15
  222.5 2.5 collective-permute-done
  225.0 2.2 fusion.19
  227.5 2.1 convolution_convert_fusion
  229.6 38.6 %reduce-scatter.2.cloned.1.call-done = bf16[256,512]{1,0:T(8,128)(2,1)} async-done(((bf16[256,4096]{1,0:T(8,128)(2,1)}), bf16[256,512]{1,0:T(8,128)(2,1)}) %reduce-scatter.2.cloned.1.call-update) | async-done | bytes 262160 | tf_op jit(solution)/shard_map/reduce_scatter | solution.py:89
  268.2 1.7 add_convert_fusion
  (61 shorter events, 11.3 us)
Async XLA Ops:
  6.5 221.0 %copy-start = (bf16[256,4096]{1,0:T(8,128)(2,1)S(1)}, bf16[256,4096]{1,0:T(8,128)(2,1)}, u32[]{:S(2)}) copy-start(bf16[256,4096]{1,0:T(8,128)(2,1)} %param.21) | copy-start | bytes 6291460
  6.5 84.9 %all-gather.5.cloned.1.call-start = ((), (), s32[]{:S(2)}) async-start(), calls=%async_computation.4 | async-start | bytes 2359296 | tf_op jit(solution)/shard_map/all_gather | solution.py:62
  14.6 7.8 %copy-start.5 = (s32[4,2]{0,1:T(2,128)S(1)}, s32[4,2]{0,1:T(2,128)}, u32[]{:S(2)}) copy-start(s32[4,2]{0,1:T(2,128)} %param.16) | copy-start | bytes 100
  14.6 7.8 %copy-start.6 = (s32[4,2]{0,1:T(2,128)S(1)}, s32[4,2]{0,1:T(2,128)}, u32[]{:S(2)}) copy-start(s32[4,2]{0,1:T(2,128)} %param.15) | copy-start | bytes 100
  14.7 8.0 %copy-start.8 = (u32[256]{0:T(256)S(1)}, u32[256]{0:T(256)}, u32[]{:S(2)}) copy-start(u32[256]{0:T(256)} %constant.48) | copy-start | bytes 3076
  14.7 43.5 %all-to-all-start = ((bf16[32,16,16,128]{3,2,1,0:T(8,128)(2,1)}), bf16[32,16,16,128]{3,2,1,0:T(8,128)(2,1)}, u32[]{:S(2)}, u32[]{:S(2)}) async-start(bf16[32,16,16,128]{3,2,1,0:T(8,128)(2,1)} %bitcast.33), calls=%async_computation | async-start | bytes 4194304 | tf_op jit(solution)/shard_map/all_to_all | solution.py:56
  22.4 156.2 %all-gather.3.cloned.1.call-start = ((), (), s32[]{:S(2)}) async-start(), calls=%async_computation.3 | async-start | bytes 9437184 | tf_op jit(solution)/shard_map/all_gather | solution.py:68
  81.6 1.3 copy-start.7
  81.6 4.9 %copy-start.3 = (bf16[4096]{0:T(1024)(128)(2,1)S(1)}, bf16[4096]{0:T(1024)(128)(2,1)}, u32[]{:S(2)}) copy-start(bf16[4096]{0:T(1024)(128)(2,1)} %param.13) | copy-start | bytes 24580
  81.6 4.9 %copy-start.4 = (bf16[4096]{0:T(1024)(128)(2,1)S(1)}, bf16[4096]{0:T(1024)(128)(2,1)}, u32[]{:S(2)}) copy-start(bf16[4096]{0:T(1024)(128)(2,1)} %param.12) | copy-start | bytes 24580
  82.9 185.3 %reduce-scatter.2.cloned.1.call-start = ((), (), s32[]{:S(2)}) async-start(), calls=%async_computation.5 | async-start | bytes 2359296 | tf_op jit(solution)/shard_map/reduce_scatter | solution.py:89
  83.6 7.2 %collective-permute-start.1 = (s32[1]{0:T(128)}, s32[1]{0:T(128)}, u32[]{:S(2)}, u32[]{:S(2)}) collective-permute-start(s32[1]{0:T(128)} %slice.15), channel_id=1, source_target_pairs={{0,8},{8,16},{16,24},{24,32},{32,40},{40,48},{48,56},{56,64},{64,7... | collective-permute-start | bytes 20 | tf_op jit(solution)/shard_map/ppermute | solution.py:15
  91.4 2.2 copy-start.1
  201.1 18.7 %collective-permute-start.2 = (bf16[256,2,128]{2,0,1:T(8,128)(2,1)}, bf16[256,2,128]{2,0,1:T(8,128)(2,1)}, u32[]{:S(2)}, u32[]{:S(2)}) collective-permute-start(bf16[256,2,128]{2,0,1:T(8,128)(2,1)} %copy.30), channel_id=1, source_target_pairs={{0,8},{8,16},{16,24},{24,32},{32,40},{40,48},{48,56},{56,64},{64,7... | collective-permute-start | bytes 393224 | tf_op jit(solution)/shard_map/ppermute | solution.py:15
  210.4 5.1 %slice-start = ((bf16[1024,256]{0,1:T(8,128)(2,1)}), bf16[256,256]{0,1:T(8,128)(2,1)S(1)}, s32[]{:S(2)}) async-start(bf16[1024,256]{0,1:T(8,128)(2,1)} %convolution_convert_fusion.2), calls=%async_computation.6 | async-start | bytes 262144 | tf_op jit(solution)/shard_map/slice | solution.py:80
  216.3 8.7 %collective-permute-start = (bf16[256,2,128]{2,0,1:T(8,128)(2,1)}, bf16[256,2,128]{2,0,1:T(8,128)(2,1)}, u32[]{:S(2)}, u32[]{:S(2)}) collective-permute-start(bf16[256,2,128]{2,0,1:T(8,128)(2,1)} %copy.28), channel_id=1, source_target_pairs={{0,8},{8,16},{16,24},{24,32},{32,40},{40,48},{48,56},{56,64},{64,7... | collective-permute-start | bytes 393224 | tf_op jit(solution)/shard_map/ppermute | solution.py:15
  229.6 38.7 %copy-start.2 = (bf16[256,512]{1,0:T(8,128)(2,1)S(1)}, bf16[256,512]{1,0:T(8,128)(2,1)}, u32[]{:S(2)}) copy-start(bf16[256,512]{1,0:T(8,128)(2,1)} %param.11) | copy-start | bytes 786436
Sparse Core Ops, SparseCore 0:
  9.2 44.4 all-gather.4
  83.0 95.5 all-gather.2
  229.7 38.4 reduce-scatter.1

commit v2 on v1

v2 whole, which is shorter than its diff:
```python
import functools

import jax
import jax.numpy as jnp
from jax import lax
from jax.experimental import pallas as pl
from jax.experimental.pallas import tpu as pltpu
from jax.sharding import PartitionSpec as P

HS = 128
NB = 2
PIECE_T = 16
PIECE_F = 128
VMEM_LIMIT = 48 * 1024 * 1024


def rms_scale(rows, gain):
    values = rows.astype(jnp.float32)
    inverse = lax.rsqrt(jnp.mean(values * values, axis=-1, keepdims=True) + 1e-06)
    return (values * inverse * gain.astype(jnp.float32)).astype(jnp.bfloat16)


def cut_kernel(db_ref, note_ref, out_ref, sems):
    shard = db_ref.shape[0]
    pieces_t = db_ref.shape[1] // PIECE_T
    pieces_f = db_ref.shape[2] // PIECE_F
    copies = []
    for f in range(pieces_f):
        for i in range(pieces_t):
            piece = f * pieces_t + i
            source = db_ref.at[:, pl.ds(i * PIECE_T, PIECE_T), pl.ds(f * PIECE_F, PIECE_F)]
            copies.append(
                pltpu.make_async_copy(
                    source, out_ref.at[piece, pl.ds(0, shard)], sems.at[0, piece]
                )
            )
            copies.append(
                pltpu.make_async_copy(note_ref, out_ref.at[piece, shard], sems.at[1, piece])
            )
    for copy in copies:
        copy.start()
    for copy in copies:
        copy.wait()


def cut(database, note):
    shard, length, part = database.shape
    pieces = (length // PIECE_T) * (part // PIECE_F)
    return pl.pallas_call(
        cut_kernel,
        in_specs=[pl.BlockSpec(memory_space=pl.ANY)] * 2,
        out_specs=pl.BlockSpec(memory_space=pl.ANY),
        out_shape=jax.ShapeDtypeStruct((pieces, shard + 1, PIECE_T, PIECE_F), database.dtype),
        scratch_shapes=[pltpu.SemaphoreType.DMA((2, pieces))],
        name="cut",
    )(database, note)


def pick_kernel(index_ref, spread_ref, low_ref, high_ref):
    n_seq, half = low_ref.shape[:2]

    def one(dest, carry):
        for j in range(half):
            low_ref[dest, j] = spread_ref[index_ref[dest, j]]
            high_ref[dest, j] = spread_ref[index_ref[dest, half + j]]
        return carry

    lax.fori_loop(0, n_seq, one, 0, unroll=2)


def pick(index, spread):
    n_seq, items = index.shape
    half = jax.ShapeDtypeStruct((n_seq, items // 2, PIECE_T, PIECE_F), spread.dtype)
    return pl.pallas_call(
        pick_kernel,
        in_specs=[
            pl.BlockSpec(memory_space=pltpu.SMEM),
            pl.BlockSpec(memory_space=pltpu.VMEM),
        ],
        out_specs=[pl.BlockSpec(memory_space=pltpu.VMEM)] * 2,
        out_shape=[half, half],
        name="pick",
    )(index, spread)


def add_block(x_ref, w_ref, start, acc, squares):
    features, pieces_t, items = x_ref.shape[:3]
    rows = pieces_t * items * PIECE_T
    pieces = [x_ref[f].reshape(rows, PIECE_F) for f in range(features)]
    for piece in pieces:
        wide = piece.astype(jnp.float32)
        squares = squares + wide * wide
    x = jnp.concatenate(pieces, axis=1)
    w = w_ref[0, start * PIECE_F : (start + features) * PIECE_F, :]
    return acc + jnp.dot(x, w, preferred_element_type=jnp.float32), squares


def gather_kernel(starts, last, where_ref, wr_ref, wl_ref, *rest):
    count = len(starts)
    x_refs = rest[:count]
    rest = rest[count:]
    if last:
        acc_ref, squares_ref, first_ref, second_ref = rest
        acc, squares = acc_ref[...], squares_ref[...]
    elif len(rest) == 4:
        acc_in_ref, squares_in_ref, acc_ref, squares_ref = rest
        acc, squares = acc_in_ref[...], squares_in_ref[...]
    else:
        acc_ref, squares_ref = rest
        acc = jnp.zeros(acc_ref.shape, jnp.float32)
        squares = jnp.zeros(squares_ref.shape, jnp.float32)
    for ref, (side, start) in zip(x_refs, starts):
        acc, squares = add_block(ref, (wr_ref, wl_ref)[side], start, acc, squares)
    if not last:
        acc_ref[...] = acc
        squares_ref[...] = squares
        return
    mean = jnp.sum(squares, axis=1, keepdims=True) * (1.0 / last)
    done = (acc * lax.rsqrt(mean + 1e-06)).astype(jnp.bfloat16)
    pieces_t, half_items = first_ref.shape[:2]
    done = done.reshape(pieces_t, 2 * half_items, PIECE_T, done.shape[-1])
    first_ref[...] = done[:, :half_items]
    second_ref[...] = done[:, half_items:]


def gather_step(blocks, starts, where, weights, state, last):
    n_ten, part, cols = weights.shape
    _, pieces_t, items = blocks[0].shape[:3]
    rows = pieces_t * items * PIECE_T
    vmem = pl.BlockSpec(memory_space=pltpu.VMEM)
    state = list(state)
    if last:
        span = jax.ShapeDtypeStruct((pieces_t, items // 2, PIECE_T, cols), jnp.bfloat16)
        out_shape = [span, span]
    else:
        out_shape = [
            jax.ShapeDtypeStruct((rows, cols), jnp.float32),
            jax.ShapeDtypeStruct((rows, PIECE_F), jnp.float32),
        ]
    return pl.pallas_call(
        functools.partial(gather_kernel, tuple(starts), n_ten * part if last else 0),
        grid_spec=pltpu.PrefetchScalarGridSpec(
            num_scalar_prefetch=1,
            grid=(1,),
            in_specs=[
                pl.BlockSpec((1, part, cols), lambda g, at: (at[0], 0, 0)),
                pl.BlockSpec((1, part, cols), lambda g, at: (at[1], 0, 0)),
            ]
            + [vmem] * (len(blocks) + len(state)),
            out_specs=[vmem] * 2,
        ),
        out_shape=out_shape,
        compiler_params=pltpu.CompilerParams(vmem_limit_bytes=VMEM_LIMIT),
        cost_estimate=pl.CostEstimate(
            flops=2 * rows * cols * PIECE_F * sum(b.shape[0] for b in blocks),
            bytes_accessed=2 * sum(b.size for b in blocks) + 4 * part * cols + 8 * rows * cols,
            transcendentals=0,
        ),
        name="gather_last" if last else "gather_step",
    )(where, weights, weights, *blocks, *state)


def ring_project(pair, weights, me, n_ten, between=None):
    right = [(i, (i + 1) % n_ten) for i in range(n_ten)]
    left = [(i, (i - 1) % n_ten) for i in range(n_ten)]
    width = pair[0].shape[0]
    go_right, go_left = list(pair), list(pair)
    here = jnp.stack([me, me]).astype(jnp.int32)
    state = gather_step(pair, [(0, 0), (0, width)], here, weights, (), False)
    last_step = n_ten // 2
    marks = None
    for step in range(1, last_step + 1):
        where = jnp.stack([(me + n_ten - step) % n_ten, (me + step) % n_ten]).astype(jnp.int32)
        last = step == last_step
        if last:
            half = width // 2
            go_right = [x[:half] for x in go_right]
            go_left = [x[half:] for x in go_left]
        if step == last_step - 1 and between is not None:
            *held, between = lax.optimization_barrier((*go_right, *go_left, between))
            go_right, go_left = held[:2], held[2:]
        for s in range(2):
            go_right[s] = lax.ppermute(go_right[s], "tensor", right)
            go_left[s] = lax.ppermute(go_left[s], "tensor", left)
        blocks, starts = [], []
        for s in range(2):
            blocks += [go_right[s], go_left[s]]
            starts += [(0, s * width), (1, s * width + (width // 2 if last else 0))]
        state = gather_step(blocks, starts, where, weights, state, last)
        if step == last_step - 1:
            marks = state
    return state, marks, between


def finish_kernel(shift, low_ref, high_ref, tokens_ref, out_ref):
    groups = low_ref.shape[0]
    sums = []
    for ref in (low_ref, high_ref):
        total = ref[0].astype(jnp.float32)
        for g in range(1, groups):
            total = total + ref[g].astype(jnp.float32)
        sums.append(total)
    total = pltpu.roll(jnp.concatenate(sums, axis=0), shift, 0)
    out_ref[...] = (tokens_ref[...].astype(jnp.float32) + total).astype(jnp.bfloat16)


def finish(low, high, tokens, shift):
    return pl.pallas_call(
        functools.partial(finish_kernel, shift),
        in_specs=[pl.BlockSpec(memory_space=pltpu.VMEM)] * 3,
        out_specs=pl.BlockSpec(memory_space=pltpu.VMEM),
        out_shape=jax.ShapeDtypeStruct(tokens.shape, jnp.bfloat16),
        compiler_params=pltpu.CompilerParams(vmem_limit_bytes=VMEM_LIMIT),
        name="finish",
    )(low, high, tokens)


def weigh(scores, count, keys_axis_owner):
    scores = jnp.where(keys_axis_owner < count, scores, jnp.float32(-1e30))
    top = jnp.max(scores, axis=-1, keepdims=True)
    expo = jnp.exp(scores - top)
    return expo / jnp.sum(expo, axis=-1, keepdims=True)


def scores_of(queries, keys):
    return lax.dot_general(
        queries, keys, (((1,), (1,)), ((), ())), preferred_element_type=jnp.float32
    )


def attend_kernel(with_prev, span_len, count_ref, q_ref, first_ref, second_ref, *rest):
    if with_prev:
        prev_ref, wo_ref, out_ref = rest
    else:
        wo_ref, out_ref = rest
    cols = q_ref.shape[1]
    heads = cols // HS
    keys = first_ref.shape[0] * first_ref.shape[1] * first_ref.shape[2]
    owner = (lax.broadcasted_iota(jnp.int32, (span_len, keys), 1) // PIECE_T) % NB
    row = lax.broadcasted_iota(jnp.int32, (span_len, keys), 0)
    blocks = []
    for span in range(2):
        pair_ref = (first_ref, second_ref)[span]
        pair = pair_ref[...].reshape(keys, 2 * cols)
        queries = q_ref[span * span_len : (span + 1) * span_len, :]
        mixed_heads = []
        for head in range(heads):
            at = slice(head * HS, (head + 1) * HS)
            value_at = slice(cols + head * HS, cols + (head + 1) * HS)
            query = queries[:, at]
            scores = scores_of(query, pair[:, at])
            if with_prev and span == 1:
                prev = prev_ref[...].reshape(keys, 2 * cols)
                own = row == 0
                scores = jnp.where(own, scores, scores_of(query, prev[:, at]))
                count = jnp.where(own, count_ref[1], count_ref[2])
                weights = weigh(scores, count, owner)
                ours = jnp.where(own, weights, 0.0).astype(jnp.bfloat16)
                theirs = jnp.where(own, 0.0, weights).astype(jnp.bfloat16)
                result = jnp.dot(
                    ours, pair[:, value_at], preferred_element_type=jnp.float32
                ) + jnp.dot(theirs, prev[:, value_at], preferred_element_type=jnp.float32)
            else:
                weights = weigh(scores, count_ref[span], owner).astype(jnp.bfloat16)
                result = jnp.dot(
                    weights, pair[:, value_at], preferred_element_type=jnp.float32
                )
            mixed_heads.append(result.astype(jnp.bfloat16))
        blocks.append(jnp.concatenate(mixed_heads, axis=1))
    attended = jnp.concatenate(blocks, axis=0)
    groups, _, width = out_ref.shape
    for g in range(groups):
        out_ref[g] = jnp.dot(
            attended, wo_ref[:, g * width : (g + 1) * width], preferred_element_type=jnp.float32
        ).astype(jnp.bfloat16)


def attend(counts, queries, first, second, prev, wo, groups):
    rows = queries.shape[0]
    span_len = rows // 2
    width = wo.shape[1] // groups
    with_prev = prev is not None
    operands = [counts, queries, first, second] + ([prev] if with_prev else []) + [wo]
    vmem = pl.BlockSpec(memory_space=pltpu.VMEM)
    return pl.pallas_call(
        functools.partial(attend_kernel, with_prev, span_len),
        in_specs=[pl.BlockSpec(memory_space=pltpu.SMEM)] + [vmem] * (len(operands) - 1),
        out_specs=vmem,
        out_shape=jax.ShapeDtypeStruct((groups, rows, width), jnp.bfloat16),
        compiler_params=pltpu.CompilerParams(vmem_limit_bytes=VMEM_LIMIT),
        cost_estimate=pl.CostEstimate(
            flops=2 * rows * wo.shape[0] * wo.shape[1] + 8 * rows * 256 * wo.shape[0],
            bytes_accessed=2 * (wo.size + rows * wo.shape[1] + 2 * first.size),
            transcendentals=0,
        ),
        name="attend_prev" if with_prev else "attend",
    )(*operands)


def body(tokens, x_gain, nbr_gain, database, nbr_shard, nbr_row, nbr_count, wq, wk, wv, wo):
    n_seq = lax.axis_size("seq")
    n_ten = lax.axis_size("tensor")
    tok_dev = tokens.shape[0]
    span_dev = nbr_shard.shape[0]
    span_len = tok_dev // span_dev
    shift = span_len - 1
    per_shard, nbr_len, d_part = database.shape
    items = span_dev * NB
    half = items // 2
    pieces_t = nbr_len // PIECE_T
    pieces_f = d_part // PIECE_F
    seq_at = lax.axis_index("seq")
    me = lax.axis_index("tensor")

    note = jnp.concatenate([nbr_shard.reshape(-1), nbr_row.reshape(-1), nbr_count])
    n_notes = note.shape[0]
    note = jnp.pad(note.astype(jnp.bfloat16)[None], ((0, PIECE_T - 1), (0, PIECE_F - n_notes)))
    spread = lax.all_to_all(cut(database, note), "seq", split_axis=0, concat_axis=0, tiled=True)
    notes = spread[:, per_shard, 0, :n_notes].astype(jnp.int32)
    index = notes[:, :items] * (per_shard + 1) + notes[:, items : 2 * items]
    prev_count = jnp.where(seq_at > 0, notes[jnp.maximum(seq_at - 1, 0), n_notes - 1], 0)
    low, high = pick(index, spread.reshape(n_seq * (per_shard + 1), PIECE_T, PIECE_F))
    whole = lax.all_gather(tokens, "tensor", axis=1, tiled=True)
    low, high, whole = lax.optimization_barrier((low, high, whole))
    high = lax.all_to_all(high, "seq", split_axis=0, concat_axis=0, tiled=True)
    low = lax.all_to_all(low, "seq", split_axis=0, concat_axis=0, tiled=True)

    both = jnp.concatenate([wk, wv], axis=1).astype(jnp.float32)
    both = (both * nbr_gain.astype(jnp.float32)[:, None]).astype(jnp.bfloat16)
    both = both.reshape(n_ten, d_part, both.shape[1])
    normed = rms_scale(whole, x_gain)
    queries = (jnp.dot(normed, wq, preferred_element_type=jnp.float32) * HS ** (-0.5)).astype(
        jnp.bfloat16
    )
    queries = jnp.concatenate([queries[shift:], queries[:shift]], axis=0)
    split = tok_dev // 2
    spans = span_dev // 2

    def streams(part):
        part = part.reshape(pieces_f, pieces_t, half, PIECE_T, PIECE_F)
        return [part[: pieces_f // 2], part[pieces_f // 2 :]]

    (third, fourth), marks, _ = ring_project(streams(high), both, me, n_ten)
    low_streams, _ = lax.optimization_barrier((streams(low), marks))
    prev = lax.ppermute(fourth, "seq", [(i, i + 1) for i in range(n_seq - 1)])
    high_counts = jnp.concatenate([nbr_count[spans:], prev_count[None]])
    high_part = attend(high_counts, queries[split:], third, fourth, prev, wo, n_ten)

    (first, second), _, high_part = ring_project(low_streams, both, me, n_ten, high_part)
    high_got = lax.all_to_all(high_part, "tensor", split_axis=0, concat_axis=0, tiled=True)
    low_part = attend(nbr_count[:spans], queries[:split], first, second, None, wo, n_ten)
    low_got = lax.all_to_all(low_part, "tensor", split_axis=0, concat_axis=0, tiled=True)
    return finish(low_got, high_got, tokens, shift)


def solution(mesh):
    placed = (
        P("seq", "tensor"),
        P(),
        P(),
        P("seq", None, "tensor"),
        P("seq", None),
        P("seq", None),
        P("seq"),
        P(None, "tensor"),
        P(None, "tensor"),
        P(None, "tensor"),
        P("tensor", None),
    )
    return jax.shard_map(
        body, mesh=mesh, in_specs=placed, out_specs=P("seq", "tensor"), check_vma=False
    )
```

time: 277 us -> 350 us (1.26); the launches traced: 276 us -> 344 us
  Pallas kernels: 0 us -> 100 us
  starting transfers between devices: 16.4 us -> 89.8 us
  waiting for transfers between devices: 128 us -> 76.4 us
  blocking collectives: 53.7 us -> 31.5 us
  matrix products: 22.9 us -> 0.76 us
  other arithmetic: 20.3 us -> 8.4 us
    pallas_call x0 -> x15, Pallas kernels: none -> 100 us  [the longest x1 69.2 us: cut(): pl.pallas_call(cut_kernel, in_specs=[pl.BlockSpec(memory_space=pl.ANY)] *...]
    all_gather x1 -> x0, waiting for transfers between devices: 82.3 us -> none  [body(): full_rows = lax.all_gather(rows, 'tensor', axis=2, tiled=True)]
    ppermute x3 -> x33, starting transfers between devices: 8.58 us -> 64.9 us  [the longest x16 51.6 us: ring_project(): go_left[s] = lax.ppermute(go_left[s], 'tensor', left)]
    reduce_scatter x1 -> x0, waiting for transfers between devices: 38.6 us -> none  [body(): lax.psum_scatter(part.astype(jnp.float32).astype(jnp.bfloat16), 'tensor',...]
    ppermute x3 -> x33, waiting for transfers between devices: 6.59 us -> 41.8 us  [the longest x16 34.1 us: ring_project(): go_right[s] = lax.ppermute(go_right[s], 'tensor', right)]
    unnamed x1 -> x0, blocking collectives: 34 us -> none
    all_to_all x1 -> x4, waiting for transfers between devices: 0.01 us -> 33.9 us  [the longest x1 28.2 us: body(): lax.all_to_all(cut(database, note), 'seq', split_axis=0, concat_axis=0, t...]
    dot_general x5 -> x0, matrix products: 19.1 us -> none  [the longest x1 7.15 us: body(): jnp.dot(encoded, wv, preferred_element_type=jnp.float32)]
  transfers between devices with their start and end apart: 7 -> 38, of which waited for: 4 -> 11; matrix products, arithmetic and copies ran while one was open for 13% -> 5% of each run, Pallas kernels for 0% -> 29%
where the time goes in v2:
time: 350 us; the launch traced here: 344 us
  Pallas kernels  100 us (29%)
  starting transfers between devices  89.8 us (26%)
  waiting for transfers between devices  76.4 us (22%)
  blocking collectives  31.5 us (9%)
  local copies, waits for them, and re-layouts  21.4 us (6%)
  between operations  15.2 us (4%)
  other arithmetic  8.4 us (2%)
    pallas_call x1, Pallas kernels, cut(): pl.pallas_call(cut_kernel, in_specs=[pl.BlockSpec(memory_space=pl.ANY)] *...  69.2 us
    ppermute x16, starting transfers between devices, ring_project(): go_left[s] = lax.ppermute(go_left[s], 'tensor', left)  51.6 us
    ppermute x16, waiting for transfers between devices, ring_project(): go_right[s] = lax.ppermute(go_right[s], 'tensor', right)  34.1 us
    all_to_all x1, blocking collectives, body(): lax.all_to_all(low_part, 'tensor', split_axis=0, concat_axis=0, tiled=True)  31.5 us
    all_to_all x1, waiting for transfers between devices, body(): lax.all_to_all(cut(database, note), 'seq', split_axis=0, concat_axis=0, t...  28.2 us
    pallas_call x10, Pallas kernels, gather_step(): pl.pallas_call(functools.partial(gather_kernel, tuple(starts), n_ten * pa...  22.4 us
    unnamed x78, local copies, waits for them, and re-layouts  13.6 us
    ppermute x16, starting transfers between devices, ring_project(): go_right[s] = lax.ppermute(go_right[s], 'tensor', right)  11.3 us
  transfers between devices with their start and end apart: 38, of which 11 were waited for; matrix products, arithmetic and copies ran while one was open for 5% of the time, Pallas kernels for 29%

profile of v2, /device:TPU:8, one launch (start us, length us, event | category | flops | bytes accessed | tf_op | source)
XLA Modules:
  0.0 343.7 jit_solution(1508329478431164891)
XLA Ops:
  10.4 69.2 %cut.1 = bf16[32,17,16,128]{3,2,1,0:T(8,128)(2,1)} custom-call(bf16[16,128,512]{2,1,0:T(8,128)(2,1)} %db_ref.1, bf16[16,128]{1,0:T(8,128)(2,1)} %fusion.21.note_ref), custom_call_target="tpu_custom_call" | custom-call | tf_op jit(solution)/shard_map/cut/pallas_call | solution.py:49
  79.5 7.6 %all-to-all-start = ((bf16[32,17,16,128]{3,2,1,0:T(8,128)(2,1)}), bf16[32,17,16,128]{3,2,1,0:T(8,128)(2,1)}, u32[]{:S(2)}, u32[]{:S(2)}) async-start(bf16[32,17,16,128]{3,2,1,0:T(8,128)(2,1)} %cut.1), calls=%async_computation | async-start | bytes 4456448 | tf_op jit(solution)/shard_map/all_to_all | solution.py:318
  87.2 28.2 %all-to-all-done = bf16[32,17,16,128]{3,2,1,0:T(8,128)(2,1)} async-done(((bf16[32,17,16,128]{3,2,1,0:T(8,128)(2,1)}), bf16[32,17,16,128]{3,2,1,0:T(8,128)(2,1)}, u32[]{:S(2)}, u32[]{:S(2)}) %all-to-all-start) | async-done | bytes 2228256 | tf_op jit(solution)/shard_map/all_to_all | solution.py:318
  120.0 7.1 %all-to-all-start.2 = ((bf16[32,4,16,128]{3,2,1,0:T(8,128)(2,1)}), bf16[32,4,16,128]{3,2,1,0:T(8,128)(2,1)S(1)}, u32[]{:S(2)}, u32[]{:S(2)}) async-start(bf16[32,4,16,128]{3,2,1,0:T(8,128)(2,1)} %get-tuple-element.41), calls=%async_computation.2 | async-start | bytes 1048576 | tf_op jit(solution)/shard_map/all_to_all | solution.py:325
  127.2 4.0 %multiply_convert_fusion.wr_ref.wl_ref = bf16[8,512,512]{2,1,0:T(8,128)(2,1)} fusion(bf16[8,512,256]{2,1,0:T(8,128)(2,1)} %bitcast.34, bf16[8,512,256]{2,1,0:T(8,128)(2,1)} %bitcast.35, f32[8,512]{1,0:T(8,128)S(1)} %reshape.81), kind=kLoop, calls=%fused_computation | loop fusion | flops 12582912 | bytes 8404992 | tf_op jit(solution)/shard_map/convert_element_type | solution.py:329
  131.3 5.6 %all-to-all-done.2 = bf16[32,4,16,128]{3,2,1,0:T(8,128)(2,1)S(1)} async-done(((bf16[32,4,16,128]{3,2,1,0:T(8,128)(2,1)}), bf16[32,4,16,128]{3,2,1,0:T(8,128)(2,1)S(1)}, u32[]{:S(2)}, u32[]{:S(2)}) %all-to-all-start.2) | async-done | bytes 524320 | tf_op jit(solution)/shard_map/all_to_all | solution.py:325
  137.0 5.9 %collective-permute-start.3 = (bf16[2,8,4,16,128]{4,3,2,1,0:T(8,128)(2,1)S(1)}, bf16[2,8,4,16,128]{4,3,2,1,0:T(8,128)(2,1)S(1)}, u32[]{:S(2)}, u32[]{:S(2)}) collective-permute-start(bf16[2,8,4,16,128]{4,3,2,1,0:T(8,128)(2,1)S(1)} %bitcast.25), channel_id=1, source_target_pairs={{0,7},{1,0},{2,1},{3,2},{4,3},{5,4},{6,5},{7,6},{8,15},{9,8},{10,9... | collective-permute-start | bytes 786440 | tf_op jit(solution)/shard_map/ppermute | solution.py:184
  142.9 3.2 collective-permute-start.9
  146.2 6.5 %all-to-all-start.1 = ((bf16[32,4,16,128]{3,2,1,0:T(8,128)(2,1)}), bf16[32,4,16,128]{3,2,1,0:T(8,128)(2,1)}, u32[]{:S(2)}, u32[]{:S(2)}) async-start(bf16[32,4,16,128]{3,2,1,0:T(8,128)(2,1)} %get-tuple-element.40), calls=%async_computation.1 | async-start | bytes 1048576 | tf_op jit(solution)/shard_map/all_to_all | solution.py:326
  152.9 3.3 collective-permute-start.4
  156.2 3.2 collective-permute-start.10
  162.8 3.8 %collective-permute-start.5 = (bf16[2,8,4,16,128]{4,3,2,1,0:T(8,128)(2,1)}, bf16[2,8,4,16,128]{4,3,2,1,0:T(8,128)(2,1)}, u32[]{:S(2)}, u32[]{:S(2)}) collective-permute-start(bf16[2,8,4,16,128]{4,3,2,1,0:T(8,128)(2,1)} %collective-permute-done.4.rest_1_), channel_id=1, source_target_pairs={{0,7},{1,0},{2,1},{3,2},{4,3},{5,4},{6,5},{7,6},{8,15},{9,8},{10,9... | collective-permute-start | bytes 786440 | tf_op jit(solution)/shard_map/ppermute | solution.py:184
  171.6 3.2 collective-permute-start.11
  174.9 8.4 %collective-permute-start.8 = (bf16[2,8,4,16,128]{4,3,2,1,0:T(8,128)(2,1)}, bf16[2,8,4,16,128]{4,3,2,1,0:T(8,128)(2,1)}, u32[]{:S(2)}, u32[]{:S(2)}) collective-permute-start(bf16[2,8,4,16,128]{4,3,2,1,0:T(8,128)(2,1)} %collective-permute-done.7.rest_2_), channel_id=1, source_target_pairs={{0,1},{1,2},{2,3},{3,4},{4,5},{5,6},{6,7},{7,0},{8,9},{9,10},{10,1... | collective-permute-start | bytes 786440 | tf_op jit(solution)/shard_map/ppermute | solution.py:183
  185.4 3.3 collective-permute-start.21
  201.6 3.3 collective-permute-start.16
  204.9 3.2 collective-permute-start.18
  215.9 6.6 %collective-permute-done.22.rest_2_ = bf16[1,8,4,16,128]{4,3,2,1,0:T(8,128)(2,1)S(1)} collective-permute-done((bf16[1,8,4,16,128]{4,3,2,1,0:T(8,128)(2,1)S(1)}, bf16[1,8,4,16,128]{4,3,2,1,0:T(8,128)(2,1)S(1)}, u32[]{:S(2)}, u32[]{:S(2)}) %collective-permute-start.22) | collective-permute-done | bytes 131104 | tf_op jit(solution)/shard_map/ppermute | solution.py:183
  229.2 3.2 collective-permute-start.19
  245.0 3.6 %all-to-all-start.4 = ((bf16[8,128,512]{2,1,0:T(8,128)(2,1)}), bf16[8,128,512]{2,1,0:T(8,128)(2,1)S(1)}, u32[]{:S(2)}, u32[]{:S(2)}) async-start(bf16[8,128,512]{2,1,0:T(8,128)(2,1)} %copy-done.5), calls=%async_computation.4 | async-start | bytes 2097152 | tf_op jit(solution)/shard_map/all_to_all | solution.py:350
  260.1 21.4 %collective-permute-done.25.rest_0_ = bf16[2,8,4,16,128]{4,3,2,1,0:T(8,128)(2,1)S(1)} collective-permute-done((bf16[2,8,4,16,128]{4,3,2,1,0:T(8,128)(2,1)}, bf16[2,8,4,16,128]{4,3,2,1,0:T(8,128)(2,1)S(1)}, u32[]{:S(2)}, u32[]{:S(2)}) %collective-permute-start.25) | collective-permute-done | bytes 262176 | tf_op jit(solution)/shard_map/ppermute | solution.py:183
  281.6 3.3 collective-permute-start.28
  287.2 3.3 collective-permute-start.32
  303.9 31.5 %all_to_all.25.low_ref = bf16[8,128,512]{2,1,0:T(8,128)(2,1)S(1)} all-to-all(bf16[8,128,512]{2,1,0:T(8,128)(2,1)} %copy-done.6), channel_id=1, replica_groups=mesh['seq'=32,'tensor'=8] {'tensor'}, dimensions={0} | all-to-all | bytes 2097152 | tf_op jit(solution)/shard_map/all_to_all | solution.py:352
  (186 shorter events, 86.4 us)
Async XLA Ops:
  6.5 113.5 %all-gather.2.cloned.1.call-start = ((), (), s32[]{:S(2)}) async-start(), calls=%async_computation.5 | async-start | bytes 2359296 | tf_op jit(solution)/shard_map/all_gather | solution.py:323
  79.5 35.9 %all-to-all-start = ((bf16[32,17,16,128]{3,2,1,0:T(8,128)(2,1)}), bf16[32,17,16,128]{3,2,1,0:T(8,128)(2,1)}, u32[]{:S(2)}, u32[]{:S(2)}) async-start(bf16[32,17,16,128]{3,2,1,0:T(8,128)(2,1)} %cut.1), calls=%async_computation | async-start | bytes 4456448 | tf_op jit(solution)/shard_map/all_to_all | solution.py:318
  120.0 16.9 %all-to-all-start.2 = ((bf16[32,4,16,128]{3,2,1,0:T(8,128)(2,1)}), bf16[32,4,16,128]{3,2,1,0:T(8,128)(2,1)S(1)}, u32[]{:S(2)}, u32[]{:S(2)}) async-start(bf16[32,4,16,128]{3,2,1,0:T(8,128)(2,1)} %get-tuple-element.41), calls=%async_computation.2 | async-start | bytes 1048576 | tf_op jit(solution)/shard_map/all_to_all | solution.py:325
  137.0 16.0 %collective-permute-start.3 = (bf16[2,8,4,16,128]{4,3,2,1,0:T(8,128)(2,1)S(1)}, bf16[2,8,4,16,128]{4,3,2,1,0:T(8,128)(2,1)S(1)}, u32[]{:S(2)}, u32[]{:S(2)}) collective-permute-start(bf16[2,8,4,16,128]{4,3,2,1,0:T(8,128)(2,1)S(1)} %bitcast.25), channel_id=1, source_target_pairs={{0,7},{1,0},{2,1},{3,2},{4,3},{5,4},{6,5},{7,6},{8,15},{9,8},{10,9... | collective-permute-start | bytes 786440 | tf_op jit(solution)/shard_map/ppermute | solution.py:184
  146.2 37.1 %all-to-all-start.1 = ((bf16[32,4,16,128]{3,2,1,0:T(8,128)(2,1)}), bf16[32,4,16,128]{3,2,1,0:T(8,128)(2,1)}, u32[]{:S(2)}, u32[]{:S(2)}) async-start(bf16[32,4,16,128]{3,2,1,0:T(8,128)(2,1)} %get-tuple-element.40), calls=%async_computation.1 | async-start | bytes 1048576 | tf_op jit(solution)/shard_map/all_to_all | solution.py:326
  156.2 15.4 %collective-permute-start.10 = (bf16[2,8,4,16,128]{4,3,2,1,0:T(8,128)(2,1)S(1)}, bf16[2,8,4,16,128]{4,3,2,1,0:T(8,128)(2,1)}, u32[]{:S(2)}, u32[]{:S(2)}) collective-permute-start(bf16[2,8,4,16,128]{4,3,2,1,0:T(8,128)(2,1)S(1)} %collective-permute-done.9.rest_3_), channel_id=1, source_target_pairs={{0,7},{1,0},{2,1},{3,2},{4,3},{5,4},{6,5},{7,6},{8,15},{9,8},{10,9... | collective-permute-start | bytes 786440 | tf_op jit(solution)/shard_map/ppermute | solution.py:184
  159.4 15.5 %collective-permute-start.7 = (bf16[2,8,4,16,128]{4,3,2,1,0:T(8,128)(2,1)}, bf16[2,8,4,16,128]{4,3,2,1,0:T(8,128)(2,1)}, u32[]{:S(2)}, u32[]{:S(2)}) collective-permute-start(bf16[2,8,4,16,128]{4,3,2,1,0:T(8,128)(2,1)} %collective-permute-done.6.rest_2_), channel_id=1, source_target_pairs={{0,1},{1,2},{2,3},{3,4},{4,5},{5,6},{6,7},{7,0},{8,9},{9,10},{10,1... | collective-permute-start | bytes 786440 | tf_op jit(solution)/shard_map/ppermute | solution.py:183
  162.8 21.5 %collective-permute-start.5 = (bf16[2,8,4,16,128]{4,3,2,1,0:T(8,128)(2,1)}, bf16[2,8,4,16,128]{4,3,2,1,0:T(8,128)(2,1)}, u32[]{:S(2)}, u32[]{:S(2)}) collective-permute-start(bf16[2,8,4,16,128]{4,3,2,1,0:T(8,128)(2,1)} %collective-permute-done.4.rest_1_), channel_id=1, source_target_pairs={{0,7},{1,0},{2,1},{3,2},{4,3},{5,4},{6,5},{7,6},{8,15},{9,8},{10,9... | collective-permute-start | bytes 786440 | tf_op jit(solution)/shard_map/ppermute | solution.py:184
  166.7 22.0 %collective-permute-start.2 = (bf16[2,8,4,16,128]{4,3,2,1,0:T(8,128)(2,1)}, bf16[2,8,4,16,128]{4,3,2,1,0:T(8,128)(2,1)}, u32[]{:S(2)}, u32[]{:S(2)}) collective-permute-start(bf16[2,8,4,16,128]{4,3,2,1,0:T(8,128)(2,1)} %collective-permute-done.1.rest_0_), channel_id=1, source_target_pairs={{0,1},{1,2},{2,3},{3,4},{4,5},{5,6},{6,7},{7,0},{8,9},{9,10},{10,1... | collective-permute-start | bytes 786440 | tf_op jit(solution)/shard_map/ppermute | solution.py:183
  171.6 27.1 %collective-permute-start.11 = (bf16[2,8,4,16,128]{4,3,2,1,0:T(8,128)(2,1)}, bf16[2,8,4,16,128]{4,3,2,1,0:T(8,128)(2,1)}, u32[]{:S(2)}, u32[]{:S(2)}) collective-permute-start(bf16[2,8,4,16,128]{4,3,2,1,0:T(8,128)(2,1)} %collective-permute-done.10.rest_3_), channel_id=1, source_target_pairs={{0,7},{1,0},{2,1},{3,2},{4,3},{5,4},{6,5},{7,6},{8,15},{9,8},{10,9... | collective-permute-start | bytes 786440 | tf_op jit(solution)/shard_map/ppermute | solution.py:184
  174.9 23.9 %collective-permute-start.8 = (bf16[2,8,4,16,128]{4,3,2,1,0:T(8,128)(2,1)}, bf16[2,8,4,16,128]{4,3,2,1,0:T(8,128)(2,1)}, u32[]{:S(2)}, u32[]{:S(2)}) collective-permute-start(bf16[2,8,4,16,128]{4,3,2,1,0:T(8,128)(2,1)} %collective-permute-done.7.rest_2_), channel_id=1, source_target_pairs={{0,1},{1,2},{2,3},{3,4},{4,5},{5,6},{6,7},{7,0},{8,9},{9,10},{10,1... | collective-permute-start | bytes 786440 | tf_op jit(solution)/shard_map/ppermute | solution.py:183
  185.4 23.7 %collective-permute-start.21 = (bf16[1,8,4,16,128]{4,3,2,1,0:T(8,128)(2,1)S(1)}, bf16[1,8,4,16,128]{4,3,2,1,0:T(8,128)(2,1)S(1)}, u32[]{:S(2)}, u32[]{:S(2)}) collective-permute-start(bf16[1,8,4,16,128]{4,3,2,1,0:T(8,128)(2,1)S(1)} %slice.112), channel_id=1, source_target_pairs={{0,7},{1,0},{2,1},{3,2},{4,3},{5,4},{6,5},{7,6},{8,15},{9,8},{10,9... | collective-permute-start | bytes 393224 | tf_op jit(solution)/shard_map/ppermute | solution.py:184
  189.6 19.6 %collective-permute-start.20 = (bf16[1,8,4,16,128]{4,3,2,1,0:T(8,128)(2,1)S(1)}, bf16[1,8,4,16,128]{4,3,2,1,0:T(8,128)(2,1)S(1)}, u32[]{:S(2)}, u32[]{:S(2)}) collective-permute-start(bf16[1,8,4,16,128]{4,3,2,1,0:T(8,128)(2,1)S(1)} %slice.111), channel_id=1, source_target_pairs={{0,1},{1,2},{2,3},{3,4},{4,5},{5,6},{6,7},{7,0},{8,9},{9,10},{10,1... | collective-permute-start | bytes 393224 | tf_op jit(solution)/shard_map/ppermute | solution.py:183
  201.6 25.4 %collective-permute-start.16 = (bf16[2,8,4,16,128]{4,3,2,1,0:T(8,128)(2,1)S(1)}, bf16[2,8,4,16,128]{4,3,2,1,0:T(8,128)(2,1)S(1)}, u32[]{:S(2)}, u32[]{:S(2)}) collective-permute-start(bf16[2,8,4,16,128]{4,3,2,1,0:T(8,128)(2,1)S(1)} %bitcast.31), channel_id=1, source_target_pairs={{0,7},{1,0},{2,1},{3,2},{4,3},{5,4},{6,5},{7,6},{8,15},{9,8},{10,9... | collective-permute-start | bytes 786440 | tf_op jit(solution)/shard_map/ppermute | solution.py:184
  204.9 24.2 %collective-permute-start.12 = (bf16[2,8,4,16,128]{4,3,2,1,0:T(8,128)(2,1)S(1)}, bf16[2,8,4,16,128]{4,3,2,1,0:T(8,128)(2,1)S(1)}, u32[]{:S(2)}, u32[]{:S(2)}) collective-permute-start(bf16[2,8,4,16,128]{4,3,2,1,0:T(8,128)(2,1)S(1)} %bitcast.32), channel_id=1, source_target_pairs={{0,1},{1,2},{2,3},{3,4},{4,5},{5,6},{6,7},{7,0},{8,9},{9,10},{10,1... | collective-permute-start | bytes 786440 | tf_op jit(solution)/shard_map/ppermute | solution.py:183
  204.9 24.2 %collective-permute-start.18 = (bf16[2,8,4,16,128]{4,3,2,1,0:T(8,128)(2,1)S(1)}, bf16[2,8,4,16,128]{4,3,2,1,0:T(8,128)(2,1)S(1)}, u32[]{:S(2)}, u32[]{:S(2)}) collective-permute-start(bf16[2,8,4,16,128]{4,3,2,1,0:T(8,128)(2,1)S(1)} %bitcast.28), channel_id=1, source_target_pairs={{0,7},{1,0},{2,1},{3,2},{4,3},{5,4},{6,5},{7,6},{8,15},{9,8},{10,9... | collective-permute-start | bytes 786440 | tf_op jit(solution)/shard_map/ppermute | solution.py:184
  209.1 23.3 %collective-permute-start.14 = (bf16[2,8,4,16,128]{4,3,2,1,0:T(8,128)(2,1)S(1)}, bf16[2,8,4,16,128]{4,3,2,1,0:T(8,128)(2,1)S(1)}, u32[]{:S(2)}, u32[]{:S(2)}) collective-permute-start(bf16[2,8,4,16,128]{4,3,2,1,0:T(8,128)(2,1)S(1)} %bitcast.29), channel_id=1, source_target_pairs={{0,1},{1,2},{2,3},{3,4},{4,5},{5,6},{6,7},{7,0},{8,9},{9,10},{10,1... | collective-permute-start | bytes 786440 | tf_op jit(solution)/shard_map/ppermute | solution.py:183
  245.0 59.0 %all-to-all-start.4 = ((bf16[8,128,512]{2,1,0:T(8,128)(2,1)}), bf16[8,128,512]{2,1,0:T(8,128)(2,1)S(1)}, u32[]{:S(2)}, u32[]{:S(2)}) async-start(bf16[8,128,512]{2,1,0:T(8,128)(2,1)} %copy-done.5), calls=%async_computation.4 | async-start | bytes 2097152 | tf_op jit(solution)/shard_map/all_to_all | solution.py:350
  248.5 33.0 %collective-permute-start.25 = (bf16[2,8,4,16,128]{4,3,2,1,0:T(8,128)(2,1)}, bf16[2,8,4,16,128]{4,3,2,1,0:T(8,128)(2,1)S(1)}, u32[]{:S(2)}, u32[]{:S(2)}) collective-permute-start(bf16[2,8,4,16,128]{4,3,2,1,0:T(8,128)(2,1)} %copy-done.28), channel_id=1, source_target_pairs={{0,1},{1,2},{2,3},{3,4},{4,5},{5,6},{6,7},{7,0},{8,9},{9,10},{10,1... | collective-permute-start | bytes 786440 | tf_op jit(solution)/shard_map/ppermute | solution.py:183
  250.4 31.2 %collective-permute-start.27 = (bf16[2,8,4,16,128]{4,3,2,1,0:T(8,128)(2,1)}, bf16[2,8,4,16,128]{4,3,2,1,0:T(8,128)(2,1)S(1)}, u32[]{:S(2)}, u32[]{:S(2)}) collective-permute-start(bf16[2,8,4,16,128]{4,3,2,1,0:T(8,128)(2,1)} %copy-done.26), channel_id=1, source_target_pairs={{0,7},{1,0},{2,1},{3,2},{4,3},{5,4},{6,5},{7,6},{8,15},{9,8},{10,9... | collective-permute-start | bytes 786440 | tf_op jit(solution)/shard_map/ppermute | solution.py:184
  251.8 35.3 %collective-permute-start.29 = (bf16[2,8,4,16,128]{4,3,2,1,0:T(8,128)(2,1)}, bf16[2,8,4,16,128]{4,3,2,1,0:T(8,128)(2,1)S(1)}, u32[]{:S(2)}, u32[]{:S(2)}) collective-permute-start(bf16[2,8,4,16,128]{4,3,2,1,0:T(8,128)(2,1)} %collective-permute-done.15.rest_2_), channel_id=1, source_target_pairs={{0,1},{1,2},{2,3},{3,4},{4,5},{5,6},{6,7},{7,0},{8,9},{9,10},{10,1... | collective-permute-start | bytes 786440 | tf_op jit(solution)/shard_map/ppermute | solution.py:183
  252.5 34.8 %collective-permute-start.31 = (bf16[2,8,4,16,128]{4,3,2,1,0:T(8,128)(2,1)}, bf16[2,8,4,16,128]{4,3,2,1,0:T(8,128)(2,1)S(1)}, u32[]{:S(2)}, u32[]{:S(2)}) collective-permute-start(bf16[2,8,4,16,128]{4,3,2,1,0:T(8,128)(2,1)} %copy-done.30), channel_id=1, source_target_pairs={{0,7},{1,0},{2,1},{3,2},{4,3},{5,4},{6,5},{7,6},{8,15},{9,8},{10,9... | collective-permute-start | bytes 786440 | tf_op jit(solution)/shard_map/ppermute | solution.py:184
  281.5 16.5 %collective-permute-start.26 = (bf16[1,8,4,16,128]{4,3,2,1,0:T(8,128)(2,1)S(1)}, bf16[1,8,4,16,128]{4,3,2,1,0:T(8,128)(2,1)S(1)}, u32[]{:S(2)}, u32[]{:S(2)}) collective-permute-start(bf16[1,8,4,16,128]{4,3,2,1,0:T(8,128)(2,1)S(1)} %slice.115), channel_id=1, source_target_pairs={{0,1},{1,2},{2,3},{3,4},{4,5},{5,6},{6,7},{7,0},{8,9},{9,10},{10,1... | collective-permute-start | bytes 393224 | tf_op jit(solution)/shard_map/ppermute | solution.py:183
  281.6 16.4 %collective-permute-start.28 = (bf16[1,8,4,16,128]{4,3,2,1,0:T(8,128)(2,1)S(1)}, bf16[1,8,4,16,128]{4,3,2,1,0:T(8,128)(2,1)S(1)}, u32[]{:S(2)}, u32[]{:S(2)}) collective-permute-start(bf16[1,8,4,16,128]{4,3,2,1,0:T(8,128)(2,1)S(1)} %slice.116), channel_id=1, source_target_pairs={{0,7},{1,0},{2,1},{3,2},{4,3},{5,4},{6,5},{7,6},{8,15},{9,8},{10,9... | collective-permute-start | bytes 393224 | tf_op jit(solution)/shard_map/ppermute | solution.py:184
  (53 other events, 768.1 us)
Sparse Core Ops, SparseCore 0:
  9.2 77.9 all-gather.1

commit v3 on v2

v3 whole, which is shorter than its diff:
```python
import functools

import jax
import jax.numpy as jnp
from jax import lax
from jax.experimental import pallas as pl
from jax.experimental.pallas import tpu as pltpu
from jax.sharding import PartitionSpec as P

HS = 128
NB = 2
PIECE_T = 16
PIECE_F = 128
FEW = 1
VMEM_LIMIT = 48 * 1024 * 1024


def rms_scale(rows, gain):
    values = rows.astype(jnp.float32)
    inverse = lax.rsqrt(jnp.mean(values * values, axis=-1, keepdims=True) + 1e-06)
    return (values * inverse * gain.astype(jnp.float32)).astype(jnp.bfloat16)


def cut_kernel(db_ref, note_ref, out_ref):
    shard = db_ref.shape[0]
    pieces_t = db_ref.shape[1] // PIECE_T
    pieces_f = db_ref.shape[2] // PIECE_F
    for f in range(pieces_f):
        for i in range(pieces_t):
            piece = f * pieces_t + i
            out_ref[piece, :shard] = db_ref[
                :, i * PIECE_T : (i + 1) * PIECE_T, f * PIECE_F : (f + 1) * PIECE_F
            ]
            out_ref[piece, shard] = note_ref[...]


def cut(database, note):
    shard, length, part = database.shape
    pieces = (length // PIECE_T) * (part // PIECE_F)
    vmem = pl.BlockSpec(memory_space=pltpu.VMEM)
    return pl.pallas_call(
        cut_kernel,
        in_specs=[vmem] * 2,
        out_specs=vmem,
        out_shape=jax.ShapeDtypeStruct((pieces, shard + 1, PIECE_T, PIECE_F), database.dtype),
        compiler_params=pltpu.CompilerParams(vmem_limit_bytes=VMEM_LIMIT),
        name="cut",
    )(database, note)


def pick_kernel(index_ref, spread_ref, low_ref, high_ref):
    n_seq, few = low_ref.shape[:2]

    def one(dest, carry):
        for j in range(few):
            low_ref[dest, j] = spread_ref[index_ref[dest, j]]
        for j in range(high_ref.shape[1]):
            high_ref[dest, j] = spread_ref[index_ref[dest, few + j]]
        return carry

    lax.fori_loop(0, n_seq, one, 0, unroll=2)


def pick(index, spread, few):
    n_seq, items = index.shape
    vmem = pl.BlockSpec(memory_space=pltpu.VMEM)
    return pl.pallas_call(
        pick_kernel,
        in_specs=[pl.BlockSpec(memory_space=pltpu.SMEM), vmem],
        out_specs=[vmem] * 2,
        out_shape=[
            jax.ShapeDtypeStruct((n_seq, count, PIECE_T, PIECE_F), spread.dtype)
            for count in (few, items - few)
        ],
        compiler_params=pltpu.CompilerParams(vmem_limit_bytes=VMEM_LIMIT),
        name="pick",
    )(index, spread)


def unpack(x_ref):
    features, pieces_t, items = x_ref.shape[:3]
    rows = pieces_t * items * PIECE_T
    pieces = [x_ref[f].reshape(rows, PIECE_F) for f in range(features)]
    squares = jnp.zeros((rows, PIECE_F), jnp.float32)
    for piece in pieces:
        wide = piece.astype(jnp.float32)
        squares = squares + wide * wide
    return jnp.concatenate(pieces, axis=1), squares


def store_spans(acc, squares, features, out_refs):
    mean = jnp.sum(squares, axis=1, keepdims=True) * (1.0 / features)
    done = (acc * lax.rsqrt(mean + 1e-06)).astype(jnp.bfloat16)
    pieces_t = out_refs[0].shape[0]
    done = done.reshape(pieces_t, NB * len(out_refs), PIECE_T, done.shape[-1])
    for span, ref in enumerate(out_refs):
        ref[...] = done[:, span * NB : (span + 1) * NB]


def project_kernel(x_ref, w_ref, *rest):
    spans = len(rest) - 2
    out_refs, (acc_ref, squares_ref) = rest[:spans], rest[spans:]
    step = pl.program_id(0)
    steps = pl.num_programs(0)
    x, squares = unpack(x_ref.at[0])
    term = jnp.dot(x, w_ref[0], preferred_element_type=jnp.float32)

    @pl.when(step == 0)
    def _():
        acc_ref[...] = term
        squares_ref[...] = squares

    @pl.when(step > 0)
    def _():
        acc_ref[...] += term
        squares_ref[...] += squares

    @pl.when(step == steps - 1)
    def _():
        store_spans(acc_ref[...], squares_ref[...], steps * x.shape[1], out_refs)


def project(x, weights):
    steps, pieces_f, pieces_t, items, _, _ = x.shape
    rows = pieces_t * items * PIECE_T
    _, part, cols = weights.shape
    span = jax.ShapeDtypeStruct((pieces_t, NB, PIECE_T, cols), jnp.bfloat16)
    return pl.pallas_call(
        project_kernel,
        grid=(steps,),
        in_specs=[
            pl.BlockSpec((1,) + x.shape[1:], lambda t: (t, 0, 0, 0, 0, 0)),
            pl.BlockSpec((1, part, cols), lambda t: (t, 0, 0)),
        ],
        out_specs=[pl.BlockSpec(span.shape, lambda t: (0, 0, 0, 0))] * (items // NB),
        out_shape=[span] * (items // NB),
        scratch_shapes=[
            pltpu.VMEM((rows, cols), jnp.float32),
            pltpu.VMEM((rows, PIECE_F), jnp.float32),
        ],
        compiler_params=pltpu.CompilerParams(vmem_limit_bytes=VMEM_LIMIT),
        cost_estimate=pl.CostEstimate(
            flops=8 * steps * rows * part * cols,
            bytes_accessed=2 * steps * part * (rows + cols),
            transcendentals=0,
        ),
        name="project",
    )(x, weights)


def project_blocks_kernel(places, where_ref, w_ref, *rest):
    count = len(places)
    x_refs, rest = rest[:count], rest[count:]
    spans = len(rest) - 2
    out_refs, (acc_ref, squares_ref) = rest[:spans], rest[spans:]
    for at, (x_ref, (place, start)) in enumerate(zip(x_refs, places)):
        x, squares = unpack(x_ref)
        first = start * PIECE_F
        w = w_ref[where_ref[place], first : first + x.shape[1], :]
        term = jnp.dot(x, w, preferred_element_type=jnp.float32)
        if at == 0:
            acc_ref[...] = term
            squares_ref[...] = squares
        else:
            acc_ref[...] += term
            squares_ref[...] += squares
    features = w_ref.shape[0] * w_ref.shape[1]
    store_spans(acc_ref[...], squares_ref[...], features, out_refs)


def project_blocks(blocks, places, where, weights):
    n_ten, part, cols = weights.shape
    _, pieces_t, items = blocks[0].shape[:3]
    rows = pieces_t * items * PIECE_T
    span = jax.ShapeDtypeStruct((pieces_t, NB, PIECE_T, cols), jnp.bfloat16)
    vmem = pl.BlockSpec(memory_space=pltpu.VMEM)
    return pl.pallas_call(
        functools.partial(project_blocks_kernel, tuple(places)),
        in_specs=[pl.BlockSpec(memory_space=pltpu.SMEM)] + [vmem] * (1 + len(blocks)),
        out_specs=[vmem] * (items // NB),
        out_shape=[span] * (items // NB),
        scratch_shapes=[
            pltpu.VMEM((rows, cols), jnp.float32),
            pltpu.VMEM((rows, PIECE_F), jnp.float32),
        ],
        compiler_params=pltpu.CompilerParams(vmem_limit_bytes=VMEM_LIMIT),
        cost_estimate=pl.CostEstimate(
            flops=8 * n_ten * rows * part * cols,
            bytes_accessed=2 * n_ten * part * (rows + cols),
            transcendentals=0,
        ),
        name="project_blocks",
    )(where, weights, *blocks)


def ring_gather(pair, me, n_ten):
    right = [(i, (i + 1) % n_ten) for i in range(n_ten)]
    left = [(i, (i - 1) % n_ten) for i in range(n_ten)]
    width = pair[0].shape[0]
    last = n_ten // 2
    go_right, go_left = list(pair), list(pair)
    blocks, places = list(pair), [(0, 0), (0, width)]
    marks = None
    for step in range(1, last + 1):
        half = width // 2 if step == last else 0
        if half:
            marks = go_right + go_left
            go_right = [x[:half] for x in go_right]
            go_left = [x[half:] for x in go_left]
        for s in range(2):
            go_right[s] = lax.ppermute(go_right[s], "tensor", right)
            go_left[s] = lax.ppermute(go_left[s], "tensor", left)
            blocks += [go_right[s], go_left[s]]
            places += [(n_ten - step, s * width), (step, s * width + half)]
    where = (me + jnp.arange(n_ten, dtype=jnp.int32)) % n_ten
    return blocks, places, where, marks


def weigh(scores, count, keys_axis_owner):
    scores = jnp.where(keys_axis_owner < count, scores, jnp.float32(-1e30))
    top = jnp.max(scores, axis=-1, keepdims=True)
    expo = jnp.exp(scores - top)
    return expo / jnp.sum(expo, axis=-1, keepdims=True)


def scores_of(queries, keys):
    return lax.dot_general(
        queries, keys, (((1,), (1,)), ((), ())), preferred_element_type=jnp.float32
    )


def attend_kernel(with_prev, span_len, count_ref, q_ref, *rest):
    pair_refs, prev_ref, out_ref = rest[: -2 if with_prev else -1], rest[-2], rest[-1]
    cols = q_ref.shape[1]
    heads = cols // HS
    spans = len(pair_refs)
    keys = pair_refs[0].shape[0] * pair_refs[0].shape[1] * pair_refs[0].shape[2]
    owner = (lax.broadcasted_iota(jnp.int32, (span_len, keys), 1) // PIECE_T) % NB
    row = lax.broadcasted_iota(jnp.int32, (span_len, keys), 0)
    for span in range(spans):
        pair = pair_refs[span][...].reshape(keys, 2 * cols)
        queries = q_ref[span * span_len : (span + 1) * span_len, :]
        mixed_heads = []
        for head in range(heads):
            at = slice(head * HS, (head + 1) * HS)
            value_at = slice(cols + head * HS, cols + (head + 1) * HS)
            query = queries[:, at]
            scores = scores_of(query, pair[:, at])
            if with_prev and span == spans - 1:
                prev = prev_ref[...].reshape(keys, 2 * cols)
                own = row == 0
                scores = jnp.where(own, scores, scores_of(query, prev[:, at]))
                count = jnp.where(own, count_ref[span], count_ref[span + 1])
                weights = weigh(scores, count, owner)
                ours = jnp.where(own, weights, 0.0).astype(jnp.bfloat16)
                theirs = jnp.where(own, 0.0, weights).astype(jnp.bfloat16)
                result = jnp.dot(
                    ours, pair[:, value_at], preferred_element_type=jnp.float32
                ) + jnp.dot(theirs, prev[:, value_at], preferred_element_type=jnp.float32)
            else:
                weights = weigh(scores, count_ref[span], owner).astype(jnp.bfloat16)
                result = jnp.dot(
                    weights, pair[:, value_at], preferred_element_type=jnp.float32
                )
            mixed_heads.append(result.astype(jnp.bfloat16))
        attended = jnp.concatenate(mixed_heads, axis=1)
        for g in range(out_ref.shape[0]):
            out_ref[g, span * span_len : (span + 1) * span_len, :] = attended


def attend(counts, queries, pairs, prev, groups):
    rows, cols = queries.shape
    with_prev = prev is not None
    operands = [counts, queries, *pairs] + ([prev] if with_prev else [])
    vmem = pl.BlockSpec(memory_space=pltpu.VMEM)
    return pl.pallas_call(
        functools.partial(attend_kernel, with_prev, rows // len(pairs)),
        in_specs=[pl.BlockSpec(memory_space=pltpu.SMEM)] + [vmem] * (len(operands) - 1),
        out_specs=vmem,
        out_shape=jax.ShapeDtypeStruct((groups, rows, cols), jnp.bfloat16),
        compiler_params=pltpu.CompilerParams(vmem_limit_bytes=VMEM_LIMIT),
        cost_estimate=pl.CostEstimate(
            flops=32 * rows * 256 * cols,
            bytes_accessed=2 * groups * rows * cols,
            transcendentals=0,
        ),
        name="attend_prev" if with_prev else "attend",
    )(*operands)


def sum_groups(attended_ref, wo_ref):
    total = None
    for g in range(wo_ref.shape[0]):
        part = jnp.dot(attended_ref[g], wo_ref[g], preferred_element_type=jnp.float32)
        part = part.astype(jnp.bfloat16).astype(jnp.float32)
        total = part if total is None else total + part
    return total


def output_kernel(attended_ref, wo_ref, out_ref):
    out_ref[...] = sum_groups(attended_ref, wo_ref)


def output(attended, wo):
    vmem = pl.BlockSpec(memory_space=pltpu.VMEM)
    return pl.pallas_call(
        output_kernel,
        in_specs=[vmem] * 2,
        out_specs=vmem,
        out_shape=jax.ShapeDtypeStruct((attended.shape[1], wo.shape[2]), jnp.float32),
        compiler_params=pltpu.CompilerParams(vmem_limit_bytes=VMEM_LIMIT),
        name="output",
    )(attended, wo)


def finish_kernel(shift, low_ref, high_ref, wo_ref, tokens_ref, out_ref):
    low = sum_groups(low_ref, wo_ref)
    total = pltpu.roll(jnp.concatenate([low, high_ref[...]], axis=0), shift, 0)
    out_ref[...] = (tokens_ref[...].astype(jnp.float32) + total).astype(jnp.bfloat16)


def finish(low, high, wo, tokens, shift):
    return pl.pallas_call(
        functools.partial(finish_kernel, shift),
        in_specs=[pl.BlockSpec(memory_space=pltpu.VMEM)] * 4,
        out_specs=pl.BlockSpec(memory_space=pltpu.VMEM),
        out_shape=jax.ShapeDtypeStruct(tokens.shape, jnp.bfloat16),
        compiler_params=pltpu.CompilerParams(vmem_limit_bytes=VMEM_LIMIT),
        name="finish",
    )(low, high, wo, tokens)


def body(tokens, x_gain, nbr_gain, database, nbr_shard, nbr_row, nbr_count, wq, wk, wv, wo):
    n_seq = lax.axis_size("seq")
    n_ten = lax.axis_size("tensor")
    tok_dev = tokens.shape[0]
    span_dev = nbr_shard.shape[0]
    span_len = tok_dev // span_dev
    shift = span_len - 1
    per_shard, nbr_len, d_part = database.shape
    items = span_dev * NB
    few = NB * FEW
    pieces_t = nbr_len // PIECE_T
    pieces_f = d_part // PIECE_F
    seq_at = lax.axis_index("seq")
    me = lax.axis_index("tensor")

    note = jnp.concatenate([nbr_shard.reshape(-1), nbr_row.reshape(-1), nbr_count])
    n_notes = note.shape[0]
    note = jnp.pad(note.astype(jnp.bfloat16)[None], ((0, PIECE_T - 1), (0, PIECE_F - n_notes)))
    pieces = cut(database, note)
    spread = lax.all_to_all(pieces, "seq", split_axis=0, concat_axis=0, tiled=True)
    notes = spread[:, per_shard, 0, :n_notes].astype(jnp.int32)
    index = notes[:, :items] * (per_shard + 1) + notes[:, items : 2 * items]
    prev_count = jnp.where(seq_at > 0, notes[jnp.maximum(seq_at - 1, 0), n_notes - 1], 0)
    low, high = pick(index, spread.reshape(n_seq * (per_shard + 1), PIECE_T, PIECE_F), few)

    own_rows = wo.shape[0] // n_seq
    wo_rows = lax.dynamic_slice_in_dim(wo, seq_at * own_rows, own_rows, axis=0)
    wo_rows, _ = lax.optimization_barrier((wo_rows, pieces))
    wo_rows = wo_rows.reshape(own_rows, n_ten, d_part).transpose(1, 0, 2)
    wo_rows = lax.all_to_all(wo_rows, "tensor", split_axis=0, concat_axis=0, tiled=True)

    whole = lax.all_gather(tokens, "tensor", axis=1, tiled=True)
    low, high, whole = lax.optimization_barrier((low, high, whole))
    high = lax.all_to_all(high, "seq", split_axis=0, concat_axis=0, tiled=True)
    low = lax.all_to_all(low, "seq", split_axis=0, concat_axis=0, tiled=True)
    wo_cols = lax.all_gather(wo_rows, "seq", axis=1, tiled=True)

    both = jnp.concatenate([wk, wv], axis=1).astype(jnp.float32)
    both = (both * nbr_gain.astype(jnp.float32)[:, None]).astype(jnp.bfloat16)
    both = both.reshape(n_ten, d_part, both.shape[1])

    high = high.reshape(pieces_f, pieces_t, items - few, PIECE_T, PIECE_F)
    streams = [high[: pieces_f // 2], high[pieces_f // 2 :]]
    blocks, places, where, marks = ring_gather(streams, me, n_ten)
    low, wo_cols, marks = lax.optimization_barrier((low, wo_cols, marks))
    low_x = lax.all_gather(low, "tensor", axis=0, tiled=True)
    low_x = low_x.reshape(n_ten, pieces_f, pieces_t, few, PIECE_T, PIECE_F)
    whole, blocks = lax.optimization_barrier((whole, blocks))

    *middle, final = project_blocks(blocks, places, where, both)
    prev = lax.ppermute(final, "seq", [(i, i + 1) for i in range(n_seq - 1)])
    normed = rms_scale(whole, x_gain)
    queries = (jnp.dot(normed, wq, preferred_element_type=jnp.float32) * HS ** (-0.5)).astype(
        jnp.bfloat16
    )
    queries = jnp.concatenate([queries[shift:], queries[:shift]], axis=0)
    split = FEW * span_len

    high_counts = jnp.concatenate([nbr_count[FEW:], prev_count[None]])
    high_rows = attend(high_counts, queries[split:], [*middle, final], prev, n_ten)
    high_rows = lax.all_to_all(high_rows, "tensor", split_axis=0, concat_axis=0, tiled=True)
    high_sum = output(high_rows, wo_cols)

    low_x, high_sum = lax.optimization_barrier((low_x, high_sum))
    low_rows = attend(nbr_count[:FEW], queries[:split], project(low_x, both), None, n_ten)
    low_rows = lax.all_to_all(low_rows, "tensor", split_axis=0, concat_axis=0, tiled=True)
    return finish(low_rows, high_sum, wo_cols, tokens, shift)


def solution(mesh):
    placed = (
        P("seq", "tensor"),
        P(),
        P(),
        P("seq", None, "tensor"),
        P("seq", None),
        P("seq", None),
        P("seq"),
        P(None, "tensor"),
        P(None, "tensor"),
        P(None, "tensor"),
        P("tensor", None),
    )
    return jax.shard_map(
        body, mesh=mesh, in_specs=placed, out_specs=P("seq", "tensor"), check_vma=False
    )
```

time: 350 us -> 244 us (0.70); the launches traced: 344 us -> 242 us
  Pallas kernels: 100 us -> 22.7 us
  starting transfers between devices: 89.8 us -> 39.3 us
  blocking collectives: 31.5 us -> 49.3 us
  waiting for transfers between devices: 76.4 us -> 87.5 us
    pallas_call x13 -> x6, Pallas kernels: 96.3 us -> 18.7 us  [the longest x1 7.04 us: project_blocks(): pl.pallas_call(functools.partial(project_blocks_kernel, tuple(places)), i...]
    ppermute x33 -> x17, starting transfers between devices: 64.9 us -> 20.1 us  [the longest x8 14.1 us: ring_gather(): go_left[s] = lax.ppermute(go_left[s], 'tensor', left)]
    all_to_all x1 -> x3, blocking collectives: 31.5 us -> 49.3 us  [the longest x1 18.3 us: body(): high = lax.all_to_all(high, 'seq', split_axis=0, concat_axis=0, tiled=True)]
    all_to_all x3 -> x2, waiting for transfers between devices: 33.9 us -> 49.2 us  [the longest x1 27.6 us: body(): lax.all_to_all(pieces, 'seq', split_axis=0, concat_axis=0, tiled=True)]
    all_to_all x3 -> x2, starting transfers between devices: 18.3 us -> 11.8 us  [the longest x1 7.51 us: body(): lax.all_to_all(pieces, 'seq', split_axis=0, concat_axis=0, tiled=True)]
    ppermute x33 -> x17, waiting for transfers between devices: 41.8 us -> 36.8 us  [the longest x8 25 us: ring_gather(): go_left[s] = lax.ppermute(go_left[s], 'tensor', left)]
    unnamed x78 -> x38, local copies, waits for them, and re-layouts: 13.6 us -> 13.2 us
  transfers between devices with their start and end apart: 38 -> 23, of which waited for: 11 -> 10; matrix products, arithmetic and copies ran while one was open for 5% -> 7% of each run, Pallas kernels for 29% -> 6%
where the time goes in v3:
time: 244 us; the launch traced here: 242 us
  waiting for transfers between devices  87.5 us (36%)
  blocking collectives  49.3 us (20%)
  starting transfers between devices  39.3 us (16%)
  Pallas kernels  22.7 us (9%)
  local copies, waits for them, and re-layouts  21.7 us (9%)
  between operations  14 us (6%)
  other arithmetic  6.81 us (3%)
    all_to_all x1, waiting for transfers between devices, body(): lax.all_to_all(pieces, 'seq', split_axis=0, concat_axis=0, tiled=True)  27.6 us
    ppermute x8, waiting for transfers between devices, ring_gather(): go_left[s] = lax.ppermute(go_left[s], 'tensor', left)  25 us
    all_to_all x1, waiting for transfers between devices, body(): lax.all_to_all(high_rows, 'tensor', split_axis=0, concat_axis=0, tiled=True)  21.7 us
    all_to_all x1, blocking collectives, body(): high = lax.all_to_all(high, 'seq', split_axis=0, concat_axis=0, tiled=True)  18.3 us
    all_to_all x1, blocking collectives, body(): lax.all_to_all(wo_rows, 'tensor', split_axis=0, concat_axis=0, tiled=True)  17.1 us
    ppermute x8, starting transfers between devices, ring_gather(): go_left[s] = lax.ppermute(go_left[s], 'tensor', left)  14.1 us
    all_to_all x1, blocking collectives, body(): lax.all_to_all(low_rows, 'tensor', split_axis=0, concat_axis=0, tiled=True)  13.9 us
    unnamed x38, local copies, waits for them, and re-layouts  13.2 us
  transfers between devices with their start and end apart: 23, of which 10 were waited for; matrix products, arithmetic and copies ran while one was open for 7% of the time, Pallas kernels for 6%

profile of v3, /device:TPU:8, one launch (start us, length us, event | category | flops | bytes accessed | tf_op | source)
XLA Modules:
  0.0 242.0 jit_solution(1730122330293098478)
XLA Ops:
  14.0 17.1 %all_to_all.30 = bf16[8,8,512]{2,1,0:T(8,128)(2,1)} all-to-all(bf16[8,8,512]{2,1,0:T(8,128)(2,1)S(1)} %bitcast.27), channel_id=1, replica_groups=mesh['seq'=32,'tensor'=8] {'tensor'}, dimensions={0} | all-to-all | bytes 131072 | tf_op jit(solution)/shard_map/all_to_all | solution.py:362
  31.1 7.5 %all-to-all-start = ((bf16[32,17,16,128]{3,2,1,0:T(8,128)(2,1)}), bf16[32,17,16,128]{3,2,1,0:T(8,128)(2,1)}, u32[]{:S(2)}, u32[]{:S(2)}) async-start(bf16[32,17,16,128]{3,2,1,0:T(8,128)(2,1)} %copy-done.1), calls=%async_computation | async-start | bytes 4456448 | tf_op jit(solution)/shard_map/all_to_all | solution.py:352
  39.4 27.6 %all-to-all-done = bf16[32,17,16,128]{3,2,1,0:T(8,128)(2,1)} async-done(((bf16[32,17,16,128]{3,2,1,0:T(8,128)(2,1)}), bf16[32,17,16,128]{3,2,1,0:T(8,128)(2,1)}, u32[]{:S(2)}, u32[]{:S(2)}) %all-to-all-start) | async-done | bytes 2228256 | tf_op jit(solution)/shard_map/all_to_all | solution.py:352
  67.9 2.7 %pick.1 = (bf16[32,2,16,128]{3,2,1,0:T(8,128)(2,1)}, bf16[32,6,16,128]{3,2,1,0:T(8,128)(2,1)S(1)}) custom-call(s32[32,8]{1,0:T(8,128)S(1)} %slice_add_fusion.index_ref, bf16[544,16,128]{2,1,0:T(8,128)(2,1)} %bitcast.2.spread_ref), custom_call_target="tpu_custom_call" | custom-call | tf_op jit(solution)/shard_map/pick/pallas_call | solution.py:67
  70.6 18.3 %all_to_all.31 = bf16[32,6,16,128]{3,2,1,0:T(8,128)(2,1)S(1)} all-to-all(bf16[32,6,16,128]{3,2,1,0:T(8,128)(2,1)S(1)} %get-tuple-element.40), channel_id=1, replica_groups=mesh['seq'=32,'tensor'=8] {'seq'}, dimensions={0} | all-to-all | bytes 1572864 | tf_op jit(solution)/shard_map/all_to_all | solution.py:366
  89.4 1.7 collective-permute-start
  93.1 7.9 %collective-permute-done.1.rest_3_ = bf16[2,8,6,16,128]{4,3,2,1,0:T(8,128)(2,1)S(1)} collective-permute-done((bf16[2,8,6,16,128]{4,3,2,1,0:T(8,128)(2,1)S(1)}, bf16[2,8,6,16,128]{4,3,2,1,0:T(8,128)(2,1)S(1)}, u32[]{:S(2)}, u32[]{:S(2)}) %collective-permute-start.1) | collective-permute-done | bytes 393248 | tf_op jit(solution)/shard_map/ppermute | solution.py:212
  104.5 4.9 %collective-permute-done.3.rest_5_ = bf16[2,8,6,16,128]{4,3,2,1,0:T(8,128)(2,1)S(1)} collective-permute-done((bf16[2,8,6,16,128]{4,3,2,1,0:T(8,128)(2,1)S(1)}, bf16[2,8,6,16,128]{4,3,2,1,0:T(8,128)(2,1)S(1)}, u32[]{:S(2)}, u32[]{:S(2)}) %collective-permute-start.3) | collective-permute-done | bytes 393248 | tf_op jit(solution)/shard_map/ppermute | solution.py:212
  113.0 5.0 %collective-permute-done.5.rest_7_ = bf16[2,8,6,16,128]{4,3,2,1,0:T(8,128)(2,1)} collective-permute-done((bf16[2,8,6,16,128]{4,3,2,1,0:T(8,128)(2,1)S(1)}, bf16[2,8,6,16,128]{4,3,2,1,0:T(8,128)(2,1)}, u32[]{:S(2)}, u32[]{:S(2)}) %collective-permute-start.5) | collective-permute-done | bytes 393248 | tf_op jit(solution)/shard_map/ppermute | solution.py:212
  120.0 6.4 %collective-permute-done.7.rest_9_ = bf16[2,8,6,16,128]{4,3,2,1,0:T(8,128)(2,1)} collective-permute-done((bf16[2,8,6,16,128]{4,3,2,1,0:T(8,128)(2,1)S(1)}, bf16[2,8,6,16,128]{4,3,2,1,0:T(8,128)(2,1)}, u32[]{:S(2)}, u32[]{:S(2)}) %collective-permute-start.7) | collective-permute-done | bytes 393248 | tf_op jit(solution)/shard_map/ppermute | solution.py:212
  128.5 7.1 %all-to-all-start.2 = ((bf16[32,2,16,128]{3,2,1,0:T(8,128)(2,1)}), bf16[32,2,16,128]{3,2,1,0:T(8,128)(2,1)}, u32[]{:S(2)}, u32[]{:S(2)}) async-start(bf16[32,2,16,128]{3,2,1,0:T(8,128)(2,1)} %get-tuple-element.42), calls=%async_computation.2 | async-start | bytes 524288 | tf_op jit(solution)/shard_map/all_to_all | solution.py:367
  135.8 4.0 %multiply_convert_fusion.w_ref = bf16[8,512,512]{2,1,0:T(8,128)(2,1)} fusion(bf16[8,512,256]{2,1,0:T(8,128)(2,1)} %bitcast.25, bf16[8,512,256]{2,1,0:T(8,128)(2,1)} %bitcast.26, f32[8,512]{1,0:T(8,128)S(1)} %reshape.86), kind=kLoop, calls=%fused_computation | loop fusion | flops 12582912 | bytes 8404992 | tf_op jit(solution)/shard_map/convert_element_type | solution.py:371
  139.9 1.6 slice.75
  141.5 2.6 %collective-permute-start.13 = (bf16[1,8,6,16,128]{4,3,2,1,0:T(8,128)(2,1)}, bf16[1,8,6,16,128]{4,3,2,1,0:T(8,128)(2,1)S(1)}, u32[]{:S(2)}, u32[]{:S(2)}) collective-permute-start(bf16[1,8,6,16,128]{4,3,2,1,0:T(8,128)(2,1)} %slice.75), channel_id=1, source_target_pairs={{0,7},{1,0},{2,1},{3,2},{4,3},{5,4},{6,5},{7,6},{8,15},{9,8},{10,9... | collective-permute-start | bytes 589832 | tf_op jit(solution)/shard_map/ppermute | solution.py:212
  146.5 3.2 %collective-permute-start.15 = (bf16[1,8,6,16,128]{4,3,2,1,0:T(8,128)(2,1)}, bf16[1,8,6,16,128]{4,3,2,1,0:T(8,128)(2,1)}, u32[]{:S(2)}, u32[]{:S(2)}) collective-permute-start(bf16[1,8,6,16,128]{4,3,2,1,0:T(8,128)(2,1)} %slice.77), channel_id=1, source_target_pairs={{0,7},{1,0},{2,1},{3,2},{4,3},{5,4},{6,5},{7,6},{8,15},{9,8},{10,9... | collective-permute-start | bytes 589832 | tf_op jit(solution)/shard_map/ppermute | solution.py:212
  154.0 5.0 %collective-permute-done.14.rest_16_ = bf16[1,8,6,16,128]{4,3,2,1,0:T(8,128)(2,1)} collective-permute-done((bf16[1,8,6,16,128]{4,3,2,1,0:T(8,128)(2,1)}, bf16[1,8,6,16,128]{4,3,2,1,0:T(8,128)(2,1)}, u32[]{:S(2)}, u32[]{:S(2)}) %collective-permute-start.14) | collective-permute-done | bytes 196640 | tf_op jit(solution)/shard_map/ppermute | solution.py:211
  163.0 7.0 %project_blocks.1 = (bf16[8,2,16,512]{3,2,1,0:T(8,128)(2,1)S(1)}, bf16[8,2,16,512]{3,2,1,0:T(8,128)(2,1)S(1)}, bf16[8,2,16,512]{3,2,1,0:T(8,128)(2,1)S(1)}) custom-call(s32[8]{0:T(128)S(1)} %and_select_fusion.where_ref, bf16[8,512,512]{2,1,0:T(8,128)(2,1)} %multiply_convert_fusion.w_ref, bf16[2,8,6,16,128]{4,3,2,1,0:T(8,128)(2,1)S(1)} %bitcast.22, ...), custom_call_target="tpu_custom_call" | custom-call | flops 12884901888 | bytes 10485760 | tf_op jit(solution)/shard_map/project_blocks/pallas_call | solution.py:177
  170.0 1.9 collective-permute-start.16
  173.4 6.5 %collective-permute-done.16.rest_3_ = bf16[8,2,16,512]{3,2,1,0:T(8,128)(2,1)S(1)} collective-permute-done((bf16[8,2,16,512]{3,2,1,0:T(8,128)(2,1)S(1)}, bf16[8,2,16,512]{3,2,1,0:T(8,128)(2,1)S(1)}, u32[]{:S(2)}, u32[]{:S(2)}) %collective-permute-start.16) | collective-permute-done | bytes 262176 | tf_op jit(solution)/shard_map/ppermute | solution.py:383
  179.8 3.5 %attend_prev.1 = bf16[8,192,256]{2,1,0:T(8,128)(2,1)} custom-call(s32[4]{0:T(128)S(1)} %pad_add_fusion.count_ref, bf16[192,256]{1,0:T(8,128)(2,1)S(1)} %pad_maximum_fusion.q_ref, bf16[8,2,16,512]{3,2,1,0:T(8,128)(2,1)S(1)} %get-tuple-element.63.rest_0_, bf16[8,2,16,512]{3,2,1,0:T(8,128)(2,1)S(1)} %get-tuple-element.64.rest_1_, ...), custom_call_target="tpu_custom_call" | custom-call | flops 402653184 | bytes 786432 | tf_op jit(solution)/shard_map/attend_prev/pallas_call | solution.py:276
  183.3 4.3 %all-to-all-start.4 = ((bf16[8,192,256]{2,1,0:T(8,128)(2,1)}), bf16[8,192,256]{2,1,0:T(8,128)(2,1)S(1)}, u32[]{:S(2)}, u32[]{:S(2)}) async-start(bf16[8,192,256]{2,1,0:T(8,128)(2,1)} %attend_prev.1), calls=%async_computation.4 | async-start | bytes 1572864 | tf_op jit(solution)/shard_map/all_to_all | solution.py:393
  187.7 21.7 %all-to-all-done.4.attended_ref = bf16[8,192,256]{2,1,0:T(8,128)(2,1)S(1)} async-done(((bf16[8,192,256]{2,1,0:T(8,128)(2,1)}), bf16[8,192,256]{2,1,0:T(8,128)(2,1)S(1)}, u32[]{:S(2)}, u32[]{:S(2)}) %all-to-all-start.4) | async-done | bytes 786464 | tf_op jit(solution)/shard_map/all_to_all | solution.py:393
  213.1 6.4 %project.1.rest_0_ = bf16[8,2,16,512]{3,2,1,0:T(8,128)(2,1)S(1)} custom-call(bf16[8,4,8,2,16,128]{5,4,3,2,1,0:T(8,128)(2,1)S(1)} %bitcast.24, bf16[8,512,512]{2,1,0:T(8,128)(2,1)} %multiply_convert_fusion.w_ref), custom_call_target="tpu_custom_call" | custom-call | flops 4294967296 | bytes 6291456 | tf_op jit(solution)/shard_map/project/pallas_call | solution.py:128
  220.4 13.9 %all_to_all.32.low_ref = bf16[8,64,256]{2,1,0:T(8,128)(2,1)S(1)} all-to-all(bf16[8,64,256]{2,1,0:T(8,128)(2,1)S(1)} %attend.1), channel_id=1, replica_groups=mesh['seq'=32,'tensor'=8] {'tensor'}, dimensions={0} | all-to-all | bytes 524288 | tf_op jit(solution)/shard_map/all_to_all | solution.py:398
  (105 shorter events, 40.2 us)
Async XLA Ops:
  6.5 165.9 %copy-start = (bf16[4096,256]{1,0:T(8,128)(2,1)S(1)}, bf16[4096,256]{1,0:T(8,128)(2,1)}, u32[]{:S(2)}) copy-start(bf16[4096,256]{1,0:T(8,128)(2,1)} %param.18) | copy-start | bytes 6291460
  6.5 64.0 %all-gather.4.cloned.1.call-start = ((), (), s32[]{:S(2)}) async-start(), calls=%async_computation.6 | async-start | bytes 2359296 | tf_op jit(solution)/shard_map/all_gather | solution.py:364
  31.1 35.8 %all-to-all-start = ((bf16[32,17,16,128]{3,2,1,0:T(8,128)(2,1)}), bf16[32,17,16,128]{3,2,1,0:T(8,128)(2,1)}, u32[]{:S(2)}, u32[]{:S(2)}) async-start(bf16[32,17,16,128]{3,2,1,0:T(8,128)(2,1)} %copy-done.1), calls=%async_computation | async-start | bytes 4456448 | tf_op jit(solution)/shard_map/all_to_all | solution.py:352
  38.6 114.1 %all-gather.6.cloned.1.call-start = ((), (), s32[]{:S(2)}) async-start(), calls=%async_computation.7 | async-start | bytes 2162688 | tf_op jit(solution)/shard_map/all_gather | solution.py:368
  89.0 12.0 %collective-permute-start.1 = (bf16[2,8,6,16,128]{4,3,2,1,0:T(8,128)(2,1)S(1)}, bf16[2,8,6,16,128]{4,3,2,1,0:T(8,128)(2,1)S(1)}, u32[]{:S(2)}, u32[]{:S(2)}) collective-permute-start(bf16[2,8,6,16,128]{4,3,2,1,0:T(8,128)(2,1)S(1)} %bitcast.20), channel_id=1, source_target_pairs={{0,7},{1,0},{2,1},{3,2},{4,3},{5,4},{6,5},{7,6},{8,15},{9,8},{10,9... | collective-permute-start | bytes 1179656 | tf_op jit(solution)/shard_map/ppermute | solution.py:212
  89.4 13.9 %collective-permute-start = (bf16[2,8,6,16,128]{4,3,2,1,0:T(8,128)(2,1)S(1)}, bf16[2,8,6,16,128]{4,3,2,1,0:T(8,128)(2,1)S(1)}, u32[]{:S(2)}, u32[]{:S(2)}) collective-permute-start(bf16[2,8,6,16,128]{4,3,2,1,0:T(8,128)(2,1)S(1)} %bitcast.21), channel_id=1, source_target_pairs={{0,1},{1,2},{2,3},{3,4},{4,5},{5,6},{6,7},{7,0},{8,9},{9,10},{10,1... | collective-permute-start | bytes 1179656 | tf_op jit(solution)/shard_map/ppermute | solution.py:211
  91.1 18.3 %collective-permute-start.3 = (bf16[2,8,6,16,128]{4,3,2,1,0:T(8,128)(2,1)S(1)}, bf16[2,8,6,16,128]{4,3,2,1,0:T(8,128)(2,1)S(1)}, u32[]{:S(2)}, u32[]{:S(2)}) collective-permute-start(bf16[2,8,6,16,128]{4,3,2,1,0:T(8,128)(2,1)S(1)} %bitcast.17), channel_id=1, source_target_pairs={{0,7},{1,0},{2,1},{3,2},{4,3},{5,4},{6,5},{7,6},{8,15},{9,8},{10,9... | collective-permute-start | bytes 1179656 | tf_op jit(solution)/shard_map/ppermute | solution.py:212
  92.6 19.1 %collective-permute-start.2 = (bf16[2,8,6,16,128]{4,3,2,1,0:T(8,128)(2,1)S(1)}, bf16[2,8,6,16,128]{4,3,2,1,0:T(8,128)(2,1)S(1)}, u32[]{:S(2)}, u32[]{:S(2)}) collective-permute-start(bf16[2,8,6,16,128]{4,3,2,1,0:T(8,128)(2,1)S(1)} %bitcast.18), channel_id=1, source_target_pairs={{0,1},{1,2},{2,3},{3,4},{4,5},{5,6},{6,7},{7,0},{8,9},{9,10},{10,1... | collective-permute-start | bytes 1179656 | tf_op jit(solution)/shard_map/ppermute | solution.py:211
  101.0 17.0 %collective-permute-start.5 = (bf16[2,8,6,16,128]{4,3,2,1,0:T(8,128)(2,1)S(1)}, bf16[2,8,6,16,128]{4,3,2,1,0:T(8,128)(2,1)}, u32[]{:S(2)}, u32[]{:S(2)}) collective-permute-start(bf16[2,8,6,16,128]{4,3,2,1,0:T(8,128)(2,1)S(1)} %collective-permute-done.1.rest_3_), channel_id=1, source_target_pairs={{0,7},{1,0},{2,1},{3,2},{4,3},{5,4},{6,5},{7,6},{8,15},{9,8},{10,9... | collective-permute-start | bytes 1179656 | tf_op jit(solution)/shard_map/ppermute | solution.py:212
  103.3 16.2 %collective-permute-start.4 = (bf16[2,8,6,16,128]{4,3,2,1,0:T(8,128)(2,1)S(1)}, bf16[2,8,6,16,128]{4,3,2,1,0:T(8,128)(2,1)}, u32[]{:S(2)}, u32[]{:S(2)}) collective-permute-start(bf16[2,8,6,16,128]{4,3,2,1,0:T(8,128)(2,1)S(1)} %collective-permute-done.rest_2_), channel_id=1, source_target_pairs={{0,1},{1,2},{2,3},{3,4},{4,5},{5,6},{6,7},{7,0},{8,9},{9,10},{10,1... | collective-permute-start | bytes 1179656 | tf_op jit(solution)/shard_map/ppermute | solution.py:211
  109.4 17.0 %collective-permute-start.7 = (bf16[2,8,6,16,128]{4,3,2,1,0:T(8,128)(2,1)S(1)}, bf16[2,8,6,16,128]{4,3,2,1,0:T(8,128)(2,1)}, u32[]{:S(2)}, u32[]{:S(2)}) collective-permute-start(bf16[2,8,6,16,128]{4,3,2,1,0:T(8,128)(2,1)S(1)} %collective-permute-done.3.rest_5_), channel_id=1, source_target_pairs={{0,7},{1,0},{2,1},{3,2},{4,3},{5,4},{6,5},{7,6},{8,15},{9,8},{10,9... | collective-permute-start | bytes 1179656 | tf_op jit(solution)/shard_map/ppermute | solution.py:212
  111.7 16.2 %collective-permute-start.6 = (bf16[2,8,6,16,128]{4,3,2,1,0:T(8,128)(2,1)S(1)}, bf16[2,8,6,16,128]{4,3,2,1,0:T(8,128)(2,1)}, u32[]{:S(2)}, u32[]{:S(2)}) collective-permute-start(bf16[2,8,6,16,128]{4,3,2,1,0:T(8,128)(2,1)S(1)} %collective-permute-done.2.rest_4_), channel_id=1, source_target_pairs={{0,1},{1,2},{2,3},{3,4},{4,5},{5,6},{6,7},{7,0},{8,9},{9,10},{10,1... | collective-permute-start | bytes 1179656 | tf_op jit(solution)/shard_map/ppermute | solution.py:211
  117.9 22.0 %collective-permute-start.9 = (bf16[2,8,6,16,128]{4,3,2,1,0:T(8,128)(2,1)}, bf16[2,8,6,16,128]{4,3,2,1,0:T(8,128)(2,1)}, u32[]{:S(2)}, u32[]{:S(2)}) collective-permute-start(bf16[2,8,6,16,128]{4,3,2,1,0:T(8,128)(2,1)} %collective-permute-done.5.rest_7_), channel_id=1, source_target_pairs={{0,7},{1,0},{2,1},{3,2},{4,3},{5,4},{6,5},{7,6},{8,15},{9,8},{10,9... | collective-permute-start | bytes 1179656 | tf_op jit(solution)/shard_map/ppermute | solution.py:212
  119.5 24.7 %collective-permute-start.8 = (bf16[2,8,6,16,128]{4,3,2,1,0:T(8,128)(2,1)}, bf16[2,8,6,16,128]{4,3,2,1,0:T(8,128)(2,1)S(1)}, u32[]{:S(2)}, u32[]{:S(2)}) collective-permute-start(bf16[2,8,6,16,128]{4,3,2,1,0:T(8,128)(2,1)} %collective-permute-done.4.rest_6_), channel_id=1, source_target_pairs={{0,1},{1,2},{2,3},{3,4},{4,5},{5,6},{6,7},{7,0},{8,9},{9,10},{10,1... | collective-permute-start | bytes 1179656 | tf_op jit(solution)/shard_map/ppermute | solution.py:211
  126.4 18.5 %collective-permute-start.11 = (bf16[2,8,6,16,128]{4,3,2,1,0:T(8,128)(2,1)}, bf16[2,8,6,16,128]{4,3,2,1,0:T(8,128)(2,1)}, u32[]{:S(2)}, u32[]{:S(2)}) collective-permute-start(bf16[2,8,6,16,128]{4,3,2,1,0:T(8,128)(2,1)} %collective-permute-done.7.rest_9_), channel_id=1, source_target_pairs={{0,7},{1,0},{2,1},{3,2},{4,3},{5,4},{6,5},{7,6},{8,15},{9,8},{10,9... | collective-permute-start | bytes 1179656 | tf_op jit(solution)/shard_map/ppermute | solution.py:212
  127.9 21.8 %collective-permute-start.10 = (bf16[2,8,6,16,128]{4,3,2,1,0:T(8,128)(2,1)}, bf16[2,8,6,16,128]{4,3,2,1,0:T(8,128)(2,1)}, u32[]{:S(2)}, u32[]{:S(2)}) collective-permute-start(bf16[2,8,6,16,128]{4,3,2,1,0:T(8,128)(2,1)} %collective-permute-done.6.rest_8_), channel_id=1, source_target_pairs={{0,1},{1,2},{2,3},{3,4},{4,5},{5,6},{6,7},{7,0},{8,9},{9,10},{10,1... | collective-permute-start | bytes 1179656 | tf_op jit(solution)/shard_map/ppermute | solution.py:211
  128.5 24.2 %all-to-all-start.2 = ((bf16[32,2,16,128]{3,2,1,0:T(8,128)(2,1)}), bf16[32,2,16,128]{3,2,1,0:T(8,128)(2,1)}, u32[]{:S(2)}, u32[]{:S(2)}) async-start(bf16[32,2,16,128]{3,2,1,0:T(8,128)(2,1)} %get-tuple-element.42), calls=%async_computation.2 | async-start | bytes 524288 | tf_op jit(solution)/shard_map/all_to_all | solution.py:367
  135.6 76.0 %all-gather.8.cloned.1.call-start = ((), (), s32[]{:S(2)}) async-start(), calls=%async_computation.8 | async-start | bytes 2359296 | tf_op jit(solution)/shard_map/all_gather | solution.py:378
  141.5 11.2 %collective-permute-start.13 = (bf16[1,8,6,16,128]{4,3,2,1,0:T(8,128)(2,1)}, bf16[1,8,6,16,128]{4,3,2,1,0:T(8,128)(2,1)S(1)}, u32[]{:S(2)}, u32[]{:S(2)}) collective-permute-start(bf16[1,8,6,16,128]{4,3,2,1,0:T(8,128)(2,1)} %slice.75), channel_id=1, source_target_pairs={{0,7},{1,0},{2,1},{3,2},{4,3},{5,4},{6,5},{7,6},{8,15},{9,8},{10,9... | collective-permute-start | bytes 589832 | tf_op jit(solution)/shard_map/ppermute | solution.py:212
  144.9 8.2 %collective-permute-start.12 = (bf16[1,8,6,16,128]{4,3,2,1,0:T(8,128)(2,1)}, bf16[1,8,6,16,128]{4,3,2,1,0:T(8,128)(2,1)}, u32[]{:S(2)}, u32[]{:S(2)}) collective-permute-start(bf16[1,8,6,16,128]{4,3,2,1,0:T(8,128)(2,1)} %slice.74), channel_id=1, source_target_pairs={{0,1},{1,2},{2,3},{3,4},{4,5},{5,6},{6,7},{7,0},{8,9},{9,10},{10,1... | collective-permute-start | bytes 589832 | tf_op jit(solution)/shard_map/ppermute | solution.py:211
  146.5 7.5 %collective-permute-start.15 = (bf16[1,8,6,16,128]{4,3,2,1,0:T(8,128)(2,1)}, bf16[1,8,6,16,128]{4,3,2,1,0:T(8,128)(2,1)}, u32[]{:S(2)}, u32[]{:S(2)}) collective-permute-start(bf16[1,8,6,16,128]{4,3,2,1,0:T(8,128)(2,1)} %slice.77), channel_id=1, source_target_pairs={{0,7},{1,0},{2,1},{3,2},{4,3},{5,4},{6,5},{7,6},{8,15},{9,8},{10,9... | collective-permute-start | bytes 589832 | tf_op jit(solution)/shard_map/ppermute | solution.py:212
  151.4 7.6 %collective-permute-start.14 = (bf16[1,8,6,16,128]{4,3,2,1,0:T(8,128)(2,1)}, bf16[1,8,6,16,128]{4,3,2,1,0:T(8,128)(2,1)}, u32[]{:S(2)}, u32[]{:S(2)}) collective-permute-start(bf16[1,8,6,16,128]{4,3,2,1,0:T(8,128)(2,1)} %slice.76), channel_id=1, source_target_pairs={{0,1},{1,2},{2,3},{3,4},{4,5},{5,6},{6,7},{7,0},{8,9},{9,10},{10,1... | collective-permute-start | bytes 589832 | tf_op jit(solution)/shard_map/ppermute | solution.py:211
  170.0 9.8 %collective-permute-start.16 = (bf16[8,2,16,512]{3,2,1,0:T(8,128)(2,1)S(1)}, bf16[8,2,16,512]{3,2,1,0:T(8,128)(2,1)S(1)}, u32[]{:S(2)}, u32[]{:S(2)}) collective-permute-start(bf16[8,2,16,512]{3,2,1,0:T(8,128)(2,1)S(1)} %get-tuple-element.65.rest_2_), channel_id=1, source_target_pairs={{0,8},{8,16},{16,24},{24,32},{32,40},{40,48},{48,56},{56,64},{64,7... | collective-permute-start | bytes 786440 | tf_op jit(solution)/shard_map/ppermute | solution.py:383
  183.3 26.0 %all-to-all-start.4 = ((bf16[8,192,256]{2,1,0:T(8,128)(2,1)}), bf16[8,192,256]{2,1,0:T(8,128)(2,1)S(1)}, u32[]{:S(2)}, u32[]{:S(2)}) async-start(bf16[8,192,256]{2,1,0:T(8,128)(2,1)} %attend_prev.1), calls=%async_computation.4 | async-start | bytes 1572864 | tf_op jit(solution)/shard_map/all_to_all | solution.py:393
  (18 other events, 133.2 us)
Sparse Core Ops, SparseCore 0:
  9.2 45.3 all-gather.3
  57.0 52.2 all-gather.5
  152.8 45.7 all-gather.7

commit v4 on v3

--- a/solution.py
+++ b/solution.py
@@ -12,40 +12,83 @@
 PIECE_T = 16
 PIECE_F = 128
 FEW = 1
+PIECES_WO = 2
 VMEM_LIMIT = 48 * 1024 * 1024
 
 
-def rms_scale(rows, gain):
-    values = rows.astype(jnp.float32)
-    inverse = lax.rsqrt(jnp.mean(values * values, axis=-1, keepdims=True) + 1e-06)
-    return (values * inverse * gain.astype(jnp.float32)).astype(jnp.bfloat16)
-
-
-def cut_kernel(db_ref, note_ref, out_ref):
+def cut_kernel(shard_ref, row_ref, count_ref, db_ref, out_ref):
     shard = db_ref.shape[0]
     pieces_t = db_ref.shape[1] // PIECE_T
     pieces_f = db_ref.shape[2] // PIECE_F
+    spans, each = shard_ref.shape
+    lane = lax.broadcasted_iota(jnp.int32, (PIECE_T, PIECE_F), 1)
+    note = jnp.zeros((PIECE_T, PIECE_F), jnp.int32)
+    for span in range(spans):
+        for j in range(each):
+            at = span * each + j
+            note = jnp.where(lane == at, shard_ref[span, j], note)
+            note = jnp.where(lane == spans * each + at, row_ref[span, j], note)
+        note = jnp.where(lane == 2 * spans * each + span, count_ref[span], note)
+    note = note.astype(jnp.float32).astype(jnp.bfloat16)
     for f in range(pieces_f):
         for i in range(pieces_t):
             piece = f * pieces_t + i
             out_ref[piece, :shard] = db_ref[
                 :, i * PIECE_T : (i + 1) * PIECE_T, f * PIECE_F : (f + 1) * PIECE_F
             ]
-            out_ref[piece, shard] = note_ref[...]
-
-
-def cut(database, note):
+            out_ref[piece, shard] = note
+
+
+def cut(nbr_shard, nbr_row, nbr_count, database):
     shard, length, part = database.shape
     pieces = (length // PIECE_T) * (part // PIECE_F)
     vmem = pl.BlockSpec(memory_space=pltpu.VMEM)
     return pl.pallas_call(
         cut_kernel,
-        in_specs=[vmem] * 2,
+        in_specs=[pl.BlockSpec(memory_space=pltpu.SMEM)] * 3 + [vmem],
         out_specs=vmem,
         out_shape=jax.ShapeDtypeStruct((pieces, shard + 1, PIECE_T, PIECE_F), database.dtype),
         compiler_params=pltpu.CompilerParams(vmem_limit_bytes=VMEM_LIMIT),
         name="cut",
-    )(database, note)
+    )(nbr_shard, nbr_row, nbr_count, database)
+
+
+def query_kernel(shift, x_ref, gain_ref, wq_ref, out_ref):
+    groups, _, part = x_ref.shape
+    rows = out_ref.shape[0]
+    squares = jnp.zeros((rows, PIECE_F), jnp.float32)
+    for g in range(groups):
+        for f in range(0, part, PIECE_F):
+            wide = x_ref[g, :rows, f : f + PIECE_F].astype(jnp.float32)
+            squares = squares + wide * wide
+    mean = jnp.sum(squares, axis=1, keepdims=True) * (1.0 / (groups * part))
+    inverse = lax.rsqrt(mean + 1e-06)
+    total = jnp.zeros(out_ref.shape, jnp.float32)
+    for g in range(groups):
+        wide = x_ref[g, :rows, :].astype(jnp.float32)
+        normed = (wide * inverse * gain_ref[g].astype(jnp.float32)).astype(jnp.bfloat16)
+        total = total + jnp.dot(normed, wq_ref[g], preferred_element_type=jnp.float32)
+    total = pltpu.roll(total * HS ** (-0.5), rows - shift, 0)
+    out_ref[...] = total.astype(jnp.bfloat16)
+
+
+def query(x, gain, wq, rows, shift):
+    groups, _, part = x.shape
+    vmem = pl.BlockSpec(memory_space=pltpu.VMEM)
+    cols = wq.shape[1]
+    return pl.pallas_call(
+        functools.partial(query_kernel, shift),
+        in_specs=[vmem] * 3,
+        out_specs=vmem,
+        out_shape=jax.ShapeDtypeStruct((rows, cols), jnp.bfloat16),
+        compiler_params=pltpu.CompilerParams(vmem_limit_bytes=VMEM_LIMIT),
+        cost_estimate=pl.CostEstimate(
+            flops=8 * rows * groups * part * cols,
+            bytes_accessed=4 * groups * part * (rows + cols),
+            transcendentals=0,
+        ),
+        name="query",
+    )(x, gain.reshape(groups, 1, part), wq.reshape(groups, part, cols))
 
 
 def pick_kernel(index_ref, spread_ref, low_ref, high_ref):
@@ -95,57 +138,6 @@
     done = done.reshape(pieces_t, NB * len(out_refs), PIECE_T, done.shape[-1])
     for span, ref in enumerate(out_refs):
         ref[...] = done[:, span * NB : (span + 1) * NB]
-
-
-def project_kernel(x_ref, w_ref, *rest):
-    spans = len(rest) - 2
-    out_refs, (acc_ref, squares_ref) = rest[:spans], rest[spans:]
-    step = pl.program_id(0)
-    steps = pl.num_programs(0)
-    x, squares = unpack(x_ref.at[0])
-    term = jnp.dot(x, w_ref[0], preferred_element_type=jnp.float32)
-
-    @pl.when(step == 0)
-    def _():
-        acc_ref[...] = term
-        squares_ref[...] = squares
-
-    @pl.when(step > 0)
-    def _():
-        acc_ref[...] += term
-        squares_ref[...] += squares
-
-    @pl.when(step == steps - 1)
-    def _():
-        store_spans(acc_ref[...], squares_ref[...], steps * x.shape[1], out_refs)
-
-
-def project(x, weights):
-    steps, pieces_f, pieces_t, items, _, _ = x.shape
-    rows = pieces_t * items * PIECE_T
-    _, part, cols = weights.shape
-    span = jax.ShapeDtypeStruct((pieces_t, NB, PIECE_T, cols), jnp.bfloat16)
-    return pl.pallas_call(
-        project_kernel,
-        grid=(steps,),
-        in_specs=[
-            pl.BlockSpec((1,) + x.shape[1:], lambda t: (t, 0, 0, 0, 0, 0)),
-            pl.BlockSpec((1, part, cols), lambda t: (t, 0, 0)),
-        ],
-        out_specs=[pl.BlockSpec(span.shape, lambda t: (0, 0, 0, 0))] * (items // NB),
-        out_shape=[span] * (items // NB),
-        scratch_shapes=[
-            pltpu.VMEM((rows, cols), jnp.float32),
-            pltpu.VMEM((rows, PIECE_F), jnp.float32),
-        ],
-        compiler_params=pltpu.CompilerParams(vmem_limit_bytes=VMEM_LIMIT),
-        cost_estimate=pl.CostEstimate(
-            flops=8 * steps * rows * part * cols,
-            bytes_accessed=2 * steps * part * (rows + cols),
-            transcendentals=0,
-        ),
-        name="project",
-    )(x, weights)
 
 
 def project_blocks_kernel(places, where_ref, w_ref, *rest):
@@ -193,27 +185,34 @@
     )(where, weights, *blocks)
 
 
-def ring_gather(pair, me, n_ten):
+def ring_gather(streams, me, n_ten):
     right = [(i, (i + 1) % n_ten) for i in range(n_ten)]
     left = [(i, (i - 1) % n_ten) for i in range(n_ten)]
-    width = pair[0].shape[0]
+    width = streams[0].shape[0]
     last = n_ten // 2
-    go_right, go_left = list(pair), list(pair)
-    blocks, places = list(pair), [(0, 0), (0, width)]
-    marks = None
-    for step in range(1, last + 1):
-        half = width // 2 if step == last else 0
-        if half:
-            marks = go_right + go_left
-            go_right = [x[:half] for x in go_right]
-            go_left = [x[half:] for x in go_left]
-        for s in range(2):
+    go_right, go_left = list(streams), list(streams)
+    blocks = list(streams)
+    places = [(0, s * width) for s in range(len(streams))]
+    arrivals = []
+    for step in range(1, last):
+        for s in range(len(streams)):
             go_right[s] = lax.ppermute(go_right[s], "tensor", right)
             go_left[s] = lax.ppermute(go_left[s], "tensor", left)
             blocks += [go_right[s], go_left[s]]
-            places += [(n_ten - step, s * width), (step, s * width + half)]
+            places += [(n_ten - step, s * width), (step, s * width)]
+        arrivals.append(go_right + go_left)
+    if len(streams) == 2:
+        from_left, from_right, start = go_right[0], go_left[1], width
+    else:
+        start = width // 2
+        from_left, from_right = go_right[0][:start], go_left[0][start:]
+    blocks += [
+        lax.ppermute(from_left, "tensor", right),
+        lax.ppermute(from_right, "tensor", left),
+    ]
+    places += [(last, 0), (last, start)]
     where = (me + jnp.arange(n_ten, dtype=jnp.int32)) % n_ten
-    return blocks, places, where, marks
+    return blocks, places, where, arrivals
 
 
 def weigh(scores, count, keys_axis_owner):
@@ -288,10 +287,19 @@
     )(*operands)
 
 
-def sum_groups(attended_ref, wo_ref):
+def sum_groups(attended_ref, mail_ref):
     total = None
-    for g in range(wo_ref.shape[0]):
-        part = jnp.dot(attended_ref[g], wo_ref[g], preferred_element_type=jnp.float32)
+    per_group = PIECES_WO
+    first = mail_ref.shape[2] - per_group * attended_ref.shape[0]
+    depth = attended_ref.shape[2]
+    for g in range(attended_ref.shape[0]):
+        tiles = [
+            mail_ref[:, h, first + g * per_group + f].reshape(depth, PIECE_F)
+            for h in range(mail_ref.shape[1])
+            for f in range(per_group)
+        ]
+        wo = jnp.concatenate(tiles, axis=1)
+        part = jnp.dot(attended_ref[g], wo, preferred_element_type=jnp.float32)
         part = part.astype(jnp.bfloat16).astype(jnp.float32)
         total = part if total is None else total + part
     return total
@@ -301,13 +309,13 @@
     out_ref[...] = sum_groups(attended_ref, wo_ref)
 
 
-def output(attended, wo):
+def output(attended, wo, width):
     vmem = pl.BlockSpec(memory_space=pltpu.VMEM)
     return pl.pallas_call(
         output_kernel,
         in_specs=[vmem] * 2,
         out_specs=vmem,
-        out_shape=jax.ShapeDtypeStruct((attended.shape[1], wo.shape[2]), jnp.float32),
+        out_shape=jax.ShapeDtypeStruct((attended.shape[1], width), jnp.float32),
         compiler_params=pltpu.CompilerParams(vmem_limit_bytes=VMEM_LIMIT),
         name="output",
     )(attended, wo)
@@ -345,58 +353,67 @@
     seq_at = lax.axis_index("seq")
     me = lax.axis_index("tensor")
 
-    note = jnp.concatenate([nbr_shard.reshape(-1), nbr_row.reshape(-1), nbr_count])
-    n_notes = note.shape[0]
-    note = jnp.pad(note.astype(jnp.bfloat16)[None], ((0, PIECE_T - 1), (0, PIECE_F - n_notes)))
-    pieces = cut(database, note)
+    pieces = cut(nbr_shard, nbr_row, nbr_count, database)
     spread = lax.all_to_all(pieces, "seq", split_axis=0, concat_axis=0, tiled=True)
+    n_notes = 2 * items + span_dev
     notes = spread[:, per_shard, 0, :n_notes].astype(jnp.int32)
     index = notes[:, :items] * (per_shard + 1) + notes[:, items : 2 * items]
     prev_count = jnp.where(seq_at > 0, notes[jnp.maximum(seq_at - 1, 0), n_notes - 1], 0)
     low, high = pick(index, spread.reshape(n_seq * (per_shard + 1), PIECE_T, PIECE_F), few)
 
-    own_rows = wo.shape[0] // n_seq
-    wo_rows = lax.dynamic_slice_in_dim(wo, seq_at * own_rows, own_rows, axis=0)
-    wo_rows, _ = lax.optimization_barrier((wo_rows, pieces))
-    wo_rows = wo_rows.reshape(own_rows, n_ten, d_part).transpose(1, 0, 2)
-    wo_rows = lax.all_to_all(wo_rows, "tensor", split_axis=0, concat_axis=0, tiled=True)
-
-    whole = lax.all_gather(tokens, "tensor", axis=1, tiled=True)
-    low, high, whole = lax.optimization_barrier((low, high, whole))
-    high = lax.all_to_all(high, "seq", split_axis=0, concat_axis=0, tiled=True)
-    low = lax.all_to_all(low, "seq", split_axis=0, concat_axis=0, tiled=True)
-    wo_cols = lax.all_gather(wo_rows, "seq", axis=1, tiled=True)
+    halves = d_part // (PIECES_WO * PIECE_F)
+    strips = n_seq // halves
+    depth = wo.shape[0] // strips
+    own = wo.reshape(strips, depth, n_ten, halves, PIECES_WO * PIECE_F)
+    own = lax.dynamic_slice(
+        own,
+        (seq_at // halves, 0, 0, seq_at % halves, 0),
+        (1, depth, n_ten, 1, PIECES_WO * PIECE_F),
+    )
+    own = own.reshape(depth, n_ten, PIECES_WO * PIECE_F).transpose(1, 0, 2)
+    own = own.reshape(n_ten, depth // halves, d_part)
+    letters = jnp.broadcast_to(tokens[None], (n_ten,) + tokens.shape)
+    letters = jnp.concatenate([letters, own], axis=1)
+    letters, _ = lax.optimization_barrier((letters, pieces))
+    letters = lax.all_to_all(letters, "tensor", split_axis=0, concat_axis=0, tiled=True)
 
     both = jnp.concatenate([wk, wv], axis=1).astype(jnp.float32)
     both = (both * nbr_gain.astype(jnp.float32)[:, None]).astype(jnp.bfloat16)
     both = both.reshape(n_ten, d_part, both.shape[1])
-
+    high, both = lax.optimization_barrier((high, both))
+    high = lax.all_to_all(high, "seq", split_axis=0, concat_axis=0, tiled=True)
     high = high.reshape(pieces_f, pieces_t, items - few, PIECE_T, PIECE_F)
     streams = [high[: pieces_f // 2], high[pieces_f // 2 :]]
-    blocks, places, where, marks = ring_gather(streams, me, n_ten)
-    low, wo_cols, marks = lax.optimization_barrier((low, wo_cols, marks))
-    low_x = lax.all_gather(low, "tensor", axis=0, tiled=True)
-    low_x = low_x.reshape(n_ten, pieces_f, pieces_t, few, PIECE_T, PIECE_F)
-    whole, blocks = lax.optimization_barrier((whole, blocks))
-
+    streams, letters = lax.optimization_barrier((streams, letters))
+    blocks, places, where, arrivals = ring_gather(streams, me, n_ten)
+
+    letters, low, _ = lax.optimization_barrier((letters, low, arrivals[0]))
+    strip = letters[:, tok_dev:].reshape(n_ten, depth, PIECES_WO, PIECE_F)
+    strip = strip.transpose(0, 2, 1, 3).reshape(1, n_ten * PIECES_WO, depth, PIECE_F)
+    mail = jnp.concatenate([low, jnp.broadcast_to(strip, (n_seq,) + strip.shape[1:])], axis=1)
+    mail = lax.all_to_all(mail, "seq", split_axis=0, concat_axis=0, tiled=True)
+    low = mail[:, :few].reshape(pieces_f, pieces_t, few, PIECE_T, PIECE_F)
+    mail = mail.reshape(strips, halves, *mail.shape[1:])
+    queries = query(letters, x_gain, wq, tok_dev, shift)
+    split = FEW * span_len
+
+    low, queries, _ = lax.optimization_barrier((low, queries, arrivals[-1]))
+    low_blocks, low_places, _, low_arrivals = ring_gather([low], me, n_ten)
+
+    blocks, _ = lax.optimization_barrier((blocks, low_arrivals[0]))
     *middle, final = project_blocks(blocks, places, where, both)
     prev = lax.ppermute(final, "seq", [(i, i + 1) for i in range(n_seq - 1)])
-    normed = rms_scale(whole, x_gain)
-    queries = (jnp.dot(normed, wq, preferred_element_type=jnp.float32) * HS ** (-0.5)).astype(
-        jnp.bfloat16
-    )
-    queries = jnp.concatenate([queries[shift:], queries[:shift]], axis=0)
-    split = FEW * span_len
-
+    prev, _ = lax.optimization_barrier((prev, low_arrivals[1]))
     high_counts = jnp.concatenate([nbr_count[FEW:], prev_count[None]])
     high_rows = attend(high_counts, queries[split:], [*middle, final], prev, n_ten)
+    low_blocks, _ = lax.optimization_barrier((low_blocks, high_rows))
     high_rows = lax.all_to_all(high_rows, "tensor", split_axis=0, concat_axis=0, tiled=True)
-    high_sum = output(high_rows, wo_cols)
-
-    low_x, high_sum = lax.optimization_barrier((low_x, high_sum))
-    low_rows = attend(nbr_count[:FEW], queries[:split], project(low_x, both), None, n_ten)
+    high_sum = output(high_rows, mail, d_part)
+
+    low_spans = project_blocks(low_blocks, low_places, where, both)
+    low_rows = attend(nbr_count[:FEW], queries[:split], low_spans, None, n_ten)
     low_rows = lax.all_to_all(low_rows, "tensor", split_axis=0, concat_axis=0, tiled=True)
-    return finish(low_rows, high_sum, wo_cols, tokens, shift)
+    return finish(low_rows, high_sum, mail, tokens, shift)
 
 
 def solution(mesh):

time: 244 us -> 303 us (1.24)
  waiting for transfers between devices: 87.5 us -> 166 us
  blocking collectives: 49.3 us -> 0 us
  starting transfers between devices: 39.3 us -> 76.8 us
  between operations: 14 us -> 0.98 us
  local copies, waits for them, and re-layouts: 21.7 us -> 26.3 us
    all_to_all x1 -> x4, waiting for transfers between devices: 0.01 us -> 69.5 us  [the longest x1 52.6 us: body(): lax.all_to_all(letters, 'tensor', split_axis=0, concat_axis=0, tiled=True)]
    ppermute x8 -> x9, waiting for transfers between devices: 5.35 us -> 62.4 us  [ring_gather(): go_right[s] = lax.ppermute(go_right[s], 'tensor', right)]
    all_to_all x3 -> x0, blocking collectives: 49.3 us -> none  [the longest x1 18.3 us: body(): high = lax.all_to_all(high, 'seq', split_axis=0, concat_axis=0, tiled=True)]
    ppermute x8 -> x9, waiting for transfers between devices: 25 us -> 0.02 us  [ring_gather(): go_left[s] = lax.ppermute(go_left[s], 'tensor', left)]
    all_to_all x1, waiting for transfers between devices: 21.7 us -> 0.01 us  [body(): lax.all_to_all(high_rows, 'tensor', split_axis=0, concat_axis=0, tiled=True)]
    all_to_all x1 -> x4, starting transfers between devices: 7.11 us -> 26.4 us  [the longest x1 8.47 us: body(): lax.all_to_all(letters, 'tensor', split_axis=0, concat_axis=0, tiled=True)]
    ppermute x8 -> x9, starting transfers between devices: 14.1 us -> 25.7 us  [ring_gather(): go_left[s] = lax.ppermute(go_left[s], 'tensor', left)]
    ppermute x0 -> x4, waiting for transfers between devices: none -> 7.77 us  [the longest x2 7.77 us: ring_gather(): lax.ppermute(from_left, 'tensor', right)]
  transfers between devices with their start and end apart: 23 -> 29, of which waited for: 10 -> 16; matrix products, arithmetic and copies ran while one was open for 7% -> 4% of each run, Pallas kernels for 6% -> 2%
where the time goes in v4:
time: 303 us; the launch traced here: 301 us
  waiting for transfers between devices  166 us (55%)
  starting transfers between devices  76.8 us (25%)
  local copies, waits for them, and re-layouts  26.3 us (9%)
  Pallas kernels  22.7 us (7%)
  other arithmetic  8.13 us (3%)
    ppermute x9, waiting for transfers between devices, ring_gather(): go_right[s] = lax.ppermute(go_right[s], 'tensor', right)  62.4 us
    all_to_all x1, waiting for transfers between devices, body(): lax.all_to_all(letters, 'tensor', split_axis=0, concat_axis=0, tiled=True)  52.6 us
    ppermute x9, starting transfers between devices, ring_gather(): go_left[s] = lax.ppermute(go_left[s], 'tensor', left)  25.7 us
    all_to_all x1, waiting for transfers between devices, body(): lax.all_to_all(pieces, 'seq', split_axis=0, concat_axis=0, tiled=True)  24.2 us
    unnamed x54, local copies, waits for them, and re-layouts  19.3 us
    pallas_call x2, Pallas kernels, project_blocks(): pl.pallas_call(functools.partial(project_blocks_kernel, tuple(places)), i...  11.2 us
    all_to_all x1, waiting for transfers between devices, body(): lax.all_to_all(low_rows, 'tensor', split_axis=0, concat_axis=0, tiled=True)  10.3 us
    all_to_all x1, starting transfers between devices, body(): lax.all_to_all(letters, 'tensor', split_axis=0, concat_axis=0, tiled=True)  8.47 us
  transfers between devices with their start and end apart: 29, of which 16 were waited for; matrix products, arithmetic and copies ran while one was open for 4% of the time, Pallas kernels for 2%

profile of v4, /device:TPU:8, one launch (start us, length us, event | category | flops | bytes accessed | tf_op | source)
XLA Modules:
  0.0 301.3 jit_solution(4777247537421524489)
XLA Ops:
  6.1 7.7 %all-to-all-start = ((bf16[32,17,16,128]{3,2,1,0:T(8,128)(2,1)}), bf16[32,17,16,128]{3,2,1,0:T(8,128)(2,1)S(1)}, u32[]{:S(2)}, u32[]{:S(2)}) async-start(bf16[32,17,16,128]{3,2,1,0:T(8,128)(2,1)} %copy-done), calls=%async_computation | async-start | bytes 4456448 | tf_op jit(solution)/shard_map/all_to_all | solution.py:357
  13.9 4.1 %multiply_convert_fusion.w_ref = bf16[8,512,512]{2,1,0:T(8,128)(2,1)} fusion(bf16[8,512,256]{2,1,0:T(8,128)(2,1)} %bitcast.35, bf16[8,512,256]{2,1,0:T(8,128)(2,1)} %bitcast.36, f32[8,512]{1,0:T(8,128)S(1)} %reshape.55), kind=kLoop, calls=%fused_computation | loop fusion | flops 12582912 | bytes 8404992 | tf_op jit(solution)/shard_map/convert_element_type | solution.py:381
  17.9 24.2 %all-to-all-done = bf16[32,17,16,128]{3,2,1,0:T(8,128)(2,1)S(1)} async-done(((bf16[32,17,16,128]{3,2,1,0:T(8,128)(2,1)}), bf16[32,17,16,128]{3,2,1,0:T(8,128)(2,1)S(1)}, u32[]{:S(2)}, u32[]{:S(2)}) %all-to-all-start) | async-done | bytes 2228256 | tf_op jit(solution)/shard_map/all_to_all | solution.py:357
  44.9 7.1 %all-to-all-start.1 = ((bf16[32,6,16,128]{3,2,1,0:T(8,128)(2,1)}), bf16[32,6,16,128]{3,2,1,0:T(8,128)(2,1)S(1)}, u32[]{:S(2)}, u32[]{:S(2)}) async-start(bf16[32,6,16,128]{3,2,1,0:T(8,128)(2,1)} %get-tuple-element.47), calls=%async_computation.1 | async-start | bytes 1572864 | tf_op jit(solution)/shard_map/all_to_all | solution.py:384
  57.4 6.6 %all-to-all-done.1 = bf16[32,6,16,128]{3,2,1,0:T(8,128)(2,1)S(1)} async-done(((bf16[32,6,16,128]{3,2,1,0:T(8,128)(2,1)}), bf16[32,6,16,128]{3,2,1,0:T(8,128)(2,1)S(1)}, u32[]{:S(2)}, u32[]{:S(2)}) %all-to-all-start.1) | async-done | bytes 786464 | tf_op jit(solution)/shard_map/all_to_all | solution.py:384
  64.9 8.5 %all-to-all-start.2 = ((bf16[8,264,512]{2,1,0:T(8,128)(2,1)}), bf16[8,264,512]{2,1,0:T(8,128)(2,1)S(1)}, u32[]{:S(2)}, u32[]{:S(2)}) async-start(bf16[8,264,512]{2,1,0:T(8,128)(2,1)} %pad_maximum_fusion.1), calls=%async_computation.2 | async-start | bytes 4325376 | tf_op jit(solution)/shard_map/all_to_all | solution.py:378
  74.6 52.6 %all-to-all-done.2.x_ref = bf16[8,264,512]{2,1,0:T(8,128)(2,1)S(1)} async-done(((bf16[8,264,512]{2,1,0:T(8,128)(2,1)}), bf16[8,264,512]{2,1,0:T(8,128)(2,1)S(1)}, u32[]{:S(2)}, u32[]{:S(2)}) %all-to-all-start.2) | async-done | bytes 2162720 | tf_op jit(solution)/shard_map/all_to_all | solution.py:378
  132.6 7.9 %collective-permute-done.rest_2_ = bf16[2,8,6,16,128]{4,3,2,1,0:T(8,128)(2,1)S(1)} collective-permute-done((bf16[2,8,6,16,128]{4,3,2,1,0:T(8,128)(2,1)S(1)}, bf16[2,8,6,16,128]{4,3,2,1,0:T(8,128)(2,1)S(1)}, u32[]{:S(2)}, u32[]{:S(2)}) %collective-permute-start) | collective-permute-done | bytes 393248 | tf_op jit(solution)/shard_map/ppermute | solution.py:199
  140.5 7.6 %collective-permute-done.1.rest_4_ = bf16[2,8,6,16,128]{4,3,2,1,0:T(8,128)(2,1)} collective-permute-done((bf16[2,8,6,16,128]{4,3,2,1,0:T(8,128)(2,1)S(1)}, bf16[2,8,6,16,128]{4,3,2,1,0:T(8,128)(2,1)}, u32[]{:S(2)}, u32[]{:S(2)}) %collective-permute-start.1) | collective-permute-done | bytes 393248 | tf_op jit(solution)/shard_map/ppermute | solution.py:199
  151.1 5.6 %all-to-all-start.3 = ((bf16[32,18,16,128]{3,2,1,0:T(8,128)(2,1)}), bf16[32,18,16,128]{3,2,1,0:T(8,128)(2,1)S(1)}, u32[]{:S(2)}, u32[]{:S(2)}) async-start(bf16[32,18,16,128]{3,2,1,0:T(8,128)(2,1)} %pad_maximum_fusion), calls=%async_computation.3 | async-start | bytes 4718592 | tf_op jit(solution)/shard_map/all_to_all | solution.py:394
  163.2 6.8 %collective-permute-done.4.rest_6_ = bf16[2,8,6,16,128]{4,3,2,1,0:T(8,128)(2,1)} collective-permute-done((bf16[2,8,6,16,128]{4,3,2,1,0:T(8,128)(2,1)S(1)}, bf16[2,8,6,16,128]{4,3,2,1,0:T(8,128)(2,1)}, u32[]{:S(2)}, u32[]{:S(2)}) %collective-permute-start.4) | collective-permute-done | bytes 393248 | tf_op jit(solution)/shard_map/ppermute | solution.py:199
  170.0 3.5 %collective-permute-start.11 = (bf16[2,8,6,16,128]{4,3,2,1,0:T(8,128)(2,1)}, bf16[2,8,6,16,128]{4,3,2,1,0:T(8,128)(2,1)}, u32[]{:S(2)}, u32[]{:S(2)}) collective-permute-start(bf16[2,8,6,16,128]{4,3,2,1,0:T(8,128)(2,1)} %collective-permute-done.10.rest_9_), channel_id=1, source_target_pairs={{0,7},{1,0},{2,1},{3,2},{4,3},{5,4},{6,5},{7,6},{8,15},{9,8},{10,9... | collective-permute-start | bytes 1179656 | tf_op jit(solution)/shard_map/ppermute | solution.py:200
  173.5 4.9 %collective-permute-done.6.rest_8_ = bf16[2,8,6,16,128]{4,3,2,1,0:T(8,128)(2,1)} collective-permute-done((bf16[2,8,6,16,128]{4,3,2,1,0:T(8,128)(2,1)}, bf16[2,8,6,16,128]{4,3,2,1,0:T(8,128)(2,1)}, u32[]{:S(2)}, u32[]{:S(2)}) %collective-permute-start.6) | collective-permute-done | bytes 393248 | tf_op jit(solution)/shard_map/ppermute | solution.py:199
  178.5 3.5 %collective-permute-start.9 = (bf16[2,8,6,16,128]{4,3,2,1,0:T(8,128)(2,1)}, bf16[2,8,6,16,128]{4,3,2,1,0:T(8,128)(2,1)}, u32[]{:S(2)}, u32[]{:S(2)}) collective-permute-start(bf16[2,8,6,16,128]{4,3,2,1,0:T(8,128)(2,1)} %collective-permute-done.8.rest_7_), channel_id=1, source_target_pairs={{0,7},{1,0},{2,1},{3,2},{4,3},{5,4},{6,5},{7,6},{8,15},{9,8},{10,9... | collective-permute-start | bytes 1179656 | tf_op jit(solution)/shard_map/ppermute | solution.py:200
  182.0 4.9 %collective-permute-done.5.rest_10_ = bf16[2,8,6,16,128]{4,3,2,1,0:T(8,128)(2,1)} collective-permute-done((bf16[2,8,6,16,128]{4,3,2,1,0:T(8,128)(2,1)}, bf16[2,8,6,16,128]{4,3,2,1,0:T(8,128)(2,1)}, u32[]{:S(2)}, u32[]{:S(2)}) %collective-permute-start.5) | collective-permute-done | bytes 393248 | tf_op jit(solution)/shard_map/ppermute | solution.py:199
  195.3 3.5 %collective-permute-start.13 = (bf16[4,8,2,16,128]{4,3,2,1,0:T(8,128)(2,1)S(1)}, bf16[4,8,2,16,128]{4,3,2,1,0:T(8,128)(2,1)}, u32[]{:S(2)}, u32[]{:S(2)}) collective-permute-start(bf16[4,8,2,16,128]{4,3,2,1,0:T(8,128)(2,1)S(1)} %bitcast.31), channel_id=1, source_target_pairs={{0,7},{1,0},{2,1},{3,2},{4,3},{5,4},{6,5},{7,6},{8,15},{9,8},{10,9... | collective-permute-start | bytes 786440 | tf_op jit(solution)/shard_map/ppermute | solution.py:200
  198.8 4.9 %collective-permute-done.20.rest_14_ = bf16[2,8,6,16,128]{4,3,2,1,0:T(8,128)(2,1)} collective-permute-done((bf16[2,8,6,16,128]{4,3,2,1,0:T(8,128)(2,1)}, bf16[2,8,6,16,128]{4,3,2,1,0:T(8,128)(2,1)}, u32[]{:S(2)}, u32[]{:S(2)}) %collective-permute-start.20) | collective-permute-done | bytes 393248 | tf_op jit(solution)/shard_map/ppermute | solution.py:210
  203.7 4.8 %collective-permute-done.12.rest_1_ = bf16[4,8,2,16,128]{4,3,2,1,0:T(8,128)(2,1)} collective-permute-done((bf16[4,8,2,16,128]{4,3,2,1,0:T(8,128)(2,1)S(1)}, bf16[4,8,2,16,128]{4,3,2,1,0:T(8,128)(2,1)}, u32[]{:S(2)}, u32[]{:S(2)}) %collective-permute-start.12) | collective-permute-done | bytes 262176 | tf_op jit(solution)/shard_map/ppermute | solution.py:199
  210.6 7.6 %project_blocks.2 = (bf16[8,2,16,512]{3,2,1,0:T(8,128)(2,1)S(1)}, bf16[8,2,16,512]{3,2,1,0:T(8,128)(2,1)S(1)}, bf16[8,2,16,512]{3,2,1,0:T(8,128)(2,1)}) custom-call(s32[8]{0:T(128)S(1)} %and_select_fusion.where_ref, bf16[8,512,512]{2,1,0:T(8,128)(2,1)} %multiply_convert_fusion.w_ref, bf16[2,8,6,16,128]{4,3,2,1,0:T(8,128)(2,1)S(1)} %bitcast.29, ...), custom_call_target="tpu_custom_call" | custom-call | flops 12884901888 | bytes 10485760 | tf_op jit(solution)/shard_map/project_blocks/pallas_call | solution.py:169
  237.4 5.1 %all-to-all-start.5 = ((bf16[8,192,256]{2,1,0:T(8,128)(2,1)}), bf16[8,192,256]{2,1,0:T(8,128)(2,1)S(1)}, u32[]{:S(2)}, u32[]{:S(2)}) async-start(bf16[8,192,256]{2,1,0:T(8,128)(2,1)} %copy-done.1), calls=%async_computation.5 | async-start | bytes 1572864 | tf_op jit(solution)/shard_map/all_to_all | solution.py:410
  245.8 23.1 %collective-permute-done.16.rest_5_ = bf16[4,8,2,16,128]{4,3,2,1,0:T(8,128)(2,1)S(1)} collective-permute-done((bf16[4,8,2,16,128]{4,3,2,1,0:T(8,128)(2,1)}, bf16[4,8,2,16,128]{4,3,2,1,0:T(8,128)(2,1)S(1)}, u32[]{:S(2)}, u32[]{:S(2)}) %collective-permute-start.16) | collective-permute-done | bytes 262176 | tf_op jit(solution)/shard_map/ppermute | solution.py:199
  277.1 3.6 %project_blocks.3.rest_0_ = bf16[8,2,16,512]{3,2,1,0:T(8,128)(2,1)S(1)} custom-call(s32[8]{0:T(128)S(1)} %and_select_fusion.where_ref, bf16[8,512,512]{2,1,0:T(8,128)(2,1)} %multiply_convert_fusion.w_ref, bf16[4,8,2,16,128]{4,3,2,1,0:T(8,128)(2,1)S(1)} %bitcast.32, bf16[4,8,2,16,128]{4,3,2,1,0:T(8,128)(2,1)} %collective-permute-done.12.rest_1_, ...), custom_call_target="tpu_custom_call" | custom-call | flops 4294967296 | bytes 6291456 | tf_op jit(solution)/shard_map/project_blocks/pallas_call | solution.py:169
  282.2 5.2 %all-to-all-start.4 = ((bf16[8,64,256]{2,1,0:T(8,128)(2,1)}), bf16[8,64,256]{2,1,0:T(8,128)(2,1)}, u32[]{:S(2)}, u32[]{:S(2)}) async-start(bf16[8,64,256]{2,1,0:T(8,128)(2,1)} %attend.1), calls=%async_computation.4 | async-start | bytes 524288 | tf_op jit(solution)/shard_map/all_to_all | solution.py:415
  287.9 10.3 %all-to-all-done.4.low_ref = bf16[8,64,256]{2,1,0:T(8,128)(2,1)} async-done(((bf16[8,64,256]{2,1,0:T(8,128)(2,1)}), bf16[8,64,256]{2,1,0:T(8,128)(2,1)}, u32[]{:S(2)}, u32[]{:S(2)}) %all-to-all-start.4) | async-done | bytes 262176 | tf_op jit(solution)/shard_map/all_to_all | solution.py:415
  (124 shorter events, 76.8 us)
Async XLA Ops:
  6.1 35.9 %all-to-all-start = ((bf16[32,17,16,128]{3,2,1,0:T(8,128)(2,1)}), bf16[32,17,16,128]{3,2,1,0:T(8,128)(2,1)S(1)}, u32[]{:S(2)}, u32[]{:S(2)}) async-start(bf16[32,17,16,128]{3,2,1,0:T(8,128)(2,1)} %copy-done), calls=%async_computation | async-start | bytes 4456448 | tf_op jit(solution)/shard_map/all_to_all | solution.py:357
  44.9 19.2 %all-to-all-start.1 = ((bf16[32,6,16,128]{3,2,1,0:T(8,128)(2,1)}), bf16[32,6,16,128]{3,2,1,0:T(8,128)(2,1)S(1)}, u32[]{:S(2)}, u32[]{:S(2)}) async-start(bf16[32,6,16,128]{3,2,1,0:T(8,128)(2,1)} %get-tuple-element.47), calls=%async_computation.1 | async-start | bytes 1572864 | tf_op jit(solution)/shard_map/all_to_all | solution.py:384
  64.9 62.4 %all-to-all-start.2 = ((bf16[8,264,512]{2,1,0:T(8,128)(2,1)}), bf16[8,264,512]{2,1,0:T(8,128)(2,1)S(1)}, u32[]{:S(2)}, u32[]{:S(2)}) async-start(bf16[8,264,512]{2,1,0:T(8,128)(2,1)} %pad_maximum_fusion.1), calls=%async_computation.2 | async-start | bytes 4325376 | tf_op jit(solution)/shard_map/all_to_all | solution.py:378
  127.3 13.2 %collective-permute-start = (bf16[2,8,6,16,128]{4,3,2,1,0:T(8,128)(2,1)S(1)}, bf16[2,8,6,16,128]{4,3,2,1,0:T(8,128)(2,1)S(1)}, u32[]{:S(2)}, u32[]{:S(2)}) collective-permute-start(bf16[2,8,6,16,128]{4,3,2,1,0:T(8,128)(2,1)S(1)} %bitcast.27), channel_id=1, source_target_pairs={{0,1},{1,2},{2,3},{3,4},{4,5},{5,6},{6,7},{7,0},{8,9},{9,10},{10,1... | collective-permute-start | bytes 1179656 | tf_op jit(solution)/shard_map/ppermute | solution.py:199
  127.7 20.3 %collective-permute-start.1 = (bf16[2,8,6,16,128]{4,3,2,1,0:T(8,128)(2,1)S(1)}, bf16[2,8,6,16,128]{4,3,2,1,0:T(8,128)(2,1)}, u32[]{:S(2)}, u32[]{:S(2)}) collective-permute-start(bf16[2,8,6,16,128]{4,3,2,1,0:T(8,128)(2,1)S(1)} %bitcast.24), channel_id=1, source_target_pairs={{0,1},{1,2},{2,3},{3,4},{4,5},{5,6},{6,7},{7,0},{8,9},{9,10},{10,1... | collective-permute-start | bytes 1179656 | tf_op jit(solution)/shard_map/ppermute | solution.py:199
  128.3 19.8 %collective-permute-start.2 = (bf16[2,8,6,16,128]{4,3,2,1,0:T(8,128)(2,1)S(1)}, bf16[2,8,6,16,128]{4,3,2,1,0:T(8,128)(2,1)}, u32[]{:S(2)}, u32[]{:S(2)}) collective-permute-start(bf16[2,8,6,16,128]{4,3,2,1,0:T(8,128)(2,1)S(1)} %bitcast.28), channel_id=1, source_target_pairs={{0,7},{1,0},{2,1},{3,2},{4,3},{5,4},{6,5},{7,6},{8,15},{9,8},{10,9... | collective-permute-start | bytes 1179656 | tf_op jit(solution)/shard_map/ppermute | solution.py:200
  131.0 17.1 %collective-permute-start.3 = (bf16[2,8,6,16,128]{4,3,2,1,0:T(8,128)(2,1)S(1)}, bf16[2,8,6,16,128]{4,3,2,1,0:T(8,128)(2,1)S(1)}, u32[]{:S(2)}, u32[]{:S(2)}) collective-permute-start(bf16[2,8,6,16,128]{4,3,2,1,0:T(8,128)(2,1)S(1)} %bitcast.25), channel_id=1, source_target_pairs={{0,7},{1,0},{2,1},{3,2},{4,3},{5,4},{6,5},{7,6},{8,15},{9,8},{10,9... | collective-permute-start | bytes 1179656 | tf_op jit(solution)/shard_map/ppermute | solution.py:200
  151.1 43.7 %all-to-all-start.3 = ((bf16[32,18,16,128]{3,2,1,0:T(8,128)(2,1)}), bf16[32,18,16,128]{3,2,1,0:T(8,128)(2,1)S(1)}, u32[]{:S(2)}, u32[]{:S(2)}) async-start(bf16[32,18,16,128]{3,2,1,0:T(8,128)(2,1)} %pad_maximum_fusion), calls=%async_computation.3 | async-start | bytes 4718592 | tf_op jit(solution)/shard_map/all_to_all | solution.py:394
  156.7 13.4 %collective-permute-start.4 = (bf16[2,8,6,16,128]{4,3,2,1,0:T(8,128)(2,1)S(1)}, bf16[2,8,6,16,128]{4,3,2,1,0:T(8,128)(2,1)}, u32[]{:S(2)}, u32[]{:S(2)}) collective-permute-start(bf16[2,8,6,16,128]{4,3,2,1,0:T(8,128)(2,1)S(1)} %copy-done.15), channel_id=1, source_target_pairs={{0,1},{1,2},{2,3},{3,4},{4,5},{5,6},{6,7},{7,0},{8,9},{9,10},{10,1... | collective-permute-start | bytes 1179656 | tf_op jit(solution)/shard_map/ppermute | solution.py:199
  156.8 13.3 %collective-permute-start.10 = (bf16[2,8,6,16,128]{4,3,2,1,0:T(8,128)(2,1)}, bf16[2,8,6,16,128]{4,3,2,1,0:T(8,128)(2,1)}, u32[]{:S(2)}, u32[]{:S(2)}) collective-permute-start(bf16[2,8,6,16,128]{4,3,2,1,0:T(8,128)(2,1)} %copy-done.17), channel_id=1, source_target_pairs={{0,7},{1,0},{2,1},{3,2},{4,3},{5,4},{6,5},{7,6},{8,15},{9,8},{10,9... | collective-permute-start | bytes 1179656 | tf_op jit(solution)/shard_map/ppermute | solution.py:200
  160.0 18.5 %collective-permute-start.6 = (bf16[2,8,6,16,128]{4,3,2,1,0:T(8,128)(2,1)}, bf16[2,8,6,16,128]{4,3,2,1,0:T(8,128)(2,1)}, u32[]{:S(2)}, u32[]{:S(2)}) collective-permute-start(bf16[2,8,6,16,128]{4,3,2,1,0:T(8,128)(2,1)} %collective-permute-done.1.rest_4_), channel_id=1, source_target_pairs={{0,1},{1,2},{2,3},{3,4},{4,5},{5,6},{6,7},{7,0},{8,9},{9,10},{10,1... | collective-permute-start | bytes 1179656 | tf_op jit(solution)/shard_map/ppermute | solution.py:199
  160.0 18.5 %collective-permute-start.8 = (bf16[2,8,6,16,128]{4,3,2,1,0:T(8,128)(2,1)}, bf16[2,8,6,16,128]{4,3,2,1,0:T(8,128)(2,1)}, u32[]{:S(2)}, u32[]{:S(2)}) collective-permute-start(bf16[2,8,6,16,128]{4,3,2,1,0:T(8,128)(2,1)} %collective-permute-done.2.rest_3_), channel_id=1, source_target_pairs={{0,7},{1,0},{2,1},{3,2},{4,3},{5,4},{6,5},{7,6},{8,15},{9,8},{10,9... | collective-permute-start | bytes 1179656 | tf_op jit(solution)/shard_map/ppermute | solution.py:200
  170.0 16.9 %collective-permute-start.5 = (bf16[2,8,6,16,128]{4,3,2,1,0:T(8,128)(2,1)}, bf16[2,8,6,16,128]{4,3,2,1,0:T(8,128)(2,1)}, u32[]{:S(2)}, u32[]{:S(2)}) collective-permute-start(bf16[2,8,6,16,128]{4,3,2,1,0:T(8,128)(2,1)} %collective-permute-done.4.rest_6_), channel_id=1, source_target_pairs={{0,1},{1,2},{2,3},{3,4},{4,5},{5,6},{6,7},{7,0},{8,9},{9,10},{10,1... | collective-permute-start | bytes 1179656 | tf_op jit(solution)/shard_map/ppermute | solution.py:199
  170.0 16.9 %collective-permute-start.11 = (bf16[2,8,6,16,128]{4,3,2,1,0:T(8,128)(2,1)}, bf16[2,8,6,16,128]{4,3,2,1,0:T(8,128)(2,1)}, u32[]{:S(2)}, u32[]{:S(2)}) collective-permute-start(bf16[2,8,6,16,128]{4,3,2,1,0:T(8,128)(2,1)} %collective-permute-done.10.rest_9_), channel_id=1, source_target_pairs={{0,7},{1,0},{2,1},{3,2},{4,3},{5,4},{6,5},{7,6},{8,15},{9,8},{10,9... | collective-permute-start | bytes 1179656 | tf_op jit(solution)/shard_map/ppermute | solution.py:200
  178.5 16.9 %collective-permute-start.7 = (bf16[2,8,6,16,128]{4,3,2,1,0:T(8,128)(2,1)}, bf16[2,8,6,16,128]{4,3,2,1,0:T(8,128)(2,1)}, u32[]{:S(2)}, u32[]{:S(2)}) collective-permute-start(bf16[2,8,6,16,128]{4,3,2,1,0:T(8,128)(2,1)} %collective-permute-done.6.rest_8_), channel_id=1, source_target_pairs={{0,1},{1,2},{2,3},{3,4},{4,5},{5,6},{6,7},{7,0},{8,9},{9,10},{10,1... | collective-permute-start | bytes 1179656 | tf_op jit(solution)/shard_map/ppermute | solution.py:199
  178.5 16.8 %collective-permute-start.9 = (bf16[2,8,6,16,128]{4,3,2,1,0:T(8,128)(2,1)}, bf16[2,8,6,16,128]{4,3,2,1,0:T(8,128)(2,1)}, u32[]{:S(2)}, u32[]{:S(2)}) collective-permute-start(bf16[2,8,6,16,128]{4,3,2,1,0:T(8,128)(2,1)} %collective-permute-done.8.rest_7_), channel_id=1, source_target_pairs={{0,7},{1,0},{2,1},{3,2},{4,3},{5,4},{6,5},{7,6},{8,15},{9,8},{10,9... | collective-permute-start | bytes 1179656 | tf_op jit(solution)/shard_map/ppermute | solution.py:200
  186.9 16.9 %collective-permute-start.20 = (bf16[2,8,6,16,128]{4,3,2,1,0:T(8,128)(2,1)}, bf16[2,8,6,16,128]{4,3,2,1,0:T(8,128)(2,1)}, u32[]{:S(2)}, u32[]{:S(2)}) collective-permute-start(bf16[2,8,6,16,128]{4,3,2,1,0:T(8,128)(2,1)} %collective-permute-done.5.rest_10_), channel_id=1, source_target_pairs={{0,1},{1,2},{2,3},{3,4},{4,5},{5,6},{6,7},{7,0},{8,9},{9,10},{10,1... | collective-permute-start | bytes 1179656 | tf_op jit(solution)/shard_map/ppermute | solution.py:210
  186.9 16.8 %collective-permute-start.21 = (bf16[2,8,6,16,128]{4,3,2,1,0:T(8,128)(2,1)}, bf16[2,8,6,16,128]{4,3,2,1,0:T(8,128)(2,1)}, u32[]{:S(2)}, u32[]{:S(2)}) collective-permute-start(bf16[2,8,6,16,128]{4,3,2,1,0:T(8,128)(2,1)} %collective-permute-done.11.rest_13_), channel_id=1, source_target_pairs={{0,7},{1,0},{2,1},{3,2},{4,3},{5,4},{6,5},{7,6},{8,15},{9,8},{10,9... | collective-permute-start | bytes 1179656 | tf_op jit(solution)/shard_map/ppermute | solution.py:211
  195.3 13.3 %collective-permute-start.12 = (bf16[4,8,2,16,128]{4,3,2,1,0:T(8,128)(2,1)S(1)}, bf16[4,8,2,16,128]{4,3,2,1,0:T(8,128)(2,1)}, u32[]{:S(2)}, u32[]{:S(2)}) collective-permute-start(bf16[4,8,2,16,128]{4,3,2,1,0:T(8,128)(2,1)S(1)} %bitcast.30), channel_id=1, source_target_pairs={{0,1},{1,2},{2,3},{3,4},{4,5},{5,6},{6,7},{7,0},{8,9},{9,10},{10,1... | collective-permute-start | bytes 786440 | tf_op jit(solution)/shard_map/ppermute | solution.py:199
  195.3 13.3 %collective-permute-start.13 = (bf16[4,8,2,16,128]{4,3,2,1,0:T(8,128)(2,1)S(1)}, bf16[4,8,2,16,128]{4,3,2,1,0:T(8,128)(2,1)}, u32[]{:S(2)}, u32[]{:S(2)}) collective-permute-start(bf16[4,8,2,16,128]{4,3,2,1,0:T(8,128)(2,1)S(1)} %bitcast.31), channel_id=1, source_target_pairs={{0,7},{1,0},{2,1},{3,2},{4,3},{5,4},{6,5},{7,6},{8,15},{9,8},{10,9... | collective-permute-start | bytes 786440 | tf_op jit(solution)/shard_map/ppermute | solution.py:200
  237.4 44.7 %all-to-all-start.5 = ((bf16[8,192,256]{2,1,0:T(8,128)(2,1)}), bf16[8,192,256]{2,1,0:T(8,128)(2,1)S(1)}, u32[]{:S(2)}, u32[]{:S(2)}) async-start(bf16[8,192,256]{2,1,0:T(8,128)(2,1)} %copy-done.1), calls=%async_computation.5 | async-start | bytes 1572864 | tf_op jit(solution)/shard_map/all_to_all | solution.py:410
  242.6 26.3 %collective-permute-start.16 = (bf16[4,8,2,16,128]{4,3,2,1,0:T(8,128)(2,1)}, bf16[4,8,2,16,128]{4,3,2,1,0:T(8,128)(2,1)S(1)}, u32[]{:S(2)}, u32[]{:S(2)}) collective-permute-start(bf16[4,8,2,16,128]{4,3,2,1,0:T(8,128)(2,1)} %copy-done.19), channel_id=1, source_target_pairs={{0,1},{1,2},{2,3},{3,4},{4,5},{5,6},{6,7},{7,0},{8,9},{9,10},{10,1... | collective-permute-start | bytes 786440 | tf_op jit(solution)/shard_map/ppermute | solution.py:199
  244.6 24.4 %collective-permute-start.17 = (bf16[4,8,2,16,128]{4,3,2,1,0:T(8,128)(2,1)}, bf16[4,8,2,16,128]{4,3,2,1,0:T(8,128)(2,1)S(1)}, u32[]{:S(2)}, u32[]{:S(2)}) collective-permute-start(bf16[4,8,2,16,128]{4,3,2,1,0:T(8,128)(2,1)} %copy-done.21), channel_id=1, source_target_pairs={{0,7},{1,0},{2,1},{3,2},{4,3},{5,4},{6,5},{7,6},{8,15},{9,8},{10,9... | collective-permute-start | bytes 786440 | tf_op jit(solution)/shard_map/ppermute | solution.py:200
  282.2 16.0 %all-to-all-start.4 = ((bf16[8,64,256]{2,1,0:T(8,128)(2,1)}), bf16[8,64,256]{2,1,0:T(8,128)(2,1)}, u32[]{:S(2)}, u32[]{:S(2)}) async-start(bf16[8,64,256]{2,1,0:T(8,128)(2,1)} %attend.1), calls=%async_computation.4 | async-start | bytes 524288 | tf_op jit(solution)/shard_map/all_to_all | solution.py:415
  (31 other events, 177.1 us)

commit v5 on v4

v5 whole, which is shorter than its diff:
```python
import functools

import jax
import jax.numpy as jnp
from jax import lax
from jax.experimental import pallas as pl
from jax.experimental.pallas import tpu as pltpu
from jax.sharding import PartitionSpec as P

HS = 128
NB = 2
PIECE_T = 16
PIECE_F = 128
PIECES_WO = 2
RING_ORDER = (0, 7, 1, 6, 2, 5, 3, 4)
VMEM_LIMIT = 48 * 1024 * 1024


def cut_kernel(shard_ref, row_ref, count_ref, db_ref, out_ref):
    shard = db_ref.shape[0]
    pieces_t = db_ref.shape[1] // PIECE_T
    pieces_f = db_ref.shape[2] // PIECE_F
    spans, each = shard_ref.shape
    lane = lax.broadcasted_iota(jnp.int32, (PIECE_T, PIECE_F), 1)
    note = jnp.zeros((PIECE_T, PIECE_F), jnp.int32)
    for span in range(spans):
        for j in range(each):
            at = span * each + j
            note = jnp.where(lane == at, shard_ref[span, j], note)
            note = jnp.where(lane == spans * each + at, row_ref[span, j], note)
        note = jnp.where(lane == 2 * spans * each + span, count_ref[span], note)
    note = note.astype(jnp.float32).astype(jnp.bfloat16)
    for f in range(pieces_f):
        for i in range(pieces_t):
            piece = f * pieces_t + i
            out_ref[piece, :shard] = db_ref[
                :, i * PIECE_T : (i + 1) * PIECE_T, f * PIECE_F : (f + 1) * PIECE_F
            ]
            out_ref[piece, shard] = note


def cut(nbr_shard, nbr_row, nbr_count, database):
    shard, length, part = database.shape
    pieces = (length // PIECE_T) * (part // PIECE_F)
    vmem = pl.BlockSpec(memory_space=pltpu.VMEM)
    return pl.pallas_call(
        cut_kernel,
        in_specs=[pl.BlockSpec(memory_space=pltpu.SMEM)] * 3 + [vmem],
        out_specs=vmem,
        out_shape=jax.ShapeDtypeStruct((pieces, shard + 1, PIECE_T, PIECE_F), database.dtype),
        compiler_params=pltpu.CompilerParams(vmem_limit_bytes=VMEM_LIMIT),
        name="cut",
    )(nbr_shard, nbr_row, nbr_count, database)


def pick_kernel(index_ref, spread_ref, out_ref):
    n_seq, items = out_ref.shape[:2]

    def one(dest, carry):
        for j in range(items):
            out_ref[dest, j] = spread_ref[index_ref[dest, j]]
        return carry

    lax.fori_loop(0, n_seq, one, 0, unroll=2)


def pick(index, spread):
    vmem = pl.BlockSpec(memory_space=pltpu.VMEM)
    return pl.pallas_call(
        pick_kernel,
        in_specs=[pl.BlockSpec(memory_space=pltpu.SMEM), vmem],
        out_specs=vmem,
        out_shape=jax.ShapeDtypeStruct(index.shape + (PIECE_T, PIECE_F), spread.dtype),
        compiler_params=pltpu.CompilerParams(vmem_limit_bytes=VMEM_LIMIT),
        name="pick",
    )(index, spread)


def letter_kernel(at_ref, tokens_ref, wo_ref, out_ref):
    rows, part = tokens_ref.shape
    pieces_t = rows // PIECE_T
    pieces_f = part // PIECE_F
    for f in range(pieces_f):
        for i in range(pieces_t):
            out_ref[f * pieces_t + i] = tokens_ref[
                i * PIECE_T : (i + 1) * PIECE_T, f * PIECE_F : (f + 1) * PIECE_F
            ]
    strip = PIECES_WO * PIECE_F
    for group in range(wo_ref.shape[1] // part):
        for f in range(PIECES_WO):
            start = pl.multiple_of(group * part + at_ref[1] * strip + f * PIECE_F, PIECE_F)
            out_ref[pieces_f * pieces_t + group * PIECES_WO + f] = wo_ref[:, pl.ds(start, PIECE_F)]


def letter(at, tokens, wo, depth):
    rows, part = tokens.shape
    tiles = rows * part // (PIECE_T * PIECE_F) + wo.shape[1] // part * PIECES_WO
    return pl.pallas_call(
        letter_kernel,
        grid_spec=pltpu.PrefetchScalarGridSpec(
            num_scalar_prefetch=1,
            grid=(1,),
            in_specs=[
                pl.BlockSpec((rows, part), lambda g, at: (0, 0)),
                pl.BlockSpec((depth, wo.shape[1]), lambda g, at: (at[0], 0)),
            ],
            out_specs=pl.BlockSpec((tiles, PIECE_T, PIECE_F), lambda g, at: (0, 0, 0)),
        ),
        out_shape=jax.ShapeDtypeStruct((tiles, PIECE_T, PIECE_F), tokens.dtype),
        name="letter",
    )(at, tokens, wo)


def unpack(x_ref):
    features, pieces_t, items = x_ref.shape[:3]
    rows = pieces_t * items * PIECE_T
    pieces = [x_ref[f].reshape(rows, PIECE_F) for f in range(features)]
    squares = jnp.zeros((rows, PIECE_F), jnp.float32)
    for piece in pieces:
        wide = piece.astype(jnp.float32)
        squares = squares + wide * wide
    return jnp.concatenate(pieces, axis=1), squares


def store_spans(acc, squares, features, out_refs):
    mean = jnp.sum(squares, axis=1, keepdims=True) * (1.0 / features)
    done = (acc * lax.rsqrt(mean + 1e-06)).astype(jnp.bfloat16)
    pieces_t = out_refs[0].shape[0]
    done = done.reshape(pieces_t, NB * len(out_refs), PIECE_T, done.shape[-1])
    for span, ref in enumerate(out_refs):
        ref[...] = done[:, span * NB : (span + 1) * NB]


def query_kernel(shift, halved, where_ref, gain_ref, wq_ref, *rest):
    x_refs, (out_ref, strip_ref) = rest[:-2], rest[-2:]
    rows = out_ref.shape[0]
    groups, _, part = gain_ref.shape
    pieces_t = rows // PIECE_T
    tiles = pieces_t * (part // PIECE_F)
    whole = list(x_refs[:-2])

    def tile_rows(k, f):
        first = f * pieces_t
        if k < groups - 1:
            return x_refs[k][first : first + pieces_t].reshape(rows, PIECE_F)
        ref, start = (x_refs[-2], 0) if first < halved else (x_refs[-1], halved)
        return ref[first - start : first - start + pieces_t].reshape(rows, PIECE_F)

    squares = jnp.zeros((rows, PIECE_F), jnp.float32)
    for k in range(groups):
        for f in range(part // PIECE_F):
            wide = tile_rows(k, f).astype(jnp.float32)
            squares = squares + wide * wide
    mean = jnp.sum(squares, axis=1, keepdims=True) * (1.0 / (groups * part))
    inverse = lax.rsqrt(mean + 1e-06)
    total = jnp.zeros(out_ref.shape, jnp.float32)
    me = where_ref[0]
    for k in range(groups):
        group = where_ref[RING_ORDER[k]]
        x = jnp.concatenate([tile_rows(k, f) for f in range(part // PIECE_F)], axis=1)
        gain = gain_ref[group].astype(jnp.float32)
        normed = (x.astype(jnp.float32) * inverse * gain).astype(jnp.bfloat16)
        total = total + jnp.dot(normed, wq_ref[group], preferred_element_type=jnp.float32)
        for f in range(PIECES_WO):
            at = tiles + me * PIECES_WO + f
            ref = whole[k] if k < groups - 1 else x_refs[-1]
            at = at if k < groups - 1 else at - halved
            strip_ref[group * PIECES_WO + f] = ref[at]
    total = pltpu.roll(total * HS ** (-0.5), rows - shift, 0)
    out_ref[...] = total.astype(jnp.bfloat16)


def query(where, letters, gain, wq, rows, shift):
    groups = where.shape[0]
    part = wq.shape[0] // groups
    cols = wq.shape[1]
    vmem = pl.BlockSpec(memory_space=pltpu.VMEM)
    return pl.pallas_call(
        functools.partial(query_kernel, shift, letters[-2].shape[0]),
        in_specs=[pl.BlockSpec(memory_space=pltpu.SMEM)] + [vmem] * (2 + len(letters)),
        out_specs=[vmem] * 2,
        out_shape=[
            jax.ShapeDtypeStruct((rows, cols), jnp.bfloat16),
            jax.ShapeDtypeStruct((groups * PIECES_WO, PIECE_T, PIECE_F), jnp.bfloat16),
        ],
        compiler_params=pltpu.CompilerParams(vmem_limit_bytes=VMEM_LIMIT),
        cost_estimate=pl.CostEstimate(
            flops=8 * rows * groups * part * cols,
            bytes_accessed=4 * groups * part * (rows + cols),
            transcendentals=0,
        ),
        name="query",
    )(where, gain.reshape(groups, 1, part), wq.reshape(groups, part, cols), *letters)


def gather_kernel(places, first, last, where_ref, w_ref, *rest):
    count = len(places)
    x_refs, rest = rest[:count], rest[count:]
    if not first:
        acc, squares = rest[0][...], rest[1][...]
        rest = rest[2:]
    for at, (x_ref, (place, start)) in enumerate(zip(x_refs, places)):
        x, more = unpack(x_ref)
        lane = start * PIECE_F
        w = w_ref[where_ref[place], lane : lane + x.shape[1], :]
        term = jnp.dot(x, w, preferred_element_type=jnp.float32)
        if first and at == 0:
            acc, squares = term, more
        else:
            acc, squares = acc + term, squares + more
    if last:
        store_spans(acc, squares, w_ref.shape[0] * w_ref.shape[1], rest)
    else:
        rest[0][...] = acc
        rest[1][...] = squares


def gather_step(blocks, places, where, weights, state, last):
    _, part, cols = weights.shape
    _, pieces_t, items = blocks[0].shape[:3]
    rows = pieces_t * items * PIECE_T
    vmem = pl.BlockSpec(memory_space=pltpu.VMEM)
    if last:
        span = jax.ShapeDtypeStruct((pieces_t, NB, PIECE_T, cols), jnp.bfloat16)
        out_shape = [span] * (items // NB)
    else:
        out_shape = [
            jax.ShapeDtypeStruct((rows, cols), jnp.float32),
            jax.ShapeDtypeStruct((rows, PIECE_F), jnp.float32),
        ]
    return pl.pallas_call(
        functools.partial(gather_kernel, tuple(places), not state, last),
        in_specs=[pl.BlockSpec(memory_space=pltpu.SMEM)]
        + [vmem] * (1 + len(blocks) + len(state)),
        out_specs=[vmem] * len(out_shape),
        out_shape=out_shape,
        compiler_params=pltpu.CompilerParams(vmem_limit_bytes=VMEM_LIMIT),
        cost_estimate=pl.CostEstimate(
            flops=8 * rows * cols * sum(block.shape[0] for block in blocks) * PIECE_F,
            bytes_accessed=2 * sum(block.size for block in blocks) + 8 * rows * cols,
            transcendentals=0,
        ),
        name="gather_last" if last else "gather_step",
    )(where, weights, *blocks, *state)


def ring_ways(n_ten):
    right = [(i, (i + 1) % n_ten) for i in range(n_ten)]
    left = [(i, (i - 1) % n_ten) for i in range(n_ten)]
    return right, left


def ring_gather(block, n_ten, cut_at):
    right, left = ring_ways(n_ten)
    go_right = go_left = block
    blocks = [block]
    for _ in range(1, n_ten // 2):
        go_right = lax.ppermute(go_right, "tensor", right)
        go_left = lax.ppermute(go_left, "tensor", left)
        blocks += [go_right, go_left]
    return blocks + [
        lax.ppermute(go_right[:cut_at], "tensor", right),
        lax.ppermute(go_left[cut_at:], "tensor", left),
    ]


def ring_project(streams, where, weights, n_ten, beside):
    right, left = ring_ways(n_ten)
    width = streams[0].shape[0]
    go_right, go_left = list(streams), list(streams)
    state = gather_step(streams, [(0, 0), (0, width)], where, weights, (), False)
    for step in range(1, n_ten // 2):
        blocks, places = [], []
        for s in range(2):
            go_right[s] = lax.ppermute(go_right[s], "tensor", right)
            go_left[s] = lax.ppermute(go_left[s], "tensor", left)
            blocks += [go_right[s], go_left[s]]
            places += [(n_ten - step, s * width), (step, s * width)]
        state = gather_step(blocks, places, where, weights, state, False)
    from_left, from_right, beside = lax.optimization_barrier((go_right[0], go_left[1], beside))
    blocks = [
        lax.ppermute(from_left, "tensor", right),
        lax.ppermute(from_right, "tensor", left),
    ]
    places = [(n_ten // 2, 0), (n_ten // 2, width)]
    return gather_step(blocks, places, where, weights, state, True), beside


def weigh(scores, count, keys_axis_owner):
    scores = jnp.where(keys_axis_owner < count, scores, jnp.float32(-1e30))
    top = jnp.max(scores, axis=-1, keepdims=True)
    expo = jnp.exp(scores - top)
    return expo / jnp.sum(expo, axis=-1, keepdims=True)


def scores_of(queries, keys):
    return lax.dot_general(
        queries, keys, (((1,), (1,)), ((), ())), preferred_element_type=jnp.float32
    )


def attend_kernel(with_prev, span_len, count_ref, q_ref, *rest):
    out_ref = rest[-1]
    if with_prev:
        prev_ref, before_ref = rest[-3:-1]
        pair_refs = rest[:-3]
        done = before_ref.shape[0]
        out_ref[:done, :] = before_ref[...]
    else:
        pair_refs = rest[:-1]
        done = 0
    cols = out_ref.shape[1]
    heads = cols // HS
    spans = len(pair_refs)
    keys = pair_refs[0].shape[0] * pair_refs[0].shape[1] * pair_refs[0].shape[2]
    owner = (lax.broadcasted_iota(jnp.int32, (span_len, keys), 1) // PIECE_T) % NB
    row = lax.broadcasted_iota(jnp.int32, (span_len, keys), 0)
    for span in range(spans):
        pair = pair_refs[span][...].reshape(keys, 2 * cols)
        rows = slice(done + span * span_len, done + (span + 1) * span_len)
        queries = q_ref[rows, :]
        mixed_heads = []
        for head in range(heads):
            at = slice(head * HS, (head + 1) * HS)
            value_at = slice(cols + head * HS, cols + (head + 1) * HS)
            query = queries[:, at]
            scores = scores_of(query, pair[:, at])
            if with_prev:
                prev = prev_ref[...].reshape(keys, 2 * cols)
                own = row == 0
                scores = jnp.where(own, scores, scores_of(query, prev[:, at]))
                count = jnp.where(own, count_ref[span], count_ref[span + 1])
                weights = weigh(scores, count, owner)
                ours = jnp.where(own, weights, 0.0).astype(jnp.bfloat16)
                theirs = jnp.where(own, 0.0, weights).astype(jnp.bfloat16)
                result = jnp.dot(
                    ours, pair[:, value_at], preferred_element_type=jnp.float32
                ) + jnp.dot(theirs, prev[:, value_at], preferred_element_type=jnp.float32)
            else:
                weights = weigh(scores, count_ref[span], owner).astype(jnp.bfloat16)
                result = jnp.dot(
                    weights, pair[:, value_at], preferred_element_type=jnp.float32
                )
            mixed_heads.append(result.astype(jnp.bfloat16))
        out_ref[rows, :] = jnp.concatenate(mixed_heads, axis=1)


def attend(counts, queries, pairs, span_len, prev=None, before=None):
    cols = queries.shape[1]
    with_prev = prev is not None
    rows = len(pairs) * span_len + (before.shape[0] if with_prev else 0)
    operands = [counts, queries, *pairs] + ([prev, before] if with_prev else [])
    vmem = pl.BlockSpec(memory_space=pltpu.VMEM)
    return pl.pallas_call(
        functools.partial(attend_kernel, with_prev, span_len),
        in_specs=[pl.BlockSpec(memory_space=pltpu.SMEM)] + [vmem] * (len(operands) - 1),
        out_specs=vmem,
        out_shape=jax.ShapeDtypeStruct((rows, cols), jnp.bfloat16),
        compiler_params=pltpu.CompilerParams(vmem_limit_bytes=VMEM_LIMIT),
        cost_estimate=pl.CostEstimate(
            flops=32 * len(pairs) * span_len * 256 * cols,
            bytes_accessed=4 * rows * cols,
            transcendentals=0,
        ),
        name="attend_prev" if with_prev else "attend",
    )(*operands)


def finish_kernel(shift, where_ref, mail_ref, tokens_ref, *rest):
    attended_refs, out_ref = rest[:-1], rest[-1]
    groups = where_ref.shape[0]
    depth = attended_refs[0].shape[1]
    total = None
    for k in range(groups):
        group = where_ref[RING_ORDER[k]]
        if k < groups - 1:
            attended = attended_refs[k][...]
        else:
            attended = jnp.concatenate([ref[...] for ref in attended_refs[k:]], axis=0)
        tiles = [
            mail_ref[:, h, group * PIECES_WO + f].reshape(depth, PIECE_F)
            for h in range(mail_ref.shape[1])
            for f in range(PIECES_WO)
        ]
        wo = jnp.concatenate(tiles, axis=1)
        part = jnp.dot(attended, wo, preferred_element_type=jnp.float32)
        part = part.astype(jnp.bfloat16).astype(jnp.float32)
        total = part if total is None else total + part
    total = pltpu.roll(total, shift, 0)
    out_ref[...] = (tokens_ref[...].astype(jnp.float32) + total).astype(jnp.bfloat16)


def finish(where, mail, tokens, attended, shift):
    vmem = pl.BlockSpec(memory_space=pltpu.VMEM)
    return pl.pallas_call(
        functools.partial(finish_kernel, shift),
        in_specs=[pl.BlockSpec(memory_space=pltpu.SMEM)] + [vmem] * (2 + len(attended)),
        out_specs=vmem,
        out_shape=jax.ShapeDtypeStruct(tokens.shape, jnp.bfloat16),
        compiler_params=pltpu.CompilerParams(vmem_limit_bytes=VMEM_LIMIT),
        name="finish",
    )(where, mail, tokens, *attended)


def body(tokens, x_gain, nbr_gain, database, nbr_shard, nbr_row, nbr_count, wq, wk, wv, wo):
    n_seq = lax.axis_size("seq")
    n_ten = lax.axis_size("tensor")
    tok_dev = tokens.shape[0]
    span_dev = nbr_shard.shape[0]
    span_len = tok_dev // span_dev
    shift = span_len - 1
    per_shard, nbr_len, d_part = database.shape
    items = span_dev * NB
    pieces_t = nbr_len // PIECE_T
    pieces_f = d_part // PIECE_F
    seq_at = lax.axis_index("seq")
    me = lax.axis_index("tensor")
    where = ((me + jnp.arange(n_ten, dtype=jnp.int32)) % n_ten).astype(jnp.int32)

    pieces = cut(nbr_shard, nbr_row, nbr_count, database)
    spread = lax.all_to_all(pieces, "seq", split_axis=0, concat_axis=0, tiled=True)
    n_notes = 2 * items + span_dev
    notes = spread[:, per_shard, 0, :n_notes].astype(jnp.int32)
    index = notes[:, :items] * (per_shard + 1) + notes[:, items : 2 * items]
    prev_count = jnp.where(seq_at > 0, notes[jnp.maximum(seq_at - 1, 0), n_notes - 1], 0)
    picked = pick(index, spread.reshape(n_seq * (per_shard + 1), PIECE_T, PIECE_F))

    halves = d_part // (PIECES_WO * PIECE_F)
    strips = n_seq // halves
    own = jnp.stack([seq_at // halves, seq_at % halves]).astype(jnp.int32)
    own, _ = lax.optimization_barrier((own, pieces))
    mine = letter(own, tokens, wo, wo.shape[0] // strips)
    letters = ring_gather(mine, n_ten, tok_dev // PIECE_T * (pieces_f // 2))

    both = jnp.concatenate([wk, wv], axis=1).astype(jnp.float32)
    both = (both * nbr_gain.astype(jnp.float32)[:, None]).astype(jnp.bfloat16)
    both = both.reshape(n_ten, d_part, both.shape[1])
    picked, both = lax.optimization_barrier((picked, both))
    rows = lax.all_to_all(picked, "seq", split_axis=0, concat_axis=0, tiled=True)
    rows = rows.reshape(pieces_f, pieces_t, items, PIECE_T, PIECE_F)
    streams = [rows[: pieces_f // 2], rows[pieces_f // 2 :]]
    queries, strip = query(where, letters, x_gain, wq, tok_dev, shift)
    streams, queries, strip = lax.optimization_barrier((streams, queries, strip))
    mail = jnp.broadcast_to(strip[None], (n_seq,) + strip.shape)
    mail = lax.all_to_all(mail, "seq", split_axis=0, concat_axis=0, tiled=True)
    mail = mail.reshape(strips, halves, *strip.shape)

    pairs, mail = ring_project(streams, where, both, n_ten, mail)
    prev = lax.ppermute(pairs[-1], "seq", [(i, i + 1) for i in range(n_seq - 1)])
    attended = attend(nbr_count[:-1], queries, pairs[:-1], span_len)
    last_counts = jnp.stack([nbr_count[-1], prev_count])
    attended = attend(last_counts, queries, pairs[-1:], span_len, prev, attended)
    gathered = ring_gather(attended, n_ten, tok_dev // 2)
    return finish(where, mail, tokens, gathered, shift)


def solution(mesh):
    placed = (
        P("seq", "tensor"),
        P(),
        P(),
        P("seq", None, "tensor"),
        P("seq", None),
        P("seq", None),
        P("seq"),
        P(None, "tensor"),
        P(None, "tensor"),
        P(None, "tensor"),
        P("tensor", None),
    )
    return jax.shard_map(
        body, mesh=mesh, in_specs=placed, out_specs=P("seq", "tensor"), check_vma=False
    )
```

time: 303 us -> 223 us (0.74)
  waiting for transfers between devices: 166 us -> 82.9 us
  Pallas kernels: 22.7 us -> 32.5 us
  local copies, waits for them, and re-layouts: 26.3 us -> 20.3 us
    all_to_all x4 -> x1, waiting for transfers between devices: 69.5 us -> 0.01 us  [body(): lax.all_to_all(picked, 'seq', split_axis=0, concat_axis=0, tiled=True)]
    ppermute x23 -> x31, starting transfers between devices: 37.6 us -> 56.6 us  [the longest x6 23.2 us: ring_gather(): go_left = lax.ppermute(go_left, 'tensor', left)]
    all_to_all x4 -> x1, starting transfers between devices: 25.9 us -> 7.97 us  [body(): lax.all_to_all(picked, 'seq', split_axis=0, concat_axis=0, tiled=True)]
    all_to_all x1, waiting for transfers between devices: 24.2 us -> 8.1 us  [body(): lax.all_to_all(pieces, 'seq', split_axis=0, concat_axis=0, tiled=True)]
    pallas_call x6 -> x9, Pallas kernels: 17.5 us -> 27.3 us  [the longest x5 19.2 us: gather_step(): pl.pallas_call(functools.partial(gather_kernel, tuple(places), not state,...]
    unnamed x54 -> x46, local copies, waits for them, and re-layouts: 19.3 us -> 15.2 us
    reshape x4 -> x0, local copies, waits for them, and re-layouts: 3.4 us -> none  [the longest x1 3.34 us: body(): own = wo.reshape(strips, depth, n_ten, halves, PIECES_WO * PIECE_F)]
    concatenate x3 -> x0, other arithmetic: 3.37 us -> none  [the longest x1 1.68 us: body(): jnp.concatenate([low, jnp.broadcast_to(strip, (n_seq,) + strip.shape[1:])...]
  transfers between devices with their start and end apart: 29 -> 34, of which waited for: 16 -> 17; matrix products, arithmetic and copies ran while one was open for 4% -> 4% of each run, Pallas kernels for 2% -> 11%
where the time goes in v5:
time: 223 us; the launch traced here: 222 us
  waiting for transfers between devices  82.9 us (37%)
  starting transfers between devices  79.4 us (36%)
  Pallas kernels  32.5 us (15%)
  local copies, waits for them, and re-layouts  20.3 us (9%)
  other arithmetic  6.11 us (3%)
    ppermute x6, waiting for transfers between devices, ring_gather(): go_right = lax.ppermute(go_right, 'tensor', right)  24.9 us
    ppermute x6, starting transfers between devices, ring_gather(): go_left = lax.ppermute(go_left, 'tensor', left)  23.2 us
    ppermute x6, waiting for transfers between devices, ring_project(): go_right[s] = lax.ppermute(go_right[s], 'tensor', right)  20.5 us
    pallas_call x5, Pallas kernels, gather_step(): pl.pallas_call(functools.partial(gather_kernel, tuple(places), not state,...  19.2 us
    ppermute x6, starting transfers between devices, ring_project(): go_left[s] = lax.ppermute(go_left[s], 'tensor', left)  17.3 us
    unnamed x46, local copies, waits for them, and re-layouts  15.2 us
    ppermute x6, waiting for transfers between devices, ring_project(): go_left[s] = lax.ppermute(go_left[s], 'tensor', left)  10.7 us
    ppermute x2, waiting for transfers between devices, ring_gather(): lax.ppermute(go_right[:cut_at], 'tensor', right)  8.27 us
  transfers between devices with their start and end apart: 34, of which 17 were waited for; matrix products, arithmetic and copies ran while one was open for 4% of the time, Pallas kernels for 11%

profile of v5, /device:TPU:8, one launch (start us, length us, event | category | flops | bytes accessed | tf_op | source)
XLA Modules:
  0.0 222.2 jit_solution(823356395821118780)
XLA Ops:
  6.1 7.5 %all-to-all-start = ((bf16[32,17,16,128]{3,2,1,0:T(8,128)(2,1)}), bf16[32,17,16,128]{3,2,1,0:T(8,128)(2,1)S(1)}, u32[]{:S(2)}, u32[]{:S(2)}) async-start(bf16[32,17,16,128]{3,2,1,0:T(8,128)(2,1)} %copy-done), calls=%async_computation | async-start | bytes 4456448 | tf_op jit(solution)/shard_map/all_to_all | solution.py:421
  16.8 5.9 %collective-permute-start.1 = (bf16[80,16,128]{2,1,0:T(8,128)(2,1)}, bf16[80,16,128]{2,1,0:T(8,128)(2,1)S(1)}, u32[]{:S(2)}, u32[]{:S(2)}) collective-permute-start(bf16[80,16,128]{2,1,0:T(8,128)(2,1)} %letter.1.rest_0_), channel_id=1, source_target_pairs={{0,7},{1,0},{2,1},{3,2},{4,3},{5,4},{6,5},{7,6},{8,15},{9,8},{10,9... | collective-permute-start | bytes 983048 | tf_op jit(solution)/shard_map/ppermute | solution.py:259
  22.7 4.1 %multiply_convert_fusion.w_ref = bf16[8,512,512]{2,1,0:T(8,128)(2,1)} fusion(bf16[8,512,256]{2,1,0:T(8,128)(2,1)} %bitcast.24, bf16[8,512,256]{2,1,0:T(8,128)(2,1)} %bitcast.25, f32[8,512]{1,0:T(8,128)S(1)} %reshape.33), kind=kLoop, calls=%fused_computation | loop fusion | flops 12582912 | bytes 8404992 | tf_op jit(solution)/shard_map/convert_element_type | solution.py:436
  26.7 3.5 %collective-permute-done.1.rest_2_ = bf16[80,16,128]{2,1,0:T(8,128)(2,1)S(1)} collective-permute-done((bf16[80,16,128]{2,1,0:T(8,128)(2,1)}, bf16[80,16,128]{2,1,0:T(8,128)(2,1)S(1)}, u32[]{:S(2)}, u32[]{:S(2)}) %collective-permute-start.1) | collective-permute-done | bytes 327712 | tf_op jit(solution)/shard_map/ppermute | solution.py:259
  30.3 3.6 %collective-permute-start.3 = (bf16[80,16,128]{2,1,0:T(8,128)(2,1)S(1)}, bf16[80,16,128]{2,1,0:T(8,128)(2,1)S(1)}, u32[]{:S(2)}, u32[]{:S(2)}) collective-permute-start(bf16[80,16,128]{2,1,0:T(8,128)(2,1)S(1)} %collective-permute-done.1.rest_2_), channel_id=1, source_target_pairs={{0,7},{1,0},{2,1},{3,2},{4,3},{5,4},{6,5},{7,6},{8,15},{9,8},{10,9... | collective-permute-start | bytes 983048 | tf_op jit(solution)/shard_map/ppermute | solution.py:259
  33.8 8.1 %all-to-all-done = bf16[32,17,16,128]{3,2,1,0:T(8,128)(2,1)S(1)} async-done(((bf16[32,17,16,128]{3,2,1,0:T(8,128)(2,1)}), bf16[32,17,16,128]{3,2,1,0:T(8,128)(2,1)S(1)}, u32[]{:S(2)}, u32[]{:S(2)}) %all-to-all-start) | async-done | bytes 2228256 | tf_op jit(solution)/shard_map/all_to_all | solution.py:421
  44.8 8.0 %all-to-all-start.1 = ((bf16[32,8,16,128]{3,2,1,0:T(8,128)(2,1)}), bf16[32,8,16,128]{3,2,1,0:T(8,128)(2,1)}, u32[]{:S(2)}, u32[]{:S(2)}) async-start(bf16[32,8,16,128]{3,2,1,0:T(8,128)(2,1)} %pick.1), calls=%async_computation.1 | async-start | bytes 2097152 | tf_op jit(solution)/shard_map/all_to_all | solution.py:439
  54.8 4.0 %collective-permute-start.5 = (bf16[80,16,128]{2,1,0:T(8,128)(2,1)S(1)}, bf16[80,16,128]{2,1,0:T(8,128)(2,1)S(1)}, u32[]{:S(2)}, u32[]{:S(2)}) collective-permute-start(bf16[80,16,128]{2,1,0:T(8,128)(2,1)S(1)} %collective-permute-done.3.rest_4_), channel_id=1, source_target_pairs={{0,7},{1,0},{2,1},{3,2},{4,3},{5,4},{6,5},{7,6},{8,15},{9,8},{10,9... | collective-permute-start | bytes 983048 | tf_op jit(solution)/shard_map/ppermute | solution.py:259
  58.8 7.9 %collective-permute-done.2.rest_3_ = bf16[80,16,128]{2,1,0:T(8,128)(2,1)S(1)} collective-permute-done((bf16[80,16,128]{2,1,0:T(8,128)(2,1)S(1)}, bf16[80,16,128]{2,1,0:T(8,128)(2,1)S(1)}, u32[]{:S(2)}, u32[]{:S(2)}) %collective-permute-start.2) | collective-permute-done | bytes 327712 | tf_op jit(solution)/shard_map/ppermute | solution.py:258
  66.8 3.3 %collective-permute-start.7 = (bf16[48,16,128]{2,1,0:T(8,128)(2,1)S(1)}, bf16[48,16,128]{2,1,0:T(8,128)(2,1)S(1)}, u32[]{:S(2)}, u32[]{:S(2)}) collective-permute-start(bf16[48,16,128]{2,1,0:T(8,128)(2,1)S(1)} %slice.58), channel_id=1, source_target_pairs={{0,7},{1,0},{2,1},{3,2},{4,3},{5,4},{6,5},{7,6},{8,15},{9,8},{10,9... | collective-permute-start | bytes 589832 | tf_op jit(solution)/shard_map/ppermute | solution.py:263
  70.1 7.2 %collective-permute-done.4.rest_5_ = bf16[80,16,128]{2,1,0:T(8,128)(2,1)S(1)} collective-permute-done((bf16[80,16,128]{2,1,0:T(8,128)(2,1)S(1)}, bf16[80,16,128]{2,1,0:T(8,128)(2,1)S(1)}, u32[]{:S(2)}, u32[]{:S(2)}) %collective-permute-start.4) | collective-permute-done | bytes 327712 | tf_op jit(solution)/shard_map/ppermute | solution.py:258
  77.5 6.1 %collective-permute-done.6.rest_7_ = bf16[32,16,128]{2,1,0:T(8,128)(2,1)S(1)} collective-permute-done((bf16[32,16,128]{2,1,0:T(8,128)(2,1)S(1)}, bf16[32,16,128]{2,1,0:T(8,128)(2,1)S(1)}, u32[]{:S(2)}, u32[]{:S(2)}) %collective-permute-start.6) | collective-permute-done | bytes 131104 | tf_op jit(solution)/shard_map/ppermute | solution.py:262
  90.2 7.3 %all-to-all-start.2 = ((bf16[32,16,16,128]{3,2,1,0:T(8,128)(2,1)}), bf16[32,16,16,128]{3,2,1,0:T(8,128)(2,1)S(1)}, u32[]{:S(2)}, u32[]{:S(2)}) async-start(bf16[32,16,16,128]{3,2,1,0:T(8,128)(2,1)} %broadcast_in_dim.2), calls=%async_computation.2 | async-start | bytes 4194304 | tf_op jit(solution)/shard_map/all_to_all | solution.py:445
  102.9 10.7 %collective-permute-done.8.rest_0_ = bf16[2,8,8,16,128]{4,3,2,1,0:T(8,128)(2,1)S(1)} collective-permute-done((bf16[2,8,8,16,128]{4,3,2,1,0:T(8,128)(2,1)S(1)}, bf16[2,8,8,16,128]{4,3,2,1,0:T(8,128)(2,1)S(1)}, u32[]{:S(2)}, u32[]{:S(2)}) %collective-permute-start.8) | collective-permute-done | bytes 524320 | tf_op jit(solution)/shard_map/ppermute | solution.py:275
  116.9 7.5 %collective-permute-done.16.rest_1_ = bf16[2,8,8,16,128]{4,3,2,1,0:T(8,128)(2,1)S(1)} collective-permute-done((bf16[2,8,8,16,128]{4,3,2,1,0:T(8,128)(2,1)S(1)}, bf16[2,8,8,16,128]{4,3,2,1,0:T(8,128)(2,1)S(1)}, u32[]{:S(2)}, u32[]{:S(2)}) %collective-permute-start.16) | collective-permute-done | bytes 524320 | tf_op jit(solution)/shard_map/ppermute | solution.py:276
  124.4 3.7 %collective-permute-start.17 = (bf16[2,8,8,16,128]{4,3,2,1,0:T(8,128)(2,1)S(1)}, bf16[2,8,8,16,128]{4,3,2,1,0:T(8,128)(2,1)}, u32[]{:S(2)}, u32[]{:S(2)}) collective-permute-start(bf16[2,8,8,16,128]{4,3,2,1,0:T(8,128)(2,1)S(1)} %collective-permute-done.16.rest_1_), channel_id=1, source_target_pairs={{0,7},{1,0},{2,1},{3,2},{4,3},{5,4},{6,5},{7,6},{8,15},{9,8},{10,9... | collective-permute-start | bytes 1572872 | tf_op jit(solution)/shard_map/ppermute | solution.py:276
  128.1 8.0 %collective-permute-done.9.rest_0_ = bf16[2,8,8,16,128]{4,3,2,1,0:T(8,128)(2,1)S(1)} collective-permute-done((bf16[2,8,8,16,128]{4,3,2,1,0:T(8,128)(2,1)S(1)}, bf16[2,8,8,16,128]{4,3,2,1,0:T(8,128)(2,1)S(1)}, u32[]{:S(2)}, u32[]{:S(2)}) %collective-permute-start.9) | collective-permute-done | bytes 524320 | tf_op jit(solution)/shard_map/ppermute | solution.py:275
  146.9 3.8 %collective-permute-start.18 = (bf16[2,8,8,16,128]{4,3,2,1,0:T(8,128)(2,1)}, bf16[2,8,8,16,128]{4,3,2,1,0:T(8,128)(2,1)}, u32[]{:S(2)}, u32[]{:S(2)}) collective-permute-start(bf16[2,8,8,16,128]{4,3,2,1,0:T(8,128)(2,1)} %collective-permute-done.17.rest_1_), channel_id=1, source_target_pairs={{0,7},{1,0},{2,1},{3,2},{4,3},{5,4},{6,5},{7,6},{8,15},{9,8},{10,9... | collective-permute-start | bytes 1572872 | tf_op jit(solution)/shard_map/ppermute | solution.py:276
  150.7 4.2 %gather_step.5 = (f32[1024,512]{1,0:T(8,128)S(1)}, f32[1024,128]{1,0:T(8,128)S(1)}) custom-call(s32[8]{0:T(128)S(1)} %and_select_fusion.where_ref, bf16[8,512,512]{2,1,0:T(8,128)(2,1)} %multiply_convert_fusion.w_ref, bf16[2,8,8,16,128]{4,3,2,1,0:T(8,128)(2,1)S(1)} %collective-permute-done.8.rest_0_, ...), custom_call_target="tpu_custom_call" | custom-call | flops 4294967296 | bytes 6291456 | tf_op jit(solution)/shard_map/gather_step/pallas_call | solution.py:231
  163.6 4.5 %gather_step.6 = (f32[1024,512]{1,0:T(8,128)S(1)}, f32[1024,128]{1,0:T(8,128)S(1)}) custom-call(s32[8]{0:T(128)S(1)} %and_select_fusion.where_ref, bf16[8,512,512]{2,1,0:T(8,128)(2,1)} %multiply_convert_fusion.w_ref, bf16[2,8,8,16,128]{4,3,2,1,0:T(8,128)(2,1)S(1)} %copy-done.8, bf16[2,8,8,16,128]{4,3,2,1,0:T(8,128)(2,1)} %collective-permute-done.17.rest_1_, ...), custom_call_target="tpu_custom_call" | custom-call | flops 4294967296 | bytes 6291456 | tf_op jit(solution)/shard_map/gather_step/pallas_call | solution.py:231
  169.9 4.6 %gather_step.7 = (f32[1024,512]{1,0:T(8,128)S(1)}, f32[1024,128]{1,0:T(8,128)S(1)}) custom-call(s32[8]{0:T(128)S(1)} %and_select_fusion.where_ref, bf16[8,512,512]{2,1,0:T(8,128)(2,1)} %multiply_convert_fusion.w_ref, bf16[2,8,8,16,128]{4,3,2,1,0:T(8,128)(2,1)S(1)} %copy-done.12, bf16[2,8,8,16,128]{4,3,2,1,0:T(8,128)(2,1)} %collective-permute-done.18.rest_1_, ...), custom_call_target="tpu_custom_call" | custom-call | flops 4294967296 | bytes 6291456 | tf_op jit(solution)/shard_map/gather_step/pallas_call | solution.py:231
  174.5 5.7 %collective-permute-done.14.rest_0_ = bf16[2,8,8,16,128]{4,3,2,1,0:T(8,128)(2,1)S(1)} collective-permute-done((bf16[2,8,8,16,128]{4,3,2,1,0:T(8,128)(2,1)}, bf16[2,8,8,16,128]{4,3,2,1,0:T(8,128)(2,1)S(1)}, u32[]{:S(2)}, u32[]{:S(2)}) %collective-permute-start.14) | collective-permute-done | bytes 524320 | tf_op jit(solution)/shard_map/ppermute | solution.py:282
  198.4 3.8 %collective-permute-done.23.rest_1_ = bf16[256,256]{1,0:T(8,128)(2,1)S(1)} collective-permute-done((bf16[256,256]{1,0:T(8,128)(2,1)S(1)}, bf16[256,256]{1,0:T(8,128)(2,1)S(1)}, u32[]{:S(2)}, u32[]{:S(2)}) %collective-permute-start.23) | collective-permute-done | bytes 131104 | tf_op jit(solution)/shard_map/ppermute | solution.py:258
  214.7 3.3 %collective-permute-start.30 = (bf16[128,256]{1,0:T(8,128)(2,1)S(1)}, bf16[128,256]{1,0:T(8,128)(2,1)S(1)}, u32[]{:S(2)}, u32[]{:S(2)}) collective-permute-start(bf16[128,256]{1,0:T(8,128)(2,1)S(1)} %slice.60), channel_id=1, source_target_pairs={{0,7},{1,0},{2,1},{3,2},{4,3},{5,4},{6,5},{7,6},{8,15},{9,8},{10,9... | collective-permute-start | bytes 196616 | tf_op jit(solution)/shard_map/ppermute | solution.py:263
  (119 shorter events, 84.8 us)
Async XLA Ops:
  6.1 35.8 %all-to-all-start = ((bf16[32,17,16,128]{3,2,1,0:T(8,128)(2,1)}), bf16[32,17,16,128]{3,2,1,0:T(8,128)(2,1)S(1)}, u32[]{:S(2)}, u32[]{:S(2)}) async-start(bf16[32,17,16,128]{3,2,1,0:T(8,128)(2,1)} %copy-done), calls=%async_computation | async-start | bytes 4456448 | tf_op jit(solution)/shard_map/all_to_all | solution.py:421
  16.8 13.5 %collective-permute-start.1 = (bf16[80,16,128]{2,1,0:T(8,128)(2,1)}, bf16[80,16,128]{2,1,0:T(8,128)(2,1)S(1)}, u32[]{:S(2)}, u32[]{:S(2)}) collective-permute-start(bf16[80,16,128]{2,1,0:T(8,128)(2,1)} %letter.1.rest_0_), channel_id=1, source_target_pairs={{0,7},{1,0},{2,1},{3,2},{4,3},{5,4},{6,5},{7,6},{8,15},{9,8},{10,9... | collective-permute-start | bytes 983048 | tf_op jit(solution)/shard_map/ppermute | solution.py:259
  22.7 30.1 %collective-permute-start = (bf16[80,16,128]{2,1,0:T(8,128)(2,1)}, bf16[80,16,128]{2,1,0:T(8,128)(2,1)S(1)}, u32[]{:S(2)}, u32[]{:S(2)}) collective-permute-start(bf16[80,16,128]{2,1,0:T(8,128)(2,1)} %letter.1.rest_0_), channel_id=1, source_target_pairs={{0,1},{1,2},{2,3},{3,4},{4,5},{5,6},{6,7},{7,0},{8,9},{9,10},{10,1... | collective-permute-start | bytes 983048 | tf_op jit(solution)/shard_map/ppermute | solution.py:258
  30.3 24.5 %collective-permute-start.3 = (bf16[80,16,128]{2,1,0:T(8,128)(2,1)S(1)}, bf16[80,16,128]{2,1,0:T(8,128)(2,1)S(1)}, u32[]{:S(2)}, u32[]{:S(2)}) collective-permute-start(bf16[80,16,128]{2,1,0:T(8,128)(2,1)S(1)} %collective-permute-done.1.rest_2_), channel_id=1, source_target_pairs={{0,7},{1,0},{2,1},{3,2},{4,3},{5,4},{6,5},{7,6},{8,15},{9,8},{10,9... | collective-permute-start | bytes 983048 | tf_op jit(solution)/shard_map/ppermute | solution.py:259
  44.8 42.1 %all-to-all-start.1 = ((bf16[32,8,16,128]{3,2,1,0:T(8,128)(2,1)}), bf16[32,8,16,128]{3,2,1,0:T(8,128)(2,1)}, u32[]{:S(2)}, u32[]{:S(2)}) async-start(bf16[32,8,16,128]{3,2,1,0:T(8,128)(2,1)} %pick.1), calls=%async_computation.1 | async-start | bytes 2097152 | tf_op jit(solution)/shard_map/all_to_all | solution.py:439
  52.8 14.0 %collective-permute-start.2 = (bf16[80,16,128]{2,1,0:T(8,128)(2,1)S(1)}, bf16[80,16,128]{2,1,0:T(8,128)(2,1)S(1)}, u32[]{:S(2)}, u32[]{:S(2)}) collective-permute-start(bf16[80,16,128]{2,1,0:T(8,128)(2,1)S(1)} %collective-permute-done.rest_1_), channel_id=1, source_target_pairs={{0,1},{1,2},{2,3},{3,4},{4,5},{5,6},{6,7},{7,0},{8,9},{9,10},{10,1... | collective-permute-start | bytes 983048 | tf_op jit(solution)/shard_map/ppermute | solution.py:258
  54.8 12.0 %collective-permute-start.5 = (bf16[80,16,128]{2,1,0:T(8,128)(2,1)S(1)}, bf16[80,16,128]{2,1,0:T(8,128)(2,1)S(1)}, u32[]{:S(2)}, u32[]{:S(2)}) collective-permute-start(bf16[80,16,128]{2,1,0:T(8,128)(2,1)S(1)} %collective-permute-done.3.rest_4_), channel_id=1, source_target_pairs={{0,7},{1,0},{2,1},{3,2},{4,3},{5,4},{6,5},{7,6},{8,15},{9,8},{10,9... | collective-permute-start | bytes 983048 | tf_op jit(solution)/shard_map/ppermute | solution.py:259
  66.8 10.6 %collective-permute-start.4 = (bf16[80,16,128]{2,1,0:T(8,128)(2,1)S(1)}, bf16[80,16,128]{2,1,0:T(8,128)(2,1)S(1)}, u32[]{:S(2)}, u32[]{:S(2)}) collective-permute-start(bf16[80,16,128]{2,1,0:T(8,128)(2,1)S(1)} %collective-permute-done.2.rest_3_), channel_id=1, source_target_pairs={{0,1},{1,2},{2,3},{3,4},{4,5},{5,6},{6,7},{7,0},{8,9},{9,10},{10,1... | collective-permute-start | bytes 983048 | tf_op jit(solution)/shard_map/ppermute | solution.py:258
  66.8 16.8 %collective-permute-start.7 = (bf16[48,16,128]{2,1,0:T(8,128)(2,1)S(1)}, bf16[48,16,128]{2,1,0:T(8,128)(2,1)S(1)}, u32[]{:S(2)}, u32[]{:S(2)}) collective-permute-start(bf16[48,16,128]{2,1,0:T(8,128)(2,1)S(1)} %slice.58), channel_id=1, source_target_pairs={{0,7},{1,0},{2,1},{3,2},{4,3},{5,4},{6,5},{7,6},{8,15},{9,8},{10,9... | collective-permute-start | bytes 589832 | tf_op jit(solution)/shard_map/ppermute | solution.py:263
  90.2 69.1 %all-to-all-start.2 = ((bf16[32,16,16,128]{3,2,1,0:T(8,128)(2,1)}), bf16[32,16,16,128]{3,2,1,0:T(8,128)(2,1)S(1)}, u32[]{:S(2)}, u32[]{:S(2)}) async-start(bf16[32,16,16,128]{3,2,1,0:T(8,128)(2,1)} %broadcast_in_dim.2), calls=%async_computation.2 | async-start | bytes 4194304 | tf_op jit(solution)/shard_map/all_to_all | solution.py:445
  97.5 16.1 %collective-permute-start.8 = (bf16[2,8,8,16,128]{4,3,2,1,0:T(8,128)(2,1)S(1)}, bf16[2,8,8,16,128]{4,3,2,1,0:T(8,128)(2,1)S(1)}, u32[]{:S(2)}, u32[]{:S(2)}) collective-permute-start(bf16[2,8,8,16,128]{4,3,2,1,0:T(8,128)(2,1)S(1)} %bitcast.19), channel_id=1, source_target_pairs={{0,1},{1,2},{2,3},{3,4},{4,5},{5,6},{6,7},{7,0},{8,9},{9,10},{10,1... | collective-permute-start | bytes 1572872 | tf_op jit(solution)/shard_map/ppermute | solution.py:275
  97.6 16.0 %collective-permute-start.11 = (bf16[2,8,8,16,128]{4,3,2,1,0:T(8,128)(2,1)S(1)}, bf16[2,8,8,16,128]{4,3,2,1,0:T(8,128)(2,1)S(1)}, u32[]{:S(2)}, u32[]{:S(2)}) collective-permute-start(bf16[2,8,8,16,128]{4,3,2,1,0:T(8,128)(2,1)S(1)} %bitcast.16), channel_id=1, source_target_pairs={{0,7},{1,0},{2,1},{3,2},{4,3},{5,4},{6,5},{7,6},{8,15},{9,8},{10,9... | collective-permute-start | bytes 1572872 | tf_op jit(solution)/shard_map/ppermute | solution.py:276
  100.8 23.6 %collective-permute-start.16 = (bf16[2,8,8,16,128]{4,3,2,1,0:T(8,128)(2,1)S(1)}, bf16[2,8,8,16,128]{4,3,2,1,0:T(8,128)(2,1)S(1)}, u32[]{:S(2)}, u32[]{:S(2)}) collective-permute-start(bf16[2,8,8,16,128]{4,3,2,1,0:T(8,128)(2,1)S(1)} %bitcast.20), channel_id=1, source_target_pairs={{0,7},{1,0},{2,1},{3,2},{4,3},{5,4},{6,5},{7,6},{8,15},{9,8},{10,9... | collective-permute-start | bytes 1572872 | tf_op jit(solution)/shard_map/ppermute | solution.py:276
  100.9 27.2 %collective-permute-start.19 = (bf16[2,8,8,16,128]{4,3,2,1,0:T(8,128)(2,1)S(1)}, bf16[2,8,8,16,128]{4,3,2,1,0:T(8,128)(2,1)S(1)}, u32[]{:S(2)}, u32[]{:S(2)}) collective-permute-start(bf16[2,8,8,16,128]{4,3,2,1,0:T(8,128)(2,1)S(1)} %bitcast.17), channel_id=1, source_target_pairs={{0,1},{1,2},{2,3},{3,4},{4,5},{5,6},{6,7},{7,0},{8,9},{9,10},{10,1... | collective-permute-start | bytes 1572872 | tf_op jit(solution)/shard_map/ppermute | solution.py:275
  113.6 22.5 %collective-permute-start.9 = (bf16[2,8,8,16,128]{4,3,2,1,0:T(8,128)(2,1)S(1)}, bf16[2,8,8,16,128]{4,3,2,1,0:T(8,128)(2,1)S(1)}, u32[]{:S(2)}, u32[]{:S(2)}) collective-permute-start(bf16[2,8,8,16,128]{4,3,2,1,0:T(8,128)(2,1)S(1)} %collective-permute-done.8.rest_0_), channel_id=1, source_target_pairs={{0,1},{1,2},{2,3},{3,4},{4,5},{5,6},{6,7},{7,0},{8,9},{9,10},{10,1... | collective-permute-start | bytes 1572872 | tf_op jit(solution)/shard_map/ppermute | solution.py:275
  113.6 22.5 %collective-permute-start.12 = (bf16[2,8,8,16,128]{4,3,2,1,0:T(8,128)(2,1)S(1)}, bf16[2,8,8,16,128]{4,3,2,1,0:T(8,128)(2,1)S(1)}, u32[]{:S(2)}, u32[]{:S(2)}) collective-permute-start(bf16[2,8,8,16,128]{4,3,2,1,0:T(8,128)(2,1)S(1)} %collective-permute-done.11.rest_3_), channel_id=1, source_target_pairs={{0,7},{1,0},{2,1},{3,2},{4,3},{5,4},{6,5},{7,6},{8,15},{9,8},{10,9... | collective-permute-start | bytes 1572872 | tf_op jit(solution)/shard_map/ppermute | solution.py:276
  124.4 22.5 %collective-permute-start.17 = (bf16[2,8,8,16,128]{4,3,2,1,0:T(8,128)(2,1)S(1)}, bf16[2,8,8,16,128]{4,3,2,1,0:T(8,128)(2,1)}, u32[]{:S(2)}, u32[]{:S(2)}) collective-permute-start(bf16[2,8,8,16,128]{4,3,2,1,0:T(8,128)(2,1)S(1)} %collective-permute-done.16.rest_1_), channel_id=1, source_target_pairs={{0,7},{1,0},{2,1},{3,2},{4,3},{5,4},{6,5},{7,6},{8,15},{9,8},{10,9... | collective-permute-start | bytes 1572872 | tf_op jit(solution)/shard_map/ppermute | solution.py:276
  128.1 22.6 %collective-permute-start.20 = (bf16[2,8,8,16,128]{4,3,2,1,0:T(8,128)(2,1)S(1)}, bf16[2,8,8,16,128]{4,3,2,1,0:T(8,128)(2,1)}, u32[]{:S(2)}, u32[]{:S(2)}) collective-permute-start(bf16[2,8,8,16,128]{4,3,2,1,0:T(8,128)(2,1)S(1)} %collective-permute-done.19.rest_2_), channel_id=1, source_target_pairs={{0,1},{1,2},{2,3},{3,4},{4,5},{5,6},{6,7},{7,0},{8,9},{9,10},{10,1... | collective-permute-start | bytes 1572872 | tf_op jit(solution)/shard_map/ppermute | solution.py:275
  136.1 22.5 %collective-permute-start.10 = (bf16[2,8,8,16,128]{4,3,2,1,0:T(8,128)(2,1)S(1)}, bf16[2,8,8,16,128]{4,3,2,1,0:T(8,128)(2,1)S(1)}, u32[]{:S(2)}, u32[]{:S(2)}) collective-permute-start(bf16[2,8,8,16,128]{4,3,2,1,0:T(8,128)(2,1)S(1)} %collective-permute-done.9.rest_0_), channel_id=1, source_target_pairs={{0,1},{1,2},{2,3},{3,4},{4,5},{5,6},{6,7},{7,0},{8,9},{9,10},{10,1... | collective-permute-start | bytes 1572872 | tf_op jit(solution)/shard_map/ppermute | solution.py:275
  136.1 23.2 %collective-permute-start.13 = (bf16[2,8,8,16,128]{4,3,2,1,0:T(8,128)(2,1)S(1)}, bf16[2,8,8,16,128]{4,3,2,1,0:T(8,128)(2,1)}, u32[]{:S(2)}, u32[]{:S(2)}) collective-permute-start(bf16[2,8,8,16,128]{4,3,2,1,0:T(8,128)(2,1)S(1)} %collective-permute-done.12.rest_3_), channel_id=1, source_target_pairs={{0,7},{1,0},{2,1},{3,2},{4,3},{5,4},{6,5},{7,6},{8,15},{9,8},{10,9... | collective-permute-start | bytes 1572872 | tf_op jit(solution)/shard_map/ppermute | solution.py:276
  146.9 22.6 %collective-permute-start.18 = (bf16[2,8,8,16,128]{4,3,2,1,0:T(8,128)(2,1)}, bf16[2,8,8,16,128]{4,3,2,1,0:T(8,128)(2,1)}, u32[]{:S(2)}, u32[]{:S(2)}) collective-permute-start(bf16[2,8,8,16,128]{4,3,2,1,0:T(8,128)(2,1)} %collective-permute-done.17.rest_1_), channel_id=1, source_target_pairs={{0,7},{1,0},{2,1},{3,2},{4,3},{5,4},{6,5},{7,6},{8,15},{9,8},{10,9... | collective-permute-start | bytes 1572872 | tf_op jit(solution)/shard_map/ppermute | solution.py:276
  150.7 19.2 %collective-permute-start.21 = (bf16[2,8,8,16,128]{4,3,2,1,0:T(8,128)(2,1)}, bf16[2,8,8,16,128]{4,3,2,1,0:T(8,128)(2,1)}, u32[]{:S(2)}, u32[]{:S(2)}) collective-permute-start(bf16[2,8,8,16,128]{4,3,2,1,0:T(8,128)(2,1)} %collective-permute-done.20.rest_2_), channel_id=1, source_target_pairs={{0,1},{1,2},{2,3},{3,4},{4,5},{5,6},{6,7},{7,0},{8,9},{9,10},{10,1... | collective-permute-start | bytes 1572872 | tf_op jit(solution)/shard_map/ppermute | solution.py:275
  159.3 20.9 %collective-permute-start.14 = (bf16[2,8,8,16,128]{4,3,2,1,0:T(8,128)(2,1)}, bf16[2,8,8,16,128]{4,3,2,1,0:T(8,128)(2,1)S(1)}, u32[]{:S(2)}, u32[]{:S(2)}) collective-permute-start(bf16[2,8,8,16,128]{4,3,2,1,0:T(8,128)(2,1)} %copy-done.11), channel_id=1, source_target_pairs={{0,1},{1,2},{2,3},{3,4},{4,5},{5,6},{6,7},{7,0},{8,9},{9,10},{10,1... | collective-permute-start | bytes 1572872 | tf_op jit(solution)/shard_map/ppermute | solution.py:282
  159.3 20.9 %collective-permute-start.15 = (bf16[2,8,8,16,128]{4,3,2,1,0:T(8,128)(2,1)}, bf16[2,8,8,16,128]{4,3,2,1,0:T(8,128)(2,1)S(1)}, u32[]{:S(2)}, u32[]{:S(2)}) collective-permute-start(bf16[2,8,8,16,128]{4,3,2,1,0:T(8,128)(2,1)} %collective-permute-done.13.rest_3_), channel_id=1, source_target_pairs={{0,7},{1,0},{2,1},{3,2},{4,3},{5,4},{6,5},{7,6},{8,15},{9,8},{10,9... | collective-permute-start | bytes 1572872 | tf_op jit(solution)/shard_map/ppermute | solution.py:283
  (32 other events, 244.7 us)

commit v6 on v5

--- a/solution.py
+++ b/solution.py
@@ -20,14 +20,14 @@
     shard = db_ref.shape[0]
     pieces_t = db_ref.shape[1] // PIECE_T
     pieces_f = db_ref.shape[2] // PIECE_F
-    spans, each = shard_ref.shape
+    each, spans = shard_ref.shape
     lane = lax.broadcasted_iota(jnp.int32, (PIECE_T, PIECE_F), 1)
     note = jnp.zeros((PIECE_T, PIECE_F), jnp.int32)
     for span in range(spans):
         for j in range(each):
             at = span * each + j
-            note = jnp.where(lane == at, shard_ref[span, j], note)
-            note = jnp.where(lane == spans * each + at, row_ref[span, j], note)
+            note = jnp.where(lane == at, shard_ref[j, span], note)
+            note = jnp.where(lane == spans * each + at, row_ref[j, span], note)
         note = jnp.where(lane == 2 * spans * each + span, count_ref[span], note)
     note = note.astype(jnp.float32).astype(jnp.bfloat16)
     for f in range(pieces_f):
@@ -50,27 +50,29 @@
         out_shape=jax.ShapeDtypeStruct((pieces, shard + 1, PIECE_T, PIECE_F), database.dtype),
         compiler_params=pltpu.CompilerParams(vmem_limit_bytes=VMEM_LIMIT),
         name="cut",
-    )(nbr_shard, nbr_row, nbr_count, database)
-
-
-def pick_kernel(index_ref, spread_ref, out_ref):
-    n_seq, items = out_ref.shape[:2]
+    )(nbr_shard.T, nbr_row.T, nbr_count, database)
+
+
+def pick_kernel(index_ref, spread_ref, *out_refs):
+    n_seq, items = out_refs[0].shape[:2]
 
     def one(dest, carry):
-        for j in range(items):
-            out_ref[dest, j] = spread_ref[index_ref[dest, j]]
+        for at, out_ref in enumerate(out_refs):
+            for j in range(items):
+                out_ref[dest, j] = spread_ref[index_ref[dest, at * items + j]]
         return carry
 
     lax.fori_loop(0, n_seq, one, 0, unroll=2)
 
 
-def pick(index, spread):
-    vmem = pl.BlockSpec(memory_space=pltpu.VMEM)
+def pick(index, spread, parts):
+    vmem = pl.BlockSpec(memory_space=pltpu.VMEM)
+    shape = (index.shape[0], index.shape[1] // parts, PIECE_T, PIECE_F)
     return pl.pallas_call(
         pick_kernel,
         in_specs=[pl.BlockSpec(memory_space=pltpu.SMEM), vmem],
-        out_specs=vmem,
-        out_shape=jax.ShapeDtypeStruct(index.shape + (PIECE_T, PIECE_F), spread.dtype),
+        out_specs=[vmem] * parts,
+        out_shape=[jax.ShapeDtypeStruct(shape, spread.dtype)] * parts,
         compiler_params=pltpu.CompilerParams(vmem_limit_bytes=VMEM_LIMIT),
         name="pick",
     )(index, spread)
@@ -165,12 +167,14 @@
             at = tiles + me * PIECES_WO + f
             ref = whole[k] if k < groups - 1 else x_refs[-1]
             at = at if k < groups - 1 else at - halved
-            strip_ref[group * PIECES_WO + f] = ref[at]
+            tile = ref[at]
+            for dest in range(strip_ref.shape[0]):
+                strip_ref[dest, group * PIECES_WO + f] = tile
     total = pltpu.roll(total * HS ** (-0.5), rows - shift, 0)
     out_ref[...] = total.astype(jnp.bfloat16)
 
 
-def query(where, letters, gain, wq, rows, shift):
+def query(where, letters, gain, wq, rows, shift, copies):
     groups = where.shape[0]
     part = wq.shape[0] // groups
     cols = wq.shape[1]
@@ -181,7 +185,7 @@
         out_specs=[vmem] * 2,
         out_shape=[
             jax.ShapeDtypeStruct((rows, cols), jnp.bfloat16),
-            jax.ShapeDtypeStruct((groups * PIECES_WO, PIECE_T, PIECE_F), jnp.bfloat16),
+            jax.ShapeDtypeStruct((copies, groups * PIECES_WO, PIECE_T, PIECE_F), jnp.bfloat16),
         ],
         compiler_params=pltpu.CompilerParams(vmem_limit_bytes=VMEM_LIMIT),
         cost_estimate=pl.CostEstimate(
@@ -264,26 +268,34 @@
     ]
 
 
-def ring_project(streams, where, weights, n_ten, beside):
+def ring_project(streams, where, weights, n_ten, send_beside):
     right, left = ring_ways(n_ten)
-    width = streams[0].shape[0]
+    half = streams[0].shape[0] // 2
     go_right, go_left = list(streams), list(streams)
-    state = gather_step(streams, [(0, 0), (0, width)], where, weights, (), False)
+    states = [gather_step([x], [(0, 0)], where, weights, (), False) for x in streams]
     for step in range(1, n_ten // 2):
-        blocks, places = [], []
-        for s in range(2):
+        for s in range(len(streams)):
             go_right[s] = lax.ppermute(go_right[s], "tensor", right)
             go_left[s] = lax.ppermute(go_left[s], "tensor", left)
-            blocks += [go_right[s], go_left[s]]
-            places += [(n_ten - step, s * width), (step, s * width)]
-        state = gather_step(blocks, places, where, weights, state, False)
-    from_left, from_right, beside = lax.optimization_barrier((go_right[0], go_left[1], beside))
-    blocks = [
-        lax.ppermute(from_left, "tensor", right),
-        lax.ppermute(from_right, "tensor", left),
-    ]
-    places = [(n_ten // 2, 0), (n_ten // 2, width)]
-    return gather_step(blocks, places, where, weights, state, True), beside
+            states[s] = gather_step(
+                [go_right[s], go_left[s]],
+                [(n_ten - step, 0), (step, 0)],
+                where,
+                weights,
+                states[s],
+                False,
+            )
+        if step == 1:
+            beside = send_beside(go_right[0])
+    places = [(n_ten // 2, 0), (n_ten // 2, half)]
+    for s in range(len(streams)):
+        from_left, from_right, beside = lax.optimization_barrier((go_right[s], go_left[s], beside))
+        blocks = [
+            lax.ppermute(from_left[:half], "tensor", right),
+            lax.ppermute(from_right[half:], "tensor", left),
+        ]
+        states[s] = gather_step(blocks, places, where, weights, states[s], True)
+    return states, beside
 
 
 def weigh(scores, count, keys_axis_owner):
@@ -299,16 +311,12 @@
     )
 
 
-def attend_kernel(with_prev, span_len, count_ref, q_ref, *rest):
+def attend_kernel(first, with_prev, span_len, count_ref, q_ref, *rest):
     out_ref = rest[-1]
-    if with_prev:
-        prev_ref, before_ref = rest[-3:-1]
-        pair_refs = rest[:-3]
-        done = before_ref.shape[0]
-        out_ref[:done, :] = before_ref[...]
-    else:
-        pair_refs = rest[:-1]
-        done = 0
+    pair_refs, other_ref = rest[:-2], rest[-2]
+    if not with_prev:
+        done = other_ref.shape[0]
+        out_ref[out_ref.shape[0] - done :, :] = other_ref[...]
     cols = out_ref.shape[1]
     heads = cols // HS
     spans = len(pair_refs)
@@ -317,19 +325,18 @@
     row = lax.broadcasted_iota(jnp.int32, (span_len, keys), 0)
     for span in range(spans):
         pair = pair_refs[span][...].reshape(keys, 2 * cols)
-        rows = slice(done + span * span_len, done + (span + 1) * span_len)
-        queries = q_ref[rows, :]
+        queries = q_ref[(first + span) * span_len : (first + span + 1) * span_len, :]
         mixed_heads = []
         for head in range(heads):
             at = slice(head * HS, (head + 1) * HS)
             value_at = slice(cols + head * HS, cols + (head + 1) * HS)
             query = queries[:, at]
             scores = scores_of(query, pair[:, at])
-            if with_prev:
-                prev = prev_ref[...].reshape(keys, 2 * cols)
+            if with_prev and span == spans - 1:
+                prev = other_ref[...].reshape(keys, 2 * cols)
                 own = row == 0
                 scores = jnp.where(own, scores, scores_of(query, prev[:, at]))
-                count = jnp.where(own, count_ref[span], count_ref[span + 1])
+                count = jnp.where(own, count_ref[first + span], count_ref[first + span + 1])
                 weights = weigh(scores, count, owner)
                 ours = jnp.where(own, weights, 0.0).astype(jnp.bfloat16)
                 theirs = jnp.where(own, 0.0, weights).astype(jnp.bfloat16)
@@ -337,22 +344,22 @@
                     ours, pair[:, value_at], preferred_element_type=jnp.float32
                 ) + jnp.dot(theirs, prev[:, value_at], preferred_element_type=jnp.float32)
             else:
-                weights = weigh(scores, count_ref[span], owner).astype(jnp.bfloat16)
+                weights = weigh(scores, count_ref[first + span], owner).astype(jnp.bfloat16)
                 result = jnp.dot(
                     weights, pair[:, value_at], preferred_element_type=jnp.float32
                 )
             mixed_heads.append(result.astype(jnp.bfloat16))
-        out_ref[rows, :] = jnp.concatenate(mixed_heads, axis=1)
-
-
-def attend(counts, queries, pairs, span_len, prev=None, before=None):
+        out_ref[span * span_len : (span + 1) * span_len, :] = jnp.concatenate(mixed_heads, axis=1)
+
+
+def attend(counts, queries, pairs, first, span_len, prev=None, after=None):
     cols = queries.shape[1]
     with_prev = prev is not None
-    rows = len(pairs) * span_len + (before.shape[0] if with_prev else 0)
-    operands = [counts, queries, *pairs] + ([prev, before] if with_prev else [])
-    vmem = pl.BlockSpec(memory_space=pltpu.VMEM)
-    return pl.pallas_call(
-        functools.partial(attend_kernel, with_prev, span_len),
+    rows = len(pairs) * span_len + (0 if with_prev else after.shape[0])
+    operands = [counts, queries, *pairs, prev if with_prev else after]
+    vmem = pl.BlockSpec(memory_space=pltpu.VMEM)
+    return pl.pallas_call(
+        functools.partial(attend_kernel, first, with_prev, span_len),
         in_specs=[pl.BlockSpec(memory_space=pltpu.SMEM)] + [vmem] * (len(operands) - 1),
         out_specs=vmem,
         out_shape=jax.ShapeDtypeStruct((rows, cols), jnp.bfloat16),
@@ -423,7 +430,7 @@
     notes = spread[:, per_shard, 0, :n_notes].astype(jnp.int32)
     index = notes[:, :items] * (per_shard + 1) + notes[:, items : 2 * items]
     prev_count = jnp.where(seq_at > 0, notes[jnp.maximum(seq_at - 1, 0), n_notes - 1], 0)
-    picked = pick(index, spread.reshape(n_seq * (per_shard + 1), PIECE_T, PIECE_F))
+    counts = jnp.concatenate([nbr_count, prev_count[None]])
 
     halves = d_part // (PIECES_WO * PIECE_F)
     strips = n_seq // halves
@@ -432,24 +439,31 @@
     mine = letter(own, tokens, wo, wo.shape[0] // strips)
     letters = ring_gather(mine, n_ten, tok_dev // PIECE_T * (pieces_f // 2))
 
+    spread, index, _ = lax.optimization_barrier((spread, index, letters[3:5]))
+    spread = spread.reshape(n_seq * (per_shard + 1), PIECE_T, PIECE_F)
+    low, high = pick(index, spread, 2)
+    nbr_gain, _ = lax.optimization_barrier((nbr_gain, high))
     both = jnp.concatenate([wk, wv], axis=1).astype(jnp.float32)
     both = (both * nbr_gain.astype(jnp.float32)[:, None]).astype(jnp.bfloat16)
     both = both.reshape(n_ten, d_part, both.shape[1])
-    picked, both = lax.optimization_barrier((picked, both))
-    rows = lax.all_to_all(picked, "seq", split_axis=0, concat_axis=0, tiled=True)
-    rows = rows.reshape(pieces_f, pieces_t, items, PIECE_T, PIECE_F)
-    streams = [rows[: pieces_f // 2], rows[pieces_f // 2 :]]
-    queries, strip = query(where, letters, x_gain, wq, tok_dev, shift)
-    streams, queries, strip = lax.optimization_barrier((streams, queries, strip))
-    mail = jnp.broadcast_to(strip[None], (n_seq,) + strip.shape)
-    mail = lax.all_to_all(mail, "seq", split_axis=0, concat_axis=0, tiled=True)
-    mail = mail.reshape(strips, halves, *strip.shape)
-
-    pairs, mail = ring_project(streams, where, both, n_ten, mail)
-    prev = lax.ppermute(pairs[-1], "seq", [(i, i + 1) for i in range(n_seq - 1)])
-    attended = attend(nbr_count[:-1], queries, pairs[:-1], span_len)
-    last_counts = jnp.stack([nbr_count[-1], prev_count])
-    attended = attend(last_counts, queries, pairs[-1:], span_len, prev, attended)
+    high = lax.all_to_all(high, "seq", split_axis=0, concat_axis=0, tiled=True)
+    high, low, letters, both, counts = lax.optimization_barrier(
+        (high, low, letters, both, counts)
+    )
+    low = lax.all_to_all(low, "seq", split_axis=0, concat_axis=0, tiled=True)
+    queries, strip = query(where, letters, x_gain, wq, tok_dev, shift, n_seq)
+
+    def send_mail(arrived):
+        mail, _ = lax.optimization_barrier((strip, arrived))
+        mail = lax.all_to_all(mail, "seq", split_axis=0, concat_axis=0, tiled=True)
+        return mail.reshape(strips, halves, *strip.shape[1:])
+
+    shape = (pieces_f, pieces_t, items // 2, PIECE_T, PIECE_F)
+    streams = [high.reshape(shape), low.reshape(shape)]
+    (late, early), mail = ring_project(streams, where, both, n_ten, send_mail)
+    prev = lax.ppermute(late[-1], "seq", [(i, i + 1) for i in range(n_seq - 1)])
+    attended = attend(counts, queries, late, span_dev // 2, span_len, prev=prev)
+    attended = attend(counts, queries, early, 0, span_len, after=attended)
     gathered = ring_gather(attended, n_ten, tok_dev // 2)
     return finish(where, mail, tokens, gathered, shift)
 

time: 223 us -> 210 us (0.942)
  waiting for transfers between devices: 82.9 us -> 54.1 us
  starting transfers between devices: 79.4 us -> 88.1 us
  Pallas kernels: 32.5 us -> 40.1 us
    ppermute x6, waiting for transfers between devices: 20.5 us -> 1.53 us  [ring_project(): go_right[s] = lax.ppermute(go_right[s], 'tensor', right)]
    ppermute x6, waiting for transfers between devices: 24.9 us -> 9.53 us  [ring_gather(): go_right = lax.ppermute(go_right, 'tensor', right)]
    ppermute x6, waiting for transfers between devices: 10.7 us -> 23.5 us  [ring_project(): go_left[s] = lax.ppermute(go_left[s], 'tensor', left)]
    ppermute x6, waiting for transfers between devices: 3.52 us -> 12.6 us  [ring_gather(): go_left = lax.ppermute(go_left, 'tensor', left)]
    all_to_all x1, waiting for transfers between devices: 8.1 us -> 0.01 us  [body(): lax.all_to_all(pieces, 'seq', split_axis=0, concat_axis=0, tiled=True)]
    pallas_call x5 -> x10, Pallas kernels: 19.2 us -> 25.4 us  [gather_step(): pl.pallas_call(functools.partial(gather_kernel, tuple(places), not state,...]
    all_to_all x2 -> x3, starting transfers between devices: 15.3 us -> 20.8 us  [the longest x1 7.39 us: body(): low = lax.all_to_all(low, 'seq', split_axis=0, concat_axis=0, tiled=True)]
    ppermute x2, waiting for transfers between devices: 8.27 us -> 2.95 us  [ring_gather(): lax.ppermute(go_right[:cut_at], 'tensor', right)]
  transfers between devices with their start and end apart: 34 -> 37, of which waited for: 17 -> 17; matrix products, arithmetic and copies ran while one was open for 4% -> 4% of each run, Pallas kernels for 11% -> 16%
where the time goes in v6:
time: 210 us; the launch traced here: 209 us
  starting transfers between devices  88.1 us (42%)
  waiting for transfers between devices  54.1 us (26%)
  Pallas kernels  40.1 us (19%)
  local copies, waits for them, and re-layouts  20.9 us (10%)
  other arithmetic  4.88 us (2%)
    pallas_call x10, Pallas kernels, gather_step(): pl.pallas_call(functools.partial(gather_kernel, tuple(places), not state,...  25.4 us
    ppermute x6, waiting for transfers between devices, ring_project(): go_left[s] = lax.ppermute(go_left[s], 'tensor', left)  23.5 us
    ppermute x6, starting transfers between devices, ring_gather(): go_left = lax.ppermute(go_left, 'tensor', left)  22.9 us
    ppermute x6, starting transfers between devices, ring_project(): go_left[s] = lax.ppermute(go_left[s], 'tensor', left)  19.4 us
    unnamed x60, local copies, waits for them, and re-layouts  18.2 us
    ppermute x6, waiting for transfers between devices, ring_gather(): go_left = lax.ppermute(go_left, 'tensor', left)  12.6 us
    ppermute x6, waiting for transfers between devices, ring_gather(): go_right = lax.ppermute(go_right, 'tensor', right)  9.53 us
    all_to_all x1, starting transfers between devices, body(): lax.all_to_all(pieces, 'seq', split_axis=0, concat_axis=0, tiled=True)  7.54 us
  transfers between devices with their start and end apart: 37, of which 17 were waited for; matrix products, arithmetic and copies ran while one was open for 4% of the time, Pallas kernels for 16%

profile of v6, /device:TPU:8, one launch (start us, length us, event | category | flops | bytes accessed | tf_op | source)
XLA Modules:
  0.0 209.3 jit_solution(1325458786354087382)
XLA Ops:
  5.9 7.5 %all-to-all-start = ((bf16[32,17,16,128]{3,2,1,0:T(8,128)(2,1)}), bf16[32,17,16,128]{3,2,1,0:T(8,128)(2,1)S(1)}, u32[]{:S(2)}, u32[]{:S(2)}) async-start(bf16[32,17,16,128]{3,2,1,0:T(8,128)(2,1)} %copy-done.1), calls=%async_computation | async-start | bytes 4456448 | tf_op jit(solution)/shard_map/all_to_all | solution.py:428
  16.5 5.9 %collective-permute-start.2 = (bf16[80,16,128]{2,1,0:T(8,128)(2,1)}, bf16[80,16,128]{2,1,0:T(8,128)(2,1)S(1)}, u32[]{:S(2)}, u32[]{:S(2)}) collective-permute-start(bf16[80,16,128]{2,1,0:T(8,128)(2,1)} %letter.1.rest_0_), channel_id=1, source_target_pairs={{0,7},{1,0},{2,1},{3,2},{4,3},{5,4},{6,5},{7,6},{8,15},{9,8},{10,9... | collective-permute-start | bytes 983048 | tf_op jit(solution)/shard_map/ppermute | solution.py:263
  22.4 7.6 %collective-permute-done.2.rest_2_ = bf16[80,16,128]{2,1,0:T(8,128)(2,1)S(1)} collective-permute-done((bf16[80,16,128]{2,1,0:T(8,128)(2,1)}, bf16[80,16,128]{2,1,0:T(8,128)(2,1)S(1)}, u32[]{:S(2)}, u32[]{:S(2)}) %collective-permute-start.2) | collective-permute-done | bytes 327712 | tf_op jit(solution)/shard_map/ppermute | solution.py:263
  30.0 3.6 %collective-permute-start.3 = (bf16[80,16,128]{2,1,0:T(8,128)(2,1)S(1)}, bf16[80,16,128]{2,1,0:T(8,128)(2,1)}, u32[]{:S(2)}, u32[]{:S(2)}) collective-permute-start(bf16[80,16,128]{2,1,0:T(8,128)(2,1)S(1)} %collective-permute-done.2.rest_2_), channel_id=1, source_target_pairs={{0,7},{1,0},{2,1},{3,2},{4,3},{5,4},{6,5},{7,6},{8,15},{9,8},{10,9... | collective-permute-start | bytes 983048 | tf_op jit(solution)/shard_map/ppermute | solution.py:263
  35.1 5.0 %collective-permute-done.3.rest_4_ = bf16[80,16,128]{2,1,0:T(8,128)(2,1)} collective-permute-done((bf16[80,16,128]{2,1,0:T(8,128)(2,1)S(1)}, bf16[80,16,128]{2,1,0:T(8,128)(2,1)}, u32[]{:S(2)}, u32[]{:S(2)}) %collective-permute-start.3) | collective-permute-done | bytes 327712 | tf_op jit(solution)/shard_map/ppermute | solution.py:263
  40.0 3.8 %collective-permute-start.5 = (bf16[80,16,128]{2,1,0:T(8,128)(2,1)}, bf16[80,16,128]{2,1,0:T(8,128)(2,1)S(1)}, u32[]{:S(2)}, u32[]{:S(2)}) collective-permute-start(bf16[80,16,128]{2,1,0:T(8,128)(2,1)} %collective-permute-done.3.rest_4_), channel_id=1, source_target_pairs={{0,7},{1,0},{2,1},{3,2},{4,3},{5,4},{6,5},{7,6},{8,15},{9,8},{10,9... | collective-permute-start | bytes 983048 | tf_op jit(solution)/shard_map/ppermute | solution.py:263
  46.6 7.4 %all-to-all-start.1 = ((bf16[32,4,16,128]{3,2,1,0:T(8,128)(2,1)}), bf16[32,4,16,128]{3,2,1,0:T(8,128)(2,1)S(1)}, u32[]{:S(2)}, u32[]{:S(2)}) async-start(bf16[32,4,16,128]{3,2,1,0:T(8,128)(2,1)} %get-tuple-element.56), calls=%async_computation.1 | async-start | bytes 1048576 | tf_op jit(solution)/shard_map/all_to_all | solution.py:449
  54.0 3.3 %collective-permute-start.7 = (bf16[48,16,128]{2,1,0:T(8,128)(2,1)S(1)}, bf16[48,16,128]{2,1,0:T(8,128)(2,1)S(1)}, u32[]{:S(2)}, u32[]{:S(2)}) collective-permute-start(bf16[48,16,128]{2,1,0:T(8,128)(2,1)S(1)} %slice.48), channel_id=1, source_target_pairs={{0,7},{1,0},{2,1},{3,2},{4,3},{5,4},{6,5},{7,6},{8,15},{9,8},{10,9... | collective-permute-start | bytes 589832 | tf_op jit(solution)/shard_map/ppermute | solution.py:267
  57.5 4.1 %multiply_convert_fusion.w_ref = bf16[8,512,512]{2,1,0:T(8,128)(2,1)} fusion(bf16[8,512,256]{2,1,0:T(8,128)(2,1)} %bitcast.25, bf16[8,512,256]{2,1,0:T(8,128)(2,1)} %bitcast.26, f32[8,512]{1,0:T(8,128)S(1)} %reshape.37), kind=kLoop, calls=%fused_computation | loop fusion | flops 12582912 | bytes 8404992 | tf_op jit(solution)/shard_map/convert_element_type | solution.py:447
  64.6 7.4 %all-to-all-start.2 = ((bf16[32,4,16,128]{3,2,1,0:T(8,128)(2,1)}), bf16[32,4,16,128]{3,2,1,0:T(8,128)(2,1)S(1)}, u32[]{:S(2)}, u32[]{:S(2)}) async-start(bf16[32,4,16,128]{3,2,1,0:T(8,128)(2,1)} %get-tuple-element.59), calls=%async_computation.2 | async-start | bytes 1048576 | tf_op jit(solution)/shard_map/all_to_all | solution.py:453
  81.7 6.0 %all-to-all-start.3 = ((bf16[32,16,16,128]{3,2,1,0:T(8,128)(2,1)}), bf16[32,16,16,128]{3,2,1,0:T(8,128)(2,1)S(1)}, u32[]{:S(2)}, u32[]{:S(2)}) async-start(bf16[32,16,16,128]{3,2,1,0:T(8,128)(2,1)} %copy-done.3), calls=%async_computation.3 | async-start | bytes 4194304 | tf_op jit(solution)/shard_map/all_to_all | solution.py:458
  87.7 3.5 %collective-permute-start.17 = (bf16[4,8,4,16,128]{4,3,2,1,0:T(8,128)(2,1)S(1)}, bf16[4,8,4,16,128]{4,3,2,1,0:T(8,128)(2,1)S(1)}, u32[]{:S(2)}, u32[]{:S(2)}) collective-permute-start(bf16[4,8,4,16,128]{4,3,2,1,0:T(8,128)(2,1)S(1)} %bitcast.18), channel_id=1, source_target_pairs={{0,7},{1,0},{2,1},{3,2},{4,3},{5,4},{6,5},{7,6},{8,15},{9,8},{10,9... | collective-permute-start | bytes 1572872 | tf_op jit(solution)/shard_map/ppermute | solution.py:279
  93.2 10.2 %collective-permute-done.17.rest_1_ = bf16[4,8,4,16,128]{4,3,2,1,0:T(8,128)(2,1)S(1)} collective-permute-done((bf16[4,8,4,16,128]{4,3,2,1,0:T(8,128)(2,1)S(1)}, bf16[4,8,4,16,128]{4,3,2,1,0:T(8,128)(2,1)S(1)}, u32[]{:S(2)}, u32[]{:S(2)}) %collective-permute-start.17) | collective-permute-done | bytes 524320 | tf_op jit(solution)/shard_map/ppermute | solution.py:279
  103.4 3.7 %collective-permute-start.18 = (bf16[4,8,4,16,128]{4,3,2,1,0:T(8,128)(2,1)S(1)}, bf16[4,8,4,16,128]{4,3,2,1,0:T(8,128)(2,1)S(1)}, u32[]{:S(2)}, u32[]{:S(2)}) collective-permute-start(bf16[4,8,4,16,128]{4,3,2,1,0:T(8,128)(2,1)S(1)} %collective-permute-done.17.rest_1_), channel_id=1, source_target_pairs={{0,7},{1,0},{2,1},{3,2},{4,3},{5,4},{6,5},{7,6},{8,15},{9,8},{10,9... | collective-permute-start | bytes 1572872 | tf_op jit(solution)/shard_map/ppermute | solution.py:279
  107.1 7.5 %collective-permute-done.11.rest_1_ = bf16[4,8,4,16,128]{4,3,2,1,0:T(8,128)(2,1)S(1)} collective-permute-done((bf16[4,8,4,16,128]{4,3,2,1,0:T(8,128)(2,1)S(1)}, bf16[4,8,4,16,128]{4,3,2,1,0:T(8,128)(2,1)S(1)}, u32[]{:S(2)}, u32[]{:S(2)}) %collective-permute-start.11) | collective-permute-done | bytes 524320 | tf_op jit(solution)/shard_map/ppermute | solution.py:279
  114.7 3.7 %collective-permute-start.12 = (bf16[4,8,4,16,128]{4,3,2,1,0:T(8,128)(2,1)S(1)}, bf16[4,8,4,16,128]{4,3,2,1,0:T(8,128)(2,1)}, u32[]{:S(2)}, u32[]{:S(2)}) collective-permute-start(bf16[4,8,4,16,128]{4,3,2,1,0:T(8,128)(2,1)S(1)} %collective-permute-done.11.rest_1_), channel_id=1, source_target_pairs={{0,7},{1,0},{2,1},{3,2},{4,3},{5,4},{6,5},{7,6},{8,15},{9,8},{10,9... | collective-permute-start | bytes 1572872 | tf_op jit(solution)/shard_map/ppermute | solution.py:279
  122.6 3.3 %collective-permute-done.18.rest_1_ = bf16[4,8,4,16,128]{4,3,2,1,0:T(8,128)(2,1)S(1)} collective-permute-done((bf16[4,8,4,16,128]{4,3,2,1,0:T(8,128)(2,1)S(1)}, bf16[4,8,4,16,128]{4,3,2,1,0:T(8,128)(2,1)S(1)}, u32[]{:S(2)}, u32[]{:S(2)}) %collective-permute-start.18) | collective-permute-done | bytes 524320 | tf_op jit(solution)/shard_map/ppermute | solution.py:279
  125.9 3.7 %collective-permute-start.19 = (bf16[4,8,4,16,128]{4,3,2,1,0:T(8,128)(2,1)S(1)}, bf16[4,8,4,16,128]{4,3,2,1,0:T(8,128)(2,1)}, u32[]{:S(2)}, u32[]{:S(2)}) collective-permute-start(bf16[4,8,4,16,128]{4,3,2,1,0:T(8,128)(2,1)S(1)} %collective-permute-done.18.rest_1_), channel_id=1, source_target_pairs={{0,7},{1,0},{2,1},{3,2},{4,3},{5,4},{6,5},{7,6},{8,15},{9,8},{10,9... | collective-permute-start | bytes 1572872 | tf_op jit(solution)/shard_map/ppermute | solution.py:279
  137.1 3.8 %collective-permute-start.13 = (bf16[4,8,4,16,128]{4,3,2,1,0:T(8,128)(2,1)}, bf16[4,8,4,16,128]{4,3,2,1,0:T(8,128)(2,1)S(1)}, u32[]{:S(2)}, u32[]{:S(2)}) collective-permute-start(bf16[4,8,4,16,128]{4,3,2,1,0:T(8,128)(2,1)} %collective-permute-done.12.rest_1_), channel_id=1, source_target_pairs={{0,7},{1,0},{2,1},{3,2},{4,3},{5,4},{6,5},{7,6},{8,15},{9,8},{10,9... | collective-permute-start | bytes 1572872 | tf_op jit(solution)/shard_map/ppermute | solution.py:279
  150.4 4.1 %collective-permute-start.23 = (bf16[2,8,4,16,128]{4,3,2,1,0:T(8,128)(2,1)S(1)}, bf16[2,8,4,16,128]{4,3,2,1,0:T(8,128)(2,1)S(1)}, u32[]{:S(2)}, u32[]{:S(2)}) collective-permute-start(bf16[2,8,4,16,128]{4,3,2,1,0:T(8,128)(2,1)S(1)} %slice.41), channel_id=1, source_target_pairs={{0,7},{1,0},{2,1},{3,2},{4,3},{5,4},{6,5},{7,6},{8,15},{9,8},{10,9... | collective-permute-start | bytes 786440 | tf_op jit(solution)/shard_map/ppermute | solution.py:295
  156.7 3.3 %gather_step.10 = (f32[512,512]{1,0:T(8,128)S(1)}, f32[512,128]{1,0:T(8,128)S(1)}) custom-call(s32[8]{0:T(128)S(1)} %and_select_fusion.where_ref, bf16[8,512,512]{2,1,0:T(8,128)(2,1)} %multiply_convert_fusion.w_ref, bf16[4,8,4,16,128]{4,3,2,1,0:T(8,128)(2,1)} %collective-permute-done.9.rest_0_, bf16[4,8,4,16,128]{4,3,2,1,0:T(8,128)(2,1)} %collective-permute-done.12.rest_1_, ...), custom_call_target="tpu_custom_call" | custom-call | flops 2147483648 | bytes 3145728 | tf_op jit(solution)/shard_map/gather_step/pallas_call | solution.py:235
  163.2 3.3 %collective-permute-start.21 = (bf16[2,8,4,16,128]{4,3,2,1,0:T(8,128)(2,1)S(1)}, bf16[2,8,4,16,128]{4,3,2,1,0:T(8,128)(2,1)S(1)}, u32[]{:S(2)}, u32[]{:S(2)}) collective-permute-start(bf16[2,8,4,16,128]{4,3,2,1,0:T(8,128)(2,1)S(1)} %slice.39), channel_id=1, source_target_pairs={{0,7},{1,0},{2,1},{3,2},{4,3},{5,4},{6,5},{7,6},{8,15},{9,8},{10,9... | collective-permute-start | bytes 786440 | tf_op jit(solution)/shard_map/ppermute | solution.py:295
  195.4 3.2 %collective-permute-start.30 = (bf16[256,256]{1,0:T(8,128)(2,1)S(1)}, bf16[256,256]{1,0:T(8,128)(2,1)S(1)}, u32[]{:S(2)}, u32[]{:S(2)}) collective-permute-start(bf16[256,256]{1,0:T(8,128)(2,1)S(1)} %collective-permute-done.28.rest_4_), channel_id=1, source_target_pairs={{0,7},{1,0},{2,1},{3,2},{4,3},{5,4},{6,5},{7,6},{8,15},{9,8},{10,9... | collective-permute-start | bytes 393224 | tf_op jit(solution)/shard_map/ppermute | solution.py:263
  201.8 3.4 %collective-permute-start.32 = (bf16[128,256]{1,0:T(8,128)(2,1)S(1)}, bf16[128,256]{1,0:T(8,128)(2,1)S(1)}, u32[]{:S(2)}, u32[]{:S(2)}) collective-permute-start(bf16[128,256]{1,0:T(8,128)(2,1)S(1)} %slice.50), channel_id=1, source_target_pairs={{0,7},{1,0},{2,1},{3,2},{4,3},{5,4},{6,5},{7,6},{8,15},{9,8},{10,9... | collective-permute-start | bytes 196616 | tf_op jit(solution)/shard_map/ppermute | solution.py:267
  (145 shorter events, 89.8 us)
Async XLA Ops:
  5.9 38.4 %all-to-all-start = ((bf16[32,17,16,128]{3,2,1,0:T(8,128)(2,1)}), bf16[32,17,16,128]{3,2,1,0:T(8,128)(2,1)S(1)}, u32[]{:S(2)}, u32[]{:S(2)}) async-start(bf16[32,17,16,128]{3,2,1,0:T(8,128)(2,1)} %copy-done.1), calls=%async_computation | async-start | bytes 4456448 | tf_op jit(solution)/shard_map/all_to_all | solution.py:428
  16.5 13.5 %collective-permute-start.2 = (bf16[80,16,128]{2,1,0:T(8,128)(2,1)}, bf16[80,16,128]{2,1,0:T(8,128)(2,1)S(1)}, u32[]{:S(2)}, u32[]{:S(2)}) collective-permute-start(bf16[80,16,128]{2,1,0:T(8,128)(2,1)} %letter.1.rest_0_), channel_id=1, source_target_pairs={{0,7},{1,0},{2,1},{3,2},{4,3},{5,4},{6,5},{7,6},{8,15},{9,8},{10,9... | collective-permute-start | bytes 983048 | tf_op jit(solution)/shard_map/ppermute | solution.py:263
  22.4 11.9 %collective-permute-start = (bf16[80,16,128]{2,1,0:T(8,128)(2,1)}, bf16[80,16,128]{2,1,0:T(8,128)(2,1)S(1)}, u32[]{:S(2)}, u32[]{:S(2)}) collective-permute-start(bf16[80,16,128]{2,1,0:T(8,128)(2,1)} %letter.1.rest_0_), channel_id=1, source_target_pairs={{0,1},{1,2},{2,3},{3,4},{4,5},{5,6},{6,7},{7,0},{8,9},{9,10},{10,1... | collective-permute-start | bytes 983048 | tf_op jit(solution)/shard_map/ppermute | solution.py:262
  40.0 14.0 %collective-permute-start.5 = (bf16[80,16,128]{2,1,0:T(8,128)(2,1)}, bf16[80,16,128]{2,1,0:T(8,128)(2,1)S(1)}, u32[]{:S(2)}, u32[]{:S(2)}) collective-permute-start(bf16[80,16,128]{2,1,0:T(8,128)(2,1)} %collective-permute-done.3.rest_4_), channel_id=1, source_target_pairs={{0,7},{1,0},{2,1},{3,2},{4,3},{5,4},{6,5},{7,6},{8,15},{9,8},{10,9... | collective-permute-start | bytes 983048 | tf_op jit(solution)/shard_map/ppermute | solution.py:263
  44.3 13.0 %collective-permute-start.4 = (bf16[80,16,128]{2,1,0:T(8,128)(2,1)}, bf16[80,16,128]{2,1,0:T(8,128)(2,1)S(1)}, u32[]{:S(2)}, u32[]{:S(2)}) collective-permute-start(bf16[80,16,128]{2,1,0:T(8,128)(2,1)} %collective-permute-done.1.rest_3_), channel_id=1, source_target_pairs={{0,1},{1,2},{2,3},{3,4},{4,5},{5,6},{6,7},{7,0},{8,9},{9,10},{10,1... | collective-permute-start | bytes 983048 | tf_op jit(solution)/shard_map/ppermute | solution.py:262
  46.6 18.0 %all-to-all-start.1 = ((bf16[32,4,16,128]{3,2,1,0:T(8,128)(2,1)}), bf16[32,4,16,128]{3,2,1,0:T(8,128)(2,1)S(1)}, u32[]{:S(2)}, u32[]{:S(2)}) async-start(bf16[32,4,16,128]{3,2,1,0:T(8,128)(2,1)} %get-tuple-element.56), calls=%async_computation.1 | async-start | bytes 1048576 | tf_op jit(solution)/shard_map/all_to_all | solution.py:449
  64.5 15.3 %collective-permute-start.14 = (bf16[4,8,4,16,128]{4,3,2,1,0:T(8,128)(2,1)S(1)}, bf16[4,8,4,16,128]{4,3,2,1,0:T(8,128)(2,1)}, u32[]{:S(2)}, u32[]{:S(2)}) collective-permute-start(bf16[4,8,4,16,128]{4,3,2,1,0:T(8,128)(2,1)S(1)} %bitcast.17), channel_id=1, source_target_pairs={{0,1},{1,2},{2,3},{3,4},{4,5},{5,6},{6,7},{7,0},{8,9},{9,10},{10,1... | collective-permute-start | bytes 1572872 | tf_op jit(solution)/shard_map/ppermute | solution.py:278
  64.6 17.1 %all-to-all-start.2 = ((bf16[32,4,16,128]{3,2,1,0:T(8,128)(2,1)}), bf16[32,4,16,128]{3,2,1,0:T(8,128)(2,1)S(1)}, u32[]{:S(2)}, u32[]{:S(2)}) async-start(bf16[32,4,16,128]{3,2,1,0:T(8,128)(2,1)} %get-tuple-element.59), calls=%async_computation.2 | async-start | bytes 1048576 | tf_op jit(solution)/shard_map/all_to_all | solution.py:453
  81.7 66.7 %all-to-all-start.3 = ((bf16[32,16,16,128]{3,2,1,0:T(8,128)(2,1)}), bf16[32,16,16,128]{3,2,1,0:T(8,128)(2,1)S(1)}, u32[]{:S(2)}, u32[]{:S(2)}) async-start(bf16[32,16,16,128]{3,2,1,0:T(8,128)(2,1)} %copy-done.3), calls=%async_computation.3 | async-start | bytes 4194304 | tf_op jit(solution)/shard_map/all_to_all | solution.py:458
  87.7 15.8 %collective-permute-start.17 = (bf16[4,8,4,16,128]{4,3,2,1,0:T(8,128)(2,1)S(1)}, bf16[4,8,4,16,128]{4,3,2,1,0:T(8,128)(2,1)S(1)}, u32[]{:S(2)}, u32[]{:S(2)}) collective-permute-start(bf16[4,8,4,16,128]{4,3,2,1,0:T(8,128)(2,1)S(1)} %bitcast.18), channel_id=1, source_target_pairs={{0,7},{1,0},{2,1},{3,2},{4,3},{5,4},{6,5},{7,6},{8,15},{9,8},{10,9... | collective-permute-start | bytes 1572872 | tf_op jit(solution)/shard_map/ppermute | solution.py:279
  91.1 23.5 %collective-permute-start.11 = (bf16[4,8,4,16,128]{4,3,2,1,0:T(8,128)(2,1)S(1)}, bf16[4,8,4,16,128]{4,3,2,1,0:T(8,128)(2,1)S(1)}, u32[]{:S(2)}, u32[]{:S(2)}) collective-permute-start(bf16[4,8,4,16,128]{4,3,2,1,0:T(8,128)(2,1)S(1)} %bitcast.20), channel_id=1, source_target_pairs={{0,7},{1,0},{2,1},{3,2},{4,3},{5,4},{6,5},{7,6},{8,15},{9,8},{10,9... | collective-permute-start | bytes 1572872 | tf_op jit(solution)/shard_map/ppermute | solution.py:279
  92.2 26.2 %collective-permute-start.8 = (bf16[4,8,4,16,128]{4,3,2,1,0:T(8,128)(2,1)S(1)}, bf16[4,8,4,16,128]{4,3,2,1,0:T(8,128)(2,1)S(1)}, u32[]{:S(2)}, u32[]{:S(2)}) collective-permute-start(bf16[4,8,4,16,128]{4,3,2,1,0:T(8,128)(2,1)S(1)} %bitcast.21), channel_id=1, source_target_pairs={{0,1},{1,2},{2,3},{3,4},{4,5},{5,6},{6,7},{7,0},{8,9},{9,10},{10,1... | collective-permute-start | bytes 1572872 | tf_op jit(solution)/shard_map/ppermute | solution.py:278
  93.2 29.4 %collective-permute-start.15 = (bf16[4,8,4,16,128]{4,3,2,1,0:T(8,128)(2,1)}, bf16[4,8,4,16,128]{4,3,2,1,0:T(8,128)(2,1)S(1)}, u32[]{:S(2)}, u32[]{:S(2)}) collective-permute-start(bf16[4,8,4,16,128]{4,3,2,1,0:T(8,128)(2,1)} %collective-permute-done.14.rest_0_), channel_id=1, source_target_pairs={{0,1},{1,2},{2,3},{3,4},{4,5},{5,6},{6,7},{7,0},{8,9},{9,10},{10,1... | collective-permute-start | bytes 1572872 | tf_op jit(solution)/shard_map/ppermute | solution.py:278
  103.4 22.5 %collective-permute-start.18 = (bf16[4,8,4,16,128]{4,3,2,1,0:T(8,128)(2,1)S(1)}, bf16[4,8,4,16,128]{4,3,2,1,0:T(8,128)(2,1)S(1)}, u32[]{:S(2)}, u32[]{:S(2)}) collective-permute-start(bf16[4,8,4,16,128]{4,3,2,1,0:T(8,128)(2,1)S(1)} %collective-permute-done.17.rest_1_), channel_id=1, source_target_pairs={{0,7},{1,0},{2,1},{3,2},{4,3},{5,4},{6,5},{7,6},{8,15},{9,8},{10,9... | collective-permute-start | bytes 1572872 | tf_op jit(solution)/shard_map/ppermute | solution.py:279
  114.7 22.5 %collective-permute-start.12 = (bf16[4,8,4,16,128]{4,3,2,1,0:T(8,128)(2,1)S(1)}, bf16[4,8,4,16,128]{4,3,2,1,0:T(8,128)(2,1)}, u32[]{:S(2)}, u32[]{:S(2)}) collective-permute-start(bf16[4,8,4,16,128]{4,3,2,1,0:T(8,128)(2,1)S(1)} %collective-permute-done.11.rest_1_), channel_id=1, source_target_pairs={{0,7},{1,0},{2,1},{3,2},{4,3},{5,4},{6,5},{7,6},{8,15},{9,8},{10,9... | collective-permute-start | bytes 1572872 | tf_op jit(solution)/shard_map/ppermute | solution.py:279
  118.4 18.3 %collective-permute-start.9 = (bf16[4,8,4,16,128]{4,3,2,1,0:T(8,128)(2,1)S(1)}, bf16[4,8,4,16,128]{4,3,2,1,0:T(8,128)(2,1)}, u32[]{:S(2)}, u32[]{:S(2)}) collective-permute-start(bf16[4,8,4,16,128]{4,3,2,1,0:T(8,128)(2,1)S(1)} %collective-permute-done.8.rest_0_), channel_id=1, source_target_pairs={{0,1},{1,2},{2,3},{3,4},{4,5},{5,6},{6,7},{7,0},{8,9},{9,10},{10,1... | collective-permute-start | bytes 1572872 | tf_op jit(solution)/shard_map/ppermute | solution.py:278
  122.6 23.1 %collective-permute-start.16 = (bf16[4,8,4,16,128]{4,3,2,1,0:T(8,128)(2,1)S(1)}, bf16[4,8,4,16,128]{4,3,2,1,0:T(8,128)(2,1)S(1)}, u32[]{:S(2)}, u32[]{:S(2)}) collective-permute-start(bf16[4,8,4,16,128]{4,3,2,1,0:T(8,128)(2,1)S(1)} %collective-permute-done.15.rest_0_), channel_id=1, source_target_pairs={{0,1},{1,2},{2,3},{3,4},{4,5},{5,6},{6,7},{7,0},{8,9},{9,10},{10,1... | collective-permute-start | bytes 1572872 | tf_op jit(solution)/shard_map/ppermute | solution.py:278
  125.9 22.5 %collective-permute-start.19 = (bf16[4,8,4,16,128]{4,3,2,1,0:T(8,128)(2,1)S(1)}, bf16[4,8,4,16,128]{4,3,2,1,0:T(8,128)(2,1)}, u32[]{:S(2)}, u32[]{:S(2)}) collective-permute-start(bf16[4,8,4,16,128]{4,3,2,1,0:T(8,128)(2,1)S(1)} %collective-permute-done.18.rest_1_), channel_id=1, source_target_pairs={{0,7},{1,0},{2,1},{3,2},{4,3},{5,4},{6,5},{7,6},{8,15},{9,8},{10,9... | collective-permute-start | bytes 1572872 | tf_op jit(solution)/shard_map/ppermute | solution.py:279
  136.6 26.4 %collective-permute-start.10 = (bf16[4,8,4,16,128]{4,3,2,1,0:T(8,128)(2,1)}, bf16[4,8,4,16,128]{4,3,2,1,0:T(8,128)(2,1)S(1)}, u32[]{:S(2)}, u32[]{:S(2)}) collective-permute-start(bf16[4,8,4,16,128]{4,3,2,1,0:T(8,128)(2,1)} %collective-permute-done.9.rest_0_), channel_id=1, source_target_pairs={{0,1},{1,2},{2,3},{3,4},{4,5},{5,6},{6,7},{7,0},{8,9},{9,10},{10,1... | collective-permute-start | bytes 1572872 | tf_op jit(solution)/shard_map/ppermute | solution.py:278
  137.1 25.9 %collective-permute-start.13 = (bf16[4,8,4,16,128]{4,3,2,1,0:T(8,128)(2,1)}, bf16[4,8,4,16,128]{4,3,2,1,0:T(8,128)(2,1)S(1)}, u32[]{:S(2)}, u32[]{:S(2)}) collective-permute-start(bf16[4,8,4,16,128]{4,3,2,1,0:T(8,128)(2,1)} %collective-permute-done.12.rest_1_), channel_id=1, source_target_pairs={{0,7},{1,0},{2,1},{3,2},{4,3},{5,4},{6,5},{7,6},{8,15},{9,8},{10,9... | collective-permute-start | bytes 1572872 | tf_op jit(solution)/shard_map/ppermute | solution.py:279
  149.3 17.2 %collective-permute-start.22 = (bf16[2,8,4,16,128]{4,3,2,1,0:T(8,128)(2,1)S(1)}, bf16[2,8,4,16,128]{4,3,2,1,0:T(8,128)(2,1)S(1)}, u32[]{:S(2)}, u32[]{:S(2)}) collective-permute-start(bf16[2,8,4,16,128]{4,3,2,1,0:T(8,128)(2,1)S(1)} %slice.40), channel_id=1, source_target_pairs={{0,1},{1,2},{2,3},{3,4},{4,5},{5,6},{6,7},{7,0},{8,9},{9,10},{10,1... | collective-permute-start | bytes 786440 | tf_op jit(solution)/shard_map/ppermute | solution.py:294
  150.4 16.1 %collective-permute-start.23 = (bf16[2,8,4,16,128]{4,3,2,1,0:T(8,128)(2,1)S(1)}, bf16[2,8,4,16,128]{4,3,2,1,0:T(8,128)(2,1)S(1)}, u32[]{:S(2)}, u32[]{:S(2)}) collective-permute-start(bf16[2,8,4,16,128]{4,3,2,1,0:T(8,128)(2,1)S(1)} %slice.41), channel_id=1, source_target_pairs={{0,7},{1,0},{2,1},{3,2},{4,3},{5,4},{6,5},{7,6},{8,15},{9,8},{10,9... | collective-permute-start | bytes 786440 | tf_op jit(solution)/shard_map/ppermute | solution.py:295
  163.1 10.9 %collective-permute-start.20 = (bf16[2,8,4,16,128]{4,3,2,1,0:T(8,128)(2,1)S(1)}, bf16[2,8,4,16,128]{4,3,2,1,0:T(8,128)(2,1)S(1)}, u32[]{:S(2)}, u32[]{:S(2)}) collective-permute-start(bf16[2,8,4,16,128]{4,3,2,1,0:T(8,128)(2,1)S(1)} %slice.38), channel_id=1, source_target_pairs={{0,1},{1,2},{2,3},{3,4},{4,5},{5,6},{6,7},{7,0},{8,9},{9,10},{10,1... | collective-permute-start | bytes 786440 | tf_op jit(solution)/shard_map/ppermute | solution.py:294
  163.2 10.8 %collective-permute-start.21 = (bf16[2,8,4,16,128]{4,3,2,1,0:T(8,128)(2,1)S(1)}, bf16[2,8,4,16,128]{4,3,2,1,0:T(8,128)(2,1)S(1)}, u32[]{:S(2)}, u32[]{:S(2)}) collective-permute-start(bf16[2,8,4,16,128]{4,3,2,1,0:T(8,128)(2,1)S(1)} %slice.39), channel_id=1, source_target_pairs={{0,7},{1,0},{2,1},{3,2},{4,3},{5,4},{6,5},{7,6},{8,15},{9,8},{10,9... | collective-permute-start | bytes 786440 | tf_op jit(solution)/shard_map/ppermute | solution.py:295
  (43 other events, 271.7 us)

commit v7 on v6

--- a/solution.py
+++ b/solution.py
@@ -26,9 +26,11 @@
     for span in range(spans):
         for j in range(each):
             at = span * each + j
-            note = jnp.where(lane == at, shard_ref[j, span], note)
-            note = jnp.where(lane == spans * each + at, row_ref[j, span], note)
-        note = jnp.where(lane == 2 * spans * each + span, count_ref[span], note)
+            note = jnp.where(lane == at, shard_ref[j : j + 1, span : span + 1], note)
+            row = row_ref[j : j + 1, span : span + 1]
+            note = jnp.where(lane == spans * each + at, row, note)
+        count = count_ref[:, span : span + 1]
+        note = jnp.where(lane == 2 * spans * each + span, count, note)
     note = note.astype(jnp.float32).astype(jnp.bfloat16)
     for f in range(pieces_f):
         for i in range(pieces_t):
@@ -45,12 +47,12 @@
     vmem = pl.BlockSpec(memory_space=pltpu.VMEM)
     return pl.pallas_call(
         cut_kernel,
-        in_specs=[pl.BlockSpec(memory_space=pltpu.SMEM)] * 3 + [vmem],
+        in_specs=[vmem] * 4,
         out_specs=vmem,
         out_shape=jax.ShapeDtypeStruct((pieces, shard + 1, PIECE_T, PIECE_F), database.dtype),
         compiler_params=pltpu.CompilerParams(vmem_limit_bytes=VMEM_LIMIT),
         name="cut",
-    )(nbr_shard.T, nbr_row.T, nbr_count, database)
+    )(nbr_shard.T, nbr_row.T, nbr_count.reshape(1, -1), database)
 
 
 def pick_kernel(index_ref, spread_ref, *out_refs):
@@ -286,10 +288,13 @@
                 False,
             )
         if step == 1:
-            beside = send_beside(go_right[0])
+            beside = send_beside(*zip(go_right, go_left))
     places = [(n_ten // 2, 0), (n_ten // 2, half)]
     for s in range(len(streams)):
-        from_left, from_right, beside = lax.optimization_barrier((go_right[s], go_left[s], beside))
+        from_left, from_right = go_right[s], go_left[s]
+        if s == len(streams) - 1:
+            held = lax.optimization_barrier((from_left, from_right, beside))
+            from_left, from_right, beside = held
         blocks = [
             lax.ppermute(from_left[:half], "tensor", right),
             lax.ppermute(from_right[half:], "tensor", left),
@@ -441,25 +446,24 @@
 
     spread, index, _ = lax.optimization_barrier((spread, index, letters[3:5]))
     spread = spread.reshape(n_seq * (per_shard + 1), PIECE_T, PIECE_F)
-    low, high = pick(index, spread, 2)
-    nbr_gain, _ = lax.optimization_barrier((nbr_gain, high))
+    (picked,) = pick(index, spread, 1)
+    nbr_gain, _ = lax.optimization_barrier((nbr_gain, picked))
     both = jnp.concatenate([wk, wv], axis=1).astype(jnp.float32)
     both = (both * nbr_gain.astype(jnp.float32)[:, None]).astype(jnp.bfloat16)
     both = both.reshape(n_ten, d_part, both.shape[1])
-    high = lax.all_to_all(high, "seq", split_axis=0, concat_axis=0, tiled=True)
-    high, low, letters, both, counts = lax.optimization_barrier(
-        (high, low, letters, both, counts)
+    rows = lax.all_to_all(picked, "seq", split_axis=0, concat_axis=0, tiled=True)
+    queries, strip = query(where, letters, x_gain, wq, tok_dev, shift, n_seq)
+    rows, queries, strip, both, counts = lax.optimization_barrier(
+        (rows, queries, strip, both, counts)
     )
-    low = lax.all_to_all(low, "seq", split_axis=0, concat_axis=0, tiled=True)
-    queries, strip = query(where, letters, x_gain, wq, tok_dev, shift, n_seq)
-
-    def send_mail(arrived):
-        mail, _ = lax.optimization_barrier((strip, arrived))
+
+    def send_mail(first, second):
+        mail, _ = lax.optimization_barrier((strip, second))
         mail = lax.all_to_all(mail, "seq", split_axis=0, concat_axis=0, tiled=True)
         return mail.reshape(strips, halves, *strip.shape[1:])
 
-    shape = (pieces_f, pieces_t, items // 2, PIECE_T, PIECE_F)
-    streams = [high.reshape(shape), low.reshape(shape)]
+    rows = rows.reshape(pieces_f, pieces_t, items, PIECE_T, PIECE_F)
+    streams = [rows[:, :, items // 2 :], rows[:, :, : items // 2]]
     (late, early), mail = ring_project(streams, where, both, n_ten, send_mail)
     prev = lax.ppermute(late[-1], "seq", [(i, i + 1) for i in range(n_seq - 1)])
     attended = attend(counts, queries, late, span_dev // 2, span_len, prev=prev)

time: 210 us -> 216 us (1.029)
  waiting for transfers between devices: 54.1 us -> 65.2 us
  starting transfers between devices: 88.1 us -> 80.3 us
    ppermute x6, waiting for transfers between devices: 1.53 us -> 17.6 us  [ring_project(): go_right[s] = lax.ppermute(go_right[s], 'tensor', right)]
    ppermute x6, waiting for transfers between devices: 23.5 us -> 9.61 us  [ring_project(): go_left[s] = lax.ppermute(go_left[s], 'tensor', left)]
    all_to_all x2 -> x1, starting transfers between devices: 14.8 us -> 7.57 us  [body(): lax.all_to_all(picked, 'seq', split_axis=0, concat_axis=0, tiled=True)]
    ppermute x2, waiting for transfers between devices: 2.95 us -> 8.56 us  [ring_gather(): lax.ppermute(go_right[:cut_at], 'tensor', right)]
    ppermute x2, waiting for transfers between devices: 0.01 us -> 5.35 us  [ring_project(): lax.ppermute(from_left[:half], 'tensor', right)]
    ppermute x6, starting transfers between devices: 19.4 us -> 17.1 us  [ring_project(): go_left[s] = lax.ppermute(go_left[s], 'tensor', left)]
    ppermute x1, waiting for transfers between devices: 2.22 us -> 0.01 us  [body(): prev = lax.ppermute(late[-1], 'seq', [(i, i + 1) for i in range(n_seq - 1)])]
    unnamed x60 -> x64, local copies, waits for them, and re-layouts: 18.2 us -> 20.1 us
  transfers between devices with their start and end apart: 37 -> 36, of which waited for: 17 -> 14; matrix products, arithmetic and copies ran while one was open for 4% -> 3% of each run, Pallas kernels for 16% -> 16%
where the time goes in v7:
time: 216 us; the launch traced here: 214 us
  starting transfers between devices  80.3 us (37%)
  waiting for transfers between devices  65.2 us (30%)
  Pallas kernels  40.6 us (19%)
  local copies, waits for them, and re-layouts  22.3 us (10%)
  other arithmetic  4.8 us (2%)
    pallas_call x10, Pallas kernels, gather_step(): pl.pallas_call(functools.partial(gather_kernel, tuple(places), not state,...  25.9 us
    ppermute x6, starting transfers between devices, ring_gather(): go_left = lax.ppermute(go_left, 'tensor', left)  22.9 us
    unnamed x64, local copies, waits for them, and re-layouts  20.1 us
    ppermute x6, waiting for transfers between devices, ring_project(): go_right[s] = lax.ppermute(go_right[s], 'tensor', right)  17.6 us
    ppermute x6, starting transfers between devices, ring_project(): go_left[s] = lax.ppermute(go_left[s], 'tensor', left)  17.1 us
    ppermute x6, waiting for transfers between devices, ring_gather(): go_left = lax.ppermute(go_left, 'tensor', left)  13.3 us
    ppermute x6, waiting for transfers between devices, ring_gather(): go_right = lax.ppermute(go_right, 'tensor', right)  10.7 us
    ppermute x6, waiting for transfers between devices, ring_project(): go_left[s] = lax.ppermute(go_left[s], 'tensor', left)  9.61 us
  transfers between devices with their start and end apart: 36, of which 14 were waited for; matrix products, arithmetic and copies ran while one was open for 3% of the time, Pallas kernels for 16%

profile of v7, /device:TPU:8, one launch (start us, length us, event | category | flops | bytes accessed | tf_op | source)
XLA Modules:
  0.0 214.4 jit_solution(9485571437170818128)
XLA Ops:
  5.3 7.5 %all-to-all-start = ((bf16[32,17,16,128]{3,2,1,0:T(8,128)(2,1)}), bf16[32,17,16,128]{3,2,1,0:T(8,128)(2,1)S(1)}, u32[]{:S(2)}, u32[]{:S(2)}) async-start(bf16[32,17,16,128]{3,2,1,0:T(8,128)(2,1)} %copy-done.1), calls=%async_computation | async-start | bytes 4456448 | tf_op jit(solution)/shard_map/all_to_all | solution.py:433
  15.9 5.9 %collective-permute-start.2 = (bf16[80,16,128]{2,1,0:T(8,128)(2,1)}, bf16[80,16,128]{2,1,0:T(8,128)(2,1)S(1)}, u32[]{:S(2)}, u32[]{:S(2)}) collective-permute-start(bf16[80,16,128]{2,1,0:T(8,128)(2,1)} %letter.1.rest_0_), channel_id=1, source_target_pairs={{0,7},{1,0},{2,1},{3,2},{4,3},{5,4},{6,5},{7,6},{8,15},{9,8},{10,9... | collective-permute-start | bytes 983048 | tf_op jit(solution)/shard_map/ppermute | solution.py:265
  21.8 7.6 %collective-permute-done.2.rest_2_ = bf16[80,16,128]{2,1,0:T(8,128)(2,1)S(1)} collective-permute-done((bf16[80,16,128]{2,1,0:T(8,128)(2,1)}, bf16[80,16,128]{2,1,0:T(8,128)(2,1)S(1)}, u32[]{:S(2)}, u32[]{:S(2)}) %collective-permute-start.2) | collective-permute-done | bytes 327712 | tf_op jit(solution)/shard_map/ppermute | solution.py:265
  29.4 3.6 %collective-permute-start.3 = (bf16[80,16,128]{2,1,0:T(8,128)(2,1)S(1)}, bf16[80,16,128]{2,1,0:T(8,128)(2,1)}, u32[]{:S(2)}, u32[]{:S(2)}) collective-permute-start(bf16[80,16,128]{2,1,0:T(8,128)(2,1)S(1)} %collective-permute-done.2.rest_2_), channel_id=1, source_target_pairs={{0,7},{1,0},{2,1},{3,2},{4,3},{5,4},{6,5},{7,6},{8,15},{9,8},{10,9... | collective-permute-start | bytes 983048 | tf_op jit(solution)/shard_map/ppermute | solution.py:265
  33.7 5.7 %collective-permute-done.3.rest_4_ = bf16[80,16,128]{2,1,0:T(8,128)(2,1)} collective-permute-done((bf16[80,16,128]{2,1,0:T(8,128)(2,1)S(1)}, bf16[80,16,128]{2,1,0:T(8,128)(2,1)}, u32[]{:S(2)}, u32[]{:S(2)}) %collective-permute-start.3) | collective-permute-done | bytes 327712 | tf_op jit(solution)/shard_map/ppermute | solution.py:265
  39.4 3.8 %collective-permute-start.5 = (bf16[80,16,128]{2,1,0:T(8,128)(2,1)}, bf16[80,16,128]{2,1,0:T(8,128)(2,1)S(1)}, u32[]{:S(2)}, u32[]{:S(2)}) collective-permute-start(bf16[80,16,128]{2,1,0:T(8,128)(2,1)} %collective-permute-done.3.rest_4_), channel_id=1, source_target_pairs={{0,7},{1,0},{2,1},{3,2},{4,3},{5,4},{6,5},{7,6},{8,15},{9,8},{10,9... | collective-permute-start | bytes 983048 | tf_op jit(solution)/shard_map/ppermute | solution.py:265
  45.6 7.6 %all-to-all-start.1 = ((bf16[32,8,16,128]{3,2,1,0:T(8,128)(2,1)}), bf16[32,8,16,128]{3,2,1,0:T(8,128)(2,1)}, u32[]{:S(2)}, u32[]{:S(2)}) async-start(bf16[32,8,16,128]{3,2,1,0:T(8,128)(2,1)} %pick.1), calls=%async_computation.1 | async-start | bytes 2097152 | tf_op jit(solution)/shard_map/all_to_all | solution.py:454
  53.2 4.2 %collective-permute-start.7 = (bf16[48,16,128]{2,1,0:T(8,128)(2,1)S(1)}, bf16[48,16,128]{2,1,0:T(8,128)(2,1)S(1)}, u32[]{:S(2)}, u32[]{:S(2)}) collective-permute-start(bf16[48,16,128]{2,1,0:T(8,128)(2,1)S(1)} %slice.56), channel_id=1, source_target_pairs={{0,7},{1,0},{2,1},{3,2},{4,3},{5,4},{6,5},{7,6},{8,15},{9,8},{10,9... | collective-permute-start | bytes 589832 | tf_op jit(solution)/shard_map/ppermute | solution.py:269
  57.6 6.4 %collective-permute-done.6.rest_7_ = bf16[32,16,128]{2,1,0:T(8,128)(2,1)S(1)} collective-permute-done((bf16[32,16,128]{2,1,0:T(8,128)(2,1)S(1)}, bf16[32,16,128]{2,1,0:T(8,128)(2,1)S(1)}, u32[]{:S(2)}, u32[]{:S(2)}) %collective-permute-start.6) | collective-permute-done | bytes 131104 | tf_op jit(solution)/shard_map/ppermute | solution.py:268
  74.7 4.0 %multiply_convert_fusion.w_ref = bf16[8,512,512]{2,1,0:T(8,128)(2,1)} fusion(bf16[8,512,256]{2,1,0:T(8,128)(2,1)} %bitcast.20, bf16[8,512,256]{2,1,0:T(8,128)(2,1)} %bitcast.21, f32[8,512]{1,0:T(8,128)S(1)} %reshape.37), kind=kLoop, calls=%fused_computation | loop fusion | flops 12582912 | bytes 8404992 | tf_op jit(solution)/shard_map/convert_element_type | solution.py:452
  85.5 9.6 %collective-permute-done.11.rest_1_ = bf16[4,8,4,16,128]{4,3,2,1,0:T(8,128)(2,1)S(1)} collective-permute-done((bf16[4,8,4,16,128]{4,3,2,1,0:T(8,128)(2,1)S(1)}, bf16[4,8,4,16,128]{4,3,2,1,0:T(8,128)(2,1)S(1)}, u32[]{:S(2)}, u32[]{:S(2)}) %collective-permute-start.11) | collective-permute-done | bytes 524320 | tf_op jit(solution)/shard_map/ppermute | solution.py:281
  98.0 7.4 %all-to-all-start.2 = ((bf16[32,16,16,128]{3,2,1,0:T(8,128)(2,1)}), bf16[32,16,16,128]{3,2,1,0:T(8,128)(2,1)S(1)}, u32[]{:S(2)}, u32[]{:S(2)}) async-start(bf16[32,16,16,128]{3,2,1,0:T(8,128)(2,1)} %copy-done.3), calls=%async_computation.2 | async-start | bytes 4194304 | tf_op jit(solution)/shard_map/all_to_all | solution.py:462
  106.7 3.2 %collective-permute-start.21 = (bf16[4,8,4,16,128]{4,3,2,1,0:T(8,128)(2,1)}, bf16[4,8,4,16,128]{4,3,2,1,0:T(8,128)(2,1)S(1)}, u32[]{:S(2)}, u32[]{:S(2)}) collective-permute-start(bf16[4,8,4,16,128]{4,3,2,1,0:T(8,128)(2,1)} %collective-permute-done.20.rest_1_), channel_id=1, source_target_pairs={{0,7},{1,0},{2,1},{3,2},{4,3},{5,4},{6,5},{7,6},{8,15},{9,8},{10,9... | collective-permute-start | bytes 1572872 | tf_op jit(solution)/shard_map/ppermute | solution.py:281
  113.1 9.8 %collective-permute-done.17.rest_0_ = bf16[4,8,4,16,128]{4,3,2,1,0:T(8,128)(2,1)S(1)} collective-permute-done((bf16[4,8,4,16,128]{4,3,2,1,0:T(8,128)(2,1)}, bf16[4,8,4,16,128]{4,3,2,1,0:T(8,128)(2,1)S(1)}, u32[]{:S(2)}, u32[]{:S(2)}) %collective-permute-start.17) | collective-permute-done | bytes 524320 | tf_op jit(solution)/shard_map/ppermute | solution.py:280
  130.4 3.3 %gather_step.13 = (f32[512,512]{1,0:T(8,128)S(1)}, f32[512,128]{1,0:T(8,128)S(1)}) custom-call(s32[8]{0:T(128)S(1)} %and_select_fusion.where_ref, bf16[8,512,512]{2,1,0:T(8,128)(2,1)} %multiply_convert_fusion.w_ref, bf16[4,8,4,16,128]{4,3,2,1,0:T(8,128)(2,1)} %collective-permute-done.16.rest_0_, bf16[4,8,4,16,128]{4,3,2,1,0:T(8,128)(2,1)} %collective-permute-done.20.rest_1_, ...), custom_call_target="tpu_custom_call" | custom-call | flops 2147483648 | bytes 3145728 | tf_op jit(solution)/shard_map/gather_step/pallas_call | solution.py:237
  141.4 4.0 %collective-permute-done.18.rest_0_ = bf16[4,8,4,16,128]{4,3,2,1,0:T(8,128)(2,1)S(1)} collective-permute-done((bf16[4,8,4,16,128]{4,3,2,1,0:T(8,128)(2,1)S(1)}, bf16[4,8,4,16,128]{4,3,2,1,0:T(8,128)(2,1)S(1)}, u32[]{:S(2)}, u32[]{:S(2)}) %collective-permute-start.18) | collective-permute-done | bytes 524320 | tf_op jit(solution)/shard_map/ppermute | solution.py:280
  145.6 3.5 %collective-permute-start.23 = (bf16[2,8,4,16,128]{4,3,2,1,0:T(8,128)(2,1)S(1)}, bf16[2,8,4,16,128]{4,3,2,1,0:T(8,128)(2,1)S(1)}, u32[]{:S(2)}, u32[]{:S(2)}) collective-permute-start(bf16[2,8,4,16,128]{4,3,2,1,0:T(8,128)(2,1)S(1)} %slice.60), channel_id=1, source_target_pairs={{0,7},{1,0},{2,1},{3,2},{4,3},{5,4},{6,5},{7,6},{8,15},{9,8},{10,9... | collective-permute-start | bytes 786440 | tf_op jit(solution)/shard_map/ppermute | solution.py:300
  154.9 5.3 %collective-permute-done.19.rest_0_ = bf16[2,8,4,16,128]{4,3,2,1,0:T(8,128)(2,1)S(1)} collective-permute-done((bf16[2,8,4,16,128]{4,3,2,1,0:T(8,128)(2,1)S(1)}, bf16[2,8,4,16,128]{4,3,2,1,0:T(8,128)(2,1)S(1)}, u32[]{:S(2)}, u32[]{:S(2)}) %collective-permute-start.19) | collective-permute-done | bytes 262176 | tf_op jit(solution)/shard_map/ppermute | solution.py:299
  160.3 3.4 %gather_last.3 = (bf16[8,2,16,512]{3,2,1,0:T(8,128)(2,1)S(1)}, bf16[8,2,16,512]{3,2,1,0:T(8,128)(2,1)}) custom-call(s32[8]{0:T(128)S(1)} %and_select_fusion.where_ref, bf16[8,512,512]{2,1,0:T(8,128)(2,1)} %multiply_convert_fusion.w_ref, bf16[2,8,4,16,128]{4,3,2,1,0:T(8,128)(2,1)S(1)} %collective-permute-done.19.rest_0_, ...), custom_call_target="tpu_custom_call" | custom-call | flops 1073741824 | bytes 2621440 | tf_op jit(solution)/shard_map/gather_last/pallas_call | solution.py:237
  165.7 3.3 %collective-permute-start.15 = (bf16[2,8,4,16,128]{4,3,2,1,0:T(8,128)(2,1)S(1)}, bf16[2,8,4,16,128]{4,3,2,1,0:T(8,128)(2,1)S(1)}, u32[]{:S(2)}, u32[]{:S(2)}) collective-permute-start(bf16[2,8,4,16,128]{4,3,2,1,0:T(8,128)(2,1)S(1)} %slice.46), channel_id=1, source_target_pairs={{0,7},{1,0},{2,1},{3,2},{4,3},{5,4},{6,5},{7,6},{8,15},{9,8},{10,9... | collective-permute-start | bytes 786440 | tf_op jit(solution)/shard_map/ppermute | solution.py:300
  189.7 4.3 %collective-permute-done.25.rest_1_ = bf16[256,256]{1,0:T(8,128)(2,1)S(1)} collective-permute-done((bf16[256,256]{1,0:T(8,128)(2,1)S(1)}, bf16[256,256]{1,0:T(8,128)(2,1)S(1)}, u32[]{:S(2)}, u32[]{:S(2)}) %collective-permute-start.25) | collective-permute-done | bytes 131104 | tf_op jit(solution)/shard_map/ppermute | solution.py:264
  194.0 3.2 %collective-permute-start.28 = (bf16[256,256]{1,0:T(8,128)(2,1)S(1)}, bf16[256,256]{1,0:T(8,128)(2,1)S(1)}, u32[]{:S(2)}, u32[]{:S(2)}) collective-permute-start(bf16[256,256]{1,0:T(8,128)(2,1)S(1)} %collective-permute-done.26.rest_2_), channel_id=1, source_target_pairs={{0,7},{1,0},{2,1},{3,2},{4,3},{5,4},{6,5},{7,6},{8,15},{9,8},{10,9... | collective-permute-start | bytes 393224 | tf_op jit(solution)/shard_map/ppermute | solution.py:265
  197.2 3.5 %collective-permute-done.27.rest_3_ = bf16[256,256]{1,0:T(8,128)(2,1)S(1)} collective-permute-done((bf16[256,256]{1,0:T(8,128)(2,1)S(1)}, bf16[256,256]{1,0:T(8,128)(2,1)S(1)}, u32[]{:S(2)}, u32[]{:S(2)}) %collective-permute-start.27) | collective-permute-done | bytes 131104 | tf_op jit(solution)/shard_map/ppermute | solution.py:264
  206.9 3.3 %collective-permute-start.32 = (bf16[128,256]{1,0:T(8,128)(2,1)S(1)}, bf16[128,256]{1,0:T(8,128)(2,1)S(1)}, u32[]{:S(2)}, u32[]{:S(2)}) collective-permute-start(bf16[128,256]{1,0:T(8,128)(2,1)S(1)} %slice.62), channel_id=1, source_target_pairs={{0,7},{1,0},{2,1},{3,2},{4,3},{5,4},{6,5},{7,6},{8,15},{9,8},{10,9... | collective-permute-start | bytes 196616 | tf_op jit(solution)/shard_map/ppermute | solution.py:269
  (148 shorter events, 89.8 us)
Async XLA Ops:
  5.3 37.9 %all-to-all-start = ((bf16[32,17,16,128]{3,2,1,0:T(8,128)(2,1)}), bf16[32,17,16,128]{3,2,1,0:T(8,128)(2,1)S(1)}, u32[]{:S(2)}, u32[]{:S(2)}) async-start(bf16[32,17,16,128]{3,2,1,0:T(8,128)(2,1)} %copy-done.1), calls=%async_computation | async-start | bytes 4456448 | tf_op jit(solution)/shard_map/all_to_all | solution.py:433
  15.9 13.5 %collective-permute-start.2 = (bf16[80,16,128]{2,1,0:T(8,128)(2,1)}, bf16[80,16,128]{2,1,0:T(8,128)(2,1)S(1)}, u32[]{:S(2)}, u32[]{:S(2)}) collective-permute-start(bf16[80,16,128]{2,1,0:T(8,128)(2,1)} %letter.1.rest_0_), channel_id=1, source_target_pairs={{0,7},{1,0},{2,1},{3,2},{4,3},{5,4},{6,5},{7,6},{8,15},{9,8},{10,9... | collective-permute-start | bytes 983048 | tf_op jit(solution)/shard_map/ppermute | solution.py:265
  39.4 13.7 %collective-permute-start.5 = (bf16[80,16,128]{2,1,0:T(8,128)(2,1)}, bf16[80,16,128]{2,1,0:T(8,128)(2,1)S(1)}, u32[]{:S(2)}, u32[]{:S(2)}) collective-permute-start(bf16[80,16,128]{2,1,0:T(8,128)(2,1)} %collective-permute-done.3.rest_4_), channel_id=1, source_target_pairs={{0,7},{1,0},{2,1},{3,2},{4,3},{5,4},{6,5},{7,6},{8,15},{9,8},{10,9... | collective-permute-start | bytes 983048 | tf_op jit(solution)/shard_map/ppermute | solution.py:265
  43.2 14.2 %collective-permute-start.4 = (bf16[80,16,128]{2,1,0:T(8,128)(2,1)}, bf16[80,16,128]{2,1,0:T(8,128)(2,1)S(1)}, u32[]{:S(2)}, u32[]{:S(2)}) collective-permute-start(bf16[80,16,128]{2,1,0:T(8,128)(2,1)} %collective-permute-done.1.rest_3_), channel_id=1, source_target_pairs={{0,1},{1,2},{2,3},{3,4},{4,5},{5,6},{6,7},{7,0},{8,9},{9,10},{10,1... | collective-permute-start | bytes 983048 | tf_op jit(solution)/shard_map/ppermute | solution.py:264
  45.6 33.1 %all-to-all-start.1 = ((bf16[32,8,16,128]{3,2,1,0:T(8,128)(2,1)}), bf16[32,8,16,128]{3,2,1,0:T(8,128)(2,1)}, u32[]{:S(2)}, u32[]{:S(2)}) async-start(bf16[32,8,16,128]{3,2,1,0:T(8,128)(2,1)} %pick.1), calls=%async_computation.1 | async-start | bytes 2097152 | tf_op jit(solution)/shard_map/all_to_all | solution.py:454
  53.2 11.4 %collective-permute-start.7 = (bf16[48,16,128]{2,1,0:T(8,128)(2,1)S(1)}, bf16[48,16,128]{2,1,0:T(8,128)(2,1)S(1)}, u32[]{:S(2)}, u32[]{:S(2)}) collective-permute-start(bf16[48,16,128]{2,1,0:T(8,128)(2,1)S(1)} %slice.56), channel_id=1, source_target_pairs={{0,7},{1,0},{2,1},{3,2},{4,3},{5,4},{6,5},{7,6},{8,15},{9,8},{10,9... | collective-permute-start | bytes 589832 | tf_op jit(solution)/shard_map/ppermute | solution.py:269
  80.1 14.9 %collective-permute-start.11 = (bf16[4,8,4,16,128]{4,3,2,1,0:T(8,128)(2,1)S(1)}, bf16[4,8,4,16,128]{4,3,2,1,0:T(8,128)(2,1)S(1)}, u32[]{:S(2)}, u32[]{:S(2)}) collective-permute-start(bf16[4,8,4,16,128]{4,3,2,1,0:T(8,128)(2,1)S(1)} %get-tuple-element.76.rest_0_), channel_id=1, source_target_pairs={{0,7},{1,0},{2,1},{3,2},{4,3},{5,4},{6,5},{7,6},{8,15},{9,8},{10,9... | collective-permute-start | bytes 1572872 | tf_op jit(solution)/shard_map/ppermute | solution.py:281
  81.1 16.1 %collective-permute-start.8 = (bf16[4,8,4,16,128]{4,3,2,1,0:T(8,128)(2,1)S(1)}, bf16[4,8,4,16,128]{4,3,2,1,0:T(8,128)(2,1)S(1)}, u32[]{:S(2)}, u32[]{:S(2)}) collective-permute-start(bf16[4,8,4,16,128]{4,3,2,1,0:T(8,128)(2,1)S(1)} %get-tuple-element.76.rest_0_), channel_id=1, source_target_pairs={{0,1},{1,2},{2,3},{3,4},{4,5},{5,6},{6,7},{7,0},{8,9},{9,10},{10,1... | collective-permute-start | bytes 1572872 | tf_op jit(solution)/shard_map/ppermute | solution.py:280
  82.2 24.4 %collective-permute-start.16 = (bf16[4,8,4,16,128]{4,3,2,1,0:T(8,128)(2,1)S(1)}, bf16[4,8,4,16,128]{4,3,2,1,0:T(8,128)(2,1)}, u32[]{:S(2)}, u32[]{:S(2)}) collective-permute-start(bf16[4,8,4,16,128]{4,3,2,1,0:T(8,128)(2,1)S(1)} %get-tuple-element.75.rest_0_), channel_id=1, source_target_pairs={{0,1},{1,2},{2,3},{3,4},{4,5},{5,6},{6,7},{7,0},{8,9},{9,10},{10,1... | collective-permute-start | bytes 1572872 | tf_op jit(solution)/shard_map/ppermute | solution.py:280
  82.3 24.4 %collective-permute-start.20 = (bf16[4,8,4,16,128]{4,3,2,1,0:T(8,128)(2,1)S(1)}, bf16[4,8,4,16,128]{4,3,2,1,0:T(8,128)(2,1)}, u32[]{:S(2)}, u32[]{:S(2)}) collective-permute-start(bf16[4,8,4,16,128]{4,3,2,1,0:T(8,128)(2,1)S(1)} %get-tuple-element.75.rest_0_), channel_id=1, source_target_pairs={{0,7},{1,0},{2,1},{3,2},{4,3},{5,4},{6,5},{7,6},{8,15},{9,8},{10,9... | collective-permute-start | bytes 1572872 | tf_op jit(solution)/shard_map/ppermute | solution.py:281
  98.0 67.6 %all-to-all-start.2 = ((bf16[32,16,16,128]{3,2,1,0:T(8,128)(2,1)}), bf16[32,16,16,128]{3,2,1,0:T(8,128)(2,1)S(1)}, u32[]{:S(2)}, u32[]{:S(2)}) async-start(bf16[32,16,16,128]{3,2,1,0:T(8,128)(2,1)} %copy-done.3), calls=%async_computation.2 | async-start | bytes 4194304 | tf_op jit(solution)/shard_map/all_to_all | solution.py:462
  106.7 16.3 %collective-permute-start.17 = (bf16[4,8,4,16,128]{4,3,2,1,0:T(8,128)(2,1)}, bf16[4,8,4,16,128]{4,3,2,1,0:T(8,128)(2,1)S(1)}, u32[]{:S(2)}, u32[]{:S(2)}) collective-permute-start(bf16[4,8,4,16,128]{4,3,2,1,0:T(8,128)(2,1)} %collective-permute-done.16.rest_0_), channel_id=1, source_target_pairs={{0,1},{1,2},{2,3},{3,4},{4,5},{5,6},{6,7},{7,0},{8,9},{9,10},{10,1... | collective-permute-start | bytes 1572872 | tf_op jit(solution)/shard_map/ppermute | solution.py:280
  106.7 16.3 %collective-permute-start.21 = (bf16[4,8,4,16,128]{4,3,2,1,0:T(8,128)(2,1)}, bf16[4,8,4,16,128]{4,3,2,1,0:T(8,128)(2,1)S(1)}, u32[]{:S(2)}, u32[]{:S(2)}) collective-permute-start(bf16[4,8,4,16,128]{4,3,2,1,0:T(8,128)(2,1)} %collective-permute-done.20.rest_1_), channel_id=1, source_target_pairs={{0,7},{1,0},{2,1},{3,2},{4,3},{5,4},{6,5},{7,6},{8,15},{9,8},{10,9... | collective-permute-start | bytes 1572872 | tf_op jit(solution)/shard_map/ppermute | solution.py:281
  109.9 24.3 %collective-permute-start.9 = (bf16[4,8,4,16,128]{4,3,2,1,0:T(8,128)(2,1)}, bf16[4,8,4,16,128]{4,3,2,1,0:T(8,128)(2,1)S(1)}, u32[]{:S(2)}, u32[]{:S(2)}) collective-permute-start(bf16[4,8,4,16,128]{4,3,2,1,0:T(8,128)(2,1)} %copy-done.16), channel_id=1, source_target_pairs={{0,1},{1,2},{2,3},{3,4},{4,5},{5,6},{6,7},{7,0},{8,9},{9,10},{10,1... | collective-permute-start | bytes 1572872 | tf_op jit(solution)/shard_map/ppermute | solution.py:280
  109.9 24.3 %collective-permute-start.12 = (bf16[4,8,4,16,128]{4,3,2,1,0:T(8,128)(2,1)}, bf16[4,8,4,16,128]{4,3,2,1,0:T(8,128)(2,1)S(1)}, u32[]{:S(2)}, u32[]{:S(2)}) collective-permute-start(bf16[4,8,4,16,128]{4,3,2,1,0:T(8,128)(2,1)} %copy-done.14), channel_id=1, source_target_pairs={{0,7},{1,0},{2,1},{3,2},{4,3},{5,4},{6,5},{7,6},{8,15},{9,8},{10,9... | collective-permute-start | bytes 1572872 | tf_op jit(solution)/shard_map/ppermute | solution.py:281
  122.9 22.5 %collective-permute-start.18 = (bf16[4,8,4,16,128]{4,3,2,1,0:T(8,128)(2,1)S(1)}, bf16[4,8,4,16,128]{4,3,2,1,0:T(8,128)(2,1)S(1)}, u32[]{:S(2)}, u32[]{:S(2)}) collective-permute-start(bf16[4,8,4,16,128]{4,3,2,1,0:T(8,128)(2,1)S(1)} %collective-permute-done.17.rest_0_), channel_id=1, source_target_pairs={{0,1},{1,2},{2,3},{3,4},{4,5},{5,6},{6,7},{7,0},{8,9},{9,10},{10,1... | collective-permute-start | bytes 1572872 | tf_op jit(solution)/shard_map/ppermute | solution.py:280
  123.0 22.6 %collective-permute-start.22 = (bf16[4,8,4,16,128]{4,3,2,1,0:T(8,128)(2,1)S(1)}, bf16[4,8,4,16,128]{4,3,2,1,0:T(8,128)(2,1)S(1)}, u32[]{:S(2)}, u32[]{:S(2)}) collective-permute-start(bf16[4,8,4,16,128]{4,3,2,1,0:T(8,128)(2,1)S(1)} %collective-permute-done.21.rest_1_), channel_id=1, source_target_pairs={{0,7},{1,0},{2,1},{3,2},{4,3},{5,4},{6,5},{7,6},{8,15},{9,8},{10,9... | collective-permute-start | bytes 1572872 | tf_op jit(solution)/shard_map/ppermute | solution.py:281
  134.2 31.4 %collective-permute-start.10 = (bf16[4,8,4,16,128]{4,3,2,1,0:T(8,128)(2,1)S(1)}, bf16[4,8,4,16,128]{4,3,2,1,0:T(8,128)(2,1)S(1)}, u32[]{:S(2)}, u32[]{:S(2)}) collective-permute-start(bf16[4,8,4,16,128]{4,3,2,1,0:T(8,128)(2,1)S(1)} %collective-permute-done.9.rest_0_), channel_id=1, source_target_pairs={{0,1},{1,2},{2,3},{3,4},{4,5},{5,6},{6,7},{7,0},{8,9},{9,10},{10,1... | collective-permute-start | bytes 1572872 | tf_op jit(solution)/shard_map/ppermute | solution.py:280
  134.2 31.4 %collective-permute-start.13 = (bf16[4,8,4,16,128]{4,3,2,1,0:T(8,128)(2,1)S(1)}, bf16[4,8,4,16,128]{4,3,2,1,0:T(8,128)(2,1)S(1)}, u32[]{:S(2)}, u32[]{:S(2)}) collective-permute-start(bf16[4,8,4,16,128]{4,3,2,1,0:T(8,128)(2,1)S(1)} %collective-permute-done.12.rest_1_), channel_id=1, source_target_pairs={{0,7},{1,0},{2,1},{3,2},{4,3},{5,4},{6,5},{7,6},{8,15},{9,8},{10,9... | collective-permute-start | bytes 1572872 | tf_op jit(solution)/shard_map/ppermute | solution.py:281
  145.4 14.8 %collective-permute-start.19 = (bf16[2,8,4,16,128]{4,3,2,1,0:T(8,128)(2,1)S(1)}, bf16[2,8,4,16,128]{4,3,2,1,0:T(8,128)(2,1)S(1)}, u32[]{:S(2)}, u32[]{:S(2)}) collective-permute-start(bf16[2,8,4,16,128]{4,3,2,1,0:T(8,128)(2,1)S(1)} %slice.59), channel_id=1, source_target_pairs={{0,1},{1,2},{2,3},{3,4},{4,5},{5,6},{6,7},{7,0},{8,9},{9,10},{10,1... | collective-permute-start | bytes 786440 | tf_op jit(solution)/shard_map/ppermute | solution.py:299
  145.6 14.7 %collective-permute-start.23 = (bf16[2,8,4,16,128]{4,3,2,1,0:T(8,128)(2,1)S(1)}, bf16[2,8,4,16,128]{4,3,2,1,0:T(8,128)(2,1)S(1)}, u32[]{:S(2)}, u32[]{:S(2)}) collective-permute-start(bf16[2,8,4,16,128]{4,3,2,1,0:T(8,128)(2,1)S(1)} %slice.60), channel_id=1, source_target_pairs={{0,7},{1,0},{2,1},{3,2},{4,3},{5,4},{6,5},{7,6},{8,15},{9,8},{10,9... | collective-permute-start | bytes 786440 | tf_op jit(solution)/shard_map/ppermute | solution.py:300
  163.6 15.6 %collective-permute-start.24 = (bf16[8,2,16,512]{3,2,1,0:T(8,128)(2,1)}, bf16[8,2,16,512]{3,2,1,0:T(8,128)(2,1)}, u32[]{:S(2)}, u32[]{:S(2)}) collective-permute-start(bf16[8,2,16,512]{3,2,1,0:T(8,128)(2,1)} %get-tuple-element.74.rest_1_), channel_id=1, source_target_pairs={{0,8},{8,16},{16,24},{24,32},{32,40},{40,48},{48,56},{56,64},{64,7... | collective-permute-start | bytes 786440 | tf_op jit(solution)/shard_map/ppermute | solution.py:468
  165.6 16.1 %collective-permute-start.14 = (bf16[2,8,4,16,128]{4,3,2,1,0:T(8,128)(2,1)S(1)}, bf16[2,8,4,16,128]{4,3,2,1,0:T(8,128)(2,1)S(1)}, u32[]{:S(2)}, u32[]{:S(2)}) collective-permute-start(bf16[2,8,4,16,128]{4,3,2,1,0:T(8,128)(2,1)S(1)} %slice.45), channel_id=1, source_target_pairs={{0,1},{1,2},{2,3},{3,4},{4,5},{5,6},{6,7},{7,0},{8,9},{9,10},{10,1... | collective-permute-start | bytes 786440 | tf_op jit(solution)/shard_map/ppermute | solution.py:299
  165.7 16.0 %collective-permute-start.15 = (bf16[2,8,4,16,128]{4,3,2,1,0:T(8,128)(2,1)S(1)}, bf16[2,8,4,16,128]{4,3,2,1,0:T(8,128)(2,1)S(1)}, u32[]{:S(2)}, u32[]{:S(2)}) collective-permute-start(bf16[2,8,4,16,128]{4,3,2,1,0:T(8,128)(2,1)S(1)} %slice.46), channel_id=1, source_target_pairs={{0,7},{1,0},{2,1},{3,2},{4,3},{5,4},{6,5},{7,6},{8,15},{9,8},{10,9... | collective-permute-start | bytes 786440 | tf_op jit(solution)/shard_map/ppermute | solution.py:300
  (44 other events, 228.4 us)

commit v8 on v7

--- a/solution.py
+++ b/solution.py
@@ -270,37 +270,33 @@
     ]
 
 
-def ring_project(streams, where, weights, n_ten, send_beside):
+def ring_project(streams, where, weights, n_ten):
     right, left = ring_ways(n_ten)
     half = streams[0].shape[0] // 2
+    last = n_ten // 2
     go_right, go_left = list(streams), list(streams)
-    states = [gather_step([x], [(0, 0)], where, weights, (), False) for x in streams]
-    for step in range(1, n_ten // 2):
+    blocks = [[x] for x in streams]
+    places = [[(0, 0)] for _ in streams]
+    states = [()] * len(streams)
+    for step in range(1, last):
         for s in range(len(streams)):
             go_right[s] = lax.ppermute(go_right[s], "tensor", right)
             go_left[s] = lax.ppermute(go_left[s], "tensor", left)
-            states[s] = gather_step(
-                [go_right[s], go_left[s]],
-                [(n_ten - step, 0), (step, 0)],
-                where,
-                weights,
-                states[s],
-                False,
-            )
-        if step == 1:
-            beside = send_beside(*zip(go_right, go_left))
-    places = [(n_ten // 2, 0), (n_ten // 2, half)]
+            blocks[s] += [go_right[s], go_left[s]]
+            places[s] += [(n_ten - step, 0), (step, 0)]
+            if step == last - 2:
+                states[s] = gather_step(blocks[s], places[s], where, weights, (), False)
+                blocks[s], places[s] = [], []
+    arrivals = None
     for s in range(len(streams)):
-        from_left, from_right = go_right[s], go_left[s]
-        if s == len(streams) - 1:
-            held = lax.optimization_barrier((from_left, from_right, beside))
-            from_left, from_right, beside = held
-        blocks = [
-            lax.ppermute(from_left[:half], "tensor", right),
-            lax.ppermute(from_right[half:], "tensor", left),
+        blocks[s] += [
+            lax.ppermute(go_right[s][:half], "tensor", right),
+            lax.ppermute(go_left[s][half:], "tensor", left),
         ]
-        states[s] = gather_step(blocks, places, where, weights, states[s], True)
-    return states, beside
+        places[s] += [(last, 0), (last, half)]
+        arrivals = blocks[s][-2:] if arrivals is None else arrivals
+        states[s] = gather_step(blocks[s], places[s], where, weights, states[s], True)
+    return states, arrivals
 
 
 def weigh(scores, count, keys_axis_owner):
@@ -444,27 +440,22 @@
     mine = letter(own, tokens, wo, wo.shape[0] // strips)
     letters = ring_gather(mine, n_ten, tok_dev // PIECE_T * (pieces_f // 2))
 
-    spread, index, _ = lax.optimization_barrier((spread, index, letters[3:5]))
-    spread = spread.reshape(n_seq * (per_shard + 1), PIECE_T, PIECE_F)
-    (picked,) = pick(index, spread, 1)
-    nbr_gain, _ = lax.optimization_barrier((nbr_gain, picked))
     both = jnp.concatenate([wk, wv], axis=1).astype(jnp.float32)
     both = (both * nbr_gain.astype(jnp.float32)[:, None]).astype(jnp.bfloat16)
     both = both.reshape(n_ten, d_part, both.shape[1])
+    spread, index, both, _ = lax.optimization_barrier((spread, index, both, letters[3:5]))
+    spread = spread.reshape(n_seq * (per_shard + 1), PIECE_T, PIECE_F)
+    (picked,) = pick(index, spread, 1)
     rows = lax.all_to_all(picked, "seq", split_axis=0, concat_axis=0, tiled=True)
     queries, strip = query(where, letters, x_gain, wq, tok_dev, shift, n_seq)
-    rows, queries, strip, both, counts = lax.optimization_barrier(
-        (rows, queries, strip, both, counts)
-    )
-
-    def send_mail(first, second):
-        mail, _ = lax.optimization_barrier((strip, second))
-        mail = lax.all_to_all(mail, "seq", split_axis=0, concat_axis=0, tiled=True)
-        return mail.reshape(strips, halves, *strip.shape[1:])
+    rows, queries, counts = lax.optimization_barrier((rows, queries, counts))
 
     rows = rows.reshape(pieces_f, pieces_t, items, PIECE_T, PIECE_F)
     streams = [rows[:, :, items // 2 :], rows[:, :, : items // 2]]
-    (late, early), mail = ring_project(streams, where, both, n_ten, send_mail)
+    (late, early), arrivals = ring_project(streams, where, both, n_ten)
+    strip, _ = lax.optimization_barrier((strip, arrivals))
+    mail = lax.all_to_all(strip, "seq", split_axis=0, concat_axis=0, tiled=True)
+    mail = mail.reshape(strips, halves, *strip.shape[1:])
     prev = lax.ppermute(late[-1], "seq", [(i, i + 1) for i in range(n_seq - 1)])
     attended = attend(counts, queries, late, span_dev // 2, span_len, prev=prev)
     attended = attend(counts, queries, early, 0, span_len, after=attended)

time: 216 us -> 226 us (1.046)
  waiting for transfers between devices: 65.2 us -> 81.3 us
  Pallas kernels: 40.6 us -> 28.7 us
  starting transfers between devices: 80.3 us -> 84.9 us
    ppermute x6, waiting for transfers between devices: 17.6 us -> 37.8 us  [ring_project(): go_right[s] = lax.ppermute(go_right[s], 'tensor', right)]
    pallas_call x10 -> x4, Pallas kernels: 25.9 us -> 14.6 us  [gather_step(): pl.pallas_call(functools.partial(gather_kernel, tuple(places), not state,...]
    ppermute x6, waiting for transfers between devices: 9.61 us -> 0.25 us  [ring_project(): go_left[s] = lax.ppermute(go_left[s], 'tensor', left)]
    all_to_all x1, waiting for transfers between devices: 0.01 us -> 7.82 us  [body(): lax.all_to_all(pieces, 'seq', split_axis=0, concat_axis=0, tiled=True)]
    ppermute x6, waiting for transfers between devices: 13.3 us -> 7.61 us  [ring_gather(): go_left = lax.ppermute(go_left, 'tensor', left)]
    ppermute x1, waiting for transfers between devices: 0.01 us -> 3.63 us  [body(): prev = lax.ppermute(late[-1], 'seq', [(i, i + 1) for i in range(n_seq - 1)])]
    ppermute x6, waiting for transfers between devices: 10.7 us -> 13.6 us  [ring_gather(): go_right = lax.ppermute(go_right, 'tensor', right)]
    ppermute x6, starting transfers between devices: 17.1 us -> 20 us  [ring_project(): go_left[s] = lax.ppermute(go_left[s], 'tensor', left)]
  transfers between devices with their start and end apart: 36 -> 36, of which waited for: 14 -> 19; matrix products, arithmetic and copies ran while one was open for 3% -> 4% of each run, Pallas kernels for 16% -> 11%
where the time goes in v8:
time: 226 us; the launch traced here: 225 us
  starting transfers between devices  84.9 us (38%)
  waiting for transfers between devices  81.3 us (36%)
  Pallas kernels  28.7 us (13%)
  local copies, waits for them, and re-layouts  23.4 us (10%)
  other arithmetic  5.48 us (2%)
    ppermute x6, waiting for transfers between devices, ring_project(): go_right[s] = lax.ppermute(go_right[s], 'tensor', right)  37.8 us
    ppermute x6, starting transfers between devices, ring_gather(): go_left = lax.ppermute(go_left, 'tensor', left)  23.5 us
    ppermute x6, starting transfers between devices, ring_project(): go_left[s] = lax.ppermute(go_left[s], 'tensor', left)  20 us
    unnamed x66, local copies, waits for them, and re-layouts  18.6 us
    pallas_call x4, Pallas kernels, gather_step(): pl.pallas_call(functools.partial(gather_kernel, tuple(places), not state,...  14.6 us
    ppermute x6, waiting for transfers between devices, ring_gather(): go_right = lax.ppermute(go_right, 'tensor', right)  13.6 us
    ppermute x2, waiting for transfers between devices, ring_gather(): lax.ppermute(go_right[:cut_at], 'tensor', right)  7.98 us
    all_to_all x1, starting transfers between devices, body(): lax.all_to_all(picked, 'seq', split_axis=0, concat_axis=0, tiled=True)  7.96 us
  transfers between devices with their start and end apart: 36, of which 19 were waited for; matrix products, arithmetic and copies ran while one was open for 4% of the time, Pallas kernels for 11%

profile of v8, /device:TPU:8, one launch (start us, length us, event | category | flops | bytes accessed | tf_op | source)
XLA Modules:
  0.0 224.8 jit_solution(5467714152228747644)
XLA Ops:
  5.4 7.5 %all-to-all-start = ((bf16[32,17,16,128]{3,2,1,0:T(8,128)(2,1)}), bf16[32,17,16,128]{3,2,1,0:T(8,128)(2,1)S(1)}, u32[]{:S(2)}, u32[]{:S(2)}) async-start(bf16[32,17,16,128]{3,2,1,0:T(8,128)(2,1)} %copy-done), calls=%async_computation | async-start | bytes 4456448 | tf_op jit(solution)/shard_map/all_to_all | solution.py:429
  18.0 3.9 %collective-permute-start.1 = (bf16[80,16,128]{2,1,0:T(8,128)(2,1)}, bf16[80,16,128]{2,1,0:T(8,128)(2,1)S(1)}, u32[]{:S(2)}, u32[]{:S(2)}) collective-permute-start(bf16[80,16,128]{2,1,0:T(8,128)(2,1)} %letter.1.rest_0_), channel_id=1, source_target_pairs={{0,7},{1,0},{2,1},{3,2},{4,3},{5,4},{6,5},{7,6},{8,15},{9,8},{10,9... | collective-permute-start | bytes 983048 | tf_op jit(solution)/shard_map/ppermute | solution.py:265
  21.9 4.1 %multiply_convert_fusion.w_ref = bf16[8,512,512]{2,1,0:T(8,128)(2,1)} fusion(bf16[8,512,256]{2,1,0:T(8,128)(2,1)} %bitcast.20, bf16[8,512,256]{2,1,0:T(8,128)(2,1)} %bitcast.21, f32[8,512]{1,0:T(8,128)S(1)} %reshape.37), kind=kLoop, calls=%fused_computation | loop fusion | flops 12582912 | bytes 8404992 | tf_op jit(solution)/shard_map/convert_element_type | solution.py:444
  26.0 4.2 %collective-permute-done.rest_1_ = bf16[80,16,128]{2,1,0:T(8,128)(2,1)S(1)} collective-permute-done((bf16[80,16,128]{2,1,0:T(8,128)(2,1)}, bf16[80,16,128]{2,1,0:T(8,128)(2,1)S(1)}, u32[]{:S(2)}, u32[]{:S(2)}) %collective-permute-start) | collective-permute-done | bytes 327712 | tf_op jit(solution)/shard_map/ppermute | solution.py:264
  33.4 7.8 %all-to-all-done = bf16[32,17,16,128]{3,2,1,0:T(8,128)(2,1)S(1)} async-done(((bf16[32,17,16,128]{3,2,1,0:T(8,128)(2,1)}), bf16[32,17,16,128]{3,2,1,0:T(8,128)(2,1)S(1)}, u32[]{:S(2)}, u32[]{:S(2)}) %all-to-all-start) | async-done | bytes 2228256 | tf_op jit(solution)/shard_map/all_to_all | solution.py:429
  44.9 8.0 %all-to-all-start.1 = ((bf16[32,8,16,128]{3,2,1,0:T(8,128)(2,1)}), bf16[32,8,16,128]{3,2,1,0:T(8,128)(2,1)}, u32[]{:S(2)}, u32[]{:S(2)}) async-start(bf16[32,8,16,128]{3,2,1,0:T(8,128)(2,1)} %pick.1), calls=%async_computation.1 | async-start | bytes 2097152 | tf_op jit(solution)/shard_map/all_to_all | solution.py:449
  52.9 5.9 %collective-permute-start.5 = (bf16[80,16,128]{2,1,0:T(8,128)(2,1)}, bf16[80,16,128]{2,1,0:T(8,128)(2,1)S(1)}, u32[]{:S(2)}, u32[]{:S(2)}) collective-permute-start(bf16[80,16,128]{2,1,0:T(8,128)(2,1)} %copy-done.27), channel_id=1, source_target_pairs={{0,7},{1,0},{2,1},{3,2},{4,3},{5,4},{6,5},{7,6},{8,15},{9,8},{10,9... | collective-permute-start | bytes 983048 | tf_op jit(solution)/shard_map/ppermute | solution.py:265
  58.8 7.6 %collective-permute-done.5.rest_6_ = bf16[80,16,128]{2,1,0:T(8,128)(2,1)S(1)} collective-permute-done((bf16[80,16,128]{2,1,0:T(8,128)(2,1)}, bf16[80,16,128]{2,1,0:T(8,128)(2,1)S(1)}, u32[]{:S(2)}, u32[]{:S(2)}) %collective-permute-start.5) | collective-permute-done | bytes 327712 | tf_op jit(solution)/shard_map/ppermute | solution.py:265
  66.4 3.7 %collective-permute-start.7 = (bf16[48,16,128]{2,1,0:T(8,128)(2,1)S(1)}, bf16[48,16,128]{2,1,0:T(8,128)(2,1)S(1)}, u32[]{:S(2)}, u32[]{:S(2)}) collective-permute-start(bf16[48,16,128]{2,1,0:T(8,128)(2,1)S(1)} %slice.53), channel_id=1, source_target_pairs={{0,7},{1,0},{2,1},{3,2},{4,3},{5,4},{6,5},{7,6},{8,15},{9,8},{10,9... | collective-permute-start | bytes 589832 | tf_op jit(solution)/shard_map/ppermute | solution.py:269
  70.3 6.1 %collective-permute-done.6.rest_7_ = bf16[32,16,128]{2,1,0:T(8,128)(2,1)S(1)} collective-permute-done((bf16[32,16,128]{2,1,0:T(8,128)(2,1)S(1)}, bf16[32,16,128]{2,1,0:T(8,128)(2,1)S(1)}, u32[]{:S(2)}, u32[]{:S(2)}) %collective-permute-start.6) | collective-permute-done | bytes 131104 | tf_op jit(solution)/shard_map/ppermute | solution.py:268
  88.6 9.8 %collective-permute-done.8.rest_1_ = bf16[4,8,4,16,128]{4,3,2,1,0:T(8,128)(2,1)S(1)} collective-permute-done((bf16[4,8,4,16,128]{4,3,2,1,0:T(8,128)(2,1)S(1)}, bf16[4,8,4,16,128]{4,3,2,1,0:T(8,128)(2,1)S(1)}, u32[]{:S(2)}, u32[]{:S(2)}) %collective-permute-start.8) | collective-permute-done | bytes 524320 | tf_op jit(solution)/shard_map/ppermute | solution.py:283
  106.4 8.0 %collective-permute-done.9.rest_3_ = bf16[4,8,4,16,128]{4,3,2,1,0:T(8,128)(2,1)S(1)} collective-permute-done((bf16[4,8,4,16,128]{4,3,2,1,0:T(8,128)(2,1)S(1)}, bf16[4,8,4,16,128]{4,3,2,1,0:T(8,128)(2,1)S(1)}, u32[]{:S(2)}, u32[]{:S(2)}) %collective-permute-start.9) | collective-permute-done | bytes 524320 | tf_op jit(solution)/shard_map/ppermute | solution.py:283
  118.5 7.2 %collective-permute-done.16.rest_1_ = bf16[4,8,4,16,128]{4,3,2,1,0:T(8,128)(2,1)S(1)} collective-permute-done((bf16[4,8,4,16,128]{4,3,2,1,0:T(8,128)(2,1)S(1)}, bf16[4,8,4,16,128]{4,3,2,1,0:T(8,128)(2,1)S(1)}, u32[]{:S(2)}, u32[]{:S(2)}) %collective-permute-start.16) | collective-permute-done | bytes 524320 | tf_op jit(solution)/shard_map/ppermute | solution.py:283
  130.6 6.4 %collective-permute-done.10.rest_0_ = bf16[4,8,4,16,128]{4,3,2,1,0:T(8,128)(2,1)S(1)} collective-permute-done((bf16[4,8,4,16,128]{4,3,2,1,0:T(8,128)(2,1)S(1)}, bf16[4,8,4,16,128]{4,3,2,1,0:T(8,128)(2,1)S(1)}, u32[]{:S(2)}, u32[]{:S(2)}) %collective-permute-start.10) | collective-permute-done | bytes 524320 | tf_op jit(solution)/shard_map/ppermute | solution.py:283
  141.8 6.4 %collective-permute-done.17.rest_3_ = bf16[4,8,4,16,128]{4,3,2,1,0:T(8,128)(2,1)} collective-permute-done((bf16[4,8,4,16,128]{4,3,2,1,0:T(8,128)(2,1)S(1)}, bf16[4,8,4,16,128]{4,3,2,1,0:T(8,128)(2,1)}, u32[]{:S(2)}, u32[]{:S(2)}) %collective-permute-start.17) | collective-permute-done | bytes 524320 | tf_op jit(solution)/shard_map/ppermute | solution.py:283
  148.5 3.8 %collective-permute-start.21 = (bf16[4,8,4,16,128]{4,3,2,1,0:T(8,128)(2,1)}, bf16[4,8,4,16,128]{4,3,2,1,0:T(8,128)(2,1)}, u32[]{:S(2)}, u32[]{:S(2)}) collective-permute-start(bf16[4,8,4,16,128]{4,3,2,1,0:T(8,128)(2,1)} %collective-permute-done.20.rest_4_), channel_id=1, source_target_pairs={{0,7},{1,0},{2,1},{3,2},{4,3},{5,4},{6,5},{7,6},{8,15},{9,8},{10,9... | collective-permute-start | bytes 1572872 | tf_op jit(solution)/shard_map/ppermute | solution.py:284
  154.8 7.3 %all-to-all-start.2 = ((bf16[32,16,16,128]{3,2,1,0:T(8,128)(2,1)}), bf16[32,16,16,128]{3,2,1,0:T(8,128)(2,1)S(1)}, u32[]{:S(2)}, u32[]{:S(2)}) async-start(bf16[32,16,16,128]{3,2,1,0:T(8,128)(2,1)} %copy-done.2), calls=%async_computation.2 | async-start | bytes 4194304 | tf_op jit(solution)/shard_map/all_to_all | solution.py:457
  166.3 3.8 %gather_step.3 = (f32[512,512]{1,0:T(8,128)S(1)}, f32[512,128]{1,0:T(8,128)S(1)}) custom-call(s32[8]{0:T(128)S(1)} %and_select_fusion.where_ref, bf16[8,512,512]{2,1,0:T(8,128)(2,1)} %multiply_convert_fusion.w_ref, bf16[4,8,4,16,128]{4,3,2,1,0:T(8,128)(2,1)S(1)} %get-tuple-element.42.rest_0_, bf16[4,8,4,16,128]{4,3,2,1,0:T(8,128)(2,1)S(1)} %copy-done.14, ...), custom_call_target="tpu_custom_call" | custom-call | flops 5368709120 | bytes 4718592 | tf_op jit(solution)/shard_map/gather_step/pallas_call | solution.py:237
  170.2 4.1 %gather_step.2 = (f32[512,512]{1,0:T(8,128)S(1)}, f32[512,128]{1,0:T(8,128)S(1)}) custom-call(s32[8]{0:T(128)S(1)} %and_select_fusion.where_ref, bf16[8,512,512]{2,1,0:T(8,128)(2,1)} %multiply_convert_fusion.w_ref, bf16[4,8,4,16,128]{4,3,2,1,0:T(8,128)(2,1)S(1)} %get-tuple-element.41.rest_0_, bf16[4,8,4,16,128]{4,3,2,1,0:T(8,128)(2,1)S(1)} %copy-done.22, ...), custom_call_target="tpu_custom_call" | custom-call | flops 5368709120 | bytes 4718592 | tf_op jit(solution)/shard_map/gather_step/pallas_call | solution.py:237
  176.6 3.8 %collective-permute-start.23 = (bf16[2,8,4,16,128]{4,3,2,1,0:T(8,128)(2,1)S(1)}, bf16[2,8,4,16,128]{4,3,2,1,0:T(8,128)(2,1)S(1)}, u32[]{:S(2)}, u32[]{:S(2)}) collective-permute-start(bf16[2,8,4,16,128]{4,3,2,1,0:T(8,128)(2,1)S(1)} %slice.62), channel_id=1, source_target_pairs={{0,7},{1,0},{2,1},{3,2},{4,3},{5,4},{6,5},{7,6},{8,15},{9,8},{10,9... | collective-permute-start | bytes 786440 | tf_op jit(solution)/shard_map/ppermute | solution.py:294
  189.8 3.6 %collective-permute-done.24.rest_2_ = bf16[8,2,16,512]{3,2,1,0:T(8,128)(2,1)S(1)} collective-permute-done((bf16[8,2,16,512]{3,2,1,0:T(8,128)(2,1)S(1)}, bf16[8,2,16,512]{3,2,1,0:T(8,128)(2,1)S(1)}, u32[]{:S(2)}, u32[]{:S(2)}) %collective-permute-start.24) | collective-permute-done | bytes 262176 | tf_op jit(solution)/shard_map/ppermute | solution.py:459
  207.2 3.8 %collective-permute-done.27.rest_3_ = bf16[256,256]{1,0:T(8,128)(2,1)S(1)} collective-permute-done((bf16[256,256]{1,0:T(8,128)(2,1)S(1)}, bf16[256,256]{1,0:T(8,128)(2,1)S(1)}, u32[]{:S(2)}, u32[]{:S(2)}) %collective-permute-start.27) | collective-permute-done | bytes 131104 | tf_op jit(solution)/shard_map/ppermute | solution.py:264
  211.1 3.6 %collective-permute-start.30 = (bf16[256,256]{1,0:T(8,128)(2,1)S(1)}, bf16[256,256]{1,0:T(8,128)(2,1)S(1)}, u32[]{:S(2)}, u32[]{:S(2)}) collective-permute-start(bf16[256,256]{1,0:T(8,128)(2,1)S(1)} %collective-permute-done.28.rest_4_), channel_id=1, source_target_pairs={{0,7},{1,0},{2,1},{3,2},{4,3},{5,4},{6,5},{7,6},{8,15},{9,8},{10,9... | collective-permute-start | bytes 393224 | tf_op jit(solution)/shard_map/ppermute | solution.py:265
  217.3 3.6 %collective-permute-start.32 = (bf16[128,256]{1,0:T(8,128)(2,1)S(1)}, bf16[128,256]{1,0:T(8,128)(2,1)S(1)}, u32[]{:S(2)}, u32[]{:S(2)}) collective-permute-start(bf16[128,256]{1,0:T(8,128)(2,1)S(1)} %slice.64), channel_id=1, source_target_pairs={{0,7},{1,0},{2,1},{3,2},{4,3},{5,4},{6,5},{7,6},{8,15},{9,8},{10,9... | collective-permute-start | bytes 196616 | tf_op jit(solution)/shard_map/ppermute | solution.py:269
  (144 shorter events, 89.7 us)
Async XLA Ops:
  5.4 35.8 %all-to-all-start = ((bf16[32,17,16,128]{3,2,1,0:T(8,128)(2,1)}), bf16[32,17,16,128]{3,2,1,0:T(8,128)(2,1)S(1)}, u32[]{:S(2)}, u32[]{:S(2)}) async-start(bf16[32,17,16,128]{3,2,1,0:T(8,128)(2,1)} %copy-done), calls=%async_computation | async-start | bytes 4456448 | tf_op jit(solution)/shard_map/all_to_all | solution.py:429
  16.1 14.1 %collective-permute-start = (bf16[80,16,128]{2,1,0:T(8,128)(2,1)}, bf16[80,16,128]{2,1,0:T(8,128)(2,1)S(1)}, u32[]{:S(2)}, u32[]{:S(2)}) collective-permute-start(bf16[80,16,128]{2,1,0:T(8,128)(2,1)} %letter.1.rest_0_), channel_id=1, source_target_pairs={{0,1},{1,2},{2,3},{3,4},{4,5},{5,6},{6,7},{7,0},{8,9},{9,10},{10,1... | collective-permute-start | bytes 983048 | tf_op jit(solution)/shard_map/ppermute | solution.py:264
  18.0 12.2 %collective-permute-start.1 = (bf16[80,16,128]{2,1,0:T(8,128)(2,1)}, bf16[80,16,128]{2,1,0:T(8,128)(2,1)S(1)}, u32[]{:S(2)}, u32[]{:S(2)}) collective-permute-start(bf16[80,16,128]{2,1,0:T(8,128)(2,1)} %letter.1.rest_0_), channel_id=1, source_target_pairs={{0,7},{1,0},{2,1},{3,2},{4,3},{5,4},{6,5},{7,6},{8,15},{9,8},{10,9... | collective-permute-start | bytes 983048 | tf_op jit(solution)/shard_map/ppermute | solution.py:265
  30.2 11.8 %collective-permute-start.2 = (bf16[80,16,128]{2,1,0:T(8,128)(2,1)S(1)}, bf16[80,16,128]{2,1,0:T(8,128)(2,1)S(1)}, u32[]{:S(2)}, u32[]{:S(2)}) collective-permute-start(bf16[80,16,128]{2,1,0:T(8,128)(2,1)S(1)} %collective-permute-done.rest_1_), channel_id=1, source_target_pairs={{0,1},{1,2},{2,3},{3,4},{4,5},{5,6},{6,7},{7,0},{8,9},{9,10},{10,1... | collective-permute-start | bytes 983048 | tf_op jit(solution)/shard_map/ppermute | solution.py:264
  30.2 11.8 %collective-permute-start.3 = (bf16[80,16,128]{2,1,0:T(8,128)(2,1)S(1)}, bf16[80,16,128]{2,1,0:T(8,128)(2,1)S(1)}, u32[]{:S(2)}, u32[]{:S(2)}) collective-permute-start(bf16[80,16,128]{2,1,0:T(8,128)(2,1)S(1)} %collective-permute-done.1.rest_2_), channel_id=1, source_target_pairs={{0,7},{1,0},{2,1},{3,2},{4,3},{5,4},{6,5},{7,6},{8,15},{9,8},{10,9... | collective-permute-start | bytes 983048 | tf_op jit(solution)/shard_map/ppermute | solution.py:265
  44.9 38.9 %all-to-all-start.1 = ((bf16[32,8,16,128]{3,2,1,0:T(8,128)(2,1)}), bf16[32,8,16,128]{3,2,1,0:T(8,128)(2,1)}, u32[]{:S(2)}, u32[]{:S(2)}) async-start(bf16[32,8,16,128]{3,2,1,0:T(8,128)(2,1)} %pick.1), calls=%async_computation.1 | async-start | bytes 2097152 | tf_op jit(solution)/shard_map/all_to_all | solution.py:449
  52.9 13.5 %collective-permute-start.5 = (bf16[80,16,128]{2,1,0:T(8,128)(2,1)}, bf16[80,16,128]{2,1,0:T(8,128)(2,1)S(1)}, u32[]{:S(2)}, u32[]{:S(2)}) collective-permute-start(bf16[80,16,128]{2,1,0:T(8,128)(2,1)} %copy-done.27), channel_id=1, source_target_pairs={{0,7},{1,0},{2,1},{3,2},{4,3},{5,4},{6,5},{7,6},{8,15},{9,8},{10,9... | collective-permute-start | bytes 983048 | tf_op jit(solution)/shard_map/ppermute | solution.py:265
  58.8 11.3 %collective-permute-start.4 = (bf16[80,16,128]{2,1,0:T(8,128)(2,1)S(1)}, bf16[80,16,128]{2,1,0:T(8,128)(2,1)S(1)}, u32[]{:S(2)}, u32[]{:S(2)}) collective-permute-start(bf16[80,16,128]{2,1,0:T(8,128)(2,1)S(1)} %collective-permute-done.2.rest_3_), channel_id=1, source_target_pairs={{0,1},{1,2},{2,3},{3,4},{4,5},{5,6},{6,7},{7,0},{8,9},{9,10},{10,1... | collective-permute-start | bytes 983048 | tf_op jit(solution)/shard_map/ppermute | solution.py:264
  85.3 13.1 %collective-permute-start.8 = (bf16[4,8,4,16,128]{4,3,2,1,0:T(8,128)(2,1)S(1)}, bf16[4,8,4,16,128]{4,3,2,1,0:T(8,128)(2,1)S(1)}, u32[]{:S(2)}, u32[]{:S(2)}) collective-permute-start(bf16[4,8,4,16,128]{4,3,2,1,0:T(8,128)(2,1)S(1)} %get-tuple-element.42.rest_0_), channel_id=1, source_target_pairs={{0,1},{1,2},{2,3},{3,4},{4,5},{5,6},{6,7},{7,0},{8,9},{9,10},{10,1... | collective-permute-start | bytes 1572872 | tf_op jit(solution)/shard_map/ppermute | solution.py:283
  85.4 13.8 %collective-permute-start.12 = (bf16[4,8,4,16,128]{4,3,2,1,0:T(8,128)(2,1)S(1)}, bf16[4,8,4,16,128]{4,3,2,1,0:T(8,128)(2,1)S(1)}, u32[]{:S(2)}, u32[]{:S(2)}) collective-permute-start(bf16[4,8,4,16,128]{4,3,2,1,0:T(8,128)(2,1)S(1)} %get-tuple-element.42.rest_0_), channel_id=1, source_target_pairs={{0,7},{1,0},{2,1},{3,2},{4,3},{5,4},{6,5},{7,6},{8,15},{9,8},{10,9... | collective-permute-start | bytes 1572872 | tf_op jit(solution)/shard_map/ppermute | solution.py:284
  98.4 16.1 %collective-permute-start.9 = (bf16[4,8,4,16,128]{4,3,2,1,0:T(8,128)(2,1)S(1)}, bf16[4,8,4,16,128]{4,3,2,1,0:T(8,128)(2,1)S(1)}, u32[]{:S(2)}, u32[]{:S(2)}) collective-permute-start(bf16[4,8,4,16,128]{4,3,2,1,0:T(8,128)(2,1)S(1)} %collective-permute-done.8.rest_1_), channel_id=1, source_target_pairs={{0,1},{1,2},{2,3},{3,4},{4,5},{5,6},{6,7},{7,0},{8,9},{9,10},{10,1... | collective-permute-start | bytes 1572872 | tf_op jit(solution)/shard_map/ppermute | solution.py:283
  99.2 16.1 %collective-permute-start.13 = (bf16[4,8,4,16,128]{4,3,2,1,0:T(8,128)(2,1)S(1)}, bf16[4,8,4,16,128]{4,3,2,1,0:T(8,128)(2,1)S(1)}, u32[]{:S(2)}, u32[]{:S(2)}) collective-permute-start(bf16[4,8,4,16,128]{4,3,2,1,0:T(8,128)(2,1)S(1)} %collective-permute-done.12.rest_2_), channel_id=1, source_target_pairs={{0,7},{1,0},{2,1},{3,2},{4,3},{5,4},{6,5},{7,6},{8,15},{9,8},{10,9... | collective-permute-start | bytes 1572872 | tf_op jit(solution)/shard_map/ppermute | solution.py:284
  103.2 22.5 %collective-permute-start.16 = (bf16[4,8,4,16,128]{4,3,2,1,0:T(8,128)(2,1)S(1)}, bf16[4,8,4,16,128]{4,3,2,1,0:T(8,128)(2,1)S(1)}, u32[]{:S(2)}, u32[]{:S(2)}) collective-permute-start(bf16[4,8,4,16,128]{4,3,2,1,0:T(8,128)(2,1)S(1)} %get-tuple-element.41.rest_0_), channel_id=1, source_target_pairs={{0,1},{1,2},{2,3},{3,4},{4,5},{5,6},{6,7},{7,0},{8,9},{9,10},{10,1... | collective-permute-start | bytes 1572872 | tf_op jit(solution)/shard_map/ppermute | solution.py:283
  103.2 23.3 %collective-permute-start.19 = (bf16[4,8,4,16,128]{4,3,2,1,0:T(8,128)(2,1)S(1)}, bf16[4,8,4,16,128]{4,3,2,1,0:T(8,128)(2,1)S(1)}, u32[]{:S(2)}, u32[]{:S(2)}) collective-permute-start(bf16[4,8,4,16,128]{4,3,2,1,0:T(8,128)(2,1)S(1)} %get-tuple-element.41.rest_0_), channel_id=1, source_target_pairs={{0,7},{1,0},{2,1},{3,2},{4,3},{5,4},{6,5},{7,6},{8,15},{9,8},{10,9... | collective-permute-start | bytes 1572872 | tf_op jit(solution)/shard_map/ppermute | solution.py:284
  114.4 22.5 %collective-permute-start.10 = (bf16[4,8,4,16,128]{4,3,2,1,0:T(8,128)(2,1)S(1)}, bf16[4,8,4,16,128]{4,3,2,1,0:T(8,128)(2,1)S(1)}, u32[]{:S(2)}, u32[]{:S(2)}) collective-permute-start(bf16[4,8,4,16,128]{4,3,2,1,0:T(8,128)(2,1)S(1)} %collective-permute-done.9.rest_3_), channel_id=1, source_target_pairs={{0,1},{1,2},{2,3},{3,4},{4,5},{5,6},{6,7},{7,0},{8,9},{9,10},{10,1... | collective-permute-start | bytes 1572872 | tf_op jit(solution)/shard_map/ppermute | solution.py:283
  115.3 22.5 %collective-permute-start.14 = (bf16[4,8,4,16,128]{4,3,2,1,0:T(8,128)(2,1)S(1)}, bf16[4,8,4,16,128]{4,3,2,1,0:T(8,128)(2,1)S(1)}, u32[]{:S(2)}, u32[]{:S(2)}) collective-permute-start(bf16[4,8,4,16,128]{4,3,2,1,0:T(8,128)(2,1)S(1)} %collective-permute-done.13.rest_4_), channel_id=1, source_target_pairs={{0,7},{1,0},{2,1},{3,2},{4,3},{5,4},{6,5},{7,6},{8,15},{9,8},{10,9... | collective-permute-start | bytes 1572872 | tf_op jit(solution)/shard_map/ppermute | solution.py:284
  125.7 22.6 %collective-permute-start.17 = (bf16[4,8,4,16,128]{4,3,2,1,0:T(8,128)(2,1)S(1)}, bf16[4,8,4,16,128]{4,3,2,1,0:T(8,128)(2,1)}, u32[]{:S(2)}, u32[]{:S(2)}) collective-permute-start(bf16[4,8,4,16,128]{4,3,2,1,0:T(8,128)(2,1)S(1)} %collective-permute-done.16.rest_1_), channel_id=1, source_target_pairs={{0,1},{1,2},{2,3},{3,4},{4,5},{5,6},{6,7},{7,0},{8,9},{9,10},{10,1... | collective-permute-start | bytes 1572872 | tf_op jit(solution)/shard_map/ppermute | solution.py:283
  126.5 22.0 %collective-permute-start.20 = (bf16[4,8,4,16,128]{4,3,2,1,0:T(8,128)(2,1)S(1)}, bf16[4,8,4,16,128]{4,3,2,1,0:T(8,128)(2,1)}, u32[]{:S(2)}, u32[]{:S(2)}) collective-permute-start(bf16[4,8,4,16,128]{4,3,2,1,0:T(8,128)(2,1)S(1)} %collective-permute-done.19.rest_2_), channel_id=1, source_target_pairs={{0,7},{1,0},{2,1},{3,2},{4,3},{5,4},{6,5},{7,6},{8,15},{9,8},{10,9... | collective-permute-start | bytes 1572872 | tf_op jit(solution)/shard_map/ppermute | solution.py:284
  137.7 16.0 %collective-permute-start.11 = (bf16[2,8,4,16,128]{4,3,2,1,0:T(8,128)(2,1)S(1)}, bf16[2,8,4,16,128]{4,3,2,1,0:T(8,128)(2,1)S(1)}, u32[]{:S(2)}, u32[]{:S(2)}) collective-permute-start(bf16[2,8,4,16,128]{4,3,2,1,0:T(8,128)(2,1)S(1)} %slice.58), channel_id=1, source_target_pairs={{0,1},{1,2},{2,3},{3,4},{4,5},{5,6},{6,7},{7,0},{8,9},{9,10},{10,1... | collective-permute-start | bytes 786440 | tf_op jit(solution)/shard_map/ppermute | solution.py:293
  138.6 15.5 %collective-permute-start.15 = (bf16[2,8,4,16,128]{4,3,2,1,0:T(8,128)(2,1)S(1)}, bf16[2,8,4,16,128]{4,3,2,1,0:T(8,128)(2,1)S(1)}, u32[]{:S(2)}, u32[]{:S(2)}) collective-permute-start(bf16[2,8,4,16,128]{4,3,2,1,0:T(8,128)(2,1)S(1)} %slice.59), channel_id=1, source_target_pairs={{0,7},{1,0},{2,1},{3,2},{4,3},{5,4},{6,5},{7,6},{8,15},{9,8},{10,9... | collective-permute-start | bytes 786440 | tf_op jit(solution)/shard_map/ppermute | solution.py:294
  148.3 26.1 %collective-permute-start.18 = (bf16[4,8,4,16,128]{4,3,2,1,0:T(8,128)(2,1)}, bf16[4,8,4,16,128]{4,3,2,1,0:T(8,128)(2,1)}, u32[]{:S(2)}, u32[]{:S(2)}) collective-permute-start(bf16[4,8,4,16,128]{4,3,2,1,0:T(8,128)(2,1)} %collective-permute-done.17.rest_3_), channel_id=1, source_target_pairs={{0,1},{1,2},{2,3},{3,4},{4,5},{5,6},{6,7},{7,0},{8,9},{9,10},{10,1... | collective-permute-start | bytes 1572872 | tf_op jit(solution)/shard_map/ppermute | solution.py:283
  148.5 27.1 %collective-permute-start.21 = (bf16[4,8,4,16,128]{4,3,2,1,0:T(8,128)(2,1)}, bf16[4,8,4,16,128]{4,3,2,1,0:T(8,128)(2,1)}, u32[]{:S(2)}, u32[]{:S(2)}) collective-permute-start(bf16[4,8,4,16,128]{4,3,2,1,0:T(8,128)(2,1)} %collective-permute-done.20.rest_4_), channel_id=1, source_target_pairs={{0,7},{1,0},{2,1},{3,2},{4,3},{5,4},{6,5},{7,6},{8,15},{9,8},{10,9... | collective-permute-start | bytes 1572872 | tf_op jit(solution)/shard_map/ppermute | solution.py:284
  154.8 67.9 %all-to-all-start.2 = ((bf16[32,16,16,128]{3,2,1,0:T(8,128)(2,1)}), bf16[32,16,16,128]{3,2,1,0:T(8,128)(2,1)S(1)}, u32[]{:S(2)}, u32[]{:S(2)}) async-start(bf16[32,16,16,128]{3,2,1,0:T(8,128)(2,1)} %copy-done.2), calls=%async_computation.2 | async-start | bytes 4194304 | tf_op jit(solution)/shard_map/all_to_all | solution.py:457
  175.3 10.6 %collective-permute-start.22 = (bf16[2,8,4,16,128]{4,3,2,1,0:T(8,128)(2,1)S(1)}, bf16[2,8,4,16,128]{4,3,2,1,0:T(8,128)(2,1)S(1)}, u32[]{:S(2)}, u32[]{:S(2)}) collective-permute-start(bf16[2,8,4,16,128]{4,3,2,1,0:T(8,128)(2,1)S(1)} %slice.61), channel_id=1, source_target_pairs={{0,1},{1,2},{2,3},{3,4},{4,5},{5,6},{6,7},{7,0},{8,9},{9,10},{10,1... | collective-permute-start | bytes 786440 | tf_op jit(solution)/shard_map/ppermute | solution.py:293
  (45 other events, 323.6 us)

commit v9 on v8

--- a/solution.py
+++ b/solution.py
@@ -270,7 +270,7 @@
     ]
 
 
-def ring_project(streams, where, weights, n_ten):
+def ring_project(streams, where, weights, n_ten, beside):
     right, left = ring_ways(n_ten)
     half = streams[0].shape[0] // 2
     last = n_ten // 2
@@ -278,25 +278,25 @@
     blocks = [[x] for x in streams]
     places = [[(0, 0)] for _ in streams]
     states = [()] * len(streams)
-    for step in range(1, last):
+    for step in range(1, last + 1):
         for s in range(len(streams)):
-            go_right[s] = lax.ppermute(go_right[s], "tensor", right)
-            go_left[s] = lax.ppermute(go_left[s], "tensor", left)
+            from_left, from_right = go_right[s], go_left[s]
+            if step == last:
+                held = lax.optimization_barrier((from_left, from_right, beside))
+                from_left, from_right, beside = held
+                from_left, from_right = from_left[:half], from_right[half:]
+            if (step, s) in ((last - 1, 1), (last, 0)):
+                other = states[1 - s]
+                held = lax.optimization_barrier((from_left, from_right, other))
+                from_left, from_right, states[1 - s] = held
+            go_right[s] = lax.ppermute(from_left, "tensor", right)
+            go_left[s] = lax.ppermute(from_right, "tensor", left)
             blocks[s] += [go_right[s], go_left[s]]
-            places[s] += [(n_ten - step, 0), (step, 0)]
-            if step == last - 2:
-                states[s] = gather_step(blocks[s], places[s], where, weights, (), False)
-                blocks[s], places[s] = [], []
-    arrivals = None
-    for s in range(len(streams)):
-        blocks[s] += [
-            lax.ppermute(go_right[s][:half], "tensor", right),
-            lax.ppermute(go_left[s][half:], "tensor", left),
-        ]
-        places[s] += [(last, 0), (last, half)]
-        arrivals = blocks[s][-2:] if arrivals is None else arrivals
-        states[s] = gather_step(blocks[s], places[s], where, weights, states[s], True)
-    return states, arrivals
+            places[s] += [(n_ten - step, 0), (step, half if step == last else 0)]
+            if step in (last - 2, last):
+                state = gather_step(blocks[s], places[s], where, weights, states[s], step == last)
+                blocks[s], places[s], states[s] = [], [], state
+    return states, beside
 
 
 def weigh(scores, count, keys_axis_owner):
@@ -427,11 +427,6 @@
 
     pieces = cut(nbr_shard, nbr_row, nbr_count, database)
     spread = lax.all_to_all(pieces, "seq", split_axis=0, concat_axis=0, tiled=True)
-    n_notes = 2 * items + span_dev
-    notes = spread[:, per_shard, 0, :n_notes].astype(jnp.int32)
-    index = notes[:, :items] * (per_shard + 1) + notes[:, items : 2 * items]
-    prev_count = jnp.where(seq_at > 0, notes[jnp.maximum(seq_at - 1, 0), n_notes - 1], 0)
-    counts = jnp.concatenate([nbr_count, prev_count[None]])
 
     halves = d_part // (PIECES_WO * PIECE_F)
     strips = n_seq // halves
@@ -443,19 +438,23 @@
     both = jnp.concatenate([wk, wv], axis=1).astype(jnp.float32)
     both = (both * nbr_gain.astype(jnp.float32)[:, None]).astype(jnp.bfloat16)
     both = both.reshape(n_ten, d_part, both.shape[1])
-    spread, index, both, _ = lax.optimization_barrier((spread, index, both, letters[3:5]))
+    spread, both, _ = lax.optimization_barrier((spread, both, letters[3:5]))
+    n_notes = 2 * items + span_dev
     spread = spread.reshape(n_seq * (per_shard + 1), PIECE_T, PIECE_F)
+    notes = spread[per_shard :: per_shard + 1, 0, :n_notes].astype(jnp.int32)
+    index = notes[:, :items] * (per_shard + 1) + notes[:, items : 2 * items]
+    prev_count = jnp.where(seq_at > 0, notes[jnp.maximum(seq_at - 1, 0), n_notes - 1], 0)
+    counts = jnp.concatenate([nbr_count, prev_count[None]])
     (picked,) = pick(index, spread, 1)
     rows = lax.all_to_all(picked, "seq", split_axis=0, concat_axis=0, tiled=True)
     queries, strip = query(where, letters, x_gain, wq, tok_dev, shift, n_seq)
-    rows, queries, counts = lax.optimization_barrier((rows, queries, counts))
+    rows, queries, strip, counts = lax.optimization_barrier((rows, queries, strip, counts))
+    mail = lax.all_to_all(strip, "seq", split_axis=0, concat_axis=0, tiled=True)
+    mail = mail.reshape(strips, halves, *strip.shape[1:])
 
     rows = rows.reshape(pieces_f, pieces_t, items, PIECE_T, PIECE_F)
     streams = [rows[:, :, items // 2 :], rows[:, :, : items // 2]]
-    (late, early), arrivals = ring_project(streams, where, both, n_ten)
-    strip, _ = lax.optimization_barrier((strip, arrivals))
-    mail = lax.all_to_all(strip, "seq", split_axis=0, concat_axis=0, tiled=True)
-    mail = mail.reshape(strips, halves, *strip.shape[1:])
+    (late, early), mail = ring_project(streams, where, both, n_ten, mail)
     prev = lax.ppermute(late[-1], "seq", [(i, i + 1) for i in range(n_seq - 1)])
     attended = attend(counts, queries, late, span_dev // 2, span_len, prev=prev)
     attended = attend(counts, queries, early, 0, span_len, after=attended)

time: 226 us -> 212 us (0.938)
  starting transfers between devices: 84.9 us -> 72.5 us
    ppermute x6, waiting for transfers between devices: 7.61 us -> 27.9 us  [ring_gather(): go_left = lax.ppermute(go_left, 'tensor', left)]
    ppermute x6, waiting for transfers between devices: 13.6 us -> 4.36 us  [ring_gather(): go_right = lax.ppermute(go_right, 'tensor', right)]
    ppermute x6, starting transfers between devices: 23.5 us -> 15.3 us  [ring_gather(): go_left = lax.ppermute(go_left, 'tensor', left)]
    all_to_all x1, waiting for transfers between devices: 7.82 us -> 0.01 us  [body(): lax.all_to_all(pieces, 'seq', split_axis=0, concat_axis=0, tiled=True)]
    ppermute x16, waiting for transfers between devices: 40.6 us -> 34.1 us  [the longest x8 20.8 us: ring_project(): go_left[s] = lax.ppermute(from_right, 'tensor', left)]
    ppermute x16, starting transfers between devices: 27.4 us -> 22 us  [the longest x8 18 us: ring_project(): go_left[s] = lax.ppermute(from_right, 'tensor', left)]
    unnamed x66 -> x48, local copies, waits for them, and re-layouts: 18.6 us -> 14.8 us
    ppermute x2, waiting for transfers between devices: 7.98 us -> 10.3 us  [ring_gather(): lax.ppermute(go_right[:cut_at], 'tensor', right)]
  transfers between devices with their start and end apart: 36 -> 36, of which waited for: 19 -> 22; matrix products, arithmetic and copies ran while one was open for 4% -> 5% of each run, Pallas kernels for 11% -> 10%
where the time goes in v9:
time: 212 us; the launch traced here: 211 us
  waiting for transfers between devices  82.7 us (39%)
  starting transfers between devices  72.5 us (34%)
  Pallas kernels  28.8 us (14%)
  local copies, waits for them, and re-layouts  21.2 us (10%)
  other arithmetic  4.87 us (2%)
    ppermute x6, waiting for transfers between devices, ring_gather(): go_left = lax.ppermute(go_left, 'tensor', left)  27.9 us
    ppermute x8, waiting for transfers between devices, ring_project(): go_left[s] = lax.ppermute(from_right, 'tensor', left)  20.8 us
    ppermute x8, starting transfers between devices, ring_project(): go_left[s] = lax.ppermute(from_right, 'tensor', left)  18 us
    ppermute x6, starting transfers between devices, ring_gather(): go_left = lax.ppermute(go_left, 'tensor', left)  15.3 us
    unnamed x48, local copies, waits for them, and re-layouts  14.8 us
    pallas_call x4, Pallas kernels, gather_step(): pl.pallas_call(functools.partial(gather_kernel, tuple(places), not state,...  14.7 us
    ppermute x8, waiting for transfers between devices, ring_project(): go_right[s] = lax.ppermute(from_left, 'tensor', right)  13.3 us
    ppermute x2, waiting for transfers between devices, ring_gather(): lax.ppermute(go_right[:cut_at], 'tensor', right)  10.3 us
  transfers between devices with their start and end apart: 36, of which 22 were waited for; matrix products, arithmetic and copies ran while one was open for 5% of the time, Pallas kernels for 10%

profile of v9, /device:TPU:8, one launch (start us, length us, event | category | flops | bytes accessed | tf_op | source)
XLA Modules:
  0.0 211.0 jit_solution(6484048656888405926)
XLA Ops:
  5.4 7.5 %all-to-all-start = ((bf16[32,17,16,128]{3,2,1,0:T(8,128)(2,1)}), bf16[32,17,16,128]{3,2,1,0:T(8,128)(2,1)S(1)}, u32[]{:S(2)}, u32[]{:S(2)}) async-start(bf16[32,17,16,128]{3,2,1,0:T(8,128)(2,1)} %copy-done), calls=%async_computation | async-start | bytes 4456448 | tf_op jit(solution)/shard_map/all_to_all | solution.py:429
  16.1 5.9 %collective-permute-start.2 = (bf16[80,16,128]{2,1,0:T(8,128)(2,1)}, bf16[80,16,128]{2,1,0:T(8,128)(2,1)S(1)}, u32[]{:S(2)}, u32[]{:S(2)}) collective-permute-start(bf16[80,16,128]{2,1,0:T(8,128)(2,1)} %letter.1.rest_0_), channel_id=1, source_target_pairs={{0,7},{1,0},{2,1},{3,2},{4,3},{5,4},{6,5},{7,6},{8,15},{9,8},{10,9... | collective-permute-start | bytes 983048 | tf_op jit(solution)/shard_map/ppermute | solution.py:265
  22.0 7.6 %collective-permute-done.2.rest_2_ = bf16[80,16,128]{2,1,0:T(8,128)(2,1)S(1)} collective-permute-done((bf16[80,16,128]{2,1,0:T(8,128)(2,1)}, bf16[80,16,128]{2,1,0:T(8,128)(2,1)S(1)}, u32[]{:S(2)}, u32[]{:S(2)}) %collective-permute-start.2) | collective-permute-done | bytes 327712 | tf_op jit(solution)/shard_map/ppermute | solution.py:265
  29.6 3.6 %collective-permute-start.3 = (bf16[80,16,128]{2,1,0:T(8,128)(2,1)S(1)}, bf16[80,16,128]{2,1,0:T(8,128)(2,1)S(1)}, u32[]{:S(2)}, u32[]{:S(2)}) collective-permute-start(bf16[80,16,128]{2,1,0:T(8,128)(2,1)S(1)} %collective-permute-done.2.rest_2_), channel_id=1, source_target_pairs={{0,7},{1,0},{2,1},{3,2},{4,3},{5,4},{6,5},{7,6},{8,15},{9,8},{10,9... | collective-permute-start | bytes 983048 | tf_op jit(solution)/shard_map/ppermute | solution.py:265
  33.1 4.0 %multiply_convert_fusion.w_ref = bf16[8,512,512]{2,1,0:T(8,128)(2,1)} fusion(bf16[8,512,256]{2,1,0:T(8,128)(2,1)} %bitcast.21, bf16[8,512,256]{2,1,0:T(8,128)(2,1)} %bitcast.22, f32[8,512]{1,0:T(8,128)S(1)} %reshape.37), kind=kLoop, calls=%fused_computation | loop fusion | flops 12582912 | bytes 8404992 | tf_op jit(solution)/shard_map/convert_element_type | solution.py:439
  39.6 3.5 %collective-permute-done.1.rest_3_ = bf16[80,16,128]{2,1,0:T(8,128)(2,1)} collective-permute-done((bf16[80,16,128]{2,1,0:T(8,128)(2,1)S(1)}, bf16[80,16,128]{2,1,0:T(8,128)(2,1)}, u32[]{:S(2)}, u32[]{:S(2)}) %collective-permute-start.1) | collective-permute-done | bytes 327712 | tf_op jit(solution)/shard_map/ppermute | solution.py:264
  45.4 7.5 %all-to-all-start.1 = ((bf16[32,8,16,128]{3,2,1,0:T(8,128)(2,1)}), bf16[32,8,16,128]{3,2,1,0:T(8,128)(2,1)S(1)}, u32[]{:S(2)}, u32[]{:S(2)}) async-start(bf16[32,8,16,128]{3,2,1,0:T(8,128)(2,1)} %pick.1), calls=%async_computation.1 | async-start | bytes 2097152 | tf_op jit(solution)/shard_map/all_to_all | solution.py:449
  52.9 3.8 %collective-permute-start.5 = (bf16[80,16,128]{2,1,0:T(8,128)(2,1)}, bf16[80,16,128]{2,1,0:T(8,128)(2,1)S(1)}, u32[]{:S(2)}, u32[]{:S(2)}) collective-permute-start(bf16[80,16,128]{2,1,0:T(8,128)(2,1)} %copy-done.11), channel_id=1, source_target_pairs={{0,7},{1,0},{2,1},{3,2},{4,3},{5,4},{6,5},{7,6},{8,15},{9,8},{10,9... | collective-permute-start | bytes 983048 | tf_op jit(solution)/shard_map/ppermute | solution.py:265
  56.7 7.6 %collective-permute-done.5.rest_6_ = bf16[80,16,128]{2,1,0:T(8,128)(2,1)S(1)} collective-permute-done((bf16[80,16,128]{2,1,0:T(8,128)(2,1)}, bf16[80,16,128]{2,1,0:T(8,128)(2,1)S(1)}, u32[]{:S(2)}, u32[]{:S(2)}) %collective-permute-start.5) | collective-permute-done | bytes 327712 | tf_op jit(solution)/shard_map/ppermute | solution.py:265
  65.0 3.6 %collective-permute-start.7 = (bf16[48,16,128]{2,1,0:T(8,128)(2,1)}, bf16[48,16,128]{2,1,0:T(8,128)(2,1)S(1)}, u32[]{:S(2)}, u32[]{:S(2)}) collective-permute-start(bf16[48,16,128]{2,1,0:T(8,128)(2,1)} %slice.55), channel_id=1, source_target_pairs={{0,7},{1,0},{2,1},{3,2},{4,3},{5,4},{6,5},{7,6},{8,15},{9,8},{10,9... | collective-permute-start | bytes 589832 | tf_op jit(solution)/shard_map/ppermute | solution.py:269
  69.3 6.4 %collective-permute-done.6.rest_7_ = bf16[32,16,128]{2,1,0:T(8,128)(2,1)S(1)} collective-permute-done((bf16[32,16,128]{2,1,0:T(8,128)(2,1)}, bf16[32,16,128]{2,1,0:T(8,128)(2,1)S(1)}, u32[]{:S(2)}, u32[]{:S(2)}) %collective-permute-start.6) | collective-permute-done | bytes 131104 | tf_op jit(solution)/shard_map/ppermute | solution.py:268
  86.7 7.4 %all-to-all-start.2 = ((bf16[32,16,16,128]{3,2,1,0:T(8,128)(2,1)}), bf16[32,16,16,128]{3,2,1,0:T(8,128)(2,1)S(1)}, u32[]{:S(2)}, u32[]{:S(2)}) async-start(bf16[32,16,16,128]{3,2,1,0:T(8,128)(2,1)} %copy-done.2), calls=%async_computation.2 | async-start | bytes 4194304 | tf_op jit(solution)/shard_map/all_to_all | solution.py:452
  99.4 9.8 %collective-permute-done.10.rest_2_ = bf16[4,8,4,16,128]{4,3,2,1,0:T(8,128)(2,1)S(1)} collective-permute-done((bf16[4,8,4,16,128]{4,3,2,1,0:T(8,128)(2,1)S(1)}, bf16[4,8,4,16,128]{4,3,2,1,0:T(8,128)(2,1)S(1)}, u32[]{:S(2)}, u32[]{:S(2)}) %collective-permute-start.10) | collective-permute-done | bytes 524320 | tf_op jit(solution)/shard_map/ppermute | solution.py:293
  112.1 8.3 %collective-permute-done.15.rest_4_ = bf16[4,8,4,16,128]{4,3,2,1,0:T(8,128)(2,1)S(1)} collective-permute-done((bf16[4,8,4,16,128]{4,3,2,1,0:T(8,128)(2,1)}, bf16[4,8,4,16,128]{4,3,2,1,0:T(8,128)(2,1)S(1)}, u32[]{:S(2)}, u32[]{:S(2)}) %collective-permute-start.15) | collective-permute-done | bytes 524320 | tf_op jit(solution)/shard_map/ppermute | solution.py:293
  123.4 4.0 %gather_step.2 = (f32[512,512]{1,0:T(8,128)S(1)}, f32[512,128]{1,0:T(8,128)S(1)}) custom-call(s32[8]{0:T(128)S(1)} %and_select_fusion.where_ref, bf16[8,512,512]{2,1,0:T(8,128)(2,1)} %multiply_convert_fusion.w_ref, bf16[4,8,4,16,128]{4,3,2,1,0:T(8,128)(2,1)S(1)} %get-tuple-element.67.rest_0_, bf16[4,8,4,16,128]{4,3,2,1,0:T(8,128)(2,1)} %collective-permute-done.12.rest_1_, ...), custom_call_target="tpu_custom_call" | custom-call | flops 5368709120 | bytes 4718592 | tf_op jit(solution)/shard_map/gather_step/pallas_call | solution.py:237
  134.7 3.2 %collective-permute-start.17 = (bf16[4,8,4,16,128]{4,3,2,1,0:T(8,128)(2,1)}, bf16[4,8,4,16,128]{4,3,2,1,0:T(8,128)(2,1)}, u32[]{:S(2)}, u32[]{:S(2)}) collective-permute-start(bf16[4,8,4,16,128]{4,3,2,1,0:T(8,128)(2,1)} %collective-permute-done.11.rest_4_), channel_id=1, source_target_pairs={{0,7},{1,0},{2,1},{3,2},{4,3},{5,4},{6,5},{7,6},{8,15},{9,8},{10,9... | collective-permute-start | bytes 1572872 | tf_op jit(solution)/shard_map/ppermute | solution.py:293
  138.0 4.0 %gather_step.3 = (f32[512,512]{1,0:T(8,128)S(1)}, f32[512,128]{1,0:T(8,128)S(1)}) custom-call(s32[8]{0:T(128)S(1)} %and_select_fusion.where_ref, bf16[8,512,512]{2,1,0:T(8,128)(2,1)} %multiply_convert_fusion.w_ref, bf16[4,8,4,16,128]{4,3,2,1,0:T(8,128)(2,1)S(1)} %get-tuple-element.68.rest_0_, bf16[4,8,4,16,128]{4,3,2,1,0:T(8,128)(2,1)S(1)} %collective-permute-done.8.rest_1_, ...), custom_call_target="tpu_custom_call" | custom-call | flops 5368709120 | bytes 4718592 | tf_op jit(solution)/shard_map/gather_step/pallas_call | solution.py:237
  151.2 5.9 %collective-permute-done.16.rest_0_ = bf16[4,8,4,16,128]{4,3,2,1,0:T(8,128)(2,1)S(1)} collective-permute-done((bf16[4,8,4,16,128]{4,3,2,1,0:T(8,128)(2,1)}, bf16[4,8,4,16,128]{4,3,2,1,0:T(8,128)(2,1)S(1)}, u32[]{:S(2)}, u32[]{:S(2)}) %collective-permute-start.16) | collective-permute-done | bytes 524320 | tf_op jit(solution)/shard_map/ppermute | solution.py:292
  165.8 3.4 %gather_last.3 = (bf16[8,2,16,512]{3,2,1,0:T(8,128)(2,1)S(1)}, bf16[8,2,16,512]{3,2,1,0:T(8,128)(2,1)S(1)}) custom-call(s32[8]{0:T(128)S(1)} %and_select_fusion.where_ref, bf16[8,512,512]{2,1,0:T(8,128)(2,1)} %multiply_convert_fusion.w_ref, bf16[4,8,4,16,128]{4,3,2,1,0:T(8,128)(2,1)} %collective-permute-done.18.rest_0_, ...), custom_call_target="tpu_custom_call" | custom-call | flops 3221225472 | bytes 3670016 | tf_op jit(solution)/shard_map/gather_last/pallas_call | solution.py:237
  171.3 3.3 %gather_last.2 = (bf16[8,2,16,512]{3,2,1,0:T(8,128)(2,1)S(1)}, bf16[8,2,16,512]{3,2,1,0:T(8,128)(2,1)S(1)}) custom-call(s32[8]{0:T(128)S(1)} %and_select_fusion.where_ref, bf16[8,512,512]{2,1,0:T(8,128)(2,1)} %multiply_convert_fusion.w_ref, bf16[4,8,4,16,128]{4,3,2,1,0:T(8,128)(2,1)S(1)} %collective-permute-done.16.rest_0_, ...), custom_call_target="tpu_custom_call" | custom-call | flops 3221225472 | bytes 3670016 | tf_op jit(solution)/shard_map/gather_last/pallas_call | solution.py:237
  174.7 4.5 %collective-permute-done.24.rest_2_ = bf16[8,2,16,512]{3,2,1,0:T(8,128)(2,1)S(1)} collective-permute-done((bf16[8,2,16,512]{3,2,1,0:T(8,128)(2,1)S(1)}, bf16[8,2,16,512]{3,2,1,0:T(8,128)(2,1)S(1)}, u32[]{:S(2)}, u32[]{:S(2)}) %collective-permute-start.24) | collective-permute-done | bytes 262176 | tf_op jit(solution)/shard_map/ppermute | solution.py:458
  185.2 4.3 %collective-permute-done.26.rest_2_ = bf16[256,256]{1,0:T(8,128)(2,1)S(1)} collective-permute-done((bf16[256,256]{1,0:T(8,128)(2,1)S(1)}, bf16[256,256]{1,0:T(8,128)(2,1)S(1)}, u32[]{:S(2)}, u32[]{:S(2)}) %collective-permute-start.26) | collective-permute-done | bytes 131104 | tf_op jit(solution)/shard_map/ppermute | solution.py:265
  191.5 3.4 %collective-permute-done.28.rest_4_ = bf16[256,256]{1,0:T(8,128)(2,1)S(1)} collective-permute-done((bf16[256,256]{1,0:T(8,128)(2,1)S(1)}, bf16[256,256]{1,0:T(8,128)(2,1)S(1)}, u32[]{:S(2)}, u32[]{:S(2)}) %collective-permute-start.28) | collective-permute-done | bytes 131104 | tf_op jit(solution)/shard_map/ppermute | solution.py:265
  205.0 3.9 %collective-permute-done.31.rest_7_ = bf16[128,256]{1,0:T(8,128)(2,1)S(1)} collective-permute-done((bf16[128,256]{1,0:T(8,128)(2,1)S(1)}, bf16[128,256]{1,0:T(8,128)(2,1)S(1)}, u32[]{:S(2)}, u32[]{:S(2)}) %collective-permute-start.31) | collective-permute-done | bytes 65568 | tf_op jit(solution)/shard_map/ppermute | solution.py:268
  (125 shorter events, 83.6 us)
Async XLA Ops:
  5.4 37.7 %all-to-all-start = ((bf16[32,17,16,128]{3,2,1,0:T(8,128)(2,1)}), bf16[32,17,16,128]{3,2,1,0:T(8,128)(2,1)S(1)}, u32[]{:S(2)}, u32[]{:S(2)}) async-start(bf16[32,17,16,128]{3,2,1,0:T(8,128)(2,1)} %copy-done), calls=%async_computation | async-start | bytes 4456448 | tf_op jit(solution)/shard_map/all_to_all | solution.py:429
  16.1 13.5 %collective-permute-start.2 = (bf16[80,16,128]{2,1,0:T(8,128)(2,1)}, bf16[80,16,128]{2,1,0:T(8,128)(2,1)S(1)}, u32[]{:S(2)}, u32[]{:S(2)}) collective-permute-start(bf16[80,16,128]{2,1,0:T(8,128)(2,1)} %letter.1.rest_0_), channel_id=1, source_target_pairs={{0,7},{1,0},{2,1},{3,2},{4,3},{5,4},{6,5},{7,6},{8,15},{9,8},{10,9... | collective-permute-start | bytes 983048 | tf_op jit(solution)/shard_map/ppermute | solution.py:265
  22.0 11.2 %collective-permute-start = (bf16[80,16,128]{2,1,0:T(8,128)(2,1)}, bf16[80,16,128]{2,1,0:T(8,128)(2,1)S(1)}, u32[]{:S(2)}, u32[]{:S(2)}) collective-permute-start(bf16[80,16,128]{2,1,0:T(8,128)(2,1)} %letter.1.rest_0_), channel_id=1, source_target_pairs={{0,1},{1,2},{2,3},{3,4},{4,5},{5,6},{6,7},{7,0},{8,9},{9,10},{10,1... | collective-permute-start | bytes 983048 | tf_op jit(solution)/shard_map/ppermute | solution.py:264
  45.4 36.7 %all-to-all-start.1 = ((bf16[32,8,16,128]{3,2,1,0:T(8,128)(2,1)}), bf16[32,8,16,128]{3,2,1,0:T(8,128)(2,1)S(1)}, u32[]{:S(2)}, u32[]{:S(2)}) async-start(bf16[32,8,16,128]{3,2,1,0:T(8,128)(2,1)} %pick.1), calls=%async_computation.1 | async-start | bytes 2097152 | tf_op jit(solution)/shard_map/all_to_all | solution.py:449
  52.9 11.4 %collective-permute-start.5 = (bf16[80,16,128]{2,1,0:T(8,128)(2,1)}, bf16[80,16,128]{2,1,0:T(8,128)(2,1)S(1)}, u32[]{:S(2)}, u32[]{:S(2)}) collective-permute-start(bf16[80,16,128]{2,1,0:T(8,128)(2,1)} %copy-done.11), channel_id=1, source_target_pairs={{0,7},{1,0},{2,1},{3,2},{4,3},{5,4},{6,5},{7,6},{8,15},{9,8},{10,9... | collective-permute-start | bytes 983048 | tf_op jit(solution)/shard_map/ppermute | solution.py:265
  56.7 11.9 %collective-permute-start.4 = (bf16[80,16,128]{2,1,0:T(8,128)(2,1)}, bf16[80,16,128]{2,1,0:T(8,128)(2,1)S(1)}, u32[]{:S(2)}, u32[]{:S(2)}) collective-permute-start(bf16[80,16,128]{2,1,0:T(8,128)(2,1)} %collective-permute-done.1.rest_3_), channel_id=1, source_target_pairs={{0,1},{1,2},{2,3},{3,4},{4,5},{5,6},{6,7},{7,0},{8,9},{9,10},{10,1... | collective-permute-start | bytes 983048 | tf_op jit(solution)/shard_map/ppermute | solution.py:264
  65.0 10.6 %collective-permute-start.7 = (bf16[48,16,128]{2,1,0:T(8,128)(2,1)}, bf16[48,16,128]{2,1,0:T(8,128)(2,1)S(1)}, u32[]{:S(2)}, u32[]{:S(2)}) collective-permute-start(bf16[48,16,128]{2,1,0:T(8,128)(2,1)} %slice.55), channel_id=1, source_target_pairs={{0,7},{1,0},{2,1},{3,2},{4,3},{5,4},{6,5},{7,6},{8,15},{9,8},{10,9... | collective-permute-start | bytes 589832 | tf_op jit(solution)/shard_map/ppermute | solution.py:269
  84.6 11.9 %collective-permute-start.13 = (bf16[4,8,4,16,128]{4,3,2,1,0:T(8,128)(2,1)S(1)}, bf16[4,8,4,16,128]{4,3,2,1,0:T(8,128)(2,1)}, u32[]{:S(2)}, u32[]{:S(2)}) collective-permute-start(bf16[4,8,4,16,128]{4,3,2,1,0:T(8,128)(2,1)S(1)} %get-tuple-element.67.rest_0_), channel_id=1, source_target_pairs={{0,7},{1,0},{2,1},{3,2},{4,3},{5,4},{6,5},{7,6},{8,15},{9,8},{10,9... | collective-permute-start | bytes 1572872 | tf_op jit(solution)/shard_map/ppermute | solution.py:293
  85.2 14.2 %collective-permute-start.12 = (bf16[4,8,4,16,128]{4,3,2,1,0:T(8,128)(2,1)S(1)}, bf16[4,8,4,16,128]{4,3,2,1,0:T(8,128)(2,1)}, u32[]{:S(2)}, u32[]{:S(2)}) collective-permute-start(bf16[4,8,4,16,128]{4,3,2,1,0:T(8,128)(2,1)S(1)} %get-tuple-element.67.rest_0_), channel_id=1, source_target_pairs={{0,1},{1,2},{2,3},{3,4},{4,5},{5,6},{6,7},{7,0},{8,9},{9,10},{10,1... | collective-permute-start | bytes 1572872 | tf_op jit(solution)/shard_map/ppermute | solution.py:292
  86.7 59.2 %all-to-all-start.2 = ((bf16[32,16,16,128]{3,2,1,0:T(8,128)(2,1)}), bf16[32,16,16,128]{3,2,1,0:T(8,128)(2,1)S(1)}, u32[]{:S(2)}, u32[]{:S(2)}) async-start(bf16[32,16,16,128]{3,2,1,0:T(8,128)(2,1)} %copy-done.2), calls=%async_computation.2 | async-start | bytes 4194304 | tf_op jit(solution)/shard_map/all_to_all | solution.py:452
  94.2 15.0 %collective-permute-start.10 = (bf16[4,8,4,16,128]{4,3,2,1,0:T(8,128)(2,1)S(1)}, bf16[4,8,4,16,128]{4,3,2,1,0:T(8,128)(2,1)S(1)}, u32[]{:S(2)}, u32[]{:S(2)}) collective-permute-start(bf16[4,8,4,16,128]{4,3,2,1,0:T(8,128)(2,1)S(1)} %get-tuple-element.68.rest_0_), channel_id=1, source_target_pairs={{0,7},{1,0},{2,1},{3,2},{4,3},{5,4},{6,5},{7,6},{8,15},{9,8},{10,9... | collective-permute-start | bytes 1572872 | tf_op jit(solution)/shard_map/ppermute | solution.py:293
  96.1 16.0 %collective-permute-start.8 = (bf16[4,8,4,16,128]{4,3,2,1,0:T(8,128)(2,1)S(1)}, bf16[4,8,4,16,128]{4,3,2,1,0:T(8,128)(2,1)S(1)}, u32[]{:S(2)}, u32[]{:S(2)}) collective-permute-start(bf16[4,8,4,16,128]{4,3,2,1,0:T(8,128)(2,1)S(1)} %get-tuple-element.68.rest_0_), channel_id=1, source_target_pairs={{0,1},{1,2},{2,3},{3,4},{4,5},{5,6},{6,7},{7,0},{8,9},{9,10},{10,1... | collective-permute-start | bytes 1572872 | tf_op jit(solution)/shard_map/ppermute | solution.py:292
  96.5 23.9 %collective-permute-start.15 = (bf16[4,8,4,16,128]{4,3,2,1,0:T(8,128)(2,1)}, bf16[4,8,4,16,128]{4,3,2,1,0:T(8,128)(2,1)S(1)}, u32[]{:S(2)}, u32[]{:S(2)}) collective-permute-start(bf16[4,8,4,16,128]{4,3,2,1,0:T(8,128)(2,1)} %collective-permute-done.13.rest_2_), channel_id=1, source_target_pairs={{0,7},{1,0},{2,1},{3,2},{4,3},{5,4},{6,5},{7,6},{8,15},{9,8},{10,9... | collective-permute-start | bytes 1572872 | tf_op jit(solution)/shard_map/ppermute | solution.py:293
  99.4 24.0 %collective-permute-start.14 = (bf16[4,8,4,16,128]{4,3,2,1,0:T(8,128)(2,1)}, bf16[4,8,4,16,128]{4,3,2,1,0:T(8,128)(2,1)S(1)}, u32[]{:S(2)}, u32[]{:S(2)}) collective-permute-start(bf16[4,8,4,16,128]{4,3,2,1,0:T(8,128)(2,1)} %collective-permute-done.12.rest_1_), channel_id=1, source_target_pairs={{0,1},{1,2},{2,3},{3,4},{4,5},{5,6},{6,7},{7,0},{8,9},{9,10},{10,1... | collective-permute-start | bytes 1572872 | tf_op jit(solution)/shard_map/ppermute | solution.py:292
  109.2 22.6 %collective-permute-start.11 = (bf16[4,8,4,16,128]{4,3,2,1,0:T(8,128)(2,1)S(1)}, bf16[4,8,4,16,128]{4,3,2,1,0:T(8,128)(2,1)}, u32[]{:S(2)}, u32[]{:S(2)}) collective-permute-start(bf16[4,8,4,16,128]{4,3,2,1,0:T(8,128)(2,1)S(1)} %collective-permute-done.10.rest_2_), channel_id=1, source_target_pairs={{0,7},{1,0},{2,1},{3,2},{4,3},{5,4},{6,5},{7,6},{8,15},{9,8},{10,9... | collective-permute-start | bytes 1572872 | tf_op jit(solution)/shard_map/ppermute | solution.py:293
  112.1 22.6 %collective-permute-start.9 = (bf16[4,8,4,16,128]{4,3,2,1,0:T(8,128)(2,1)S(1)}, bf16[4,8,4,16,128]{4,3,2,1,0:T(8,128)(2,1)}, u32[]{:S(2)}, u32[]{:S(2)}) collective-permute-start(bf16[4,8,4,16,128]{4,3,2,1,0:T(8,128)(2,1)S(1)} %collective-permute-done.8.rest_1_), channel_id=1, source_target_pairs={{0,1},{1,2},{2,3},{3,4},{4,5},{5,6},{6,7},{7,0},{8,9},{9,10},{10,1... | collective-permute-start | bytes 1572872 | tf_op jit(solution)/shard_map/ppermute | solution.py:292
  120.4 22.6 %collective-permute-start.19 = (bf16[4,8,4,16,128]{4,3,2,1,0:T(8,128)(2,1)S(1)}, bf16[4,8,4,16,128]{4,3,2,1,0:T(8,128)(2,1)S(1)}, u32[]{:S(2)}, u32[]{:S(2)}) collective-permute-start(bf16[4,8,4,16,128]{4,3,2,1,0:T(8,128)(2,1)S(1)} %collective-permute-done.15.rest_4_), channel_id=1, source_target_pairs={{0,7},{1,0},{2,1},{3,2},{4,3},{5,4},{6,5},{7,6},{8,15},{9,8},{10,9... | collective-permute-start | bytes 1572872 | tf_op jit(solution)/shard_map/ppermute | solution.py:293
  123.4 22.6 %collective-permute-start.18 = (bf16[4,8,4,16,128]{4,3,2,1,0:T(8,128)(2,1)S(1)}, bf16[4,8,4,16,128]{4,3,2,1,0:T(8,128)(2,1)}, u32[]{:S(2)}, u32[]{:S(2)}) collective-permute-start(bf16[4,8,4,16,128]{4,3,2,1,0:T(8,128)(2,1)S(1)} %collective-permute-done.14.rest_3_), channel_id=1, source_target_pairs={{0,1},{1,2},{2,3},{3,4},{4,5},{5,6},{6,7},{7,0},{8,9},{9,10},{10,1... | collective-permute-start | bytes 1572872 | tf_op jit(solution)/shard_map/ppermute | solution.py:292
  134.7 22.4 %collective-permute-start.16 = (bf16[4,8,4,16,128]{4,3,2,1,0:T(8,128)(2,1)}, bf16[4,8,4,16,128]{4,3,2,1,0:T(8,128)(2,1)S(1)}, u32[]{:S(2)}, u32[]{:S(2)}) collective-permute-start(bf16[4,8,4,16,128]{4,3,2,1,0:T(8,128)(2,1)} %collective-permute-done.9.rest_3_), channel_id=1, source_target_pairs={{0,1},{1,2},{2,3},{3,4},{4,5},{5,6},{6,7},{7,0},{8,9},{9,10},{10,1... | collective-permute-start | bytes 1572872 | tf_op jit(solution)/shard_map/ppermute | solution.py:292
  134.7 22.4 %collective-permute-start.17 = (bf16[4,8,4,16,128]{4,3,2,1,0:T(8,128)(2,1)}, bf16[4,8,4,16,128]{4,3,2,1,0:T(8,128)(2,1)}, u32[]{:S(2)}, u32[]{:S(2)}) collective-permute-start(bf16[4,8,4,16,128]{4,3,2,1,0:T(8,128)(2,1)} %collective-permute-done.11.rest_4_), channel_id=1, source_target_pairs={{0,7},{1,0},{2,1},{3,2},{4,3},{5,4},{6,5},{7,6},{8,15},{9,8},{10,9... | collective-permute-start | bytes 1572872 | tf_op jit(solution)/shard_map/ppermute | solution.py:293
  147.9 14.7 %collective-permute-start.22 = (bf16[2,8,4,16,128]{4,3,2,1,0:T(8,128)(2,1)S(1)}, bf16[2,8,4,16,128]{4,3,2,1,0:T(8,128)(2,1)S(1)}, u32[]{:S(2)}, u32[]{:S(2)}) collective-permute-start(bf16[2,8,4,16,128]{4,3,2,1,0:T(8,128)(2,1)S(1)} %slice.48), channel_id=1, source_target_pairs={{0,1},{1,2},{2,3},{3,4},{4,5},{5,6},{6,7},{7,0},{8,9},{9,10},{10,1... | collective-permute-start | bytes 786440 | tf_op jit(solution)/shard_map/ppermute | solution.py:292
  148.0 14.6 %collective-permute-start.23 = (bf16[2,8,4,16,128]{4,3,2,1,0:T(8,128)(2,1)S(1)}, bf16[2,8,4,16,128]{4,3,2,1,0:T(8,128)(2,1)S(1)}, u32[]{:S(2)}, u32[]{:S(2)}) collective-permute-start(bf16[2,8,4,16,128]{4,3,2,1,0:T(8,128)(2,1)S(1)} %slice.49), channel_id=1, source_target_pairs={{0,7},{1,0},{2,1},{3,2},{4,3},{5,4},{6,5},{7,6},{8,15},{9,8},{10,9... | collective-permute-start | bytes 786440 | tf_op jit(solution)/shard_map/ppermute | solution.py:293
  158.1 13.2 %collective-permute-start.21 = (bf16[2,8,4,16,128]{4,3,2,1,0:T(8,128)(2,1)S(1)}, bf16[2,8,4,16,128]{4,3,2,1,0:T(8,128)(2,1)S(1)}, u32[]{:S(2)}, u32[]{:S(2)}) collective-permute-start(bf16[2,8,4,16,128]{4,3,2,1,0:T(8,128)(2,1)S(1)} %slice.47), channel_id=1, source_target_pairs={{0,7},{1,0},{2,1},{3,2},{4,3},{5,4},{6,5},{7,6},{8,15},{9,8},{10,9... | collective-permute-start | bytes 786440 | tf_op jit(solution)/shard_map/ppermute | solution.py:293
  158.4 12.9 %collective-permute-start.20 = (bf16[2,8,4,16,128]{4,3,2,1,0:T(8,128)(2,1)S(1)}, bf16[2,8,4,16,128]{4,3,2,1,0:T(8,128)(2,1)S(1)}, u32[]{:S(2)}, u32[]{:S(2)}) collective-permute-start(bf16[2,8,4,16,128]{4,3,2,1,0:T(8,128)(2,1)S(1)} %slice.46), channel_id=1, source_target_pairs={{0,1},{1,2},{2,3},{3,4},{4,5},{5,6},{6,7},{7,0},{8,9},{9,10},{10,1... | collective-permute-start | bytes 786440 | tf_op jit(solution)/shard_map/ppermute | solution.py:292
  (36 other events, 256.0 us)

commit v10 on v9

--- a/solution.py
+++ b/solution.py
@@ -278,6 +278,7 @@
     blocks = [[x] for x in streams]
     places = [[(0, 0)] for _ in streams]
     states = [()] * len(streams)
+    first_parts = []
     for step in range(1, last + 1):
         for s in range(len(streams)):
             from_left, from_right = go_right[s], go_left[s]
@@ -285,17 +286,21 @@
                 held = lax.optimization_barrier((from_left, from_right, beside))
                 from_left, from_right, beside = held
                 from_left, from_right = from_left[:half], from_right[half:]
-            if (step, s) in ((last - 1, 1), (last, 0)):
-                other = states[1 - s]
-                held = lax.optimization_barrier((from_left, from_right, other))
-                from_left, from_right, states[1 - s] = held
+            if (step, s) == (last - 1, 1):
+                held = lax.optimization_barrier((from_left, from_right, first_parts[0]))
+                from_left, from_right, _ = held
+            if (step, s) == (last, 0):
+                held = lax.optimization_barrier((from_left, from_right, first_parts[1]))
+                from_left, from_right, _ = held
             go_right[s] = lax.ppermute(from_left, "tensor", right)
             go_left[s] = lax.ppermute(from_right, "tensor", left)
             blocks[s] += [go_right[s], go_left[s]]
             places[s] += [(n_ten - step, 0), (step, half if step == last else 0)]
-            if step in (last - 2, last):
+            if step >= last - 2:
                 state = gather_step(blocks[s], places[s], where, weights, states[s], step == last)
                 blocks[s], places[s], states[s] = [], [], state
+                if step == last - 2:
+                    first_parts.append(state)
     return states, beside
 
 
@@ -314,10 +319,11 @@
 
 def attend_kernel(first, with_prev, span_len, count_ref, q_ref, *rest):
     out_ref = rest[-1]
-    pair_refs, other_ref = rest[:-2], rest[-2]
-    if not with_prev:
-        done = other_ref.shape[0]
-        out_ref[out_ref.shape[0] - done :, :] = other_ref[...]
+    pair_refs, prev_ref, done = rest[:-1], None, 0
+    if with_prev:
+        pair_refs, (prev_ref, before_ref) = rest[:-3], rest[-3:-1]
+        done = before_ref.shape[0]
+        out_ref[:done, :] = before_ref[...]
     cols = out_ref.shape[1]
     heads = cols // HS
     spans = len(pair_refs)
@@ -334,7 +340,7 @@
             query = queries[:, at]
             scores = scores_of(query, pair[:, at])
             if with_prev and span == spans - 1:
-                prev = other_ref[...].reshape(keys, 2 * cols)
+                prev = prev_ref[...].reshape(keys, 2 * cols)
                 own = row == 0
                 scores = jnp.where(own, scores, scores_of(query, prev[:, at]))
                 count = jnp.where(own, count_ref[first + span], count_ref[first + span + 1])
@@ -350,14 +356,15 @@
                     weights, pair[:, value_at], preferred_element_type=jnp.float32
                 )
             mixed_heads.append(result.astype(jnp.bfloat16))
-        out_ref[span * span_len : (span + 1) * span_len, :] = jnp.concatenate(mixed_heads, axis=1)
-
-
-def attend(counts, queries, pairs, first, span_len, prev=None, after=None):
+        rows = slice(done + span * span_len, done + (span + 1) * span_len)
+        out_ref[rows, :] = jnp.concatenate(mixed_heads, axis=1)
+
+
+def attend(counts, queries, pairs, first, span_len, prev=None, before=None):
     cols = queries.shape[1]
     with_prev = prev is not None
-    rows = len(pairs) * span_len + (0 if with_prev else after.shape[0])
-    operands = [counts, queries, *pairs, prev if with_prev else after]
+    rows = len(pairs) * span_len + (before.shape[0] if with_prev else 0)
+    operands = [counts, queries, *pairs] + ([prev, before] if with_prev else [])
     vmem = pl.BlockSpec(memory_space=pltpu.VMEM)
     return pl.pallas_call(
         functools.partial(attend_kernel, first, with_prev, span_len),
@@ -435,10 +442,7 @@
     mine = letter(own, tokens, wo, wo.shape[0] // strips)
     letters = ring_gather(mine, n_ten, tok_dev // PIECE_T * (pieces_f // 2))
 
-    both = jnp.concatenate([wk, wv], axis=1).astype(jnp.float32)
-    both = (both * nbr_gain.astype(jnp.float32)[:, None]).astype(jnp.bfloat16)
-    both = both.reshape(n_ten, d_part, both.shape[1])
-    spread, both, _ = lax.optimization_barrier((spread, both, letters[3:5]))
+    spread, _ = lax.optimization_barrier((spread, letters[3:5]))
     n_notes = 2 * items + span_dev
     spread = spread.reshape(n_seq * (per_shard + 1), PIECE_T, PIECE_F)
     notes = spread[per_shard :: per_shard + 1, 0, :n_notes].astype(jnp.int32)
@@ -447,6 +451,12 @@
     counts = jnp.concatenate([nbr_count, prev_count[None]])
     (picked,) = pick(index, spread, 1)
     rows = lax.all_to_all(picked, "seq", split_axis=0, concat_axis=0, tiled=True)
+    nbr_gain, _ = lax.optimization_barrier((nbr_gain, picked))
+    both = jnp.concatenate([wk, wv], axis=1).astype(jnp.float32)
+    both = (both * nbr_gain.astype(jnp.float32)[:, None]).astype(jnp.bfloat16)
+    both = both.reshape(n_ten, d_part, both.shape[1])
+    *tail, both = lax.optimization_barrier((*letters[7:], both))
+    letters = letters[:7] + tail
     queries, strip = query(where, letters, x_gain, wq, tok_dev, shift, n_seq)
     rows, queries, strip, counts = lax.optimization_barrier((rows, queries, strip, counts))
     mail = lax.all_to_all(strip, "seq", split_axis=0, concat_axis=0, tiled=True)
@@ -456,8 +466,8 @@
     streams = [rows[:, :, items // 2 :], rows[:, :, : items // 2]]
     (late, early), mail = ring_project(streams, where, both, n_ten, mail)
     prev = lax.ppermute(late[-1], "seq", [(i, i + 1) for i in range(n_seq - 1)])
-    attended = attend(counts, queries, late, span_dev // 2, span_len, prev=prev)
-    attended = attend(counts, queries, early, 0, span_len, after=attended)
+    attended = attend(counts, queries, early, 0, span_len)
+    attended = attend(counts, queries, late, span_dev // 2, span_len, prev, attended)
     gathered = ring_gather(attended, n_ten, tok_dev // 2)
     return finish(where, mail, tokens, gathered, shift)
 

time: 212 us -> 204 us (0.962)
  waiting for transfers between devices: 82.7 us -> 69.4 us
  Pallas kernels: 28.8 us -> 33.5 us
  starting transfers between devices: 72.5 us -> 76.2 us
  local copies, waits for them, and re-layouts: 21.2 us -> 18.1 us
    ppermute x2, waiting for transfers between devices: 10.3 us -> 5.03 us  [ring_gather(): lax.ppermute(go_right[:cut_at], 'tensor', right)]
    ppermute x8, waiting for transfers between devices: 13.3 us -> 8.2 us  [ring_project(): go_right[s] = lax.ppermute(from_left, 'tensor', right)]
    pallas_call x4 -> x6, Pallas kernels: 14.7 us -> 19.5 us  [gather_step(): pl.pallas_call(functools.partial(gather_kernel, tuple(places), not state,...]
    ppermute x1, waiting for transfers between devices: 4.51 us -> 0.2 us  [body(): prev = lax.ppermute(late[-1], 'seq', [(i, i + 1) for i in range(n_seq - 1)])]
    ppermute x8, starting transfers between devices: 18 us -> 22.3 us  [ring_project(): go_left[s] = lax.ppermute(from_right, 'tensor', left)]
    ppermute x6, waiting for transfers between devices: 27.9 us -> 31.8 us  [ring_gather(): go_left = lax.ppermute(go_left, 'tensor', left)]
    ppermute x8, waiting for transfers between devices: 20.8 us -> 18.4 us  [ring_project(): go_left[s] = lax.ppermute(from_right, 'tensor', left)]
    unnamed x48 -> x42, local copies, waits for them, and re-layouts: 14.8 us -> 13.1 us
  transfers between devices with their start and end apart: 36 -> 36, of which waited for: 22 -> 19; matrix products, arithmetic and copies ran while one was open for 5% -> 4% of each run, Pallas kernels for 10% -> 13%
where the time goes in v10:
time: 204 us; the launch traced here: 203 us
  starting transfers between devices  76.2 us (37%)
  waiting for transfers between devices  69.4 us (34%)
  Pallas kernels  33.5 us (16%)
  local copies, waits for them, and re-layouts  18.1 us (9%)
  other arithmetic  4.97 us (2%)
    ppermute x6, waiting for transfers between devices, ring_gather(): go_left = lax.ppermute(go_left, 'tensor', left)  31.8 us
    ppermute x8, starting transfers between devices, ring_project(): go_left[s] = lax.ppermute(from_right, 'tensor', left)  22.3 us
    pallas_call x6, Pallas kernels, gather_step(): pl.pallas_call(functools.partial(gather_kernel, tuple(places), not state,...  19.5 us
    ppermute x8, waiting for transfers between devices, ring_project(): go_left[s] = lax.ppermute(from_right, 'tensor', left)  18.4 us
    ppermute x6, starting transfers between devices, ring_gather(): go_left = lax.ppermute(go_left, 'tensor', left)  17 us
    unnamed x42, local copies, waits for them, and re-layouts  13.1 us
    ppermute x8, waiting for transfers between devices, ring_project(): go_right[s] = lax.ppermute(from_left, 'tensor', right)  8.2 us
    all_to_all x1, starting transfers between devices, body(): lax.all_to_all(pieces, 'seq', split_axis=0, concat_axis=0, tiled=True)  7.54 us
  transfers between devices with their start and end apart: 36, of which 19 were waited for; matrix products, arithmetic and copies ran while one was open for 4% of the time, Pallas kernels for 13%

profile of v10, /device:TPU:8, one launch (start us, length us, event | category | flops | bytes accessed | tf_op | source)
XLA Modules:
  0.0 203.2 jit_solution(8067305185549062533)
XLA Ops:
  5.3 7.5 %all-to-all-start = ((bf16[32,17,16,128]{3,2,1,0:T(8,128)(2,1)}), bf16[32,17,16,128]{3,2,1,0:T(8,128)(2,1)S(1)}, u32[]{:S(2)}, u32[]{:S(2)}) async-start(bf16[32,17,16,128]{3,2,1,0:T(8,128)(2,1)} %copy-done), calls=%async_computation | async-start | bytes 4456448 | tf_op jit(solution)/shard_map/all_to_all | solution.py:436
  16.0 5.9 %collective-permute-start.2 = (bf16[80,16,128]{2,1,0:T(8,128)(2,1)}, bf16[80,16,128]{2,1,0:T(8,128)(2,1)S(1)}, u32[]{:S(2)}, u32[]{:S(2)}) collective-permute-start(bf16[80,16,128]{2,1,0:T(8,128)(2,1)} %letter.1.rest_0_), channel_id=1, source_target_pairs={{0,7},{1,0},{2,1},{3,2},{4,3},{5,4},{6,5},{7,6},{8,15},{9,8},{10,9... | collective-permute-start | bytes 983048 | tf_op jit(solution)/shard_map/ppermute | solution.py:265
  21.9 7.6 %collective-permute-done.2.rest_2_ = bf16[80,16,128]{2,1,0:T(8,128)(2,1)S(1)} collective-permute-done((bf16[80,16,128]{2,1,0:T(8,128)(2,1)}, bf16[80,16,128]{2,1,0:T(8,128)(2,1)S(1)}, u32[]{:S(2)}, u32[]{:S(2)}) %collective-permute-start.2) | collective-permute-done | bytes 327712 | tf_op jit(solution)/shard_map/ppermute | solution.py:265
  29.5 3.6 %collective-permute-start.3 = (bf16[80,16,128]{2,1,0:T(8,128)(2,1)S(1)}, bf16[80,16,128]{2,1,0:T(8,128)(2,1)S(1)}, u32[]{:S(2)}, u32[]{:S(2)}) collective-permute-start(bf16[80,16,128]{2,1,0:T(8,128)(2,1)S(1)} %collective-permute-done.2.rest_2_), channel_id=1, source_target_pairs={{0,7},{1,0},{2,1},{3,2},{4,3},{5,4},{6,5},{7,6},{8,15},{9,8},{10,9... | collective-permute-start | bytes 983048 | tf_op jit(solution)/shard_map/ppermute | solution.py:265
  33.0 6.4 %collective-permute-done.3.rest_4_ = bf16[80,16,128]{2,1,0:T(8,128)(2,1)S(1)} collective-permute-done((bf16[80,16,128]{2,1,0:T(8,128)(2,1)S(1)}, bf16[80,16,128]{2,1,0:T(8,128)(2,1)S(1)}, u32[]{:S(2)}, u32[]{:S(2)}) %collective-permute-start.3) | collective-permute-done | bytes 327712 | tf_op jit(solution)/shard_map/ppermute | solution.py:265
  39.5 3.5 %collective-permute-done.1.rest_3_ = bf16[80,16,128]{2,1,0:T(8,128)(2,1)} collective-permute-done((bf16[80,16,128]{2,1,0:T(8,128)(2,1)S(1)}, bf16[80,16,128]{2,1,0:T(8,128)(2,1)}, u32[]{:S(2)}, u32[]{:S(2)}) %collective-permute-start.1) | collective-permute-done | bytes 327712 | tf_op jit(solution)/shard_map/ppermute | solution.py:264
  45.3 7.4 %all-to-all-start.1 = ((bf16[32,8,16,128]{3,2,1,0:T(8,128)(2,1)}), bf16[32,8,16,128]{3,2,1,0:T(8,128)(2,1)}, u32[]{:S(2)}, u32[]{:S(2)}) async-start(bf16[32,8,16,128]{3,2,1,0:T(8,128)(2,1)} %pick.1), calls=%async_computation.1 | async-start | bytes 2097152 | tf_op jit(solution)/shard_map/all_to_all | solution.py:453
  52.8 4.4 %collective-permute-start.5 = (bf16[80,16,128]{2,1,0:T(8,128)(2,1)S(1)}, bf16[80,16,128]{2,1,0:T(8,128)(2,1)S(1)}, u32[]{:S(2)}, u32[]{:S(2)}) collective-permute-start(bf16[80,16,128]{2,1,0:T(8,128)(2,1)S(1)} %collective-permute-done.3.rest_4_), channel_id=1, source_target_pairs={{0,7},{1,0},{2,1},{3,2},{4,3},{5,4},{6,5},{7,6},{8,15},{9,8},{10,9... | collective-permute-start | bytes 983048 | tf_op jit(solution)/shard_map/ppermute | solution.py:265
  57.3 7.2 %collective-permute-done.5.rest_6_ = bf16[80,16,128]{2,1,0:T(8,128)(2,1)S(1)} collective-permute-done((bf16[80,16,128]{2,1,0:T(8,128)(2,1)S(1)}, bf16[80,16,128]{2,1,0:T(8,128)(2,1)S(1)}, u32[]{:S(2)}, u32[]{:S(2)}) %collective-permute-start.5) | collective-permute-done | bytes 327712 | tf_op jit(solution)/shard_map/ppermute | solution.py:265
  64.5 3.8 %collective-permute-start.7 = (bf16[48,16,128]{2,1,0:T(8,128)(2,1)S(1)}, bf16[48,16,128]{2,1,0:T(8,128)(2,1)S(1)}, u32[]{:S(2)}, u32[]{:S(2)}) collective-permute-start(bf16[48,16,128]{2,1,0:T(8,128)(2,1)S(1)} %slice.55), channel_id=1, source_target_pairs={{0,7},{1,0},{2,1},{3,2},{4,3},{5,4},{6,5},{7,6},{8,15},{9,8},{10,9... | collective-permute-start | bytes 589832 | tf_op jit(solution)/shard_map/ppermute | solution.py:269
  68.5 4.1 %multiply_convert_fusion.w_ref = bf16[8,512,512]{2,1,0:T(8,128)(2,1)} fusion(bf16[8,512,256]{2,1,0:T(8,128)(2,1)} %bitcast.20, bf16[8,512,256]{2,1,0:T(8,128)(2,1)} %bitcast.21, f32[8,512]{1,0:T(8,128)S(1)} %reshape.37), kind=kLoop, calls=%fused_computation | loop fusion | flops 12582912 | bytes 8404992 | tf_op jit(solution)/shard_map/convert_element_type | solution.py:456
  83.4 7.4 %all-to-all-start.2 = ((bf16[32,16,16,128]{3,2,1,0:T(8,128)(2,1)}), bf16[32,16,16,128]{3,2,1,0:T(8,128)(2,1)S(1)}, u32[]{:S(2)}, u32[]{:S(2)}) async-start(bf16[32,16,16,128]{3,2,1,0:T(8,128)(2,1)} %copy-done.2), calls=%async_computation.2 | async-start | bytes 4194304 | tf_op jit(solution)/shard_map/all_to_all | solution.py:462
  90.8 3.3 %collective-permute-start.10 = (bf16[4,8,4,16,128]{4,3,2,1,0:T(8,128)(2,1)S(1)}, bf16[4,8,4,16,128]{4,3,2,1,0:T(8,128)(2,1)S(1)}, u32[]{:S(2)}, u32[]{:S(2)}) collective-permute-start(bf16[4,8,4,16,128]{4,3,2,1,0:T(8,128)(2,1)S(1)} %get-tuple-element.74.rest_0_), channel_id=1, source_target_pairs={{0,7},{1,0},{2,1},{3,2},{4,3},{5,4},{6,5},{7,6},{8,15},{9,8},{10,9... | collective-permute-start | bytes 1572872 | tf_op jit(solution)/shard_map/ppermute | solution.py:296
  97.4 9.0 %collective-permute-done.10.rest_2_ = bf16[4,8,4,16,128]{4,3,2,1,0:T(8,128)(2,1)S(1)} collective-permute-done((bf16[4,8,4,16,128]{4,3,2,1,0:T(8,128)(2,1)S(1)}, bf16[4,8,4,16,128]{4,3,2,1,0:T(8,128)(2,1)S(1)}, u32[]{:S(2)}, u32[]{:S(2)}) %collective-permute-start.10) | collective-permute-done | bytes 524320 | tf_op jit(solution)/shard_map/ppermute | solution.py:296
  106.4 3.7 %collective-permute-start.11 = (bf16[4,8,4,16,128]{4,3,2,1,0:T(8,128)(2,1)S(1)}, bf16[4,8,4,16,128]{4,3,2,1,0:T(8,128)(2,1)}, u32[]{:S(2)}, u32[]{:S(2)}) collective-permute-start(bf16[4,8,4,16,128]{4,3,2,1,0:T(8,128)(2,1)S(1)} %collective-permute-done.10.rest_2_), channel_id=1, source_target_pairs={{0,7},{1,0},{2,1},{3,2},{4,3},{5,4},{6,5},{7,6},{8,15},{9,8},{10,9... | collective-permute-start | bytes 1572872 | tf_op jit(solution)/shard_map/ppermute | solution.py:296
  110.2 7.6 %collective-permute-done.15.rest_4_ = bf16[4,8,4,16,128]{4,3,2,1,0:T(8,128)(2,1)S(1)} collective-permute-done((bf16[4,8,4,16,128]{4,3,2,1,0:T(8,128)(2,1)}, bf16[4,8,4,16,128]{4,3,2,1,0:T(8,128)(2,1)S(1)}, u32[]{:S(2)}, u32[]{:S(2)}) %collective-permute-start.15) | collective-permute-done | bytes 524320 | tf_op jit(solution)/shard_map/ppermute | solution.py:296
  117.8 3.6 %collective-permute-start.19 = (bf16[4,8,4,16,128]{4,3,2,1,0:T(8,128)(2,1)S(1)}, bf16[4,8,4,16,128]{4,3,2,1,0:T(8,128)(2,1)S(1)}, u32[]{:S(2)}, u32[]{:S(2)}) collective-permute-start(bf16[4,8,4,16,128]{4,3,2,1,0:T(8,128)(2,1)S(1)} %collective-permute-done.15.rest_4_), channel_id=1, source_target_pairs={{0,7},{1,0},{2,1},{3,2},{4,3},{5,4},{6,5},{7,6},{8,15},{9,8},{10,9... | collective-permute-start | bytes 1572872 | tf_op jit(solution)/shard_map/ppermute | solution.py:296
  121.4 4.0 %gather_step.4 = (f32[512,512]{1,0:T(8,128)S(1)}, f32[512,128]{1,0:T(8,128)S(1)}) custom-call(s32[8]{0:T(128)S(1)} %and_select_fusion.where_ref, bf16[8,512,512]{2,1,0:T(8,128)(2,1)} %multiply_convert_fusion.w_ref, bf16[4,8,4,16,128]{4,3,2,1,0:T(8,128)(2,1)S(1)} %get-tuple-element.73.rest_0_, bf16[4,8,4,16,128]{4,3,2,1,0:T(8,128)(2,1)} %collective-permute-done.12.rest_1_, ...), custom_call_target="tpu_custom_call" | custom-call | flops 5368709120 | bytes 4718592 | tf_op jit(solution)/shard_map/gather_step/pallas_call | solution.py:237
  128.9 3.8 %collective-permute-done.9.rest_3_ = bf16[4,8,4,16,128]{4,3,2,1,0:T(8,128)(2,1)} collective-permute-done((bf16[4,8,4,16,128]{4,3,2,1,0:T(8,128)(2,1)S(1)}, bf16[4,8,4,16,128]{4,3,2,1,0:T(8,128)(2,1)}, u32[]{:S(2)}, u32[]{:S(2)}) %collective-permute-start.9) | collective-permute-done | bytes 524320 | tf_op jit(solution)/shard_map/ppermute | solution.py:295
  136.0 4.0 %gather_step.5 = (f32[512,512]{1,0:T(8,128)S(1)}, f32[512,128]{1,0:T(8,128)S(1)}) custom-call(s32[8]{0:T(128)S(1)} %and_select_fusion.where_ref, bf16[8,512,512]{2,1,0:T(8,128)(2,1)} %multiply_convert_fusion.w_ref, bf16[4,8,4,16,128]{4,3,2,1,0:T(8,128)(2,1)S(1)} %get-tuple-element.74.rest_0_, bf16[4,8,4,16,128]{4,3,2,1,0:T(8,128)(2,1)S(1)} %collective-permute-done.8.rest_1_, ...), custom_call_target="tpu_custom_call" | custom-call | flops 5368709120 | bytes 4718592 | tf_op jit(solution)/shard_map/gather_step/pallas_call | solution.py:237
  177.3 4.0 %collective-permute-done.26.rest_2_ = bf16[256,256]{1,0:T(8,128)(2,1)S(1)} collective-permute-done((bf16[256,256]{1,0:T(8,128)(2,1)S(1)}, bf16[256,256]{1,0:T(8,128)(2,1)S(1)}, u32[]{:S(2)}, u32[]{:S(2)}) %collective-permute-start.26) | collective-permute-done | bytes 131104 | tf_op jit(solution)/shard_map/ppermute | solution.py:265
  183.6 3.6 %collective-permute-done.28.rest_4_ = bf16[256,256]{1,0:T(8,128)(2,1)S(1)} collective-permute-done((bf16[256,256]{1,0:T(8,128)(2,1)S(1)}, bf16[256,256]{1,0:T(8,128)(2,1)S(1)}, u32[]{:S(2)}, u32[]{:S(2)}) %collective-permute-start.28) | collective-permute-done | bytes 131104 | tf_op jit(solution)/shard_map/ppermute | solution.py:265
  192.3 3.4 %collective-permute-start.32 = (bf16[128,256]{1,0:T(8,128)(2,1)S(1)}, bf16[128,256]{1,0:T(8,128)(2,1)S(1)}, u32[]{:S(2)}, u32[]{:S(2)}) collective-permute-start(bf16[128,256]{1,0:T(8,128)(2,1)S(1)} %slice.59), channel_id=1, source_target_pairs={{0,7},{1,0},{2,1},{3,2},{4,3},{5,4},{6,5},{7,6},{8,15},{9,8},{10,9... | collective-permute-start | bytes 196616 | tf_op jit(solution)/shard_map/ppermute | solution.py:269
  197.5 3.7 %collective-permute-done.31.rest_7_ = bf16[128,256]{1,0:T(8,128)(2,1)S(1)} collective-permute-done((bf16[128,256]{1,0:T(8,128)(2,1)S(1)}, bf16[128,256]{1,0:T(8,128)(2,1)S(1)}, u32[]{:S(2)}, u32[]{:S(2)}) %collective-permute-start.31) | collective-permute-done | bytes 65568 | tf_op jit(solution)/shard_map/ppermute | solution.py:268
  (121 shorter events, 79.4 us)
Async XLA Ops:
  5.3 37.7 %all-to-all-start = ((bf16[32,17,16,128]{3,2,1,0:T(8,128)(2,1)}), bf16[32,17,16,128]{3,2,1,0:T(8,128)(2,1)S(1)}, u32[]{:S(2)}, u32[]{:S(2)}) async-start(bf16[32,17,16,128]{3,2,1,0:T(8,128)(2,1)} %copy-done), calls=%async_computation | async-start | bytes 4456448 | tf_op jit(solution)/shard_map/all_to_all | solution.py:436
  16.0 13.5 %collective-permute-start.2 = (bf16[80,16,128]{2,1,0:T(8,128)(2,1)}, bf16[80,16,128]{2,1,0:T(8,128)(2,1)S(1)}, u32[]{:S(2)}, u32[]{:S(2)}) collective-permute-start(bf16[80,16,128]{2,1,0:T(8,128)(2,1)} %letter.1.rest_0_), channel_id=1, source_target_pairs={{0,7},{1,0},{2,1},{3,2},{4,3},{5,4},{6,5},{7,6},{8,15},{9,8},{10,9... | collective-permute-start | bytes 983048 | tf_op jit(solution)/shard_map/ppermute | solution.py:265
  21.9 11.2 %collective-permute-start = (bf16[80,16,128]{2,1,0:T(8,128)(2,1)}, bf16[80,16,128]{2,1,0:T(8,128)(2,1)S(1)}, u32[]{:S(2)}, u32[]{:S(2)}) collective-permute-start(bf16[80,16,128]{2,1,0:T(8,128)(2,1)} %letter.1.rest_0_), channel_id=1, source_target_pairs={{0,1},{1,2},{2,3},{3,4},{4,5},{5,6},{6,7},{7,0},{8,9},{9,10},{10,1... | collective-permute-start | bytes 983048 | tf_op jit(solution)/shard_map/ppermute | solution.py:264
  45.3 34.5 %all-to-all-start.1 = ((bf16[32,8,16,128]{3,2,1,0:T(8,128)(2,1)}), bf16[32,8,16,128]{3,2,1,0:T(8,128)(2,1)}, u32[]{:S(2)}, u32[]{:S(2)}) async-start(bf16[32,8,16,128]{3,2,1,0:T(8,128)(2,1)} %pick.1), calls=%async_computation.1 | async-start | bytes 2097152 | tf_op jit(solution)/shard_map/all_to_all | solution.py:453
  52.8 11.7 %collective-permute-start.5 = (bf16[80,16,128]{2,1,0:T(8,128)(2,1)S(1)}, bf16[80,16,128]{2,1,0:T(8,128)(2,1)S(1)}, u32[]{:S(2)}, u32[]{:S(2)}) collective-permute-start(bf16[80,16,128]{2,1,0:T(8,128)(2,1)S(1)} %collective-permute-done.3.rest_4_), channel_id=1, source_target_pairs={{0,7},{1,0},{2,1},{3,2},{4,3},{5,4},{6,5},{7,6},{8,15},{9,8},{10,9... | collective-permute-start | bytes 983048 | tf_op jit(solution)/shard_map/ppermute | solution.py:265
  57.2 11.1 %collective-permute-start.4 = (bf16[80,16,128]{2,1,0:T(8,128)(2,1)}, bf16[80,16,128]{2,1,0:T(8,128)(2,1)S(1)}, u32[]{:S(2)}, u32[]{:S(2)}) collective-permute-start(bf16[80,16,128]{2,1,0:T(8,128)(2,1)} %collective-permute-done.1.rest_3_), channel_id=1, source_target_pairs={{0,1},{1,2},{2,3},{3,4},{4,5},{5,6},{6,7},{7,0},{8,9},{9,10},{10,1... | collective-permute-start | bytes 983048 | tf_op jit(solution)/shard_map/ppermute | solution.py:264
  64.5 10.0 %collective-permute-start.7 = (bf16[48,16,128]{2,1,0:T(8,128)(2,1)S(1)}, bf16[48,16,128]{2,1,0:T(8,128)(2,1)S(1)}, u32[]{:S(2)}, u32[]{:S(2)}) collective-permute-start(bf16[48,16,128]{2,1,0:T(8,128)(2,1)S(1)} %slice.55), channel_id=1, source_target_pairs={{0,7},{1,0},{2,1},{3,2},{4,3},{5,4},{6,5},{7,6},{8,15},{9,8},{10,9... | collective-permute-start | bytes 589832 | tf_op jit(solution)/shard_map/ppermute | solution.py:269
  81.3 12.9 %collective-permute-start.13 = (bf16[4,8,4,16,128]{4,3,2,1,0:T(8,128)(2,1)S(1)}, bf16[4,8,4,16,128]{4,3,2,1,0:T(8,128)(2,1)}, u32[]{:S(2)}, u32[]{:S(2)}) collective-permute-start(bf16[4,8,4,16,128]{4,3,2,1,0:T(8,128)(2,1)S(1)} %get-tuple-element.73.rest_0_), channel_id=1, source_target_pairs={{0,7},{1,0},{2,1},{3,2},{4,3},{5,4},{6,5},{7,6},{8,15},{9,8},{10,9... | collective-permute-start | bytes 1572872 | tf_op jit(solution)/shard_map/ppermute | solution.py:296
  83.2 14.2 %collective-permute-start.12 = (bf16[4,8,4,16,128]{4,3,2,1,0:T(8,128)(2,1)S(1)}, bf16[4,8,4,16,128]{4,3,2,1,0:T(8,128)(2,1)}, u32[]{:S(2)}, u32[]{:S(2)}) collective-permute-start(bf16[4,8,4,16,128]{4,3,2,1,0:T(8,128)(2,1)S(1)} %get-tuple-element.73.rest_0_), channel_id=1, source_target_pairs={{0,1},{1,2},{2,3},{3,4},{4,5},{5,6},{6,7},{7,0},{8,9},{9,10},{10,1... | collective-permute-start | bytes 1572872 | tf_op jit(solution)/shard_map/ppermute | solution.py:295
  83.4 60.6 %all-to-all-start.2 = ((bf16[32,16,16,128]{3,2,1,0:T(8,128)(2,1)}), bf16[32,16,16,128]{3,2,1,0:T(8,128)(2,1)S(1)}, u32[]{:S(2)}, u32[]{:S(2)}) async-start(bf16[32,16,16,128]{3,2,1,0:T(8,128)(2,1)} %copy-done.2), calls=%async_computation.2 | async-start | bytes 4194304 | tf_op jit(solution)/shard_map/all_to_all | solution.py:462
  90.8 15.6 %collective-permute-start.10 = (bf16[4,8,4,16,128]{4,3,2,1,0:T(8,128)(2,1)S(1)}, bf16[4,8,4,16,128]{4,3,2,1,0:T(8,128)(2,1)S(1)}, u32[]{:S(2)}, u32[]{:S(2)}) collective-permute-start(bf16[4,8,4,16,128]{4,3,2,1,0:T(8,128)(2,1)S(1)} %get-tuple-element.74.rest_0_), channel_id=1, source_target_pairs={{0,7},{1,0},{2,1},{3,2},{4,3},{5,4},{6,5},{7,6},{8,15},{9,8},{10,9... | collective-permute-start | bytes 1572872 | tf_op jit(solution)/shard_map/ppermute | solution.py:296
  94.1 16.0 %collective-permute-start.8 = (bf16[4,8,4,16,128]{4,3,2,1,0:T(8,128)(2,1)S(1)}, bf16[4,8,4,16,128]{4,3,2,1,0:T(8,128)(2,1)S(1)}, u32[]{:S(2)}, u32[]{:S(2)}) collective-permute-start(bf16[4,8,4,16,128]{4,3,2,1,0:T(8,128)(2,1)S(1)} %get-tuple-element.74.rest_0_), channel_id=1, source_target_pairs={{0,1},{1,2},{2,3},{3,4},{4,5},{5,6},{6,7},{7,0},{8,9},{9,10},{10,1... | collective-permute-start | bytes 1572872 | tf_op jit(solution)/shard_map/ppermute | solution.py:295
  94.2 23.6 %collective-permute-start.15 = (bf16[4,8,4,16,128]{4,3,2,1,0:T(8,128)(2,1)}, bf16[4,8,4,16,128]{4,3,2,1,0:T(8,128)(2,1)S(1)}, u32[]{:S(2)}, u32[]{:S(2)}) collective-permute-start(bf16[4,8,4,16,128]{4,3,2,1,0:T(8,128)(2,1)} %collective-permute-done.13.rest_2_), channel_id=1, source_target_pairs={{0,7},{1,0},{2,1},{3,2},{4,3},{5,4},{6,5},{7,6},{8,15},{9,8},{10,9... | collective-permute-start | bytes 1572872 | tf_op jit(solution)/shard_map/ppermute | solution.py:296
  97.4 24.0 %collective-permute-start.14 = (bf16[4,8,4,16,128]{4,3,2,1,0:T(8,128)(2,1)}, bf16[4,8,4,16,128]{4,3,2,1,0:T(8,128)(2,1)S(1)}, u32[]{:S(2)}, u32[]{:S(2)}) collective-permute-start(bf16[4,8,4,16,128]{4,3,2,1,0:T(8,128)(2,1)} %collective-permute-done.12.rest_1_), channel_id=1, source_target_pairs={{0,1},{1,2},{2,3},{3,4},{4,5},{5,6},{6,7},{7,0},{8,9},{9,10},{10,1... | collective-permute-start | bytes 1572872 | tf_op jit(solution)/shard_map/ppermute | solution.py:295
  106.4 22.5 %collective-permute-start.11 = (bf16[4,8,4,16,128]{4,3,2,1,0:T(8,128)(2,1)S(1)}, bf16[4,8,4,16,128]{4,3,2,1,0:T(8,128)(2,1)}, u32[]{:S(2)}, u32[]{:S(2)}) collective-permute-start(bf16[4,8,4,16,128]{4,3,2,1,0:T(8,128)(2,1)S(1)} %collective-permute-done.10.rest_2_), channel_id=1, source_target_pairs={{0,7},{1,0},{2,1},{3,2},{4,3},{5,4},{6,5},{7,6},{8,15},{9,8},{10,9... | collective-permute-start | bytes 1572872 | tf_op jit(solution)/shard_map/ppermute | solution.py:296
  110.2 22.6 %collective-permute-start.9 = (bf16[4,8,4,16,128]{4,3,2,1,0:T(8,128)(2,1)S(1)}, bf16[4,8,4,16,128]{4,3,2,1,0:T(8,128)(2,1)}, u32[]{:S(2)}, u32[]{:S(2)}) collective-permute-start(bf16[4,8,4,16,128]{4,3,2,1,0:T(8,128)(2,1)S(1)} %collective-permute-done.8.rest_1_), channel_id=1, source_target_pairs={{0,1},{1,2},{2,3},{3,4},{4,5},{5,6},{6,7},{7,0},{8,9},{9,10},{10,1... | collective-permute-start | bytes 1572872 | tf_op jit(solution)/shard_map/ppermute | solution.py:295
  117.8 23.2 %collective-permute-start.19 = (bf16[4,8,4,16,128]{4,3,2,1,0:T(8,128)(2,1)S(1)}, bf16[4,8,4,16,128]{4,3,2,1,0:T(8,128)(2,1)S(1)}, u32[]{:S(2)}, u32[]{:S(2)}) collective-permute-start(bf16[4,8,4,16,128]{4,3,2,1,0:T(8,128)(2,1)S(1)} %collective-permute-done.15.rest_4_), channel_id=1, source_target_pairs={{0,7},{1,0},{2,1},{3,2},{4,3},{5,4},{6,5},{7,6},{8,15},{9,8},{10,9... | collective-permute-start | bytes 1572872 | tf_op jit(solution)/shard_map/ppermute | solution.py:296
  121.4 22.6 %collective-permute-start.18 = (bf16[4,8,4,16,128]{4,3,2,1,0:T(8,128)(2,1)S(1)}, bf16[4,8,4,16,128]{4,3,2,1,0:T(8,128)(2,1)}, u32[]{:S(2)}, u32[]{:S(2)}) collective-permute-start(bf16[4,8,4,16,128]{4,3,2,1,0:T(8,128)(2,1)S(1)} %collective-permute-done.14.rest_3_), channel_id=1, source_target_pairs={{0,1},{1,2},{2,3},{3,4},{4,5},{5,6},{6,7},{7,0},{8,9},{9,10},{10,1... | collective-permute-start | bytes 1572872 | tf_op jit(solution)/shard_map/ppermute | solution.py:295
  132.7 22.8 %collective-permute-start.16 = (bf16[4,8,4,16,128]{4,3,2,1,0:T(8,128)(2,1)}, bf16[4,8,4,16,128]{4,3,2,1,0:T(8,128)(2,1)S(1)}, u32[]{:S(2)}, u32[]{:S(2)}) collective-permute-start(bf16[4,8,4,16,128]{4,3,2,1,0:T(8,128)(2,1)} %collective-permute-done.9.rest_3_), channel_id=1, source_target_pairs={{0,1},{1,2},{2,3},{3,4},{4,5},{5,6},{6,7},{7,0},{8,9},{9,10},{10,1... | collective-permute-start | bytes 1572872 | tf_op jit(solution)/shard_map/ppermute | solution.py:295
  132.7 22.8 %collective-permute-start.17 = (bf16[4,8,4,16,128]{4,3,2,1,0:T(8,128)(2,1)}, bf16[4,8,4,16,128]{4,3,2,1,0:T(8,128)(2,1)}, u32[]{:S(2)}, u32[]{:S(2)}) collective-permute-start(bf16[4,8,4,16,128]{4,3,2,1,0:T(8,128)(2,1)} %collective-permute-done.11.rest_4_), channel_id=1, source_target_pairs={{0,7},{1,0},{2,1},{3,2},{4,3},{5,4},{6,5},{7,6},{8,15},{9,8},{10,9... | collective-permute-start | bytes 1572872 | tf_op jit(solution)/shard_map/ppermute | solution.py:296
  145.9 14.8 %collective-permute-start.20 = (bf16[2,8,4,16,128]{4,3,2,1,0:T(8,128)(2,1)S(1)}, bf16[2,8,4,16,128]{4,3,2,1,0:T(8,128)(2,1)S(1)}, u32[]{:S(2)}, u32[]{:S(2)}) collective-permute-start(bf16[2,8,4,16,128]{4,3,2,1,0:T(8,128)(2,1)S(1)} %slice.46), channel_id=1, source_target_pairs={{0,1},{1,2},{2,3},{3,4},{4,5},{5,6},{6,7},{7,0},{8,9},{9,10},{10,1... | collective-permute-start | bytes 786440 | tf_op jit(solution)/shard_map/ppermute | solution.py:295
  146.0 14.7 %collective-permute-start.21 = (bf16[2,8,4,16,128]{4,3,2,1,0:T(8,128)(2,1)S(1)}, bf16[2,8,4,16,128]{4,3,2,1,0:T(8,128)(2,1)S(1)}, u32[]{:S(2)}, u32[]{:S(2)}) collective-permute-start(bf16[2,8,4,16,128]{4,3,2,1,0:T(8,128)(2,1)S(1)} %slice.47), channel_id=1, source_target_pairs={{0,7},{1,0},{2,1},{3,2},{4,3},{5,4},{6,5},{7,6},{8,15},{9,8},{10,9... | collective-permute-start | bytes 786440 | tf_op jit(solution)/shard_map/ppermute | solution.py:296
  156.5 11.9 %collective-permute-start.24 = (bf16[2,8,4,16,128]{4,3,2,1,0:T(8,128)(2,1)S(1)}, bf16[2,8,4,16,128]{4,3,2,1,0:T(8,128)(2,1)S(1)}, u32[]{:S(2)}, u32[]{:S(2)}) collective-permute-start(bf16[2,8,4,16,128]{4,3,2,1,0:T(8,128)(2,1)S(1)} %slice.49), channel_id=1, source_target_pairs={{0,7},{1,0},{2,1},{3,2},{4,3},{5,4},{6,5},{7,6},{8,15},{9,8},{10,9... | collective-permute-start | bytes 786440 | tf_op jit(solution)/shard_map/ppermute | solution.py:296
  156.6 11.8 %collective-permute-start.23 = (bf16[2,8,4,16,128]{4,3,2,1,0:T(8,128)(2,1)S(1)}, bf16[2,8,4,16,128]{4,3,2,1,0:T(8,128)(2,1)S(1)}, u32[]{:S(2)}, u32[]{:S(2)}) collective-permute-start(bf16[2,8,4,16,128]{4,3,2,1,0:T(8,128)(2,1)S(1)} %slice.48), channel_id=1, source_target_pairs={{0,1},{1,2},{2,3},{3,4},{4,5},{5,6},{6,7},{7,0},{8,9},{9,10},{10,1... | collective-permute-start | bytes 786440 | tf_op jit(solution)/shard_map/ppermute | solution.py:295
  (33 other events, 205.3 us)

commit v11 on v10

--- a/solution.py
+++ b/solution.py
@@ -296,7 +296,7 @@
             go_left[s] = lax.ppermute(from_right, "tensor", left)
             blocks[s] += [go_right[s], go_left[s]]
             places[s] += [(n_ten - step, 0), (step, half if step == last else 0)]
-            if step >= last - 2:
+            if step in (last - 2, last) or (step, s) == (last - 1, 0):
                 state = gather_step(blocks[s], places[s], where, weights, states[s], step == last)
                 blocks[s], places[s], states[s] = [], [], state
                 if step == last - 2:
@@ -457,8 +457,8 @@
     both = both.reshape(n_ten, d_part, both.shape[1])
     *tail, both = lax.optimization_barrier((*letters[7:], both))
     letters = letters[:7] + tail
+    rows, letters, counts = lax.optimization_barrier((rows, letters, counts))
     queries, strip = query(where, letters, x_gain, wq, tok_dev, shift, n_seq)
-    rows, queries, strip, counts = lax.optimization_barrier((rows, queries, strip, counts))
     mail = lax.all_to_all(strip, "seq", split_axis=0, concat_axis=0, tiled=True)
     mail = mail.reshape(strips, halves, *strip.shape[1:])
 

time: 204 us -> 212 us (1.039)
  local copies, waits for them, and re-layouts: 18.1 us -> 25.3 us
  starting transfers between devices: 76.2 us -> 80.9 us
  Pallas kernels: 33.5 us -> 31.1 us
    ppermute x6, waiting for transfers between devices: 31.8 us -> 7.25 us  [ring_gather(): go_left = lax.ppermute(go_left, 'tensor', left)]
    ppermute x6, waiting for transfers between devices: 4.01 us -> 23.4 us  [ring_gather(): go_right = lax.ppermute(go_right, 'tensor', right)]
    ppermute x8, waiting for transfers between devices: 8.2 us -> 19.1 us  [ring_project(): go_right[s] = lax.ppermute(from_left, 'tensor', right)]
    ppermute x8, waiting for transfers between devices: 18.4 us -> 10.5 us  [ring_project(): go_left[s] = lax.ppermute(from_right, 'tensor', left)]
    unnamed x42 -> x70, local copies, waits for them, and re-layouts: 13.1 us -> 20.2 us
    ppermute x6, starting transfers between devices: 17 us -> 22.8 us  [ring_gather(): go_left = lax.ppermute(go_left, 'tensor', left)]
    ppermute x8, starting transfers between devices: 22.3 us -> 18 us  [ring_project(): go_left[s] = lax.ppermute(from_right, 'tensor', left)]
    ppermute x8, starting transfers between devices: 2.3 us -> 6.27 us  [ring_project(): go_right[s] = lax.ppermute(from_left, 'tensor', right)]
  transfers between devices with their start and end apart: 36 -> 36, of which waited for: 19 -> 17; matrix products, arithmetic and copies ran while one was open for 4% -> 4% of each run, Pallas kernels for 13% -> 12%
where the time goes in v11:
time: 212 us; the launch traced here: 211 us
  starting transfers between devices  80.9 us (38%)
  waiting for transfers between devices  67.7 us (32%)
  Pallas kernels  31.1 us (15%)
  local copies, waits for them, and re-layouts  25.3 us (12%)
  other arithmetic  4.85 us (2%)
    ppermute x6, waiting for transfers between devices, ring_gather(): go_right = lax.ppermute(go_right, 'tensor', right)  23.4 us
    ppermute x6, starting transfers between devices, ring_gather(): go_left = lax.ppermute(go_left, 'tensor', left)  22.8 us
    unnamed x70, local copies, waits for them, and re-layouts  20.2 us
    ppermute x8, waiting for transfers between devices, ring_project(): go_right[s] = lax.ppermute(from_left, 'tensor', right)  19.1 us
    ppermute x8, starting transfers between devices, ring_project(): go_left[s] = lax.ppermute(from_right, 'tensor', left)  18 us
    pallas_call x5, Pallas kernels, gather_step(): pl.pallas_call(functools.partial(gather_kernel, tuple(places), not state,...  17.1 us
    ppermute x8, waiting for transfers between devices, ring_project(): go_left[s] = lax.ppermute(from_right, 'tensor', left)  10.5 us
    all_to_all x1, starting transfers between devices, body(): lax.all_to_all(picked, 'seq', split_axis=0, concat_axis=0, tiled=True)  7.83 us
  transfers between devices with their start and end apart: 36, of which 17 were waited for; matrix products, arithmetic and copies ran while one was open for 4% of the time, Pallas kernels for 12%

profile of v11, /device:TPU:8, one launch (start us, length us, event | category | flops | bytes accessed | tf_op | source)
XLA Modules:
  0.0 210.9 jit_solution(18332539363120986397)
XLA Ops:
  5.3 7.5 %all-to-all-start = ((bf16[32,17,16,128]{3,2,1,0:T(8,128)(2,1)}), bf16[32,17,16,128]{3,2,1,0:T(8,128)(2,1)S(1)}, u32[]{:S(2)}, u32[]{:S(2)}) async-start(bf16[32,17,16,128]{3,2,1,0:T(8,128)(2,1)} %copy-done), calls=%async_computation | async-start | bytes 4456448 | tf_op jit(solution)/shard_map/all_to_all | solution.py:436
  17.8 3.9 %collective-permute-start.2 = (bf16[80,16,128]{2,1,0:T(8,128)(2,1)}, bf16[80,16,128]{2,1,0:T(8,128)(2,1)S(1)}, u32[]{:S(2)}, u32[]{:S(2)}) collective-permute-start(bf16[80,16,128]{2,1,0:T(8,128)(2,1)} %letter.1.rest_0_), channel_id=1, source_target_pairs={{0,7},{1,0},{2,1},{3,2},{4,3},{5,4},{6,5},{7,6},{8,15},{9,8},{10,9... | collective-permute-start | bytes 983048 | tf_op jit(solution)/shard_map/ppermute | solution.py:265
  21.8 8.2 %collective-permute-done.rest_1_ = bf16[80,16,128]{2,1,0:T(8,128)(2,1)S(1)} collective-permute-done((bf16[80,16,128]{2,1,0:T(8,128)(2,1)}, bf16[80,16,128]{2,1,0:T(8,128)(2,1)S(1)}, u32[]{:S(2)}, u32[]{:S(2)}) %collective-permute-start) | collective-permute-done | bytes 327712 | tf_op jit(solution)/shard_map/ppermute | solution.py:264
  30.8 3.2 %collective-permute-start.3 = (bf16[80,16,128]{2,1,0:T(8,128)(2,1)S(1)}, bf16[80,16,128]{2,1,0:T(8,128)(2,1)S(1)}, u32[]{:S(2)}, u32[]{:S(2)}) collective-permute-start(bf16[80,16,128]{2,1,0:T(8,128)(2,1)S(1)} %collective-permute-done.2.rest_2_), channel_id=1, source_target_pairs={{0,7},{1,0},{2,1},{3,2},{4,3},{5,4},{6,5},{7,6},{8,15},{9,8},{10,9... | collective-permute-start | bytes 983048 | tf_op jit(solution)/shard_map/ppermute | solution.py:265
  34.7 5.7 %collective-permute-done.1.rest_3_ = bf16[80,16,128]{2,1,0:T(8,128)(2,1)S(1)} collective-permute-done((bf16[80,16,128]{2,1,0:T(8,128)(2,1)S(1)}, bf16[80,16,128]{2,1,0:T(8,128)(2,1)S(1)}, u32[]{:S(2)}, u32[]{:S(2)}) %collective-permute-start.1) | collective-permute-done | bytes 327712 | tf_op jit(solution)/shard_map/ppermute | solution.py:264
  43.4 7.8 %all-to-all-start.1 = ((bf16[32,8,16,128]{3,2,1,0:T(8,128)(2,1)}), bf16[32,8,16,128]{3,2,1,0:T(8,128)(2,1)}, u32[]{:S(2)}, u32[]{:S(2)}) async-start(bf16[32,8,16,128]{3,2,1,0:T(8,128)(2,1)} %pick.1), calls=%async_computation.1 | async-start | bytes 2097152 | tf_op jit(solution)/shard_map/all_to_all | solution.py:453
  51.2 5.9 %collective-permute-start.5 = (bf16[80,16,128]{2,1,0:T(8,128)(2,1)S(1)}, bf16[80,16,128]{2,1,0:T(8,128)(2,1)S(1)}, u32[]{:S(2)}, u32[]{:S(2)}) collective-permute-start(bf16[80,16,128]{2,1,0:T(8,128)(2,1)S(1)} %collective-permute-done.3.rest_4_), channel_id=1, source_target_pairs={{0,7},{1,0},{2,1},{3,2},{4,3},{5,4},{6,5},{7,6},{8,15},{9,8},{10,9... | collective-permute-start | bytes 983048 | tf_op jit(solution)/shard_map/ppermute | solution.py:265
  57.2 7.2 %collective-permute-done.5.rest_6_ = bf16[80,16,128]{2,1,0:T(8,128)(2,1)S(1)} collective-permute-done((bf16[80,16,128]{2,1,0:T(8,128)(2,1)S(1)}, bf16[80,16,128]{2,1,0:T(8,128)(2,1)S(1)}, u32[]{:S(2)}, u32[]{:S(2)}) %collective-permute-start.5) | collective-permute-done | bytes 327712 | tf_op jit(solution)/shard_map/ppermute | solution.py:265
  64.5 3.8 %collective-permute-start.7 = (bf16[48,16,128]{2,1,0:T(8,128)(2,1)S(1)}, bf16[48,16,128]{2,1,0:T(8,128)(2,1)S(1)}, u32[]{:S(2)}, u32[]{:S(2)}) collective-permute-start(bf16[48,16,128]{2,1,0:T(8,128)(2,1)S(1)} %slice.55), channel_id=1, source_target_pairs={{0,7},{1,0},{2,1},{3,2},{4,3},{5,4},{6,5},{7,6},{8,15},{9,8},{10,9... | collective-permute-start | bytes 589832 | tf_op jit(solution)/shard_map/ppermute | solution.py:269
  68.5 4.1 %multiply_convert_fusion.w_ref = bf16[8,512,512]{2,1,0:T(8,128)(2,1)} fusion(bf16[8,512,256]{2,1,0:T(8,128)(2,1)} %bitcast.20, bf16[8,512,256]{2,1,0:T(8,128)(2,1)} %bitcast.21, f32[8,512]{1,0:T(8,128)S(1)} %reshape.37), kind=kLoop, calls=%fused_computation | loop fusion | flops 12582912 | bytes 8404992 | tf_op jit(solution)/shard_map/convert_element_type | solution.py:456
  77.5 3.2 %collective-permute-start.13 = (bf16[4,8,4,16,128]{4,3,2,1,0:T(8,128)(2,1)S(1)}, bf16[4,8,4,16,128]{4,3,2,1,0:T(8,128)(2,1)}, u32[]{:S(2)}, u32[]{:S(2)}) collective-permute-start(bf16[4,8,4,16,128]{4,3,2,1,0:T(8,128)(2,1)S(1)} %get-tuple-element.83.rest_0_), channel_id=1, source_target_pairs={{0,7},{1,0},{2,1},{3,2},{4,3},{5,4},{6,5},{7,6},{8,15},{9,8},{10,9... | collective-permute-start | bytes 1572872 | tf_op jit(solution)/shard_map/ppermute | solution.py:296
  89.9 7.5 %all-to-all-start.2 = ((bf16[32,16,16,128]{3,2,1,0:T(8,128)(2,1)}), bf16[32,16,16,128]{3,2,1,0:T(8,128)(2,1)S(1)}, u32[]{:S(2)}, u32[]{:S(2)}) async-start(bf16[32,16,16,128]{3,2,1,0:T(8,128)(2,1)} %copy-done.2), calls=%async_computation.2 | async-start | bytes 4194304 | tf_op jit(solution)/shard_map/all_to_all | solution.py:462
  99.7 3.2 %collective-permute-start.15 = (bf16[4,8,4,16,128]{4,3,2,1,0:T(8,128)(2,1)}, bf16[4,8,4,16,128]{4,3,2,1,0:T(8,128)(2,1)S(1)}, u32[]{:S(2)}, u32[]{:S(2)}) collective-permute-start(bf16[4,8,4,16,128]{4,3,2,1,0:T(8,128)(2,1)} %collective-permute-done.13.rest_2_), channel_id=1, source_target_pairs={{0,7},{1,0},{2,1},{3,2},{4,3},{5,4},{6,5},{7,6},{8,15},{9,8},{10,9... | collective-permute-start | bytes 1572872 | tf_op jit(solution)/shard_map/ppermute | solution.py:296
  102.9 9.5 %collective-permute-done.10.rest_2_ = bf16[4,8,4,16,128]{4,3,2,1,0:T(8,128)(2,1)S(1)} collective-permute-done((bf16[4,8,4,16,128]{4,3,2,1,0:T(8,128)(2,1)S(1)}, bf16[4,8,4,16,128]{4,3,2,1,0:T(8,128)(2,1)S(1)}, u32[]{:S(2)}, u32[]{:S(2)}) %collective-permute-start.10) | collective-permute-done | bytes 524320 | tf_op jit(solution)/shard_map/ppermute | solution.py:296
  114.5 10.5 %collective-permute-done.14.rest_3_ = bf16[4,8,4,16,128]{4,3,2,1,0:T(8,128)(2,1)S(1)} collective-permute-done((bf16[4,8,4,16,128]{4,3,2,1,0:T(8,128)(2,1)}, bf16[4,8,4,16,128]{4,3,2,1,0:T(8,128)(2,1)S(1)}, u32[]{:S(2)}, u32[]{:S(2)}) %collective-permute-start.14) | collective-permute-done | bytes 524320 | tf_op jit(solution)/shard_map/ppermute | solution.py:295
  128.2 4.0 %gather_step.3 = (f32[512,512]{1,0:T(8,128)S(1)}, f32[512,128]{1,0:T(8,128)S(1)}) custom-call(s32[8]{0:T(128)S(1)} %and_select_fusion.where_ref, bf16[8,512,512]{2,1,0:T(8,128)(2,1)} %multiply_convert_fusion.w_ref, bf16[4,8,4,16,128]{4,3,2,1,0:T(8,128)(2,1)S(1)} %get-tuple-element.83.rest_0_, bf16[4,8,4,16,128]{4,3,2,1,0:T(8,128)(2,1)} %collective-permute-done.12.rest_1_, ...), custom_call_target="tpu_custom_call" | custom-call | flops 5368709120 | bytes 4718592 | tf_op jit(solution)/shard_map/gather_step/pallas_call | solution.py:237
  139.5 4.0 %gather_step.4 = (f32[512,512]{1,0:T(8,128)S(1)}, f32[512,128]{1,0:T(8,128)S(1)}) custom-call(s32[8]{0:T(128)S(1)} %and_select_fusion.where_ref, bf16[8,512,512]{2,1,0:T(8,128)(2,1)} %multiply_convert_fusion.w_ref, bf16[4,8,4,16,128]{4,3,2,1,0:T(8,128)(2,1)S(1)} %get-tuple-element.84.rest_0_, bf16[4,8,4,16,128]{4,3,2,1,0:T(8,128)(2,1)S(1)} %collective-permute-done.8.rest_1_, ...), custom_call_target="tpu_custom_call" | custom-call | flops 5368709120 | bytes 4718592 | tf_op jit(solution)/shard_map/gather_step/pallas_call | solution.py:237
  153.5 5.2 %collective-permute-done.16.rest_0_ = bf16[4,8,4,16,128]{4,3,2,1,0:T(8,128)(2,1)S(1)} collective-permute-done((bf16[4,8,4,16,128]{4,3,2,1,0:T(8,128)(2,1)}, bf16[4,8,4,16,128]{4,3,2,1,0:T(8,128)(2,1)S(1)}, u32[]{:S(2)}, u32[]{:S(2)}) %collective-permute-start.16) | collective-permute-done | bytes 524320 | tf_op jit(solution)/shard_map/ppermute | solution.py:295
  174.3 3.3 %gather_last.3 = (bf16[8,2,16,512]{3,2,1,0:T(8,128)(2,1)S(1)}, bf16[8,2,16,512]{3,2,1,0:T(8,128)(2,1)S(1)}) custom-call(s32[8]{0:T(128)S(1)} %and_select_fusion.where_ref, bf16[8,512,512]{2,1,0:T(8,128)(2,1)} %multiply_convert_fusion.w_ref, bf16[4,8,4,16,128]{4,3,2,1,0:T(8,128)(2,1)S(1)} %collective-permute-done.16.rest_0_, ...), custom_call_target="tpu_custom_call" | custom-call | flops 3221225472 | bytes 3670016 | tf_op jit(solution)/shard_map/gather_last/pallas_call | solution.py:237
  184.2 3.2 %collective-permute-start.26 = (bf16[256,256]{1,0:T(8,128)(2,1)S(1)}, bf16[256,256]{1,0:T(8,128)(2,1)S(1)}, u32[]{:S(2)}, u32[]{:S(2)}) collective-permute-start(bf16[256,256]{1,0:T(8,128)(2,1)S(1)} %attend_prev.1.rest_0_), channel_id=1, source_target_pairs={{0,7},{1,0},{2,1},{3,2},{4,3},{5,4},{6,5},{7,6},{8,15},{9,8},{10,9... | collective-permute-start | bytes 393224 | tf_op jit(solution)/shard_map/ppermute | solution.py:265
  190.3 3.2 %collective-permute-start.28 = (bf16[256,256]{1,0:T(8,128)(2,1)S(1)}, bf16[256,256]{1,0:T(8,128)(2,1)S(1)}, u32[]{:S(2)}, u32[]{:S(2)}) collective-permute-start(bf16[256,256]{1,0:T(8,128)(2,1)S(1)} %collective-permute-done.26.rest_2_), channel_id=1, source_target_pairs={{0,7},{1,0},{2,1},{3,2},{4,3},{5,4},{6,5},{7,6},{8,15},{9,8},{10,9... | collective-permute-start | bytes 393224 | tf_op jit(solution)/shard_map/ppermute | solution.py:265
  196.5 3.2 %collective-permute-start.30 = (bf16[256,256]{1,0:T(8,128)(2,1)S(1)}, bf16[256,256]{1,0:T(8,128)(2,1)S(1)}, u32[]{:S(2)}, u32[]{:S(2)}) collective-permute-start(bf16[256,256]{1,0:T(8,128)(2,1)S(1)} %collective-permute-done.28.rest_4_), channel_id=1, source_target_pairs={{0,7},{1,0},{2,1},{3,2},{4,3},{5,4},{6,5},{7,6},{8,15},{9,8},{10,9... | collective-permute-start | bytes 393224 | tf_op jit(solution)/shard_map/ppermute | solution.py:265
  199.8 3.6 %collective-permute-done.29.rest_5_ = bf16[256,256]{1,0:T(8,128)(2,1)S(1)} collective-permute-done((bf16[256,256]{1,0:T(8,128)(2,1)S(1)}, bf16[256,256]{1,0:T(8,128)(2,1)S(1)}, u32[]{:S(2)}, u32[]{:S(2)}) %collective-permute-start.29) | collective-permute-done | bytes 131104 | tf_op jit(solution)/shard_map/ppermute | solution.py:264
  203.4 3.3 %collective-permute-start.32 = (bf16[128,256]{1,0:T(8,128)(2,1)S(1)}, bf16[128,256]{1,0:T(8,128)(2,1)S(1)}, u32[]{:S(2)}, u32[]{:S(2)}) collective-permute-start(bf16[128,256]{1,0:T(8,128)(2,1)S(1)} %slice.59), channel_id=1, source_target_pairs={{0,7},{1,0},{2,1},{3,2},{4,3},{5,4},{6,5},{7,6},{8,15},{9,8},{10,9... | collective-permute-start | bytes 196616 | tf_op jit(solution)/shard_map/ppermute | solution.py:269
  (148 shorter events, 85.3 us)
Async XLA Ops:
  5.3 35.8 %all-to-all-start = ((bf16[32,17,16,128]{3,2,1,0:T(8,128)(2,1)}), bf16[32,17,16,128]{3,2,1,0:T(8,128)(2,1)S(1)}, u32[]{:S(2)}, u32[]{:S(2)}) async-start(bf16[32,17,16,128]{3,2,1,0:T(8,128)(2,1)} %copy-done), calls=%async_computation | async-start | bytes 4456448 | tf_op jit(solution)/shard_map/all_to_all | solution.py:436
  15.9 14.1 %collective-permute-start = (bf16[80,16,128]{2,1,0:T(8,128)(2,1)}, bf16[80,16,128]{2,1,0:T(8,128)(2,1)S(1)}, u32[]{:S(2)}, u32[]{:S(2)}) collective-permute-start(bf16[80,16,128]{2,1,0:T(8,128)(2,1)} %letter.1.rest_0_), channel_id=1, source_target_pairs={{0,1},{1,2},{2,3},{3,4},{4,5},{5,6},{6,7},{7,0},{8,9},{9,10},{10,1... | collective-permute-start | bytes 983048 | tf_op jit(solution)/shard_map/ppermute | solution.py:264
  17.8 12.9 %collective-permute-start.2 = (bf16[80,16,128]{2,1,0:T(8,128)(2,1)}, bf16[80,16,128]{2,1,0:T(8,128)(2,1)S(1)}, u32[]{:S(2)}, u32[]{:S(2)}) collective-permute-start(bf16[80,16,128]{2,1,0:T(8,128)(2,1)} %letter.1.rest_0_), channel_id=1, source_target_pairs={{0,7},{1,0},{2,1},{3,2},{4,3},{5,4},{6,5},{7,6},{8,15},{9,8},{10,9... | collective-permute-start | bytes 983048 | tf_op jit(solution)/shard_map/ppermute | solution.py:265
  30.0 10.5 %collective-permute-start.1 = (bf16[80,16,128]{2,1,0:T(8,128)(2,1)S(1)}, bf16[80,16,128]{2,1,0:T(8,128)(2,1)S(1)}, u32[]{:S(2)}, u32[]{:S(2)}) collective-permute-start(bf16[80,16,128]{2,1,0:T(8,128)(2,1)S(1)} %collective-permute-done.rest_1_), channel_id=1, source_target_pairs={{0,1},{1,2},{2,3},{3,4},{4,5},{5,6},{6,7},{7,0},{8,9},{9,10},{10,1... | collective-permute-start | bytes 983048 | tf_op jit(solution)/shard_map/ppermute | solution.py:264
  43.4 32.5 %all-to-all-start.1 = ((bf16[32,8,16,128]{3,2,1,0:T(8,128)(2,1)}), bf16[32,8,16,128]{3,2,1,0:T(8,128)(2,1)}, u32[]{:S(2)}, u32[]{:S(2)}) async-start(bf16[32,8,16,128]{3,2,1,0:T(8,128)(2,1)} %pick.1), calls=%async_computation.1 | async-start | bytes 2097152 | tf_op jit(solution)/shard_map/all_to_all | solution.py:453
  51.2 13.2 %collective-permute-start.5 = (bf16[80,16,128]{2,1,0:T(8,128)(2,1)S(1)}, bf16[80,16,128]{2,1,0:T(8,128)(2,1)S(1)}, u32[]{:S(2)}, u32[]{:S(2)}) collective-permute-start(bf16[80,16,128]{2,1,0:T(8,128)(2,1)S(1)} %collective-permute-done.3.rest_4_), channel_id=1, source_target_pairs={{0,7},{1,0},{2,1},{3,2},{4,3},{5,4},{6,5},{7,6},{8,15},{9,8},{10,9... | collective-permute-start | bytes 983048 | tf_op jit(solution)/shard_map/ppermute | solution.py:265
  57.2 11.1 %collective-permute-start.4 = (bf16[80,16,128]{2,1,0:T(8,128)(2,1)S(1)}, bf16[80,16,128]{2,1,0:T(8,128)(2,1)S(1)}, u32[]{:S(2)}, u32[]{:S(2)}) collective-permute-start(bf16[80,16,128]{2,1,0:T(8,128)(2,1)S(1)} %collective-permute-done.1.rest_3_), channel_id=1, source_target_pairs={{0,1},{1,2},{2,3},{3,4},{4,5},{5,6},{6,7},{7,0},{8,9},{9,10},{10,1... | collective-permute-start | bytes 983048 | tf_op jit(solution)/shard_map/ppermute | solution.py:264
  77.4 22.3 %collective-permute-start.12 = (bf16[4,8,4,16,128]{4,3,2,1,0:T(8,128)(2,1)S(1)}, bf16[4,8,4,16,128]{4,3,2,1,0:T(8,128)(2,1)}, u32[]{:S(2)}, u32[]{:S(2)}) collective-permute-start(bf16[4,8,4,16,128]{4,3,2,1,0:T(8,128)(2,1)S(1)} %get-tuple-element.83.rest_0_), channel_id=1, source_target_pairs={{0,1},{1,2},{2,3},{3,4},{4,5},{5,6},{6,7},{7,0},{8,9},{9,10},{10,1... | collective-permute-start | bytes 1572872 | tf_op jit(solution)/shard_map/ppermute | solution.py:295
  77.5 22.2 %collective-permute-start.13 = (bf16[4,8,4,16,128]{4,3,2,1,0:T(8,128)(2,1)S(1)}, bf16[4,8,4,16,128]{4,3,2,1,0:T(8,128)(2,1)}, u32[]{:S(2)}, u32[]{:S(2)}) collective-permute-start(bf16[4,8,4,16,128]{4,3,2,1,0:T(8,128)(2,1)S(1)} %get-tuple-element.83.rest_0_), channel_id=1, source_target_pairs={{0,7},{1,0},{2,1},{3,2},{4,3},{5,4},{6,5},{7,6},{8,15},{9,8},{10,9... | collective-permute-start | bytes 1572872 | tf_op jit(solution)/shard_map/ppermute | solution.py:296
  89.9 58.3 %all-to-all-start.2 = ((bf16[32,16,16,128]{3,2,1,0:T(8,128)(2,1)}), bf16[32,16,16,128]{3,2,1,0:T(8,128)(2,1)S(1)}, u32[]{:S(2)}, u32[]{:S(2)}) async-start(bf16[32,16,16,128]{3,2,1,0:T(8,128)(2,1)} %copy-done.2), calls=%async_computation.2 | async-start | bytes 4194304 | tf_op jit(solution)/shard_map/all_to_all | solution.py:462
  97.4 15.0 %collective-permute-start.10 = (bf16[4,8,4,16,128]{4,3,2,1,0:T(8,128)(2,1)S(1)}, bf16[4,8,4,16,128]{4,3,2,1,0:T(8,128)(2,1)S(1)}, u32[]{:S(2)}, u32[]{:S(2)}) collective-permute-start(bf16[4,8,4,16,128]{4,3,2,1,0:T(8,128)(2,1)S(1)} %get-tuple-element.84.rest_0_), channel_id=1, source_target_pairs={{0,7},{1,0},{2,1},{3,2},{4,3},{5,4},{6,5},{7,6},{8,15},{9,8},{10,9... | collective-permute-start | bytes 1572872 | tf_op jit(solution)/shard_map/ppermute | solution.py:296
  97.7 16.0 %collective-permute-start.8 = (bf16[4,8,4,16,128]{4,3,2,1,0:T(8,128)(2,1)S(1)}, bf16[4,8,4,16,128]{4,3,2,1,0:T(8,128)(2,1)S(1)}, u32[]{:S(2)}, u32[]{:S(2)}) collective-permute-start(bf16[4,8,4,16,128]{4,3,2,1,0:T(8,128)(2,1)S(1)} %get-tuple-element.84.rest_0_), channel_id=1, source_target_pairs={{0,1},{1,2},{2,3},{3,4},{4,5},{5,6},{6,7},{7,0},{8,9},{9,10},{10,1... | collective-permute-start | bytes 1572872 | tf_op jit(solution)/shard_map/ppermute | solution.py:295
  99.7 25.3 %collective-permute-start.14 = (bf16[4,8,4,16,128]{4,3,2,1,0:T(8,128)(2,1)}, bf16[4,8,4,16,128]{4,3,2,1,0:T(8,128)(2,1)S(1)}, u32[]{:S(2)}, u32[]{:S(2)}) collective-permute-start(bf16[4,8,4,16,128]{4,3,2,1,0:T(8,128)(2,1)} %collective-permute-done.12.rest_1_), channel_id=1, source_target_pairs={{0,1},{1,2},{2,3},{3,4},{4,5},{5,6},{6,7},{7,0},{8,9},{9,10},{10,1... | collective-permute-start | bytes 1572872 | tf_op jit(solution)/shard_map/ppermute | solution.py:295
  99.7 26.0 %collective-permute-start.15 = (bf16[4,8,4,16,128]{4,3,2,1,0:T(8,128)(2,1)}, bf16[4,8,4,16,128]{4,3,2,1,0:T(8,128)(2,1)S(1)}, u32[]{:S(2)}, u32[]{:S(2)}) collective-permute-start(bf16[4,8,4,16,128]{4,3,2,1,0:T(8,128)(2,1)} %collective-permute-done.13.rest_2_), channel_id=1, source_target_pairs={{0,7},{1,0},{2,1},{3,2},{4,3},{5,4},{6,5},{7,6},{8,15},{9,8},{10,9... | collective-permute-start | bytes 1572872 | tf_op jit(solution)/shard_map/ppermute | solution.py:296
  112.4 22.6 %collective-permute-start.11 = (bf16[4,8,4,16,128]{4,3,2,1,0:T(8,128)(2,1)S(1)}, bf16[4,8,4,16,128]{4,3,2,1,0:T(8,128)(2,1)}, u32[]{:S(2)}, u32[]{:S(2)}) collective-permute-start(bf16[4,8,4,16,128]{4,3,2,1,0:T(8,128)(2,1)S(1)} %collective-permute-done.10.rest_2_), channel_id=1, source_target_pairs={{0,7},{1,0},{2,1},{3,2},{4,3},{5,4},{6,5},{7,6},{8,15},{9,8},{10,9... | collective-permute-start | bytes 1572872 | tf_op jit(solution)/shard_map/ppermute | solution.py:296
  113.7 22.6 %collective-permute-start.9 = (bf16[4,8,4,16,128]{4,3,2,1,0:T(8,128)(2,1)S(1)}, bf16[4,8,4,16,128]{4,3,2,1,0:T(8,128)(2,1)}, u32[]{:S(2)}, u32[]{:S(2)}) collective-permute-start(bf16[4,8,4,16,128]{4,3,2,1,0:T(8,128)(2,1)S(1)} %collective-permute-done.8.rest_1_), channel_id=1, source_target_pairs={{0,1},{1,2},{2,3},{3,4},{4,5},{5,6},{6,7},{7,0},{8,9},{9,10},{10,1... | collective-permute-start | bytes 1572872 | tf_op jit(solution)/shard_map/ppermute | solution.py:295
  125.0 22.5 %collective-permute-start.18 = (bf16[4,8,4,16,128]{4,3,2,1,0:T(8,128)(2,1)S(1)}, bf16[4,8,4,16,128]{4,3,2,1,0:T(8,128)(2,1)S(1)}, u32[]{:S(2)}, u32[]{:S(2)}) collective-permute-start(bf16[4,8,4,16,128]{4,3,2,1,0:T(8,128)(2,1)S(1)} %collective-permute-done.14.rest_3_), channel_id=1, source_target_pairs={{0,1},{1,2},{2,3},{3,4},{4,5},{5,6},{6,7},{7,0},{8,9},{9,10},{10,1... | collective-permute-start | bytes 1572872 | tf_op jit(solution)/shard_map/ppermute | solution.py:295
  125.7 22.5 %collective-permute-start.19 = (bf16[4,8,4,16,128]{4,3,2,1,0:T(8,128)(2,1)S(1)}, bf16[4,8,4,16,128]{4,3,2,1,0:T(8,128)(2,1)}, u32[]{:S(2)}, u32[]{:S(2)}) collective-permute-start(bf16[4,8,4,16,128]{4,3,2,1,0:T(8,128)(2,1)S(1)} %collective-permute-done.15.rest_4_), channel_id=1, source_target_pairs={{0,7},{1,0},{2,1},{3,2},{4,3},{5,4},{6,5},{7,6},{8,15},{9,8},{10,9... | collective-permute-start | bytes 1572872 | tf_op jit(solution)/shard_map/ppermute | solution.py:296
  136.3 22.4 %collective-permute-start.16 = (bf16[4,8,4,16,128]{4,3,2,1,0:T(8,128)(2,1)}, bf16[4,8,4,16,128]{4,3,2,1,0:T(8,128)(2,1)S(1)}, u32[]{:S(2)}, u32[]{:S(2)}) collective-permute-start(bf16[4,8,4,16,128]{4,3,2,1,0:T(8,128)(2,1)} %collective-permute-done.9.rest_3_), channel_id=1, source_target_pairs={{0,1},{1,2},{2,3},{3,4},{4,5},{5,6},{6,7},{7,0},{8,9},{9,10},{10,1... | collective-permute-start | bytes 1572872 | tf_op jit(solution)/shard_map/ppermute | solution.py:295
  137.1 21.6 %collective-permute-start.17 = (bf16[4,8,4,16,128]{4,3,2,1,0:T(8,128)(2,1)}, bf16[4,8,4,16,128]{4,3,2,1,0:T(8,128)(2,1)}, u32[]{:S(2)}, u32[]{:S(2)}) collective-permute-start(bf16[4,8,4,16,128]{4,3,2,1,0:T(8,128)(2,1)} %collective-permute-done.11.rest_4_), channel_id=1, source_target_pairs={{0,7},{1,0},{2,1},{3,2},{4,3},{5,4},{6,5},{7,6},{8,15},{9,8},{10,9... | collective-permute-start | bytes 1572872 | tf_op jit(solution)/shard_map/ppermute | solution.py:296
  150.2 19.3 %collective-permute-start.20 = (bf16[2,8,4,16,128]{4,3,2,1,0:T(8,128)(2,1)S(1)}, bf16[2,8,4,16,128]{4,3,2,1,0:T(8,128)(2,1)S(1)}, u32[]{:S(2)}, u32[]{:S(2)}) collective-permute-start(bf16[2,8,4,16,128]{4,3,2,1,0:T(8,128)(2,1)S(1)} %slice.46), channel_id=1, source_target_pairs={{0,1},{1,2},{2,3},{3,4},{4,5},{5,6},{6,7},{7,0},{8,9},{9,10},{10,1... | collective-permute-start | bytes 786440 | tf_op jit(solution)/shard_map/ppermute | solution.py:295
  151.0 18.5 %collective-permute-start.21 = (bf16[2,8,4,16,128]{4,3,2,1,0:T(8,128)(2,1)S(1)}, bf16[2,8,4,16,128]{4,3,2,1,0:T(8,128)(2,1)S(1)}, u32[]{:S(2)}, u32[]{:S(2)}) collective-permute-start(bf16[2,8,4,16,128]{4,3,2,1,0:T(8,128)(2,1)S(1)} %slice.47), channel_id=1, source_target_pairs={{0,7},{1,0},{2,1},{3,2},{4,3},{5,4},{6,5},{7,6},{8,15},{9,8},{10,9... | collective-permute-start | bytes 786440 | tf_op jit(solution)/shard_map/ppermute | solution.py:296
  158.7 15.6 %collective-permute-start.23 = (bf16[2,8,4,16,128]{4,3,2,1,0:T(8,128)(2,1)S(1)}, bf16[2,8,4,16,128]{4,3,2,1,0:T(8,128)(2,1)S(1)}, u32[]{:S(2)}, u32[]{:S(2)}) collective-permute-start(bf16[2,8,4,16,128]{4,3,2,1,0:T(8,128)(2,1)S(1)} %slice.48), channel_id=1, source_target_pairs={{0,1},{1,2},{2,3},{3,4},{4,5},{5,6},{6,7},{7,0},{8,9},{9,10},{10,1... | collective-permute-start | bytes 786440 | tf_op jit(solution)/shard_map/ppermute | solution.py:295
  160.7 13.5 %collective-permute-start.24 = (bf16[2,8,4,16,128]{4,3,2,1,0:T(8,128)(2,1)S(1)}, bf16[2,8,4,16,128]{4,3,2,1,0:T(8,128)(2,1)S(1)}, u32[]{:S(2)}, u32[]{:S(2)}) collective-permute-start(bf16[2,8,4,16,128]{4,3,2,1,0:T(8,128)(2,1)S(1)} %slice.49), channel_id=1, source_target_pairs={{0,7},{1,0},{2,1},{3,2},{4,3},{5,4},{6,5},{7,6},{8,15},{9,8},{10,9... | collective-permute-start | bytes 786440 | tf_op jit(solution)/shard_map/ppermute | solution.py:296
  (47 other events, 275.2 us)

commit v12 on v11

--- a/solution.py
+++ b/solution.py
@@ -457,8 +457,8 @@
     both = both.reshape(n_ten, d_part, both.shape[1])
     *tail, both = lax.optimization_barrier((*letters[7:], both))
     letters = letters[:7] + tail
-    rows, letters, counts = lax.optimization_barrier((rows, letters, counts))
     queries, strip = query(where, letters, x_gain, wq, tok_dev, shift, n_seq)
+    rows, queries, strip, counts = lax.optimization_barrier((rows, queries, strip, counts))
     mail = lax.all_to_all(strip, "seq", split_axis=0, concat_axis=0, tiled=True)
     mail = mail.reshape(strips, halves, *strip.shape[1:])
 

time: 212 us -> 207 us (0.976)
  local copies, waits for them, and re-layouts: 25.3 us -> 17.2 us
  waiting for transfers between devices: 67.7 us -> 73.5 us
  starting transfers between devices: 80.9 us -> 78.7 us
    ppermute x6, waiting for transfers between devices: 7.25 us -> 30.1 us  [ring_gather(): go_left = lax.ppermute(go_left, 'tensor', left)]
    ppermute x6, waiting for transfers between devices: 23.4 us -> 3.58 us  [ring_gather(): go_right = lax.ppermute(go_right, 'tensor', right)]
    ppermute x8, waiting for transfers between devices: 10.5 us -> 19.2 us  [ring_project(): go_left[s] = lax.ppermute(from_right, 'tensor', left)]
    unnamed x70 -> x42, local copies, waits for them, and re-layouts: 20.2 us -> 12.1 us
    ppermute x8, waiting for transfers between devices: 19.1 us -> 11.2 us  [ring_project(): go_right[s] = lax.ppermute(from_left, 'tensor', right)]
    ppermute x8, starting transfers between devices: 18 us -> 22.5 us  [ring_project(): go_left[s] = lax.ppermute(from_right, 'tensor', left)]
    ppermute x8, starting transfers between devices: 6.27 us -> 2.27 us  [ring_project(): go_right[s] = lax.ppermute(from_left, 'tensor', right)]
  transfers between devices with their start and end apart: 36 -> 36, of which waited for: 17 -> 18; matrix products, arithmetic and copies ran while one was open for 4% -> 4% of each run, Pallas kernels for 12% -> 12%
where the time goes in v12:
time: 207 us; the launch traced here: 206 us
  starting transfers between devices  78.7 us (38%)
  waiting for transfers between devices  73.5 us (36%)
  Pallas kernels  31.2 us (15%)
  local copies, waits for them, and re-layouts  17.2 us (8%)
  other arithmetic  4.88 us (2%)
    ppermute x6, waiting for transfers between devices, ring_gather(): go_left = lax.ppermute(go_left, 'tensor', left)  30.1 us
    ppermute x8, starting transfers between devices, ring_project(): go_left[s] = lax.ppermute(from_right, 'tensor', left)  22.5 us
    ppermute x6, starting transfers between devices, ring_gather(): go_left = lax.ppermute(go_left, 'tensor', left)  21.3 us
    ppermute x8, waiting for transfers between devices, ring_project(): go_left[s] = lax.ppermute(from_right, 'tensor', left)  19.2 us
    pallas_call x5, Pallas kernels, gather_step(): pl.pallas_call(functools.partial(gather_kernel, tuple(places), not state,...  17.1 us
    unnamed x42, local copies, waits for them, and re-layouts  12.1 us
    ppermute x8, waiting for transfers between devices, ring_project(): go_right[s] = lax.ppermute(from_left, 'tensor', right)  11.2 us
    all_to_all x1, starting transfers between devices, body(): lax.all_to_all(pieces, 'seq', split_axis=0, concat_axis=0, tiled=True)  7.54 us
  transfers between devices with their start and end apart: 36, of which 18 were waited for; matrix products, arithmetic and copies ran while one was open for 4% of the time, Pallas kernels for 12%

profile of v12, /device:TPU:8, one launch (start us, length us, event | category | flops | bytes accessed | tf_op | source)
XLA Modules:
  0.0 206.5 jit_solution(7642105368852222087)
XLA Ops:
  5.4 7.5 %all-to-all-start = ((bf16[32,17,16,128]{3,2,1,0:T(8,128)(2,1)}), bf16[32,17,16,128]{3,2,1,0:T(8,128)(2,1)S(1)}, u32[]{:S(2)}, u32[]{:S(2)}) async-start(bf16[32,17,16,128]{3,2,1,0:T(8,128)(2,1)} %copy-done), calls=%async_computation | async-start | bytes 4456448 | tf_op jit(solution)/shard_map/all_to_all | solution.py:436
  15.9 5.9 %collective-permute-start.2 = (bf16[80,16,128]{2,1,0:T(8,128)(2,1)}, bf16[80,16,128]{2,1,0:T(8,128)(2,1)S(1)}, u32[]{:S(2)}, u32[]{:S(2)}) collective-permute-start(bf16[80,16,128]{2,1,0:T(8,128)(2,1)} %letter.1.rest_0_), channel_id=1, source_target_pairs={{0,7},{1,0},{2,1},{3,2},{4,3},{5,4},{6,5},{7,6},{8,15},{9,8},{10,9... | collective-permute-start | bytes 983048 | tf_op jit(solution)/shard_map/ppermute | solution.py:265
  21.8 7.6 %collective-permute-done.2.rest_2_ = bf16[80,16,128]{2,1,0:T(8,128)(2,1)S(1)} collective-permute-done((bf16[80,16,128]{2,1,0:T(8,128)(2,1)}, bf16[80,16,128]{2,1,0:T(8,128)(2,1)S(1)}, u32[]{:S(2)}, u32[]{:S(2)}) %collective-permute-start.2) | collective-permute-done | bytes 327712 | tf_op jit(solution)/shard_map/ppermute | solution.py:265
  29.4 3.6 %collective-permute-start.3 = (bf16[80,16,128]{2,1,0:T(8,128)(2,1)S(1)}, bf16[80,16,128]{2,1,0:T(8,128)(2,1)S(1)}, u32[]{:S(2)}, u32[]{:S(2)}) collective-permute-start(bf16[80,16,128]{2,1,0:T(8,128)(2,1)S(1)} %collective-permute-done.2.rest_2_), channel_id=1, source_target_pairs={{0,7},{1,0},{2,1},{3,2},{4,3},{5,4},{6,5},{7,6},{8,15},{9,8},{10,9... | collective-permute-start | bytes 983048 | tf_op jit(solution)/shard_map/ppermute | solution.py:265
  33.0 6.4 %collective-permute-done.3.rest_4_ = bf16[80,16,128]{2,1,0:T(8,128)(2,1)S(1)} collective-permute-done((bf16[80,16,128]{2,1,0:T(8,128)(2,1)S(1)}, bf16[80,16,128]{2,1,0:T(8,128)(2,1)S(1)}, u32[]{:S(2)}, u32[]{:S(2)}) %collective-permute-start.3) | collective-permute-done | bytes 327712 | tf_op jit(solution)/shard_map/ppermute | solution.py:265
  39.4 3.5 %collective-permute-done.1.rest_3_ = bf16[80,16,128]{2,1,0:T(8,128)(2,1)} collective-permute-done((bf16[80,16,128]{2,1,0:T(8,128)(2,1)S(1)}, bf16[80,16,128]{2,1,0:T(8,128)(2,1)}, u32[]{:S(2)}, u32[]{:S(2)}) %collective-permute-start.1) | collective-permute-done | bytes 327712 | tf_op jit(solution)/shard_map/ppermute | solution.py:264
  45.3 7.4 %all-to-all-start.1 = ((bf16[32,8,16,128]{3,2,1,0:T(8,128)(2,1)}), bf16[32,8,16,128]{3,2,1,0:T(8,128)(2,1)}, u32[]{:S(2)}, u32[]{:S(2)}) async-start(bf16[32,8,16,128]{3,2,1,0:T(8,128)(2,1)} %pick.1), calls=%async_computation.1 | async-start | bytes 2097152 | tf_op jit(solution)/shard_map/all_to_all | solution.py:453
  52.7 4.5 %collective-permute-start.5 = (bf16[80,16,128]{2,1,0:T(8,128)(2,1)S(1)}, bf16[80,16,128]{2,1,0:T(8,128)(2,1)S(1)}, u32[]{:S(2)}, u32[]{:S(2)}) collective-permute-start(bf16[80,16,128]{2,1,0:T(8,128)(2,1)S(1)} %collective-permute-done.3.rest_4_), channel_id=1, source_target_pairs={{0,7},{1,0},{2,1},{3,2},{4,3},{5,4},{6,5},{7,6},{8,15},{9,8},{10,9... | collective-permute-start | bytes 983048 | tf_op jit(solution)/shard_map/ppermute | solution.py:265
  57.3 7.2 %collective-permute-done.5.rest_6_ = bf16[80,16,128]{2,1,0:T(8,128)(2,1)S(1)} collective-permute-done((bf16[80,16,128]{2,1,0:T(8,128)(2,1)S(1)}, bf16[80,16,128]{2,1,0:T(8,128)(2,1)S(1)}, u32[]{:S(2)}, u32[]{:S(2)}) %collective-permute-start.5) | collective-permute-done | bytes 327712 | tf_op jit(solution)/shard_map/ppermute | solution.py:265
  64.6 3.8 %collective-permute-start.7 = (bf16[48,16,128]{2,1,0:T(8,128)(2,1)S(1)}, bf16[48,16,128]{2,1,0:T(8,128)(2,1)S(1)}, u32[]{:S(2)}, u32[]{:S(2)}) collective-permute-start(bf16[48,16,128]{2,1,0:T(8,128)(2,1)S(1)} %slice.55), channel_id=1, source_target_pairs={{0,7},{1,0},{2,1},{3,2},{4,3},{5,4},{6,5},{7,6},{8,15},{9,8},{10,9... | collective-permute-start | bytes 589832 | tf_op jit(solution)/shard_map/ppermute | solution.py:269
  68.5 4.1 %multiply_convert_fusion.w_ref = bf16[8,512,512]{2,1,0:T(8,128)(2,1)} fusion(bf16[8,512,256]{2,1,0:T(8,128)(2,1)} %bitcast.20, bf16[8,512,256]{2,1,0:T(8,128)(2,1)} %bitcast.21, f32[8,512]{1,0:T(8,128)S(1)} %reshape.37), kind=kLoop, calls=%fused_computation | loop fusion | flops 12582912 | bytes 8404992 | tf_op jit(solution)/shard_map/convert_element_type | solution.py:456
  83.4 7.5 %all-to-all-start.2 = ((bf16[32,16,16,128]{3,2,1,0:T(8,128)(2,1)}), bf16[32,16,16,128]{3,2,1,0:T(8,128)(2,1)S(1)}, u32[]{:S(2)}, u32[]{:S(2)}) async-start(bf16[32,16,16,128]{3,2,1,0:T(8,128)(2,1)} %copy-done.2), calls=%async_computation.2 | async-start | bytes 4194304 | tf_op jit(solution)/shard_map/all_to_all | solution.py:462
  97.4 9.0 %collective-permute-done.10.rest_2_ = bf16[4,8,4,16,128]{4,3,2,1,0:T(8,128)(2,1)S(1)} collective-permute-done((bf16[4,8,4,16,128]{4,3,2,1,0:T(8,128)(2,1)S(1)}, bf16[4,8,4,16,128]{4,3,2,1,0:T(8,128)(2,1)S(1)}, u32[]{:S(2)}, u32[]{:S(2)}) %collective-permute-start.10) | collective-permute-done | bytes 524320 | tf_op jit(solution)/shard_map/ppermute | solution.py:296
  106.4 3.7 %collective-permute-start.11 = (bf16[4,8,4,16,128]{4,3,2,1,0:T(8,128)(2,1)S(1)}, bf16[4,8,4,16,128]{4,3,2,1,0:T(8,128)(2,1)}, u32[]{:S(2)}, u32[]{:S(2)}) collective-permute-start(bf16[4,8,4,16,128]{4,3,2,1,0:T(8,128)(2,1)S(1)} %collective-permute-done.10.rest_2_), channel_id=1, source_target_pairs={{0,7},{1,0},{2,1},{3,2},{4,3},{5,4},{6,5},{7,6},{8,15},{9,8},{10,9... | collective-permute-start | bytes 1572872 | tf_op jit(solution)/shard_map/ppermute | solution.py:296
  110.2 7.6 %collective-permute-done.15.rest_4_ = bf16[4,8,4,16,128]{4,3,2,1,0:T(8,128)(2,1)S(1)} collective-permute-done((bf16[4,8,4,16,128]{4,3,2,1,0:T(8,128)(2,1)}, bf16[4,8,4,16,128]{4,3,2,1,0:T(8,128)(2,1)S(1)}, u32[]{:S(2)}, u32[]{:S(2)}) %collective-permute-start.15) | collective-permute-done | bytes 524320 | tf_op jit(solution)/shard_map/ppermute | solution.py:296
  117.8 3.6 %collective-permute-start.19 = (bf16[4,8,4,16,128]{4,3,2,1,0:T(8,128)(2,1)S(1)}, bf16[4,8,4,16,128]{4,3,2,1,0:T(8,128)(2,1)S(1)}, u32[]{:S(2)}, u32[]{:S(2)}) collective-permute-start(bf16[4,8,4,16,128]{4,3,2,1,0:T(8,128)(2,1)S(1)} %collective-permute-done.15.rest_4_), channel_id=1, source_target_pairs={{0,7},{1,0},{2,1},{3,2},{4,3},{5,4},{6,5},{7,6},{8,15},{9,8},{10,9... | collective-permute-start | bytes 1572872 | tf_op jit(solution)/shard_map/ppermute | solution.py:296
  121.4 4.0 %gather_step.3 = (f32[512,512]{1,0:T(8,128)S(1)}, f32[512,128]{1,0:T(8,128)S(1)}) custom-call(s32[8]{0:T(128)S(1)} %and_select_fusion.where_ref, bf16[8,512,512]{2,1,0:T(8,128)(2,1)} %multiply_convert_fusion.w_ref, bf16[4,8,4,16,128]{4,3,2,1,0:T(8,128)(2,1)S(1)} %get-tuple-element.69.rest_0_, bf16[4,8,4,16,128]{4,3,2,1,0:T(8,128)(2,1)} %collective-permute-done.12.rest_1_, ...), custom_call_target="tpu_custom_call" | custom-call | flops 5368709120 | bytes 4718592 | tf_op jit(solution)/shard_map/gather_step/pallas_call | solution.py:237
  128.9 3.8 %collective-permute-done.9.rest_3_ = bf16[4,8,4,16,128]{4,3,2,1,0:T(8,128)(2,1)} collective-permute-done((bf16[4,8,4,16,128]{4,3,2,1,0:T(8,128)(2,1)S(1)}, bf16[4,8,4,16,128]{4,3,2,1,0:T(8,128)(2,1)}, u32[]{:S(2)}, u32[]{:S(2)}) %collective-permute-start.9) | collective-permute-done | bytes 524320 | tf_op jit(solution)/shard_map/ppermute | solution.py:295
  136.0 4.0 %gather_step.4 = (f32[512,512]{1,0:T(8,128)S(1)}, f32[512,128]{1,0:T(8,128)S(1)}) custom-call(s32[8]{0:T(128)S(1)} %and_select_fusion.where_ref, bf16[8,512,512]{2,1,0:T(8,128)(2,1)} %multiply_convert_fusion.w_ref, bf16[4,8,4,16,128]{4,3,2,1,0:T(8,128)(2,1)S(1)} %get-tuple-element.70.rest_0_, bf16[4,8,4,16,128]{4,3,2,1,0:T(8,128)(2,1)S(1)} %collective-permute-done.8.rest_1_, ...), custom_call_target="tpu_custom_call" | custom-call | flops 5368709120 | bytes 4718592 | tf_op jit(solution)/shard_map/gather_step/pallas_call | solution.py:237
  149.2 5.9 %collective-permute-done.16.rest_0_ = bf16[4,8,4,16,128]{4,3,2,1,0:T(8,128)(2,1)S(1)} collective-permute-done((bf16[4,8,4,16,128]{4,3,2,1,0:T(8,128)(2,1)}, bf16[4,8,4,16,128]{4,3,2,1,0:T(8,128)(2,1)S(1)}, u32[]{:S(2)}, u32[]{:S(2)}) %collective-permute-start.16) | collective-permute-done | bytes 524320 | tf_op jit(solution)/shard_map/ppermute | solution.py:295
  168.5 3.3 %gather_last.3 = (bf16[8,2,16,512]{3,2,1,0:T(8,128)(2,1)S(1)}, bf16[8,2,16,512]{3,2,1,0:T(8,128)(2,1)S(1)}) custom-call(s32[8]{0:T(128)S(1)} %and_select_fusion.where_ref, bf16[8,512,512]{2,1,0:T(8,128)(2,1)} %multiply_convert_fusion.w_ref, bf16[4,8,4,16,128]{4,3,2,1,0:T(8,128)(2,1)S(1)} %collective-permute-done.16.rest_0_, ...), custom_call_target="tpu_custom_call" | custom-call | flops 3221225472 | bytes 3670016 | tf_op jit(solution)/shard_map/gather_last/pallas_call | solution.py:237
  188.6 3.4 %collective-permute-start.30 = (bf16[256,256]{1,0:T(8,128)(2,1)S(1)}, bf16[256,256]{1,0:T(8,128)(2,1)S(1)}, u32[]{:S(2)}, u32[]{:S(2)}) collective-permute-start(bf16[256,256]{1,0:T(8,128)(2,1)S(1)} %collective-permute-done.28.rest_4_), channel_id=1, source_target_pairs={{0,7},{1,0},{2,1},{3,2},{4,3},{5,4},{6,5},{7,6},{8,15},{9,8},{10,9... | collective-permute-start | bytes 393224 | tf_op jit(solution)/shard_map/ppermute | solution.py:265
  195.2 3.7 %collective-permute-start.32 = (bf16[128,256]{1,0:T(8,128)(2,1)S(1)}, bf16[128,256]{1,0:T(8,128)(2,1)S(1)}, u32[]{:S(2)}, u32[]{:S(2)}) collective-permute-start(bf16[128,256]{1,0:T(8,128)(2,1)S(1)} %slice.59), channel_id=1, source_target_pairs={{0,7},{1,0},{2,1},{3,2},{4,3},{5,4},{6,5},{7,6},{8,15},{9,8},{10,9... | collective-permute-start | bytes 196616 | tf_op jit(solution)/shard_map/ppermute | solution.py:269
  200.8 3.7 %collective-permute-done.31.rest_7_ = bf16[128,256]{1,0:T(8,128)(2,1)S(1)} collective-permute-done((bf16[128,256]{1,0:T(8,128)(2,1)S(1)}, bf16[128,256]{1,0:T(8,128)(2,1)S(1)}, u32[]{:S(2)}, u32[]{:S(2)}) %collective-permute-start.31) | collective-permute-done | bytes 65568 | tf_op jit(solution)/shard_map/ppermute | solution.py:268
  (120 shorter events, 80.6 us)
Async XLA Ops:
  5.4 37.6 %all-to-all-start = ((bf16[32,17,16,128]{3,2,1,0:T(8,128)(2,1)}), bf16[32,17,16,128]{3,2,1,0:T(8,128)(2,1)S(1)}, u32[]{:S(2)}, u32[]{:S(2)}) async-start(bf16[32,17,16,128]{3,2,1,0:T(8,128)(2,1)} %copy-done), calls=%async_computation | async-start | bytes 4456448 | tf_op jit(solution)/shard_map/all_to_all | solution.py:436
  15.9 13.5 %collective-permute-start.2 = (bf16[80,16,128]{2,1,0:T(8,128)(2,1)}, bf16[80,16,128]{2,1,0:T(8,128)(2,1)S(1)}, u32[]{:S(2)}, u32[]{:S(2)}) collective-permute-start(bf16[80,16,128]{2,1,0:T(8,128)(2,1)} %letter.1.rest_0_), channel_id=1, source_target_pairs={{0,7},{1,0},{2,1},{3,2},{4,3},{5,4},{6,5},{7,6},{8,15},{9,8},{10,9... | collective-permute-start | bytes 983048 | tf_op jit(solution)/shard_map/ppermute | solution.py:265
  21.8 11.2 %collective-permute-start = (bf16[80,16,128]{2,1,0:T(8,128)(2,1)}, bf16[80,16,128]{2,1,0:T(8,128)(2,1)S(1)}, u32[]{:S(2)}, u32[]{:S(2)}) collective-permute-start(bf16[80,16,128]{2,1,0:T(8,128)(2,1)} %letter.1.rest_0_), channel_id=1, source_target_pairs={{0,1},{1,2},{2,3},{3,4},{4,5},{5,6},{6,7},{7,0},{8,9},{9,10},{10,1... | collective-permute-start | bytes 983048 | tf_op jit(solution)/shard_map/ppermute | solution.py:264
  45.3 34.5 %all-to-all-start.1 = ((bf16[32,8,16,128]{3,2,1,0:T(8,128)(2,1)}), bf16[32,8,16,128]{3,2,1,0:T(8,128)(2,1)}, u32[]{:S(2)}, u32[]{:S(2)}) async-start(bf16[32,8,16,128]{3,2,1,0:T(8,128)(2,1)} %pick.1), calls=%async_computation.1 | async-start | bytes 2097152 | tf_op jit(solution)/shard_map/all_to_all | solution.py:453
  52.7 11.8 %collective-permute-start.5 = (bf16[80,16,128]{2,1,0:T(8,128)(2,1)S(1)}, bf16[80,16,128]{2,1,0:T(8,128)(2,1)S(1)}, u32[]{:S(2)}, u32[]{:S(2)}) collective-permute-start(bf16[80,16,128]{2,1,0:T(8,128)(2,1)S(1)} %collective-permute-done.3.rest_4_), channel_id=1, source_target_pairs={{0,7},{1,0},{2,1},{3,2},{4,3},{5,4},{6,5},{7,6},{8,15},{9,8},{10,9... | collective-permute-start | bytes 983048 | tf_op jit(solution)/shard_map/ppermute | solution.py:265
  57.3 11.1 %collective-permute-start.4 = (bf16[80,16,128]{2,1,0:T(8,128)(2,1)}, bf16[80,16,128]{2,1,0:T(8,128)(2,1)S(1)}, u32[]{:S(2)}, u32[]{:S(2)}) collective-permute-start(bf16[80,16,128]{2,1,0:T(8,128)(2,1)} %collective-permute-done.1.rest_3_), channel_id=1, source_target_pairs={{0,1},{1,2},{2,3},{3,4},{4,5},{5,6},{6,7},{7,0},{8,9},{9,10},{10,1... | collective-permute-start | bytes 983048 | tf_op jit(solution)/shard_map/ppermute | solution.py:264
  64.6 10.0 %collective-permute-start.7 = (bf16[48,16,128]{2,1,0:T(8,128)(2,1)S(1)}, bf16[48,16,128]{2,1,0:T(8,128)(2,1)S(1)}, u32[]{:S(2)}, u32[]{:S(2)}) collective-permute-start(bf16[48,16,128]{2,1,0:T(8,128)(2,1)S(1)} %slice.55), channel_id=1, source_target_pairs={{0,7},{1,0},{2,1},{3,2},{4,3},{5,4},{6,5},{7,6},{8,15},{9,8},{10,9... | collective-permute-start | bytes 589832 | tf_op jit(solution)/shard_map/ppermute | solution.py:269
  81.3 12.9 %collective-permute-start.13 = (bf16[4,8,4,16,128]{4,3,2,1,0:T(8,128)(2,1)S(1)}, bf16[4,8,4,16,128]{4,3,2,1,0:T(8,128)(2,1)}, u32[]{:S(2)}, u32[]{:S(2)}) collective-permute-start(bf16[4,8,4,16,128]{4,3,2,1,0:T(8,128)(2,1)S(1)} %get-tuple-element.69.rest_0_), channel_id=1, source_target_pairs={{0,7},{1,0},{2,1},{3,2},{4,3},{5,4},{6,5},{7,6},{8,15},{9,8},{10,9... | collective-permute-start | bytes 1572872 | tf_op jit(solution)/shard_map/ppermute | solution.py:296
  83.2 14.2 %collective-permute-start.12 = (bf16[4,8,4,16,128]{4,3,2,1,0:T(8,128)(2,1)S(1)}, bf16[4,8,4,16,128]{4,3,2,1,0:T(8,128)(2,1)}, u32[]{:S(2)}, u32[]{:S(2)}) collective-permute-start(bf16[4,8,4,16,128]{4,3,2,1,0:T(8,128)(2,1)S(1)} %get-tuple-element.69.rest_0_), channel_id=1, source_target_pairs={{0,1},{1,2},{2,3},{3,4},{4,5},{5,6},{6,7},{7,0},{8,9},{9,10},{10,1... | collective-permute-start | bytes 1572872 | tf_op jit(solution)/shard_map/ppermute | solution.py:295
  83.4 60.6 %all-to-all-start.2 = ((bf16[32,16,16,128]{3,2,1,0:T(8,128)(2,1)}), bf16[32,16,16,128]{3,2,1,0:T(8,128)(2,1)S(1)}, u32[]{:S(2)}, u32[]{:S(2)}) async-start(bf16[32,16,16,128]{3,2,1,0:T(8,128)(2,1)} %copy-done.2), calls=%async_computation.2 | async-start | bytes 4194304 | tf_op jit(solution)/shard_map/all_to_all | solution.py:462
  90.9 15.6 %collective-permute-start.10 = (bf16[4,8,4,16,128]{4,3,2,1,0:T(8,128)(2,1)S(1)}, bf16[4,8,4,16,128]{4,3,2,1,0:T(8,128)(2,1)S(1)}, u32[]{:S(2)}, u32[]{:S(2)}) collective-permute-start(bf16[4,8,4,16,128]{4,3,2,1,0:T(8,128)(2,1)S(1)} %get-tuple-element.70.rest_0_), channel_id=1, source_target_pairs={{0,7},{1,0},{2,1},{3,2},{4,3},{5,4},{6,5},{7,6},{8,15},{9,8},{10,9... | collective-permute-start | bytes 1572872 | tf_op jit(solution)/shard_map/ppermute | solution.py:296
  94.2 16.0 %collective-permute-start.8 = (bf16[4,8,4,16,128]{4,3,2,1,0:T(8,128)(2,1)S(1)}, bf16[4,8,4,16,128]{4,3,2,1,0:T(8,128)(2,1)S(1)}, u32[]{:S(2)}, u32[]{:S(2)}) collective-permute-start(bf16[4,8,4,16,128]{4,3,2,1,0:T(8,128)(2,1)S(1)} %get-tuple-element.70.rest_0_), channel_id=1, source_target_pairs={{0,1},{1,2},{2,3},{3,4},{4,5},{5,6},{6,7},{7,0},{8,9},{9,10},{10,1... | collective-permute-start | bytes 1572872 | tf_op jit(solution)/shard_map/ppermute | solution.py:295
  94.2 23.6 %collective-permute-start.15 = (bf16[4,8,4,16,128]{4,3,2,1,0:T(8,128)(2,1)}, bf16[4,8,4,16,128]{4,3,2,1,0:T(8,128)(2,1)S(1)}, u32[]{:S(2)}, u32[]{:S(2)}) collective-permute-start(bf16[4,8,4,16,128]{4,3,2,1,0:T(8,128)(2,1)} %collective-permute-done.13.rest_2_), channel_id=1, source_target_pairs={{0,7},{1,0},{2,1},{3,2},{4,3},{5,4},{6,5},{7,6},{8,15},{9,8},{10,9... | collective-permute-start | bytes 1572872 | tf_op jit(solution)/shard_map/ppermute | solution.py:296
  97.4 24.0 %collective-permute-start.14 = (bf16[4,8,4,16,128]{4,3,2,1,0:T(8,128)(2,1)}, bf16[4,8,4,16,128]{4,3,2,1,0:T(8,128)(2,1)S(1)}, u32[]{:S(2)}, u32[]{:S(2)}) collective-permute-start(bf16[4,8,4,16,128]{4,3,2,1,0:T(8,128)(2,1)} %collective-permute-done.12.rest_1_), channel_id=1, source_target_pairs={{0,1},{1,2},{2,3},{3,4},{4,5},{5,6},{6,7},{7,0},{8,9},{9,10},{10,1... | collective-permute-start | bytes 1572872 | tf_op jit(solution)/shard_map/ppermute | solution.py:295
  106.4 22.5 %collective-permute-start.11 = (bf16[4,8,4,16,128]{4,3,2,1,0:T(8,128)(2,1)S(1)}, bf16[4,8,4,16,128]{4,3,2,1,0:T(8,128)(2,1)}, u32[]{:S(2)}, u32[]{:S(2)}) collective-permute-start(bf16[4,8,4,16,128]{4,3,2,1,0:T(8,128)(2,1)S(1)} %collective-permute-done.10.rest_2_), channel_id=1, source_target_pairs={{0,7},{1,0},{2,1},{3,2},{4,3},{5,4},{6,5},{7,6},{8,15},{9,8},{10,9... | collective-permute-start | bytes 1572872 | tf_op jit(solution)/shard_map/ppermute | solution.py:296
  110.2 22.6 %collective-permute-start.9 = (bf16[4,8,4,16,128]{4,3,2,1,0:T(8,128)(2,1)S(1)}, bf16[4,8,4,16,128]{4,3,2,1,0:T(8,128)(2,1)}, u32[]{:S(2)}, u32[]{:S(2)}) collective-permute-start(bf16[4,8,4,16,128]{4,3,2,1,0:T(8,128)(2,1)S(1)} %collective-permute-done.8.rest_1_), channel_id=1, source_target_pairs={{0,1},{1,2},{2,3},{3,4},{4,5},{5,6},{6,7},{7,0},{8,9},{9,10},{10,1... | collective-permute-start | bytes 1572872 | tf_op jit(solution)/shard_map/ppermute | solution.py:295
  117.8 24.0 %collective-permute-start.19 = (bf16[4,8,4,16,128]{4,3,2,1,0:T(8,128)(2,1)S(1)}, bf16[4,8,4,16,128]{4,3,2,1,0:T(8,128)(2,1)S(1)}, u32[]{:S(2)}, u32[]{:S(2)}) collective-permute-start(bf16[4,8,4,16,128]{4,3,2,1,0:T(8,128)(2,1)S(1)} %collective-permute-done.15.rest_4_), channel_id=1, source_target_pairs={{0,7},{1,0},{2,1},{3,2},{4,3},{5,4},{6,5},{7,6},{8,15},{9,8},{10,9... | collective-permute-start | bytes 1572872 | tf_op jit(solution)/shard_map/ppermute | solution.py:296
  121.4 22.6 %collective-permute-start.18 = (bf16[4,8,4,16,128]{4,3,2,1,0:T(8,128)(2,1)S(1)}, bf16[4,8,4,16,128]{4,3,2,1,0:T(8,128)(2,1)}, u32[]{:S(2)}, u32[]{:S(2)}) collective-permute-start(bf16[4,8,4,16,128]{4,3,2,1,0:T(8,128)(2,1)S(1)} %collective-permute-done.14.rest_3_), channel_id=1, source_target_pairs={{0,1},{1,2},{2,3},{3,4},{4,5},{5,6},{6,7},{7,0},{8,9},{9,10},{10,1... | collective-permute-start | bytes 1572872 | tf_op jit(solution)/shard_map/ppermute | solution.py:295
  132.7 22.4 %collective-permute-start.16 = (bf16[4,8,4,16,128]{4,3,2,1,0:T(8,128)(2,1)}, bf16[4,8,4,16,128]{4,3,2,1,0:T(8,128)(2,1)S(1)}, u32[]{:S(2)}, u32[]{:S(2)}) collective-permute-start(bf16[4,8,4,16,128]{4,3,2,1,0:T(8,128)(2,1)} %collective-permute-done.9.rest_3_), channel_id=1, source_target_pairs={{0,1},{1,2},{2,3},{3,4},{4,5},{5,6},{6,7},{7,0},{8,9},{9,10},{10,1... | collective-permute-start | bytes 1572872 | tf_op jit(solution)/shard_map/ppermute | solution.py:295
  132.7 22.4 %collective-permute-start.17 = (bf16[4,8,4,16,128]{4,3,2,1,0:T(8,128)(2,1)}, bf16[4,8,4,16,128]{4,3,2,1,0:T(8,128)(2,1)}, u32[]{:S(2)}, u32[]{:S(2)}) collective-permute-start(bf16[4,8,4,16,128]{4,3,2,1,0:T(8,128)(2,1)} %collective-permute-done.11.rest_4_), channel_id=1, source_target_pairs={{0,7},{1,0},{2,1},{3,2},{4,3},{5,4},{6,5},{7,6},{8,15},{9,8},{10,9... | collective-permute-start | bytes 1572872 | tf_op jit(solution)/shard_map/ppermute | solution.py:296
  145.9 17.8 %collective-permute-start.20 = (bf16[2,8,4,16,128]{4,3,2,1,0:T(8,128)(2,1)S(1)}, bf16[2,8,4,16,128]{4,3,2,1,0:T(8,128)(2,1)S(1)}, u32[]{:S(2)}, u32[]{:S(2)}) collective-permute-start(bf16[2,8,4,16,128]{4,3,2,1,0:T(8,128)(2,1)S(1)} %slice.46), channel_id=1, source_target_pairs={{0,1},{1,2},{2,3},{3,4},{4,5},{5,6},{6,7},{7,0},{8,9},{9,10},{10,1... | collective-permute-start | bytes 786440 | tf_op jit(solution)/shard_map/ppermute | solution.py:295
  146.0 17.7 %collective-permute-start.21 = (bf16[2,8,4,16,128]{4,3,2,1,0:T(8,128)(2,1)S(1)}, bf16[2,8,4,16,128]{4,3,2,1,0:T(8,128)(2,1)S(1)}, u32[]{:S(2)}, u32[]{:S(2)}) collective-permute-start(bf16[2,8,4,16,128]{4,3,2,1,0:T(8,128)(2,1)S(1)} %slice.47), channel_id=1, source_target_pairs={{0,7},{1,0},{2,1},{3,2},{4,3},{5,4},{6,5},{7,6},{8,15},{9,8},{10,9... | collective-permute-start | bytes 786440 | tf_op jit(solution)/shard_map/ppermute | solution.py:296
  156.1 12.4 %collective-permute-start.24 = (bf16[2,8,4,16,128]{4,3,2,1,0:T(8,128)(2,1)S(1)}, bf16[2,8,4,16,128]{4,3,2,1,0:T(8,128)(2,1)S(1)}, u32[]{:S(2)}, u32[]{:S(2)}) collective-permute-start(bf16[2,8,4,16,128]{4,3,2,1,0:T(8,128)(2,1)S(1)} %slice.49), channel_id=1, source_target_pairs={{0,7},{1,0},{2,1},{3,2},{4,3},{5,4},{6,5},{7,6},{8,15},{9,8},{10,9... | collective-permute-start | bytes 786440 | tf_op jit(solution)/shard_map/ppermute | solution.py:296
  156.5 12.0 %collective-permute-start.23 = (bf16[2,8,4,16,128]{4,3,2,1,0:T(8,128)(2,1)S(1)}, bf16[2,8,4,16,128]{4,3,2,1,0:T(8,128)(2,1)S(1)}, u32[]{:S(2)}, u32[]{:S(2)}) collective-permute-start(bf16[2,8,4,16,128]{4,3,2,1,0:T(8,128)(2,1)S(1)} %slice.48), channel_id=1, source_target_pairs={{0,1},{1,2},{2,3},{3,4},{4,5},{5,6},{6,7},{7,0},{8,9},{9,10},{10,1... | collective-permute-start | bytes 786440 | tf_op jit(solution)/shard_map/ppermute | solution.py:295
  (33 other events, 210.9 us)

commit v13 on v12

--- a/solution.py
+++ b/solution.py
@@ -289,8 +289,8 @@
             if (step, s) == (last - 1, 1):
                 held = lax.optimization_barrier((from_left, from_right, first_parts[0]))
                 from_left, from_right, _ = held
-            if (step, s) == (last, 0):
-                held = lax.optimization_barrier((from_left, from_right, first_parts[1]))
+            if step == last:
+                held = lax.optimization_barrier((from_left, from_right, first_parts[1 + s]))
                 from_left, from_right, _ = held
             go_right[s] = lax.ppermute(from_left, "tensor", right)
             go_left[s] = lax.ppermute(from_right, "tensor", left)
@@ -299,7 +299,7 @@
             if step in (last - 2, last) or (step, s) == (last - 1, 0):
                 state = gather_step(blocks[s], places[s], where, weights, states[s], step == last)
                 blocks[s], places[s], states[s] = [], [], state
-                if step == last - 2:
+                if step < last:
                     first_parts.append(state)
     return states, beside
 
@@ -317,33 +317,29 @@
     )
 
 
-def attend_kernel(first, with_prev, span_len, count_ref, q_ref, *rest):
-    out_ref = rest[-1]
-    pair_refs, prev_ref, done = rest[:-1], None, 0
-    if with_prev:
-        pair_refs, (prev_ref, before_ref) = rest[:-3], rest[-3:-1]
-        done = before_ref.shape[0]
-        out_ref[:done, :] = before_ref[...]
+def attend_kernel(span_len, count_ref, q_ref, prev_ref, *rest):
+    pair_refs, out_ref = rest[:-1], rest[-1]
     cols = out_ref.shape[1]
     heads = cols // HS
     spans = len(pair_refs)
-    keys = pair_refs[0].shape[0] * pair_refs[0].shape[1] * pair_refs[0].shape[2]
+    keys = prev_ref.shape[0] * prev_ref.shape[1] * prev_ref.shape[2]
     owner = (lax.broadcasted_iota(jnp.int32, (span_len, keys), 1) // PIECE_T) % NB
     row = lax.broadcasted_iota(jnp.int32, (span_len, keys), 0)
     for span in range(spans):
         pair = pair_refs[span][...].reshape(keys, 2 * cols)
-        queries = q_ref[(first + span) * span_len : (first + span + 1) * span_len, :]
+        rows = slice(span * span_len, (span + 1) * span_len)
+        queries = q_ref[rows, :]
         mixed_heads = []
         for head in range(heads):
             at = slice(head * HS, (head + 1) * HS)
             value_at = slice(cols + head * HS, cols + (head + 1) * HS)
             query = queries[:, at]
             scores = scores_of(query, pair[:, at])
-            if with_prev and span == spans - 1:
+            if span == spans - 1:
                 prev = prev_ref[...].reshape(keys, 2 * cols)
                 own = row == 0
                 scores = jnp.where(own, scores, scores_of(query, prev[:, at]))
-                count = jnp.where(own, count_ref[first + span], count_ref[first + span + 1])
+                count = jnp.where(own, count_ref[span], count_ref[span + 1])
                 weights = weigh(scores, count, owner)
                 ours = jnp.where(own, weights, 0.0).astype(jnp.bfloat16)
                 theirs = jnp.where(own, 0.0, weights).astype(jnp.bfloat16)
@@ -351,34 +347,29 @@
                     ours, pair[:, value_at], preferred_element_type=jnp.float32
                 ) + jnp.dot(theirs, prev[:, value_at], preferred_element_type=jnp.float32)
             else:
-                weights = weigh(scores, count_ref[first + span], owner).astype(jnp.bfloat16)
+                weights = weigh(scores, count_ref[span], owner).astype(jnp.bfloat16)
                 result = jnp.dot(
                     weights, pair[:, value_at], preferred_element_type=jnp.float32
                 )
             mixed_heads.append(result.astype(jnp.bfloat16))
-        rows = slice(done + span * span_len, done + (span + 1) * span_len)
         out_ref[rows, :] = jnp.concatenate(mixed_heads, axis=1)
 
 
-def attend(counts, queries, pairs, first, span_len, prev=None, before=None):
+def attend(counts, queries, pairs, prev, span_len):
     cols = queries.shape[1]
-    with_prev = prev is not None
-    rows = len(pairs) * span_len + (before.shape[0] if with_prev else 0)
-    operands = [counts, queries, *pairs] + ([prev, before] if with_prev else [])
-    vmem = pl.BlockSpec(memory_space=pltpu.VMEM)
-    return pl.pallas_call(
-        functools.partial(attend_kernel, first, with_prev, span_len),
-        in_specs=[pl.BlockSpec(memory_space=pltpu.SMEM)] + [vmem] * (len(operands) - 1),
+    rows = len(pairs) * span_len
+    vmem = pl.BlockSpec(memory_space=pltpu.VMEM)
+    return pl.pallas_call(
+        functools.partial(attend_kernel, span_len),
+        in_specs=[pl.BlockSpec(memory_space=pltpu.SMEM)] + [vmem] * (2 + len(pairs)),
         out_specs=vmem,
         out_shape=jax.ShapeDtypeStruct((rows, cols), jnp.bfloat16),
         compiler_params=pltpu.CompilerParams(vmem_limit_bytes=VMEM_LIMIT),
         cost_estimate=pl.CostEstimate(
-            flops=32 * len(pairs) * span_len * 256 * cols,
-            bytes_accessed=4 * rows * cols,
-            transcendentals=0,
+            flops=32 * rows * 256 * cols, bytes_accessed=4 * rows * cols, transcendentals=0
         ),
-        name="attend_prev" if with_prev else "attend",
-    )(*operands)
+        name="attend",
+    )(counts, queries, prev, *pairs)
 
 
 def finish_kernel(shift, where_ref, mail_ref, tokens_ref, *rest):
@@ -466,8 +457,7 @@
     streams = [rows[:, :, items // 2 :], rows[:, :, : items // 2]]
     (late, early), mail = ring_project(streams, where, both, n_ten, mail)
     prev = lax.ppermute(late[-1], "seq", [(i, i + 1) for i in range(n_seq - 1)])
-    attended = attend(counts, queries, early, 0, span_len)
-    attended = attend(counts, queries, late, span_dev // 2, span_len, prev, attended)
+    attended = attend(counts, queries, [*early, *late], prev, span_len)
     gathered = ring_gather(attended, n_ten, tok_dev // 2)
     return finish(where, mail, tokens, gathered, shift)
 

time: 207 us -> 207 us (level)
  local copies, waits for them, and re-layouts: 17.2 us -> 20.2 us
  starting transfers between devices: 78.7 us -> 76.1 us
    ppermute x6, starting transfers between devices: 21.3 us -> 15.4 us  [ring_gather(): go_left = lax.ppermute(go_left, 'tensor', left)]
    ppermute x8, waiting for transfers between devices: 11.2 us -> 7.24 us  [ring_project(): go_right[s] = lax.ppermute(from_left, 'tensor', right)]
    ppermute x6, starting transfers between devices: 0.74 us -> 3.85 us  [ring_gather(): go_right = lax.ppermute(go_right, 'tensor', right)]
    ppermute x8, starting transfers between devices: 22.5 us -> 25 us  [ring_project(): go_left[s] = lax.ppermute(from_right, 'tensor', left)]
    unnamed x42 -> x44, local copies, waits for them, and re-layouts: 12.1 us -> 13.8 us
  transfers between devices with their start and end apart: 36 -> 36, of which waited for: 18 -> 21; matrix products, arithmetic and copies ran while one was open for 4% -> 5% of each run, Pallas kernels for 12% -> 11%
where the time goes in v13:
time: 207 us; the launch traced here: 206 us
  starting transfers between devices  76.1 us (37%)
  waiting for transfers between devices  74 us (36%)
  Pallas kernels  30.3 us (15%)
  local copies, waits for them, and re-layouts  20.2 us (10%)
  other arithmetic  4.96 us (2%)
    ppermute x6, waiting for transfers between devices, ring_gather(): go_left = lax.ppermute(go_left, 'tensor', left)  31.6 us
    ppermute x8, starting transfers between devices, ring_project(): go_left[s] = lax.ppermute(from_right, 'tensor', left)  25 us
    ppermute x8, waiting for transfers between devices, ring_project(): go_left[s] = lax.ppermute(from_right, 'tensor', left)  19.1 us
    pallas_call x5, Pallas kernels, gather_step(): pl.pallas_call(functools.partial(gather_kernel, tuple(places), not state,...  17 us
    ppermute x6, starting transfers between devices, ring_gather(): go_left = lax.ppermute(go_left, 'tensor', left)  15.4 us
    unnamed x44, local copies, waits for them, and re-layouts  13.8 us
    all_to_all x1, starting transfers between devices, body(): lax.all_to_all(pieces, 'seq', split_axis=0, concat_axis=0, tiled=True)  7.54 us
    all_to_all x1, starting transfers between devices, body(): mail = lax.all_to_all(strip, 'seq', split_axis=0, concat_axis=0, tiled=True)  7.45 us
  transfers between devices with their start and end apart: 36, of which 21 were waited for; matrix products, arithmetic and copies ran while one was open for 5% of the time, Pallas kernels for 11%

profile of v13, /device:TPU:8, one launch (start us, length us, event | category | flops | bytes accessed | tf_op | source)
XLA Modules:
  0.0 206.5 jit_solution(1059582355693997256)
XLA Ops:
  5.3 7.5 %all-to-all-start = ((bf16[32,17,16,128]{3,2,1,0:T(8,128)(2,1)}), bf16[32,17,16,128]{3,2,1,0:T(8,128)(2,1)S(1)}, u32[]{:S(2)}, u32[]{:S(2)}) async-start(bf16[32,17,16,128]{3,2,1,0:T(8,128)(2,1)} %copy-done), calls=%async_computation | async-start | bytes 4456448 | tf_op jit(solution)/shard_map/all_to_all | solution.py:427
  16.0 5.9 %collective-permute-start.2 = (bf16[80,16,128]{2,1,0:T(8,128)(2,1)}, bf16[80,16,128]{2,1,0:T(8,128)(2,1)S(1)}, u32[]{:S(2)}, u32[]{:S(2)}) collective-permute-start(bf16[80,16,128]{2,1,0:T(8,128)(2,1)} %letter.1.rest_0_), channel_id=1, source_target_pairs={{0,7},{1,0},{2,1},{3,2},{4,3},{5,4},{6,5},{7,6},{8,15},{9,8},{10,9... | collective-permute-start | bytes 983048 | tf_op jit(solution)/shard_map/ppermute | solution.py:265
  21.9 7.6 %collective-permute-done.2.rest_2_ = bf16[80,16,128]{2,1,0:T(8,128)(2,1)S(1)} collective-permute-done((bf16[80,16,128]{2,1,0:T(8,128)(2,1)}, bf16[80,16,128]{2,1,0:T(8,128)(2,1)S(1)}, u32[]{:S(2)}, u32[]{:S(2)}) %collective-permute-start.2) | collective-permute-done | bytes 327712 | tf_op jit(solution)/shard_map/ppermute | solution.py:265
  29.5 3.6 %collective-permute-start.3 = (bf16[80,16,128]{2,1,0:T(8,128)(2,1)S(1)}, bf16[80,16,128]{2,1,0:T(8,128)(2,1)S(1)}, u32[]{:S(2)}, u32[]{:S(2)}) collective-permute-start(bf16[80,16,128]{2,1,0:T(8,128)(2,1)S(1)} %collective-permute-done.2.rest_2_), channel_id=1, source_target_pairs={{0,7},{1,0},{2,1},{3,2},{4,3},{5,4},{6,5},{7,6},{8,15},{9,8},{10,9... | collective-permute-start | bytes 983048 | tf_op jit(solution)/shard_map/ppermute | solution.py:265
  33.0 6.4 %collective-permute-done.3.rest_4_ = bf16[80,16,128]{2,1,0:T(8,128)(2,1)S(1)} collective-permute-done((bf16[80,16,128]{2,1,0:T(8,128)(2,1)S(1)}, bf16[80,16,128]{2,1,0:T(8,128)(2,1)S(1)}, u32[]{:S(2)}, u32[]{:S(2)}) %collective-permute-start.3) | collective-permute-done | bytes 327712 | tf_op jit(solution)/shard_map/ppermute | solution.py:265
  39.5 3.5 %collective-permute-done.1.rest_3_ = bf16[80,16,128]{2,1,0:T(8,128)(2,1)} collective-permute-done((bf16[80,16,128]{2,1,0:T(8,128)(2,1)S(1)}, bf16[80,16,128]{2,1,0:T(8,128)(2,1)}, u32[]{:S(2)}, u32[]{:S(2)}) %collective-permute-start.1) | collective-permute-done | bytes 327712 | tf_op jit(solution)/shard_map/ppermute | solution.py:264
  45.3 7.4 %all-to-all-start.1 = ((bf16[32,8,16,128]{3,2,1,0:T(8,128)(2,1)}), bf16[32,8,16,128]{3,2,1,0:T(8,128)(2,1)S(1)}, u32[]{:S(2)}, u32[]{:S(2)}) async-start(bf16[32,8,16,128]{3,2,1,0:T(8,128)(2,1)} %pick.1), calls=%async_computation.1 | async-start | bytes 2097152 | tf_op jit(solution)/shard_map/all_to_all | solution.py:444
  52.7 3.8 %collective-permute-start.5 = (bf16[80,16,128]{2,1,0:T(8,128)(2,1)S(1)}, bf16[80,16,128]{2,1,0:T(8,128)(2,1)S(1)}, u32[]{:S(2)}, u32[]{:S(2)}) collective-permute-start(bf16[80,16,128]{2,1,0:T(8,128)(2,1)S(1)} %collective-permute-done.3.rest_4_), channel_id=1, source_target_pairs={{0,7},{1,0},{2,1},{3,2},{4,3},{5,4},{6,5},{7,6},{8,15},{9,8},{10,9... | collective-permute-start | bytes 983048 | tf_op jit(solution)/shard_map/ppermute | solution.py:265
  56.5 7.2 %collective-permute-done.5.rest_6_ = bf16[80,16,128]{2,1,0:T(8,128)(2,1)S(1)} collective-permute-done((bf16[80,16,128]{2,1,0:T(8,128)(2,1)S(1)}, bf16[80,16,128]{2,1,0:T(8,128)(2,1)S(1)}, u32[]{:S(2)}, u32[]{:S(2)}) %collective-permute-start.5) | collective-permute-done | bytes 327712 | tf_op jit(solution)/shard_map/ppermute | solution.py:265
  64.5 3.7 %collective-permute-start.7 = (bf16[48,16,128]{2,1,0:T(8,128)(2,1)}, bf16[48,16,128]{2,1,0:T(8,128)(2,1)S(1)}, u32[]{:S(2)}, u32[]{:S(2)}) collective-permute-start(bf16[48,16,128]{2,1,0:T(8,128)(2,1)} %slice.55), channel_id=1, source_target_pairs={{0,7},{1,0},{2,1},{3,2},{4,3},{5,4},{6,5},{7,6},{8,15},{9,8},{10,9... | collective-permute-start | bytes 589832 | tf_op jit(solution)/shard_map/ppermute | solution.py:269
  68.9 4.1 %multiply_convert_fusion.w_ref = bf16[8,512,512]{2,1,0:T(8,128)(2,1)} fusion(bf16[8,512,256]{2,1,0:T(8,128)(2,1)} %bitcast.21, bf16[8,512,256]{2,1,0:T(8,128)(2,1)} %bitcast.22, f32[8,512]{1,0:T(8,128)S(1)} %reshape.37), kind=kLoop, calls=%fused_computation | loop fusion | flops 12582912 | bytes 8404992 | tf_op jit(solution)/shard_map/convert_element_type | solution.py:447
  85.7 7.4 %all-to-all-start.2 = ((bf16[32,16,16,128]{3,2,1,0:T(8,128)(2,1)}), bf16[32,16,16,128]{3,2,1,0:T(8,128)(2,1)S(1)}, u32[]{:S(2)}, u32[]{:S(2)}) async-start(bf16[32,16,16,128]{3,2,1,0:T(8,128)(2,1)} %copy-done.2), calls=%async_computation.2 | async-start | bytes 4194304 | tf_op jit(solution)/shard_map/all_to_all | solution.py:453
  99.5 9.0 %collective-permute-done.10.rest_2_ = bf16[4,8,4,16,128]{4,3,2,1,0:T(8,128)(2,1)S(1)} collective-permute-done((bf16[4,8,4,16,128]{4,3,2,1,0:T(8,128)(2,1)S(1)}, bf16[4,8,4,16,128]{4,3,2,1,0:T(8,128)(2,1)S(1)}, u32[]{:S(2)}, u32[]{:S(2)}) %collective-permute-start.10) | collective-permute-done | bytes 524320 | tf_op jit(solution)/shard_map/ppermute | solution.py:296
  108.5 3.7 %collective-permute-start.11 = (bf16[4,8,4,16,128]{4,3,2,1,0:T(8,128)(2,1)S(1)}, bf16[4,8,4,16,128]{4,3,2,1,0:T(8,128)(2,1)}, u32[]{:S(2)}, u32[]{:S(2)}) collective-permute-start(bf16[4,8,4,16,128]{4,3,2,1,0:T(8,128)(2,1)S(1)} %collective-permute-done.10.rest_2_), channel_id=1, source_target_pairs={{0,7},{1,0},{2,1},{3,2},{4,3},{5,4},{6,5},{7,6},{8,15},{9,8},{10,9... | collective-permute-start | bytes 1572872 | tf_op jit(solution)/shard_map/ppermute | solution.py:296
  112.2 7.6 %collective-permute-done.15.rest_4_ = bf16[4,8,4,16,128]{4,3,2,1,0:T(8,128)(2,1)S(1)} collective-permute-done((bf16[4,8,4,16,128]{4,3,2,1,0:T(8,128)(2,1)}, bf16[4,8,4,16,128]{4,3,2,1,0:T(8,128)(2,1)S(1)}, u32[]{:S(2)}, u32[]{:S(2)}) %collective-permute-start.15) | collective-permute-done | bytes 524320 | tf_op jit(solution)/shard_map/ppermute | solution.py:296
  119.8 3.6 %collective-permute-start.19 = (bf16[4,8,4,16,128]{4,3,2,1,0:T(8,128)(2,1)S(1)}, bf16[4,8,4,16,128]{4,3,2,1,0:T(8,128)(2,1)S(1)}, u32[]{:S(2)}, u32[]{:S(2)}) collective-permute-start(bf16[4,8,4,16,128]{4,3,2,1,0:T(8,128)(2,1)S(1)} %collective-permute-done.15.rest_4_), channel_id=1, source_target_pairs={{0,7},{1,0},{2,1},{3,2},{4,3},{5,4},{6,5},{7,6},{8,15},{9,8},{10,9... | collective-permute-start | bytes 1572872 | tf_op jit(solution)/shard_map/ppermute | solution.py:296
  123.5 4.0 %gather_step.3 = (f32[512,512]{1,0:T(8,128)S(1)}, f32[512,128]{1,0:T(8,128)S(1)}) custom-call(s32[8]{0:T(128)S(1)} %and_select_fusion.where_ref, bf16[8,512,512]{2,1,0:T(8,128)(2,1)} %multiply_convert_fusion.w_ref, bf16[4,8,4,16,128]{4,3,2,1,0:T(8,128)(2,1)S(1)} %get-tuple-element.73.rest_0_, bf16[4,8,4,16,128]{4,3,2,1,0:T(8,128)(2,1)} %collective-permute-done.12.rest_1_, ...), custom_call_target="tpu_custom_call" | custom-call | flops 5368709120 | bytes 4718592 | tf_op jit(solution)/shard_map/gather_step/pallas_call | solution.py:237
  131.0 3.8 %collective-permute-done.9.rest_3_ = bf16[4,8,4,16,128]{4,3,2,1,0:T(8,128)(2,1)} collective-permute-done((bf16[4,8,4,16,128]{4,3,2,1,0:T(8,128)(2,1)S(1)}, bf16[4,8,4,16,128]{4,3,2,1,0:T(8,128)(2,1)}, u32[]{:S(2)}, u32[]{:S(2)}) %collective-permute-start.9) | collective-permute-done | bytes 524320 | tf_op jit(solution)/shard_map/ppermute | solution.py:295
  138.0 4.0 %gather_step.4 = (f32[512,512]{1,0:T(8,128)S(1)}, f32[512,128]{1,0:T(8,128)S(1)}) custom-call(s32[8]{0:T(128)S(1)} %and_select_fusion.where_ref, bf16[8,512,512]{2,1,0:T(8,128)(2,1)} %multiply_convert_fusion.w_ref, bf16[4,8,4,16,128]{4,3,2,1,0:T(8,128)(2,1)S(1)} %get-tuple-element.74.rest_0_, bf16[4,8,4,16,128]{4,3,2,1,0:T(8,128)(2,1)S(1)} %collective-permute-done.8.rest_1_, ...), custom_call_target="tpu_custom_call" | custom-call | flops 5368709120 | bytes 4718592 | tf_op jit(solution)/shard_map/gather_step/pallas_call | solution.py:237
  167.5 3.3 %gather_last.3 = (bf16[8,2,16,512]{3,2,1,0:T(8,128)(2,1)S(1)}, bf16[8,2,16,512]{3,2,1,0:T(8,128)(2,1)S(1)}) custom-call(s32[8]{0:T(128)S(1)} %and_select_fusion.where_ref, bf16[8,512,512]{2,1,0:T(8,128)(2,1)} %multiply_convert_fusion.w_ref, bf16[4,8,4,16,128]{4,3,2,1,0:T(8,128)(2,1)S(1)} %collective-permute-done.16.rest_0_, ...), custom_call_target="tpu_custom_call" | custom-call | flops 3221225472 | bytes 3670016 | tf_op jit(solution)/shard_map/gather_last/pallas_call | solution.py:237
  170.9 4.5 %collective-permute-done.22.prev_ref = bf16[8,2,16,512]{3,2,1,0:T(8,128)(2,1)S(1)} collective-permute-done((bf16[8,2,16,512]{3,2,1,0:T(8,128)(2,1)S(1)}, bf16[8,2,16,512]{3,2,1,0:T(8,128)(2,1)S(1)}, u32[]{:S(2)}, u32[]{:S(2)}) %collective-permute-start.22) | collective-permute-done | bytes 262176 | tf_op jit(solution)/shard_map/ppermute | solution.py:459
  180.7 4.3 %collective-permute-done.26.rest_2_ = bf16[256,256]{1,0:T(8,128)(2,1)S(1)} collective-permute-done((bf16[256,256]{1,0:T(8,128)(2,1)S(1)}, bf16[256,256]{1,0:T(8,128)(2,1)S(1)}, u32[]{:S(2)}, u32[]{:S(2)}) %collective-permute-start.26) | collective-permute-done | bytes 131104 | tf_op jit(solution)/shard_map/ppermute | solution.py:265
  187.0 3.4 %collective-permute-done.28.rest_4_ = bf16[256,256]{1,0:T(8,128)(2,1)S(1)} collective-permute-done((bf16[256,256]{1,0:T(8,128)(2,1)S(1)}, bf16[256,256]{1,0:T(8,128)(2,1)S(1)}, u32[]{:S(2)}, u32[]{:S(2)}) %collective-permute-start.28) | collective-permute-done | bytes 131104 | tf_op jit(solution)/shard_map/ppermute | solution.py:265
  200.5 3.9 %collective-permute-done.31.rest_7_ = bf16[128,256]{1,0:T(8,128)(2,1)S(1)} collective-permute-done((bf16[128,256]{1,0:T(8,128)(2,1)S(1)}, bf16[128,256]{1,0:T(8,128)(2,1)S(1)}, u32[]{:S(2)}, u32[]{:S(2)}) %collective-permute-start.31) | collective-permute-done | bytes 65568 | tf_op jit(solution)/shard_map/ppermute | solution.py:268
  (121 shorter events, 82.0 us)
Async XLA Ops:
  5.3 37.7 %all-to-all-start = ((bf16[32,17,16,128]{3,2,1,0:T(8,128)(2,1)}), bf16[32,17,16,128]{3,2,1,0:T(8,128)(2,1)S(1)}, u32[]{:S(2)}, u32[]{:S(2)}) async-start(bf16[32,17,16,128]{3,2,1,0:T(8,128)(2,1)} %copy-done), calls=%async_computation | async-start | bytes 4456448 | tf_op jit(solution)/shard_map/all_to_all | solution.py:427
  16.0 13.5 %collective-permute-start.2 = (bf16[80,16,128]{2,1,0:T(8,128)(2,1)}, bf16[80,16,128]{2,1,0:T(8,128)(2,1)S(1)}, u32[]{:S(2)}, u32[]{:S(2)}) collective-permute-start(bf16[80,16,128]{2,1,0:T(8,128)(2,1)} %letter.1.rest_0_), channel_id=1, source_target_pairs={{0,7},{1,0},{2,1},{3,2},{4,3},{5,4},{6,5},{7,6},{8,15},{9,8},{10,9... | collective-permute-start | bytes 983048 | tf_op jit(solution)/shard_map/ppermute | solution.py:265
  21.9 11.2 %collective-permute-start = (bf16[80,16,128]{2,1,0:T(8,128)(2,1)}, bf16[80,16,128]{2,1,0:T(8,128)(2,1)S(1)}, u32[]{:S(2)}, u32[]{:S(2)}) collective-permute-start(bf16[80,16,128]{2,1,0:T(8,128)(2,1)} %letter.1.rest_0_), channel_id=1, source_target_pairs={{0,1},{1,2},{2,3},{3,4},{4,5},{5,6},{6,7},{7,0},{8,9},{9,10},{10,1... | collective-permute-start | bytes 983048 | tf_op jit(solution)/shard_map/ppermute | solution.py:264
  29.5 10.0 %collective-permute-start.3 = (bf16[80,16,128]{2,1,0:T(8,128)(2,1)S(1)}, bf16[80,16,128]{2,1,0:T(8,128)(2,1)S(1)}, u32[]{:S(2)}, u32[]{:S(2)}) collective-permute-start(bf16[80,16,128]{2,1,0:T(8,128)(2,1)S(1)} %collective-permute-done.2.rest_2_), channel_id=1, source_target_pairs={{0,7},{1,0},{2,1},{3,2},{4,3},{5,4},{6,5},{7,6},{8,15},{9,8},{10,9... | collective-permute-start | bytes 983048 | tf_op jit(solution)/shard_map/ppermute | solution.py:265
  33.0 10.0 %collective-permute-start.1 = (bf16[80,16,128]{2,1,0:T(8,128)(2,1)S(1)}, bf16[80,16,128]{2,1,0:T(8,128)(2,1)}, u32[]{:S(2)}, u32[]{:S(2)}) collective-permute-start(bf16[80,16,128]{2,1,0:T(8,128)(2,1)S(1)} %collective-permute-done.rest_1_), channel_id=1, source_target_pairs={{0,1},{1,2},{2,3},{3,4},{4,5},{5,6},{6,7},{7,0},{8,9},{9,10},{10,1... | collective-permute-start | bytes 983048 | tf_op jit(solution)/shard_map/ppermute | solution.py:264
  45.3 35.8 %all-to-all-start.1 = ((bf16[32,8,16,128]{3,2,1,0:T(8,128)(2,1)}), bf16[32,8,16,128]{3,2,1,0:T(8,128)(2,1)S(1)}, u32[]{:S(2)}, u32[]{:S(2)}) async-start(bf16[32,8,16,128]{3,2,1,0:T(8,128)(2,1)} %pick.1), calls=%async_computation.1 | async-start | bytes 2097152 | tf_op jit(solution)/shard_map/all_to_all | solution.py:444
  52.7 11.1 %collective-permute-start.5 = (bf16[80,16,128]{2,1,0:T(8,128)(2,1)S(1)}, bf16[80,16,128]{2,1,0:T(8,128)(2,1)S(1)}, u32[]{:S(2)}, u32[]{:S(2)}) collective-permute-start(bf16[80,16,128]{2,1,0:T(8,128)(2,1)S(1)} %collective-permute-done.3.rest_4_), channel_id=1, source_target_pairs={{0,7},{1,0},{2,1},{3,2},{4,3},{5,4},{6,5},{7,6},{8,15},{9,8},{10,9... | collective-permute-start | bytes 983048 | tf_op jit(solution)/shard_map/ppermute | solution.py:265
  56.5 11.7 %collective-permute-start.4 = (bf16[80,16,128]{2,1,0:T(8,128)(2,1)}, bf16[80,16,128]{2,1,0:T(8,128)(2,1)S(1)}, u32[]{:S(2)}, u32[]{:S(2)}) collective-permute-start(bf16[80,16,128]{2,1,0:T(8,128)(2,1)} %collective-permute-done.1.rest_3_), channel_id=1, source_target_pairs={{0,1},{1,2},{2,3},{3,4},{4,5},{5,6},{6,7},{7,0},{8,9},{9,10},{10,1... | collective-permute-start | bytes 983048 | tf_op jit(solution)/shard_map/ppermute | solution.py:264
  64.5 10.8 %collective-permute-start.7 = (bf16[48,16,128]{2,1,0:T(8,128)(2,1)}, bf16[48,16,128]{2,1,0:T(8,128)(2,1)S(1)}, u32[]{:S(2)}, u32[]{:S(2)}) collective-permute-start(bf16[48,16,128]{2,1,0:T(8,128)(2,1)} %slice.55), channel_id=1, source_target_pairs={{0,7},{1,0},{2,1},{3,2},{4,3},{5,4},{6,5},{7,6},{8,15},{9,8},{10,9... | collective-permute-start | bytes 589832 | tf_op jit(solution)/shard_map/ppermute | solution.py:269
  83.6 12.6 %collective-permute-start.13 = (bf16[4,8,4,16,128]{4,3,2,1,0:T(8,128)(2,1)S(1)}, bf16[4,8,4,16,128]{4,3,2,1,0:T(8,128)(2,1)}, u32[]{:S(2)}, u32[]{:S(2)}) collective-permute-start(bf16[4,8,4,16,128]{4,3,2,1,0:T(8,128)(2,1)S(1)} %get-tuple-element.73.rest_0_), channel_id=1, source_target_pairs={{0,7},{1,0},{2,1},{3,2},{4,3},{5,4},{6,5},{7,6},{8,15},{9,8},{10,9... | collective-permute-start | bytes 1572872 | tf_op jit(solution)/shard_map/ppermute | solution.py:296
  85.3 14.2 %collective-permute-start.12 = (bf16[4,8,4,16,128]{4,3,2,1,0:T(8,128)(2,1)S(1)}, bf16[4,8,4,16,128]{4,3,2,1,0:T(8,128)(2,1)}, u32[]{:S(2)}, u32[]{:S(2)}) collective-permute-start(bf16[4,8,4,16,128]{4,3,2,1,0:T(8,128)(2,1)S(1)} %get-tuple-element.73.rest_0_), channel_id=1, source_target_pairs={{0,1},{1,2},{2,3},{3,4},{4,5},{5,6},{6,7},{7,0},{8,9},{9,10},{10,1... | collective-permute-start | bytes 1572872 | tf_op jit(solution)/shard_map/ppermute | solution.py:295
  85.7 60.4 %all-to-all-start.2 = ((bf16[32,16,16,128]{3,2,1,0:T(8,128)(2,1)}), bf16[32,16,16,128]{3,2,1,0:T(8,128)(2,1)S(1)}, u32[]{:S(2)}, u32[]{:S(2)}) async-start(bf16[32,16,16,128]{3,2,1,0:T(8,128)(2,1)} %copy-done.2), calls=%async_computation.2 | async-start | bytes 4194304 | tf_op jit(solution)/shard_map/all_to_all | solution.py:453
  93.1 15.4 %collective-permute-start.10 = (bf16[4,8,4,16,128]{4,3,2,1,0:T(8,128)(2,1)S(1)}, bf16[4,8,4,16,128]{4,3,2,1,0:T(8,128)(2,1)S(1)}, u32[]{:S(2)}, u32[]{:S(2)}) collective-permute-start(bf16[4,8,4,16,128]{4,3,2,1,0:T(8,128)(2,1)S(1)} %get-tuple-element.74.rest_0_), channel_id=1, source_target_pairs={{0,7},{1,0},{2,1},{3,2},{4,3},{5,4},{6,5},{7,6},{8,15},{9,8},{10,9... | collective-permute-start | bytes 1572872 | tf_op jit(solution)/shard_map/ppermute | solution.py:296
  96.2 16.0 %collective-permute-start.8 = (bf16[4,8,4,16,128]{4,3,2,1,0:T(8,128)(2,1)S(1)}, bf16[4,8,4,16,128]{4,3,2,1,0:T(8,128)(2,1)S(1)}, u32[]{:S(2)}, u32[]{:S(2)}) collective-permute-start(bf16[4,8,4,16,128]{4,3,2,1,0:T(8,128)(2,1)S(1)} %get-tuple-element.74.rest_0_), channel_id=1, source_target_pairs={{0,1},{1,2},{2,3},{3,4},{4,5},{5,6},{6,7},{7,0},{8,9},{9,10},{10,1... | collective-permute-start | bytes 1572872 | tf_op jit(solution)/shard_map/ppermute | solution.py:295
  96.2 23.6 %collective-permute-start.15 = (bf16[4,8,4,16,128]{4,3,2,1,0:T(8,128)(2,1)}, bf16[4,8,4,16,128]{4,3,2,1,0:T(8,128)(2,1)S(1)}, u32[]{:S(2)}, u32[]{:S(2)}) collective-permute-start(bf16[4,8,4,16,128]{4,3,2,1,0:T(8,128)(2,1)} %collective-permute-done.13.rest_2_), channel_id=1, source_target_pairs={{0,7},{1,0},{2,1},{3,2},{4,3},{5,4},{6,5},{7,6},{8,15},{9,8},{10,9... | collective-permute-start | bytes 1572872 | tf_op jit(solution)/shard_map/ppermute | solution.py:296
  99.5 24.0 %collective-permute-start.14 = (bf16[4,8,4,16,128]{4,3,2,1,0:T(8,128)(2,1)}, bf16[4,8,4,16,128]{4,3,2,1,0:T(8,128)(2,1)S(1)}, u32[]{:S(2)}, u32[]{:S(2)}) collective-permute-start(bf16[4,8,4,16,128]{4,3,2,1,0:T(8,128)(2,1)} %collective-permute-done.12.rest_1_), channel_id=1, source_target_pairs={{0,1},{1,2},{2,3},{3,4},{4,5},{5,6},{6,7},{7,0},{8,9},{9,10},{10,1... | collective-permute-start | bytes 1572872 | tf_op jit(solution)/shard_map/ppermute | solution.py:295
  108.5 22.5 %collective-permute-start.11 = (bf16[4,8,4,16,128]{4,3,2,1,0:T(8,128)(2,1)S(1)}, bf16[4,8,4,16,128]{4,3,2,1,0:T(8,128)(2,1)}, u32[]{:S(2)}, u32[]{:S(2)}) collective-permute-start(bf16[4,8,4,16,128]{4,3,2,1,0:T(8,128)(2,1)S(1)} %collective-permute-done.10.rest_2_), channel_id=1, source_target_pairs={{0,7},{1,0},{2,1},{3,2},{4,3},{5,4},{6,5},{7,6},{8,15},{9,8},{10,9... | collective-permute-start | bytes 1572872 | tf_op jit(solution)/shard_map/ppermute | solution.py:296
  112.2 22.6 %collective-permute-start.9 = (bf16[4,8,4,16,128]{4,3,2,1,0:T(8,128)(2,1)S(1)}, bf16[4,8,4,16,128]{4,3,2,1,0:T(8,128)(2,1)}, u32[]{:S(2)}, u32[]{:S(2)}) collective-permute-start(bf16[4,8,4,16,128]{4,3,2,1,0:T(8,128)(2,1)S(1)} %collective-permute-done.8.rest_1_), channel_id=1, source_target_pairs={{0,1},{1,2},{2,3},{3,4},{4,5},{5,6},{6,7},{7,0},{8,9},{9,10},{10,1... | collective-permute-start | bytes 1572872 | tf_op jit(solution)/shard_map/ppermute | solution.py:295
  119.8 23.9 %collective-permute-start.19 = (bf16[4,8,4,16,128]{4,3,2,1,0:T(8,128)(2,1)S(1)}, bf16[4,8,4,16,128]{4,3,2,1,0:T(8,128)(2,1)S(1)}, u32[]{:S(2)}, u32[]{:S(2)}) collective-permute-start(bf16[4,8,4,16,128]{4,3,2,1,0:T(8,128)(2,1)S(1)} %collective-permute-done.15.rest_4_), channel_id=1, source_target_pairs={{0,7},{1,0},{2,1},{3,2},{4,3},{5,4},{6,5},{7,6},{8,15},{9,8},{10,9... | collective-permute-start | bytes 1572872 | tf_op jit(solution)/shard_map/ppermute | solution.py:296
  123.5 22.6 %collective-permute-start.18 = (bf16[4,8,4,16,128]{4,3,2,1,0:T(8,128)(2,1)S(1)}, bf16[4,8,4,16,128]{4,3,2,1,0:T(8,128)(2,1)}, u32[]{:S(2)}, u32[]{:S(2)}) collective-permute-start(bf16[4,8,4,16,128]{4,3,2,1,0:T(8,128)(2,1)S(1)} %collective-permute-done.14.rest_3_), channel_id=1, source_target_pairs={{0,1},{1,2},{2,3},{3,4},{4,5},{5,6},{6,7},{7,0},{8,9},{9,10},{10,1... | collective-permute-start | bytes 1572872 | tf_op jit(solution)/shard_map/ppermute | solution.py:295
  134.8 22.4 %collective-permute-start.16 = (bf16[4,8,4,16,128]{4,3,2,1,0:T(8,128)(2,1)}, bf16[4,8,4,16,128]{4,3,2,1,0:T(8,128)(2,1)S(1)}, u32[]{:S(2)}, u32[]{:S(2)}) collective-permute-start(bf16[4,8,4,16,128]{4,3,2,1,0:T(8,128)(2,1)} %collective-permute-done.9.rest_3_), channel_id=1, source_target_pairs={{0,1},{1,2},{2,3},{3,4},{4,5},{5,6},{6,7},{7,0},{8,9},{9,10},{10,1... | collective-permute-start | bytes 1572872 | tf_op jit(solution)/shard_map/ppermute | solution.py:295
  134.8 22.4 %collective-permute-start.17 = (bf16[4,8,4,16,128]{4,3,2,1,0:T(8,128)(2,1)}, bf16[4,8,4,16,128]{4,3,2,1,0:T(8,128)(2,1)}, u32[]{:S(2)}, u32[]{:S(2)}) collective-permute-start(bf16[4,8,4,16,128]{4,3,2,1,0:T(8,128)(2,1)} %collective-permute-done.11.rest_4_), channel_id=1, source_target_pairs={{0,7},{1,0},{2,1},{3,2},{4,3},{5,4},{6,5},{7,6},{8,15},{9,8},{10,9... | collective-permute-start | bytes 1572872 | tf_op jit(solution)/shard_map/ppermute | solution.py:296
  148.0 14.8 %collective-permute-start.20 = (bf16[2,8,4,16,128]{4,3,2,1,0:T(8,128)(2,1)S(1)}, bf16[2,8,4,16,128]{4,3,2,1,0:T(8,128)(2,1)S(1)}, u32[]{:S(2)}, u32[]{:S(2)}) collective-permute-start(bf16[2,8,4,16,128]{4,3,2,1,0:T(8,128)(2,1)S(1)} %slice.46), channel_id=1, source_target_pairs={{0,1},{1,2},{2,3},{3,4},{4,5},{5,6},{6,7},{7,0},{8,9},{9,10},{10,1... | collective-permute-start | bytes 786440 | tf_op jit(solution)/shard_map/ppermute | solution.py:295
  148.1 14.7 %collective-permute-start.21 = (bf16[2,8,4,16,128]{4,3,2,1,0:T(8,128)(2,1)S(1)}, bf16[2,8,4,16,128]{4,3,2,1,0:T(8,128)(2,1)S(1)}, u32[]{:S(2)}, u32[]{:S(2)}) collective-permute-start(bf16[2,8,4,16,128]{4,3,2,1,0:T(8,128)(2,1)S(1)} %slice.47), channel_id=1, source_target_pairs={{0,7},{1,0},{2,1},{3,2},{4,3},{5,4},{6,5},{7,6},{8,15},{9,8},{10,9... | collective-permute-start | bytes 786440 | tf_op jit(solution)/shard_map/ppermute | solution.py:296
  (34 other events, 211.7 us)

commit v14 on v12

--- a/solution.py
+++ b/solution.py
@@ -289,8 +289,8 @@
             if (step, s) == (last - 1, 1):
                 held = lax.optimization_barrier((from_left, from_right, first_parts[0]))
                 from_left, from_right, _ = held
-            if (step, s) == (last, 0):
-                held = lax.optimization_barrier((from_left, from_right, first_parts[1]))
+            if step == last:
+                held = lax.optimization_barrier((from_left, from_right, first_parts[1 + s]))
                 from_left, from_right, _ = held
             go_right[s] = lax.ppermute(from_left, "tensor", right)
             go_left[s] = lax.ppermute(from_right, "tensor", left)
@@ -299,7 +299,7 @@
             if step in (last - 2, last) or (step, s) == (last - 1, 0):
                 state = gather_step(blocks[s], places[s], where, weights, states[s], step == last)
                 blocks[s], places[s], states[s] = [], [], state
-                if step == last - 2:
+                if step < last:
                     first_parts.append(state)
     return states, beside
 

time: 207 us -> 203 us (0.981)
  waiting for transfers between devices: 73.5 us -> 71.2 us
  starting transfers between devices: 78.7 us -> 76.6 us
    ppermute x6, starting transfers between devices: 21.3 us -> 17 us  [ring_gather(): go_left = lax.ppermute(go_left, 'tensor', left)]
    ppermute x8, waiting for transfers between devices: 11.2 us -> 7.24 us  [ring_project(): go_right[s] = lax.ppermute(from_left, 'tensor', right)]
    ppermute x8, starting transfers between devices: 22.5 us -> 25.4 us  [ring_project(): go_left[s] = lax.ppermute(from_right, 'tensor', left)]
    ppermute x6, starting transfers between devices: 0.74 us -> 2.99 us  [ring_gather(): go_right = lax.ppermute(go_right, 'tensor', right)]
  transfers between devices with their start and end apart: 36 -> 36, of which waited for: 18 -> 21; matrix products, arithmetic and copies ran while one was open for 4% -> 4% of each run, Pallas kernels for 12% -> 12%
where the time goes in v14:
time: 203 us; the launch traced here: 202 us
  starting transfers between devices  76.6 us (38%)
  waiting for transfers between devices  71.2 us (35%)
  Pallas kernels  31.1 us (15%)
  local copies, waits for them, and re-layouts  17.2 us (8%)
  other arithmetic  4.88 us (2%)
    ppermute x6, waiting for transfers between devices, ring_gather(): go_left = lax.ppermute(go_left, 'tensor', left)  31.4 us
    ppermute x8, starting transfers between devices, ring_project(): go_left[s] = lax.ppermute(from_right, 'tensor', left)  25.4 us
    ppermute x8, waiting for transfers between devices, ring_project(): go_left[s] = lax.ppermute(from_right, 'tensor', left)  19.1 us
    pallas_call x5, Pallas kernels, gather_step(): pl.pallas_call(functools.partial(gather_kernel, tuple(places), not state,...  17 us
    ppermute x6, starting transfers between devices, ring_gather(): go_left = lax.ppermute(go_left, 'tensor', left)  17 us
    unnamed x42, local copies, waits for them, and re-layouts  12.1 us
    all_to_all x1, starting transfers between devices, body(): lax.all_to_all(pieces, 'seq', split_axis=0, concat_axis=0, tiled=True)  7.54 us
    all_to_all x1, starting transfers between devices, body(): mail = lax.all_to_all(strip, 'seq', split_axis=0, concat_axis=0, tiled=True)  7.45 us
  transfers between devices with their start and end apart: 36, of which 21 were waited for; matrix products, arithmetic and copies ran while one was open for 4% of the time, Pallas kernels for 12%

profile of v14, /device:TPU:8, one launch (start us, length us, event | category | flops | bytes accessed | tf_op | source)
XLA Modules:
  0.0 202.0 jit_solution(15098387136597592734)
XLA Ops:
  5.4 7.5 %all-to-all-start = ((bf16[32,17,16,128]{3,2,1,0:T(8,128)(2,1)}), bf16[32,17,16,128]{3,2,1,0:T(8,128)(2,1)S(1)}, u32[]{:S(2)}, u32[]{:S(2)}) async-start(bf16[32,17,16,128]{3,2,1,0:T(8,128)(2,1)} %copy-done), calls=%async_computation | async-start | bytes 4456448 | tf_op jit(solution)/shard_map/all_to_all | solution.py:436
  15.9 5.9 %collective-permute-start.2 = (bf16[80,16,128]{2,1,0:T(8,128)(2,1)}, bf16[80,16,128]{2,1,0:T(8,128)(2,1)S(1)}, u32[]{:S(2)}, u32[]{:S(2)}) collective-permute-start(bf16[80,16,128]{2,1,0:T(8,128)(2,1)} %letter.1.rest_0_), channel_id=1, source_target_pairs={{0,7},{1,0},{2,1},{3,2},{4,3},{5,4},{6,5},{7,6},{8,15},{9,8},{10,9... | collective-permute-start | bytes 983048 | tf_op jit(solution)/shard_map/ppermute | solution.py:265
  21.8 7.6 %collective-permute-done.2.rest_2_ = bf16[80,16,128]{2,1,0:T(8,128)(2,1)S(1)} collective-permute-done((bf16[80,16,128]{2,1,0:T(8,128)(2,1)}, bf16[80,16,128]{2,1,0:T(8,128)(2,1)S(1)}, u32[]{:S(2)}, u32[]{:S(2)}) %collective-permute-start.2) | collective-permute-done | bytes 327712 | tf_op jit(solution)/shard_map/ppermute | solution.py:265
  29.4 3.6 %collective-permute-start.3 = (bf16[80,16,128]{2,1,0:T(8,128)(2,1)S(1)}, bf16[80,16,128]{2,1,0:T(8,128)(2,1)S(1)}, u32[]{:S(2)}, u32[]{:S(2)}) collective-permute-start(bf16[80,16,128]{2,1,0:T(8,128)(2,1)S(1)} %collective-permute-done.2.rest_2_), channel_id=1, source_target_pairs={{0,7},{1,0},{2,1},{3,2},{4,3},{5,4},{6,5},{7,6},{8,15},{9,8},{10,9... | collective-permute-start | bytes 983048 | tf_op jit(solution)/shard_map/ppermute | solution.py:265
  33.0 6.4 %collective-permute-done.3.rest_4_ = bf16[80,16,128]{2,1,0:T(8,128)(2,1)S(1)} collective-permute-done((bf16[80,16,128]{2,1,0:T(8,128)(2,1)S(1)}, bf16[80,16,128]{2,1,0:T(8,128)(2,1)S(1)}, u32[]{:S(2)}, u32[]{:S(2)}) %collective-permute-start.3) | collective-permute-done | bytes 327712 | tf_op jit(solution)/shard_map/ppermute | solution.py:265
  39.4 3.5 %collective-permute-done.1.rest_3_ = bf16[80,16,128]{2,1,0:T(8,128)(2,1)} collective-permute-done((bf16[80,16,128]{2,1,0:T(8,128)(2,1)S(1)}, bf16[80,16,128]{2,1,0:T(8,128)(2,1)}, u32[]{:S(2)}, u32[]{:S(2)}) %collective-permute-start.1) | collective-permute-done | bytes 327712 | tf_op jit(solution)/shard_map/ppermute | solution.py:264
  45.3 7.4 %all-to-all-start.1 = ((bf16[32,8,16,128]{3,2,1,0:T(8,128)(2,1)}), bf16[32,8,16,128]{3,2,1,0:T(8,128)(2,1)}, u32[]{:S(2)}, u32[]{:S(2)}) async-start(bf16[32,8,16,128]{3,2,1,0:T(8,128)(2,1)} %pick.1), calls=%async_computation.1 | async-start | bytes 2097152 | tf_op jit(solution)/shard_map/all_to_all | solution.py:453
  52.7 4.5 %collective-permute-start.5 = (bf16[80,16,128]{2,1,0:T(8,128)(2,1)S(1)}, bf16[80,16,128]{2,1,0:T(8,128)(2,1)S(1)}, u32[]{:S(2)}, u32[]{:S(2)}) collective-permute-start(bf16[80,16,128]{2,1,0:T(8,128)(2,1)S(1)} %collective-permute-done.3.rest_4_), channel_id=1, source_target_pairs={{0,7},{1,0},{2,1},{3,2},{4,3},{5,4},{6,5},{7,6},{8,15},{9,8},{10,9... | collective-permute-start | bytes 983048 | tf_op jit(solution)/shard_map/ppermute | solution.py:265
  57.3 7.2 %collective-permute-done.5.rest_6_ = bf16[80,16,128]{2,1,0:T(8,128)(2,1)S(1)} collective-permute-done((bf16[80,16,128]{2,1,0:T(8,128)(2,1)S(1)}, bf16[80,16,128]{2,1,0:T(8,128)(2,1)S(1)}, u32[]{:S(2)}, u32[]{:S(2)}) %collective-permute-start.5) | collective-permute-done | bytes 327712 | tf_op jit(solution)/shard_map/ppermute | solution.py:265
  64.6 3.8 %collective-permute-start.7 = (bf16[48,16,128]{2,1,0:T(8,128)(2,1)S(1)}, bf16[48,16,128]{2,1,0:T(8,128)(2,1)S(1)}, u32[]{:S(2)}, u32[]{:S(2)}) collective-permute-start(bf16[48,16,128]{2,1,0:T(8,128)(2,1)S(1)} %slice.55), channel_id=1, source_target_pairs={{0,7},{1,0},{2,1},{3,2},{4,3},{5,4},{6,5},{7,6},{8,15},{9,8},{10,9... | collective-permute-start | bytes 589832 | tf_op jit(solution)/shard_map/ppermute | solution.py:269
  68.5 4.1 %multiply_convert_fusion.w_ref = bf16[8,512,512]{2,1,0:T(8,128)(2,1)} fusion(bf16[8,512,256]{2,1,0:T(8,128)(2,1)} %bitcast.20, bf16[8,512,256]{2,1,0:T(8,128)(2,1)} %bitcast.21, f32[8,512]{1,0:T(8,128)S(1)} %reshape.37), kind=kLoop, calls=%fused_computation | loop fusion | flops 12582912 | bytes 8404992 | tf_op jit(solution)/shard_map/convert_element_type | solution.py:456
  83.4 7.5 %all-to-all-start.2 = ((bf16[32,16,16,128]{3,2,1,0:T(8,128)(2,1)}), bf16[32,16,16,128]{3,2,1,0:T(8,128)(2,1)S(1)}, u32[]{:S(2)}, u32[]{:S(2)}) async-start(bf16[32,16,16,128]{3,2,1,0:T(8,128)(2,1)} %copy-done.2), calls=%async_computation.2 | async-start | bytes 4194304 | tf_op jit(solution)/shard_map/all_to_all | solution.py:462
  90.9 3.3 %collective-permute-start.10 = (bf16[4,8,4,16,128]{4,3,2,1,0:T(8,128)(2,1)S(1)}, bf16[4,8,4,16,128]{4,3,2,1,0:T(8,128)(2,1)S(1)}, u32[]{:S(2)}, u32[]{:S(2)}) collective-permute-start(bf16[4,8,4,16,128]{4,3,2,1,0:T(8,128)(2,1)S(1)} %get-tuple-element.74.rest_0_), channel_id=1, source_target_pairs={{0,7},{1,0},{2,1},{3,2},{4,3},{5,4},{6,5},{7,6},{8,15},{9,8},{10,9... | collective-permute-start | bytes 1572872 | tf_op jit(solution)/shard_map/ppermute | solution.py:296
  97.4 9.0 %collective-permute-done.10.rest_2_ = bf16[4,8,4,16,128]{4,3,2,1,0:T(8,128)(2,1)S(1)} collective-permute-done((bf16[4,8,4,16,128]{4,3,2,1,0:T(8,128)(2,1)S(1)}, bf16[4,8,4,16,128]{4,3,2,1,0:T(8,128)(2,1)S(1)}, u32[]{:S(2)}, u32[]{:S(2)}) %collective-permute-start.10) | collective-permute-done | bytes 524320 | tf_op jit(solution)/shard_map/ppermute | solution.py:296
  106.4 3.7 %collective-permute-start.11 = (bf16[4,8,4,16,128]{4,3,2,1,0:T(8,128)(2,1)S(1)}, bf16[4,8,4,16,128]{4,3,2,1,0:T(8,128)(2,1)}, u32[]{:S(2)}, u32[]{:S(2)}) collective-permute-start(bf16[4,8,4,16,128]{4,3,2,1,0:T(8,128)(2,1)S(1)} %collective-permute-done.10.rest_2_), channel_id=1, source_target_pairs={{0,7},{1,0},{2,1},{3,2},{4,3},{5,4},{6,5},{7,6},{8,15},{9,8},{10,9... | collective-permute-start | bytes 1572872 | tf_op jit(solution)/shard_map/ppermute | solution.py:296
  110.2 7.6 %collective-permute-done.15.rest_4_ = bf16[4,8,4,16,128]{4,3,2,1,0:T(8,128)(2,1)S(1)} collective-permute-done((bf16[4,8,4,16,128]{4,3,2,1,0:T(8,128)(2,1)}, bf16[4,8,4,16,128]{4,3,2,1,0:T(8,128)(2,1)S(1)}, u32[]{:S(2)}, u32[]{:S(2)}) %collective-permute-start.15) | collective-permute-done | bytes 524320 | tf_op jit(solution)/shard_map/ppermute | solution.py:296
  117.8 3.6 %collective-permute-start.19 = (bf16[4,8,4,16,128]{4,3,2,1,0:T(8,128)(2,1)S(1)}, bf16[4,8,4,16,128]{4,3,2,1,0:T(8,128)(2,1)S(1)}, u32[]{:S(2)}, u32[]{:S(2)}) collective-permute-start(bf16[4,8,4,16,128]{4,3,2,1,0:T(8,128)(2,1)S(1)} %collective-permute-done.15.rest_4_), channel_id=1, source_target_pairs={{0,7},{1,0},{2,1},{3,2},{4,3},{5,4},{6,5},{7,6},{8,15},{9,8},{10,9... | collective-permute-start | bytes 1572872 | tf_op jit(solution)/shard_map/ppermute | solution.py:296
  121.4 4.0 %gather_step.3 = (f32[512,512]{1,0:T(8,128)S(1)}, f32[512,128]{1,0:T(8,128)S(1)}) custom-call(s32[8]{0:T(128)S(1)} %and_select_fusion.where_ref, bf16[8,512,512]{2,1,0:T(8,128)(2,1)} %multiply_convert_fusion.w_ref, bf16[4,8,4,16,128]{4,3,2,1,0:T(8,128)(2,1)S(1)} %get-tuple-element.73.rest_0_, bf16[4,8,4,16,128]{4,3,2,1,0:T(8,128)(2,1)} %collective-permute-done.12.rest_1_, ...), custom_call_target="tpu_custom_call" | custom-call | flops 5368709120 | bytes 4718592 | tf_op jit(solution)/shard_map/gather_step/pallas_call | solution.py:237
  128.9 3.8 %collective-permute-done.9.rest_3_ = bf16[4,8,4,16,128]{4,3,2,1,0:T(8,128)(2,1)} collective-permute-done((bf16[4,8,4,16,128]{4,3,2,1,0:T(8,128)(2,1)S(1)}, bf16[4,8,4,16,128]{4,3,2,1,0:T(8,128)(2,1)}, u32[]{:S(2)}, u32[]{:S(2)}) %collective-permute-start.9) | collective-permute-done | bytes 524320 | tf_op jit(solution)/shard_map/ppermute | solution.py:295
  136.0 4.0 %gather_step.4 = (f32[512,512]{1,0:T(8,128)S(1)}, f32[512,128]{1,0:T(8,128)S(1)}) custom-call(s32[8]{0:T(128)S(1)} %and_select_fusion.where_ref, bf16[8,512,512]{2,1,0:T(8,128)(2,1)} %multiply_convert_fusion.w_ref, bf16[4,8,4,16,128]{4,3,2,1,0:T(8,128)(2,1)S(1)} %get-tuple-element.74.rest_0_, bf16[4,8,4,16,128]{4,3,2,1,0:T(8,128)(2,1)S(1)} %collective-permute-done.8.rest_1_, ...), custom_call_target="tpu_custom_call" | custom-call | flops 5368709120 | bytes 4718592 | tf_op jit(solution)/shard_map/gather_step/pallas_call | solution.py:237
  165.3 3.3 %gather_last.3 = (bf16[8,2,16,512]{3,2,1,0:T(8,128)(2,1)S(1)}, bf16[8,2,16,512]{3,2,1,0:T(8,128)(2,1)S(1)}) custom-call(s32[8]{0:T(128)S(1)} %and_select_fusion.where_ref, bf16[8,512,512]{2,1,0:T(8,128)(2,1)} %multiply_convert_fusion.w_ref, bf16[4,8,4,16,128]{4,3,2,1,0:T(8,128)(2,1)S(1)} %collective-permute-done.16.rest_0_, ...), custom_call_target="tpu_custom_call" | custom-call | flops 3221225472 | bytes 3670016 | tf_op jit(solution)/shard_map/gather_last/pallas_call | solution.py:237
  182.2 3.7 %collective-permute-done.28.rest_4_ = bf16[256,256]{1,0:T(8,128)(2,1)S(1)} collective-permute-done((bf16[256,256]{1,0:T(8,128)(2,1)S(1)}, bf16[256,256]{1,0:T(8,128)(2,1)S(1)}, u32[]{:S(2)}, u32[]{:S(2)}) %collective-permute-start.28) | collective-permute-done | bytes 131104 | tf_op jit(solution)/shard_map/ppermute | solution.py:265
  187.9 3.5 %collective-permute-done.30.rest_6_ = bf16[256,256]{1,0:T(8,128)(2,1)S(1)} collective-permute-done((bf16[256,256]{1,0:T(8,128)(2,1)S(1)}, bf16[256,256]{1,0:T(8,128)(2,1)S(1)}, u32[]{:S(2)}, u32[]{:S(2)}) %collective-permute-start.30) | collective-permute-done | bytes 131104 | tf_op jit(solution)/shard_map/ppermute | solution.py:265
  196.0 4.0 %collective-permute-done.31.rest_7_ = bf16[128,256]{1,0:T(8,128)(2,1)S(1)} collective-permute-done((bf16[128,256]{1,0:T(8,128)(2,1)S(1)}, bf16[128,256]{1,0:T(8,128)(2,1)S(1)}, u32[]{:S(2)}, u32[]{:S(2)}) %collective-permute-start.31) | collective-permute-done | bytes 65568 | tf_op jit(solution)/shard_map/ppermute | solution.py:268
  (120 shorter events, 78.4 us)
Async XLA Ops:
  5.4 37.6 %all-to-all-start = ((bf16[32,17,16,128]{3,2,1,0:T(8,128)(2,1)}), bf16[32,17,16,128]{3,2,1,0:T(8,128)(2,1)S(1)}, u32[]{:S(2)}, u32[]{:S(2)}) async-start(bf16[32,17,16,128]{3,2,1,0:T(8,128)(2,1)} %copy-done), calls=%async_computation | async-start | bytes 4456448 | tf_op jit(solution)/shard_map/all_to_all | solution.py:436
  15.9 13.5 %collective-permute-start.2 = (bf16[80,16,128]{2,1,0:T(8,128)(2,1)}, bf16[80,16,128]{2,1,0:T(8,128)(2,1)S(1)}, u32[]{:S(2)}, u32[]{:S(2)}) collective-permute-start(bf16[80,16,128]{2,1,0:T(8,128)(2,1)} %letter.1.rest_0_), channel_id=1, source_target_pairs={{0,7},{1,0},{2,1},{3,2},{4,3},{5,4},{6,5},{7,6},{8,15},{9,8},{10,9... | collective-permute-start | bytes 983048 | tf_op jit(solution)/shard_map/ppermute | solution.py:265
  21.8 11.2 %collective-permute-start = (bf16[80,16,128]{2,1,0:T(8,128)(2,1)}, bf16[80,16,128]{2,1,0:T(8,128)(2,1)S(1)}, u32[]{:S(2)}, u32[]{:S(2)}) collective-permute-start(bf16[80,16,128]{2,1,0:T(8,128)(2,1)} %letter.1.rest_0_), channel_id=1, source_target_pairs={{0,1},{1,2},{2,3},{3,4},{4,5},{5,6},{6,7},{7,0},{8,9},{9,10},{10,1... | collective-permute-start | bytes 983048 | tf_op jit(solution)/shard_map/ppermute | solution.py:264
  29.4 10.0 %collective-permute-start.3 = (bf16[80,16,128]{2,1,0:T(8,128)(2,1)S(1)}, bf16[80,16,128]{2,1,0:T(8,128)(2,1)S(1)}, u32[]{:S(2)}, u32[]{:S(2)}) collective-permute-start(bf16[80,16,128]{2,1,0:T(8,128)(2,1)S(1)} %collective-permute-done.2.rest_2_), channel_id=1, source_target_pairs={{0,7},{1,0},{2,1},{3,2},{4,3},{5,4},{6,5},{7,6},{8,15},{9,8},{10,9... | collective-permute-start | bytes 983048 | tf_op jit(solution)/shard_map/ppermute | solution.py:265
  33.0 10.0 %collective-permute-start.1 = (bf16[80,16,128]{2,1,0:T(8,128)(2,1)S(1)}, bf16[80,16,128]{2,1,0:T(8,128)(2,1)}, u32[]{:S(2)}, u32[]{:S(2)}) collective-permute-start(bf16[80,16,128]{2,1,0:T(8,128)(2,1)S(1)} %collective-permute-done.rest_1_), channel_id=1, source_target_pairs={{0,1},{1,2},{2,3},{3,4},{4,5},{5,6},{6,7},{7,0},{8,9},{9,10},{10,1... | collective-permute-start | bytes 983048 | tf_op jit(solution)/shard_map/ppermute | solution.py:264
  45.3 34.5 %all-to-all-start.1 = ((bf16[32,8,16,128]{3,2,1,0:T(8,128)(2,1)}), bf16[32,8,16,128]{3,2,1,0:T(8,128)(2,1)}, u32[]{:S(2)}, u32[]{:S(2)}) async-start(bf16[32,8,16,128]{3,2,1,0:T(8,128)(2,1)} %pick.1), calls=%async_computation.1 | async-start | bytes 2097152 | tf_op jit(solution)/shard_map/all_to_all | solution.py:453
  52.7 11.8 %collective-permute-start.5 = (bf16[80,16,128]{2,1,0:T(8,128)(2,1)S(1)}, bf16[80,16,128]{2,1,0:T(8,128)(2,1)S(1)}, u32[]{:S(2)}, u32[]{:S(2)}) collective-permute-start(bf16[80,16,128]{2,1,0:T(8,128)(2,1)S(1)} %collective-permute-done.3.rest_4_), channel_id=1, source_target_pairs={{0,7},{1,0},{2,1},{3,2},{4,3},{5,4},{6,5},{7,6},{8,15},{9,8},{10,9... | collective-permute-start | bytes 983048 | tf_op jit(solution)/shard_map/ppermute | solution.py:265
  57.3 11.1 %collective-permute-start.4 = (bf16[80,16,128]{2,1,0:T(8,128)(2,1)}, bf16[80,16,128]{2,1,0:T(8,128)(2,1)S(1)}, u32[]{:S(2)}, u32[]{:S(2)}) collective-permute-start(bf16[80,16,128]{2,1,0:T(8,128)(2,1)} %collective-permute-done.1.rest_3_), channel_id=1, source_target_pairs={{0,1},{1,2},{2,3},{3,4},{4,5},{5,6},{6,7},{7,0},{8,9},{9,10},{10,1... | collective-permute-start | bytes 983048 | tf_op jit(solution)/shard_map/ppermute | solution.py:264
  64.6 10.0 %collective-permute-start.7 = (bf16[48,16,128]{2,1,0:T(8,128)(2,1)S(1)}, bf16[48,16,128]{2,1,0:T(8,128)(2,1)S(1)}, u32[]{:S(2)}, u32[]{:S(2)}) collective-permute-start(bf16[48,16,128]{2,1,0:T(8,128)(2,1)S(1)} %slice.55), channel_id=1, source_target_pairs={{0,7},{1,0},{2,1},{3,2},{4,3},{5,4},{6,5},{7,6},{8,15},{9,8},{10,9... | collective-permute-start | bytes 589832 | tf_op jit(solution)/shard_map/ppermute | solution.py:269
  81.3 12.9 %collective-permute-start.13 = (bf16[4,8,4,16,128]{4,3,2,1,0:T(8,128)(2,1)S(1)}, bf16[4,8,4,16,128]{4,3,2,1,0:T(8,128)(2,1)}, u32[]{:S(2)}, u32[]{:S(2)}) collective-permute-start(bf16[4,8,4,16,128]{4,3,2,1,0:T(8,128)(2,1)S(1)} %get-tuple-element.73.rest_0_), channel_id=1, source_target_pairs={{0,7},{1,0},{2,1},{3,2},{4,3},{5,4},{6,5},{7,6},{8,15},{9,8},{10,9... | collective-permute-start | bytes 1572872 | tf_op jit(solution)/shard_map/ppermute | solution.py:296
  83.2 14.2 %collective-permute-start.12 = (bf16[4,8,4,16,128]{4,3,2,1,0:T(8,128)(2,1)S(1)}, bf16[4,8,4,16,128]{4,3,2,1,0:T(8,128)(2,1)}, u32[]{:S(2)}, u32[]{:S(2)}) collective-permute-start(bf16[4,8,4,16,128]{4,3,2,1,0:T(8,128)(2,1)S(1)} %get-tuple-element.73.rest_0_), channel_id=1, source_target_pairs={{0,1},{1,2},{2,3},{3,4},{4,5},{5,6},{6,7},{7,0},{8,9},{9,10},{10,1... | collective-permute-start | bytes 1572872 | tf_op jit(solution)/shard_map/ppermute | solution.py:295
  83.4 60.6 %all-to-all-start.2 = ((bf16[32,16,16,128]{3,2,1,0:T(8,128)(2,1)}), bf16[32,16,16,128]{3,2,1,0:T(8,128)(2,1)S(1)}, u32[]{:S(2)}, u32[]{:S(2)}) async-start(bf16[32,16,16,128]{3,2,1,0:T(8,128)(2,1)} %copy-done.2), calls=%async_computation.2 | async-start | bytes 4194304 | tf_op jit(solution)/shard_map/all_to_all | solution.py:462
  90.9 15.6 %collective-permute-start.10 = (bf16[4,8,4,16,128]{4,3,2,1,0:T(8,128)(2,1)S(1)}, bf16[4,8,4,16,128]{4,3,2,1,0:T(8,128)(2,1)S(1)}, u32[]{:S(2)}, u32[]{:S(2)}) collective-permute-start(bf16[4,8,4,16,128]{4,3,2,1,0:T(8,128)(2,1)S(1)} %get-tuple-element.74.rest_0_), channel_id=1, source_target_pairs={{0,7},{1,0},{2,1},{3,2},{4,3},{5,4},{6,5},{7,6},{8,15},{9,8},{10,9... | collective-permute-start | bytes 1572872 | tf_op jit(solution)/shard_map/ppermute | solution.py:296
  94.2 16.0 %collective-permute-start.8 = (bf16[4,8,4,16,128]{4,3,2,1,0:T(8,128)(2,1)S(1)}, bf16[4,8,4,16,128]{4,3,2,1,0:T(8,128)(2,1)S(1)}, u32[]{:S(2)}, u32[]{:S(2)}) collective-permute-start(bf16[4,8,4,16,128]{4,3,2,1,0:T(8,128)(2,1)S(1)} %get-tuple-element.74.rest_0_), channel_id=1, source_target_pairs={{0,1},{1,2},{2,3},{3,4},{4,5},{5,6},{6,7},{7,0},{8,9},{9,10},{10,1... | collective-permute-start | bytes 1572872 | tf_op jit(solution)/shard_map/ppermute | solution.py:295
  94.2 23.6 %collective-permute-start.15 = (bf16[4,8,4,16,128]{4,3,2,1,0:T(8,128)(2,1)}, bf16[4,8,4,16,128]{4,3,2,1,0:T(8,128)(2,1)S(1)}, u32[]{:S(2)}, u32[]{:S(2)}) collective-permute-start(bf16[4,8,4,16,128]{4,3,2,1,0:T(8,128)(2,1)} %collective-permute-done.13.rest_2_), channel_id=1, source_target_pairs={{0,7},{1,0},{2,1},{3,2},{4,3},{5,4},{6,5},{7,6},{8,15},{9,8},{10,9... | collective-permute-start | bytes 1572872 | tf_op jit(solution)/shard_map/ppermute | solution.py:296
  97.4 24.0 %collective-permute-start.14 = (bf16[4,8,4,16,128]{4,3,2,1,0:T(8,128)(2,1)}, bf16[4,8,4,16,128]{4,3,2,1,0:T(8,128)(2,1)S(1)}, u32[]{:S(2)}, u32[]{:S(2)}) collective-permute-start(bf16[4,8,4,16,128]{4,3,2,1,0:T(8,128)(2,1)} %collective-permute-done.12.rest_1_), channel_id=1, source_target_pairs={{0,1},{1,2},{2,3},{3,4},{4,5},{5,6},{6,7},{7,0},{8,9},{9,10},{10,1... | collective-permute-start | bytes 1572872 | tf_op jit(solution)/shard_map/ppermute | solution.py:295
  106.4 22.5 %collective-permute-start.11 = (bf16[4,8,4,16,128]{4,3,2,1,0:T(8,128)(2,1)S(1)}, bf16[4,8,4,16,128]{4,3,2,1,0:T(8,128)(2,1)}, u32[]{:S(2)}, u32[]{:S(2)}) collective-permute-start(bf16[4,8,4,16,128]{4,3,2,1,0:T(8,128)(2,1)S(1)} %collective-permute-done.10.rest_2_), channel_id=1, source_target_pairs={{0,7},{1,0},{2,1},{3,2},{4,3},{5,4},{6,5},{7,6},{8,15},{9,8},{10,9... | collective-permute-start | bytes 1572872 | tf_op jit(solution)/shard_map/ppermute | solution.py:296
  110.2 22.6 %collective-permute-start.9 = (bf16[4,8,4,16,128]{4,3,2,1,0:T(8,128)(2,1)S(1)}, bf16[4,8,4,16,128]{4,3,2,1,0:T(8,128)(2,1)}, u32[]{:S(2)}, u32[]{:S(2)}) collective-permute-start(bf16[4,8,4,16,128]{4,3,2,1,0:T(8,128)(2,1)S(1)} %collective-permute-done.8.rest_1_), channel_id=1, source_target_pairs={{0,1},{1,2},{2,3},{3,4},{4,5},{5,6},{6,7},{7,0},{8,9},{9,10},{10,1... | collective-permute-start | bytes 1572872 | tf_op jit(solution)/shard_map/ppermute | solution.py:295
  117.8 23.9 %collective-permute-start.19 = (bf16[4,8,4,16,128]{4,3,2,1,0:T(8,128)(2,1)S(1)}, bf16[4,8,4,16,128]{4,3,2,1,0:T(8,128)(2,1)S(1)}, u32[]{:S(2)}, u32[]{:S(2)}) collective-permute-start(bf16[4,8,4,16,128]{4,3,2,1,0:T(8,128)(2,1)S(1)} %collective-permute-done.15.rest_4_), channel_id=1, source_target_pairs={{0,7},{1,0},{2,1},{3,2},{4,3},{5,4},{6,5},{7,6},{8,15},{9,8},{10,9... | collective-permute-start | bytes 1572872 | tf_op jit(solution)/shard_map/ppermute | solution.py:296
  121.4 22.6 %collective-permute-start.18 = (bf16[4,8,4,16,128]{4,3,2,1,0:T(8,128)(2,1)S(1)}, bf16[4,8,4,16,128]{4,3,2,1,0:T(8,128)(2,1)}, u32[]{:S(2)}, u32[]{:S(2)}) collective-permute-start(bf16[4,8,4,16,128]{4,3,2,1,0:T(8,128)(2,1)S(1)} %collective-permute-done.14.rest_3_), channel_id=1, source_target_pairs={{0,1},{1,2},{2,3},{3,4},{4,5},{5,6},{6,7},{7,0},{8,9},{9,10},{10,1... | collective-permute-start | bytes 1572872 | tf_op jit(solution)/shard_map/ppermute | solution.py:295
  132.7 22.4 %collective-permute-start.16 = (bf16[4,8,4,16,128]{4,3,2,1,0:T(8,128)(2,1)}, bf16[4,8,4,16,128]{4,3,2,1,0:T(8,128)(2,1)S(1)}, u32[]{:S(2)}, u32[]{:S(2)}) collective-permute-start(bf16[4,8,4,16,128]{4,3,2,1,0:T(8,128)(2,1)} %collective-permute-done.9.rest_3_), channel_id=1, source_target_pairs={{0,1},{1,2},{2,3},{3,4},{4,5},{5,6},{6,7},{7,0},{8,9},{9,10},{10,1... | collective-permute-start | bytes 1572872 | tf_op jit(solution)/shard_map/ppermute | solution.py:295
  132.7 22.4 %collective-permute-start.17 = (bf16[4,8,4,16,128]{4,3,2,1,0:T(8,128)(2,1)}, bf16[4,8,4,16,128]{4,3,2,1,0:T(8,128)(2,1)}, u32[]{:S(2)}, u32[]{:S(2)}) collective-permute-start(bf16[4,8,4,16,128]{4,3,2,1,0:T(8,128)(2,1)} %collective-permute-done.11.rest_4_), channel_id=1, source_target_pairs={{0,7},{1,0},{2,1},{3,2},{4,3},{5,4},{6,5},{7,6},{8,15},{9,8},{10,9... | collective-permute-start | bytes 1572872 | tf_op jit(solution)/shard_map/ppermute | solution.py:296
  145.9 14.8 %collective-permute-start.20 = (bf16[2,8,4,16,128]{4,3,2,1,0:T(8,128)(2,1)S(1)}, bf16[2,8,4,16,128]{4,3,2,1,0:T(8,128)(2,1)S(1)}, u32[]{:S(2)}, u32[]{:S(2)}) collective-permute-start(bf16[2,8,4,16,128]{4,3,2,1,0:T(8,128)(2,1)S(1)} %slice.46), channel_id=1, source_target_pairs={{0,1},{1,2},{2,3},{3,4},{4,5},{5,6},{6,7},{7,0},{8,9},{9,10},{10,1... | collective-permute-start | bytes 786440 | tf_op jit(solution)/shard_map/ppermute | solution.py:295
  146.0 14.7 %collective-permute-start.21 = (bf16[2,8,4,16,128]{4,3,2,1,0:T(8,128)(2,1)S(1)}, bf16[2,8,4,16,128]{4,3,2,1,0:T(8,128)(2,1)S(1)}, u32[]{:S(2)}, u32[]{:S(2)}) collective-permute-start(bf16[2,8,4,16,128]{4,3,2,1,0:T(8,128)(2,1)S(1)} %slice.47), channel_id=1, source_target_pairs={{0,7},{1,0},{2,1},{3,2},{4,3},{5,4},{6,5},{7,6},{8,15},{9,8},{10,9... | collective-permute-start | bytes 786440 | tf_op jit(solution)/shard_map/ppermute | solution.py:296
  (33 other events, 215.1 us)

commit v15 on v14

--- a/solution.py
+++ b/solution.py
@@ -16,21 +16,19 @@
 VMEM_LIMIT = 48 * 1024 * 1024
 
 
-def cut_kernel(shard_ref, row_ref, count_ref, db_ref, out_ref):
+def cut_kernel(notes_ref, db_ref, out_ref):
     shard = db_ref.shape[0]
     pieces_t = db_ref.shape[1] // PIECE_T
     pieces_f = db_ref.shape[2] // PIECE_F
-    each, spans = shard_ref.shape
+    kinds, spans = notes_ref.shape
+    each = (kinds - 1) // 2
     lane = lax.broadcasted_iota(jnp.int32, (PIECE_T, PIECE_F), 1)
     note = jnp.zeros((PIECE_T, PIECE_F), jnp.int32)
     for span in range(spans):
-        for j in range(each):
-            at = span * each + j
-            note = jnp.where(lane == at, shard_ref[j : j + 1, span : span + 1], note)
-            row = row_ref[j : j + 1, span : span + 1]
-            note = jnp.where(lane == spans * each + at, row, note)
-        count = count_ref[:, span : span + 1]
-        note = jnp.where(lane == 2 * spans * each + span, count, note)
+        for kind in range(kinds):
+            at = (kind // each * spans + span) * each + kind % each
+            at = at if kind < 2 * each else 2 * each * spans + span
+            note = jnp.where(lane == at, notes_ref[kind : kind + 1, span : span + 1], note)
     note = note.astype(jnp.float32).astype(jnp.bfloat16)
     for f in range(pieces_f):
         for i in range(pieces_t):
@@ -41,18 +39,18 @@
             out_ref[piece, shard] = note
 
 
-def cut(nbr_shard, nbr_row, nbr_count, database):
+def cut(notes, database):
     shard, length, part = database.shape
     pieces = (length // PIECE_T) * (part // PIECE_F)
     vmem = pl.BlockSpec(memory_space=pltpu.VMEM)
     return pl.pallas_call(
         cut_kernel,
-        in_specs=[vmem] * 4,
+        in_specs=[vmem] * 2,
         out_specs=vmem,
         out_shape=jax.ShapeDtypeStruct((pieces, shard + 1, PIECE_T, PIECE_F), database.dtype),
         compiler_params=pltpu.CompilerParams(vmem_limit_bytes=VMEM_LIMIT),
         name="cut",
-    )(nbr_shard.T, nbr_row.T, nbr_count.reshape(1, -1), database)
+    )(notes, database)
 
 
 def pick_kernel(index_ref, spread_ref, *out_refs):
@@ -432,7 +430,8 @@
     me = lax.axis_index("tensor")
     where = ((me + jnp.arange(n_ten, dtype=jnp.int32)) % n_ten).astype(jnp.int32)
 
-    pieces = cut(nbr_shard, nbr_row, nbr_count, database)
+    notes = jnp.concatenate([nbr_shard.T, nbr_row.T, nbr_count[None]], axis=0)
+    pieces = cut(notes, database)
     spread = lax.all_to_all(pieces, "seq", split_axis=0, concat_axis=0, tiled=True)
 
     halves = d_part // (PIECES_WO * PIECE_F)

time: 203 us -> 201 us (level)
    unnamed x42 -> x36, local copies, waits for them, and re-layouts: 12.1 us -> 10.1 us
where the time goes in v15:
time: 201 us
  starting transfers between devices  76.6 us (38%)
  waiting for transfers between devices  71.2 us (35%)
  Pallas kernels  31.1 us (15%)
  local copies, waits for them, and re-layouts  15.2 us (8%)
  other arithmetic  5.59 us (3%)
    ppermute x6, waiting for transfers between devices, ring_gather(): go_left = lax.ppermute(go_left, 'tensor', left)  31.4 us
    ppermute x8, starting transfers between devices, ring_project(): go_left[s] = lax.ppermute(from_right, 'tensor', left)  25.3 us
    ppermute x8, waiting for transfers between devices, ring_project(): go_left[s] = lax.ppermute(from_right, 'tensor', left)  19.1 us
    pallas_call x5, Pallas kernels, gather_step(): pl.pallas_call(functools.partial(gather_kernel, tuple(places), not state,...  17 us
    ppermute x6, starting transfers between devices, ring_gather(): go_left = lax.ppermute(go_left, 'tensor', left)  16.9 us
    unnamed x36, local copies, waits for them, and re-layouts  10.1 us
    all_to_all x1, starting transfers between devices, body(): lax.all_to_all(pieces, 'seq', split_axis=0, concat_axis=0, tiled=True)  7.54 us
    all_to_all x1, starting transfers between devices, body(): mail = lax.all_to_all(strip, 'seq', split_axis=0, concat_axis=0, tiled=True)  7.45 us
  transfers between devices with their start and end apart: 36, of which 21 were waited for; matrix products, arithmetic and copies ran while one was open for 4% of the time, Pallas kernels for 12%

profile of v15, /device:TPU:8, one launch (start us, length us, event | category | flops | bytes accessed | tf_op | source)
XLA Modules:
  0.0 200.7 jit_solution(4951653406220487462)
XLA Ops:
  4.1 7.5 %all-to-all-start = ((bf16[32,17,16,128]{3,2,1,0:T(8,128)(2,1)}), bf16[32,17,16,128]{3,2,1,0:T(8,128)(2,1)S(1)}, u32[]{:S(2)}, u32[]{:S(2)}) async-start(bf16[32,17,16,128]{3,2,1,0:T(8,128)(2,1)} %copy-done), calls=%async_computation | async-start | bytes 4456448 | tf_op jit(solution)/shard_map/all_to_all | solution.py:435
  14.7 5.9 %collective-permute-start.2 = (bf16[80,16,128]{2,1,0:T(8,128)(2,1)}, bf16[80,16,128]{2,1,0:T(8,128)(2,1)S(1)}, u32[]{:S(2)}, u32[]{:S(2)}) collective-permute-start(bf16[80,16,128]{2,1,0:T(8,128)(2,1)} %letter.1.rest_0_), channel_id=1, source_target_pairs={{0,7},{1,0},{2,1},{3,2},{4,3},{5,4},{6,5},{7,6},{8,15},{9,8},{10,9... | collective-permute-start | bytes 983048 | tf_op jit(solution)/shard_map/ppermute | solution.py:263
  20.5 7.6 %collective-permute-done.2.rest_2_ = bf16[80,16,128]{2,1,0:T(8,128)(2,1)S(1)} collective-permute-done((bf16[80,16,128]{2,1,0:T(8,128)(2,1)}, bf16[80,16,128]{2,1,0:T(8,128)(2,1)S(1)}, u32[]{:S(2)}, u32[]{:S(2)}) %collective-permute-start.2) | collective-permute-done | bytes 327712 | tf_op jit(solution)/shard_map/ppermute | solution.py:263
  28.1 3.6 %collective-permute-start.3 = (bf16[80,16,128]{2,1,0:T(8,128)(2,1)S(1)}, bf16[80,16,128]{2,1,0:T(8,128)(2,1)S(1)}, u32[]{:S(2)}, u32[]{:S(2)}) collective-permute-start(bf16[80,16,128]{2,1,0:T(8,128)(2,1)S(1)} %collective-permute-done.2.rest_2_), channel_id=1, source_target_pairs={{0,7},{1,0},{2,1},{3,2},{4,3},{5,4},{6,5},{7,6},{8,15},{9,8},{10,9... | collective-permute-start | bytes 983048 | tf_op jit(solution)/shard_map/ppermute | solution.py:263
  31.7 6.4 %collective-permute-done.3.rest_4_ = bf16[80,16,128]{2,1,0:T(8,128)(2,1)S(1)} collective-permute-done((bf16[80,16,128]{2,1,0:T(8,128)(2,1)S(1)}, bf16[80,16,128]{2,1,0:T(8,128)(2,1)S(1)}, u32[]{:S(2)}, u32[]{:S(2)}) %collective-permute-start.3) | collective-permute-done | bytes 327712 | tf_op jit(solution)/shard_map/ppermute | solution.py:263
  38.2 3.5 %collective-permute-done.1.rest_3_ = bf16[80,16,128]{2,1,0:T(8,128)(2,1)} collective-permute-done((bf16[80,16,128]{2,1,0:T(8,128)(2,1)S(1)}, bf16[80,16,128]{2,1,0:T(8,128)(2,1)}, u32[]{:S(2)}, u32[]{:S(2)}) %collective-permute-start.1) | collective-permute-done | bytes 327712 | tf_op jit(solution)/shard_map/ppermute | solution.py:262
  44.0 7.4 %all-to-all-start.1 = ((bf16[32,8,16,128]{3,2,1,0:T(8,128)(2,1)}), bf16[32,8,16,128]{3,2,1,0:T(8,128)(2,1)}, u32[]{:S(2)}, u32[]{:S(2)}) async-start(bf16[32,8,16,128]{3,2,1,0:T(8,128)(2,1)} %pick.1), calls=%async_computation.1 | async-start | bytes 2097152 | tf_op jit(solution)/shard_map/all_to_all | solution.py:452
  51.5 4.5 %collective-permute-start.5 = (bf16[80,16,128]{2,1,0:T(8,128)(2,1)S(1)}, bf16[80,16,128]{2,1,0:T(8,128)(2,1)S(1)}, u32[]{:S(2)}, u32[]{:S(2)}) collective-permute-start(bf16[80,16,128]{2,1,0:T(8,128)(2,1)S(1)} %collective-permute-done.3.rest_4_), channel_id=1, source_target_pairs={{0,7},{1,0},{2,1},{3,2},{4,3},{5,4},{6,5},{7,6},{8,15},{9,8},{10,9... | collective-permute-start | bytes 983048 | tf_op jit(solution)/shard_map/ppermute | solution.py:263
  56.0 7.2 %collective-permute-done.5.rest_6_ = bf16[80,16,128]{2,1,0:T(8,128)(2,1)S(1)} collective-permute-done((bf16[80,16,128]{2,1,0:T(8,128)(2,1)S(1)}, bf16[80,16,128]{2,1,0:T(8,128)(2,1)S(1)}, u32[]{:S(2)}, u32[]{:S(2)}) %collective-permute-start.5) | collective-permute-done | bytes 327712 | tf_op jit(solution)/shard_map/ppermute | solution.py:263
  63.3 3.8 %collective-permute-start.7 = (bf16[48,16,128]{2,1,0:T(8,128)(2,1)S(1)}, bf16[48,16,128]{2,1,0:T(8,128)(2,1)S(1)}, u32[]{:S(2)}, u32[]{:S(2)}) collective-permute-start(bf16[48,16,128]{2,1,0:T(8,128)(2,1)S(1)} %slice.55), channel_id=1, source_target_pairs={{0,7},{1,0},{2,1},{3,2},{4,3},{5,4},{6,5},{7,6},{8,15},{9,8},{10,9... | collective-permute-start | bytes 589832 | tf_op jit(solution)/shard_map/ppermute | solution.py:267
  67.2 4.1 %multiply_convert_fusion.w_ref = bf16[8,512,512]{2,1,0:T(8,128)(2,1)} fusion(bf16[8,512,256]{2,1,0:T(8,128)(2,1)} %bitcast.17, bf16[8,512,256]{2,1,0:T(8,128)(2,1)} %bitcast.18, f32[8,512]{1,0:T(8,128)S(1)} %reshape.33), kind=kLoop, calls=%fused_computation | loop fusion | flops 12582912 | bytes 8404992 | tf_op jit(solution)/shard_map/convert_element_type | solution.py:455
  82.1 7.4 %all-to-all-start.2 = ((bf16[32,16,16,128]{3,2,1,0:T(8,128)(2,1)}), bf16[32,16,16,128]{3,2,1,0:T(8,128)(2,1)S(1)}, u32[]{:S(2)}, u32[]{:S(2)}) async-start(bf16[32,16,16,128]{3,2,1,0:T(8,128)(2,1)} %copy-done.2), calls=%async_computation.2 | async-start | bytes 4194304 | tf_op jit(solution)/shard_map/all_to_all | solution.py:461
  89.6 3.3 %collective-permute-start.10 = (bf16[4,8,4,16,128]{4,3,2,1,0:T(8,128)(2,1)S(1)}, bf16[4,8,4,16,128]{4,3,2,1,0:T(8,128)(2,1)S(1)}, u32[]{:S(2)}, u32[]{:S(2)}) collective-permute-start(bf16[4,8,4,16,128]{4,3,2,1,0:T(8,128)(2,1)S(1)} %get-tuple-element.74.rest_0_), channel_id=1, source_target_pairs={{0,7},{1,0},{2,1},{3,2},{4,3},{5,4},{6,5},{7,6},{8,15},{9,8},{10,9... | collective-permute-start | bytes 1572872 | tf_op jit(solution)/shard_map/ppermute | solution.py:294
  96.1 9.0 %collective-permute-done.10.rest_2_ = bf16[4,8,4,16,128]{4,3,2,1,0:T(8,128)(2,1)S(1)} collective-permute-done((bf16[4,8,4,16,128]{4,3,2,1,0:T(8,128)(2,1)S(1)}, bf16[4,8,4,16,128]{4,3,2,1,0:T(8,128)(2,1)S(1)}, u32[]{:S(2)}, u32[]{:S(2)}) %collective-permute-start.10) | collective-permute-done | bytes 524320 | tf_op jit(solution)/shard_map/ppermute | solution.py:294
  105.1 3.7 %collective-permute-start.11 = (bf16[4,8,4,16,128]{4,3,2,1,0:T(8,128)(2,1)S(1)}, bf16[4,8,4,16,128]{4,3,2,1,0:T(8,128)(2,1)}, u32[]{:S(2)}, u32[]{:S(2)}) collective-permute-start(bf16[4,8,4,16,128]{4,3,2,1,0:T(8,128)(2,1)S(1)} %collective-permute-done.10.rest_2_), channel_id=1, source_target_pairs={{0,7},{1,0},{2,1},{3,2},{4,3},{5,4},{6,5},{7,6},{8,15},{9,8},{10,9... | collective-permute-start | bytes 1572872 | tf_op jit(solution)/shard_map/ppermute | solution.py:294
  108.9 7.6 %collective-permute-done.15.rest_4_ = bf16[4,8,4,16,128]{4,3,2,1,0:T(8,128)(2,1)S(1)} collective-permute-done((bf16[4,8,4,16,128]{4,3,2,1,0:T(8,128)(2,1)}, bf16[4,8,4,16,128]{4,3,2,1,0:T(8,128)(2,1)S(1)}, u32[]{:S(2)}, u32[]{:S(2)}) %collective-permute-start.15) | collective-permute-done | bytes 524320 | tf_op jit(solution)/shard_map/ppermute | solution.py:294
  116.5 3.6 %collective-permute-start.19 = (bf16[4,8,4,16,128]{4,3,2,1,0:T(8,128)(2,1)S(1)}, bf16[4,8,4,16,128]{4,3,2,1,0:T(8,128)(2,1)S(1)}, u32[]{:S(2)}, u32[]{:S(2)}) collective-permute-start(bf16[4,8,4,16,128]{4,3,2,1,0:T(8,128)(2,1)S(1)} %collective-permute-done.15.rest_4_), channel_id=1, source_target_pairs={{0,7},{1,0},{2,1},{3,2},{4,3},{5,4},{6,5},{7,6},{8,15},{9,8},{10,9... | collective-permute-start | bytes 1572872 | tf_op jit(solution)/shard_map/ppermute | solution.py:294
  120.1 4.0 %gather_step.3 = (f32[512,512]{1,0:T(8,128)S(1)}, f32[512,128]{1,0:T(8,128)S(1)}) custom-call(s32[8]{0:T(128)S(1)} %and_select_fusion.where_ref, bf16[8,512,512]{2,1,0:T(8,128)(2,1)} %multiply_convert_fusion.w_ref, bf16[4,8,4,16,128]{4,3,2,1,0:T(8,128)(2,1)S(1)} %get-tuple-element.73.rest_0_, bf16[4,8,4,16,128]{4,3,2,1,0:T(8,128)(2,1)} %collective-permute-done.12.rest_1_, ...), custom_call_target="tpu_custom_call" | custom-call | flops 5368709120 | bytes 4718592 | tf_op jit(solution)/shard_map/gather_step/pallas_call | solution.py:235
  127.6 3.8 %collective-permute-done.9.rest_3_ = bf16[4,8,4,16,128]{4,3,2,1,0:T(8,128)(2,1)} collective-permute-done((bf16[4,8,4,16,128]{4,3,2,1,0:T(8,128)(2,1)S(1)}, bf16[4,8,4,16,128]{4,3,2,1,0:T(8,128)(2,1)}, u32[]{:S(2)}, u32[]{:S(2)}) %collective-permute-start.9) | collective-permute-done | bytes 524320 | tf_op jit(solution)/shard_map/ppermute | solution.py:293
  134.7 4.0 %gather_step.4 = (f32[512,512]{1,0:T(8,128)S(1)}, f32[512,128]{1,0:T(8,128)S(1)}) custom-call(s32[8]{0:T(128)S(1)} %and_select_fusion.where_ref, bf16[8,512,512]{2,1,0:T(8,128)(2,1)} %multiply_convert_fusion.w_ref, bf16[4,8,4,16,128]{4,3,2,1,0:T(8,128)(2,1)S(1)} %get-tuple-element.74.rest_0_, bf16[4,8,4,16,128]{4,3,2,1,0:T(8,128)(2,1)S(1)} %collective-permute-done.8.rest_1_, ...), custom_call_target="tpu_custom_call" | custom-call | flops 5368709120 | bytes 4718592 | tf_op jit(solution)/shard_map/gather_step/pallas_call | solution.py:235
  164.0 3.3 %gather_last.3 = (bf16[8,2,16,512]{3,2,1,0:T(8,128)(2,1)S(1)}, bf16[8,2,16,512]{3,2,1,0:T(8,128)(2,1)S(1)}) custom-call(s32[8]{0:T(128)S(1)} %and_select_fusion.where_ref, bf16[8,512,512]{2,1,0:T(8,128)(2,1)} %multiply_convert_fusion.w_ref, bf16[4,8,4,16,128]{4,3,2,1,0:T(8,128)(2,1)S(1)} %collective-permute-done.16.rest_0_, ...), custom_call_target="tpu_custom_call" | custom-call | flops 3221225472 | bytes 3670016 | tf_op jit(solution)/shard_map/gather_last/pallas_call | solution.py:235
  180.9 3.7 %collective-permute-done.28.rest_4_ = bf16[256,256]{1,0:T(8,128)(2,1)S(1)} collective-permute-done((bf16[256,256]{1,0:T(8,128)(2,1)S(1)}, bf16[256,256]{1,0:T(8,128)(2,1)S(1)}, u32[]{:S(2)}, u32[]{:S(2)}) %collective-permute-start.28) | collective-permute-done | bytes 131104 | tf_op jit(solution)/shard_map/ppermute | solution.py:263
  186.6 3.5 %collective-permute-done.30.rest_6_ = bf16[256,256]{1,0:T(8,128)(2,1)S(1)} collective-permute-done((bf16[256,256]{1,0:T(8,128)(2,1)S(1)}, bf16[256,256]{1,0:T(8,128)(2,1)S(1)}, u32[]{:S(2)}, u32[]{:S(2)}) %collective-permute-start.30) | collective-permute-done | bytes 131104 | tf_op jit(solution)/shard_map/ppermute | solution.py:263
  194.7 3.9 %collective-permute-done.31.rest_7_ = bf16[128,256]{1,0:T(8,128)(2,1)S(1)} collective-permute-done((bf16[128,256]{1,0:T(8,128)(2,1)S(1)}, bf16[128,256]{1,0:T(8,128)(2,1)S(1)}, u32[]{:S(2)}, u32[]{:S(2)}) %collective-permute-start.31) | collective-permute-done | bytes 65568 | tf_op jit(solution)/shard_map/ppermute | solution.py:266
  (115 shorter events, 77.2 us)
Async XLA Ops:
  4.1 37.6 %all-to-all-start = ((bf16[32,17,16,128]{3,2,1,0:T(8,128)(2,1)}), bf16[32,17,16,128]{3,2,1,0:T(8,128)(2,1)S(1)}, u32[]{:S(2)}, u32[]{:S(2)}) async-start(bf16[32,17,16,128]{3,2,1,0:T(8,128)(2,1)} %copy-done), calls=%async_computation | async-start | bytes 4456448 | tf_op jit(solution)/shard_map/all_to_all | solution.py:435
  14.7 13.5 %collective-permute-start.2 = (bf16[80,16,128]{2,1,0:T(8,128)(2,1)}, bf16[80,16,128]{2,1,0:T(8,128)(2,1)S(1)}, u32[]{:S(2)}, u32[]{:S(2)}) collective-permute-start(bf16[80,16,128]{2,1,0:T(8,128)(2,1)} %letter.1.rest_0_), channel_id=1, source_target_pairs={{0,7},{1,0},{2,1},{3,2},{4,3},{5,4},{6,5},{7,6},{8,15},{9,8},{10,9... | collective-permute-start | bytes 983048 | tf_op jit(solution)/shard_map/ppermute | solution.py:263
  20.5 11.2 %collective-permute-start = (bf16[80,16,128]{2,1,0:T(8,128)(2,1)}, bf16[80,16,128]{2,1,0:T(8,128)(2,1)S(1)}, u32[]{:S(2)}, u32[]{:S(2)}) collective-permute-start(bf16[80,16,128]{2,1,0:T(8,128)(2,1)} %letter.1.rest_0_), channel_id=1, source_target_pairs={{0,1},{1,2},{2,3},{3,4},{4,5},{5,6},{6,7},{7,0},{8,9},{9,10},{10,1... | collective-permute-start | bytes 983048 | tf_op jit(solution)/shard_map/ppermute | solution.py:262
  28.1 10.0 %collective-permute-start.3 = (bf16[80,16,128]{2,1,0:T(8,128)(2,1)S(1)}, bf16[80,16,128]{2,1,0:T(8,128)(2,1)S(1)}, u32[]{:S(2)}, u32[]{:S(2)}) collective-permute-start(bf16[80,16,128]{2,1,0:T(8,128)(2,1)S(1)} %collective-permute-done.2.rest_2_), channel_id=1, source_target_pairs={{0,7},{1,0},{2,1},{3,2},{4,3},{5,4},{6,5},{7,6},{8,15},{9,8},{10,9... | collective-permute-start | bytes 983048 | tf_op jit(solution)/shard_map/ppermute | solution.py:263
  31.7 10.0 %collective-permute-start.1 = (bf16[80,16,128]{2,1,0:T(8,128)(2,1)S(1)}, bf16[80,16,128]{2,1,0:T(8,128)(2,1)}, u32[]{:S(2)}, u32[]{:S(2)}) collective-permute-start(bf16[80,16,128]{2,1,0:T(8,128)(2,1)S(1)} %collective-permute-done.rest_1_), channel_id=1, source_target_pairs={{0,1},{1,2},{2,3},{3,4},{4,5},{5,6},{6,7},{7,0},{8,9},{9,10},{10,1... | collective-permute-start | bytes 983048 | tf_op jit(solution)/shard_map/ppermute | solution.py:262
  44.0 34.5 %all-to-all-start.1 = ((bf16[32,8,16,128]{3,2,1,0:T(8,128)(2,1)}), bf16[32,8,16,128]{3,2,1,0:T(8,128)(2,1)}, u32[]{:S(2)}, u32[]{:S(2)}) async-start(bf16[32,8,16,128]{3,2,1,0:T(8,128)(2,1)} %pick.1), calls=%async_computation.1 | async-start | bytes 2097152 | tf_op jit(solution)/shard_map/all_to_all | solution.py:452
  51.5 11.8 %collective-permute-start.5 = (bf16[80,16,128]{2,1,0:T(8,128)(2,1)S(1)}, bf16[80,16,128]{2,1,0:T(8,128)(2,1)S(1)}, u32[]{:S(2)}, u32[]{:S(2)}) collective-permute-start(bf16[80,16,128]{2,1,0:T(8,128)(2,1)S(1)} %collective-permute-done.3.rest_4_), channel_id=1, source_target_pairs={{0,7},{1,0},{2,1},{3,2},{4,3},{5,4},{6,5},{7,6},{8,15},{9,8},{10,9... | collective-permute-start | bytes 983048 | tf_op jit(solution)/shard_map/ppermute | solution.py:263
  56.0 11.1 %collective-permute-start.4 = (bf16[80,16,128]{2,1,0:T(8,128)(2,1)}, bf16[80,16,128]{2,1,0:T(8,128)(2,1)S(1)}, u32[]{:S(2)}, u32[]{:S(2)}) collective-permute-start(bf16[80,16,128]{2,1,0:T(8,128)(2,1)} %collective-permute-done.1.rest_3_), channel_id=1, source_target_pairs={{0,1},{1,2},{2,3},{3,4},{4,5},{5,6},{6,7},{7,0},{8,9},{9,10},{10,1... | collective-permute-start | bytes 983048 | tf_op jit(solution)/shard_map/ppermute | solution.py:262
  63.3 10.0 %collective-permute-start.7 = (bf16[48,16,128]{2,1,0:T(8,128)(2,1)S(1)}, bf16[48,16,128]{2,1,0:T(8,128)(2,1)S(1)}, u32[]{:S(2)}, u32[]{:S(2)}) collective-permute-start(bf16[48,16,128]{2,1,0:T(8,128)(2,1)S(1)} %slice.55), channel_id=1, source_target_pairs={{0,7},{1,0},{2,1},{3,2},{4,3},{5,4},{6,5},{7,6},{8,15},{9,8},{10,9... | collective-permute-start | bytes 589832 | tf_op jit(solution)/shard_map/ppermute | solution.py:267
  80.0 12.8 %collective-permute-start.13 = (bf16[4,8,4,16,128]{4,3,2,1,0:T(8,128)(2,1)S(1)}, bf16[4,8,4,16,128]{4,3,2,1,0:T(8,128)(2,1)}, u32[]{:S(2)}, u32[]{:S(2)}) collective-permute-start(bf16[4,8,4,16,128]{4,3,2,1,0:T(8,128)(2,1)S(1)} %get-tuple-element.73.rest_0_), channel_id=1, source_target_pairs={{0,7},{1,0},{2,1},{3,2},{4,3},{5,4},{6,5},{7,6},{8,15},{9,8},{10,9... | collective-permute-start | bytes 1572872 | tf_op jit(solution)/shard_map/ppermute | solution.py:294
  81.9 14.2 %collective-permute-start.12 = (bf16[4,8,4,16,128]{4,3,2,1,0:T(8,128)(2,1)S(1)}, bf16[4,8,4,16,128]{4,3,2,1,0:T(8,128)(2,1)}, u32[]{:S(2)}, u32[]{:S(2)}) collective-permute-start(bf16[4,8,4,16,128]{4,3,2,1,0:T(8,128)(2,1)S(1)} %get-tuple-element.73.rest_0_), channel_id=1, source_target_pairs={{0,1},{1,2},{2,3},{3,4},{4,5},{5,6},{6,7},{7,0},{8,9},{9,10},{10,1... | collective-permute-start | bytes 1572872 | tf_op jit(solution)/shard_map/ppermute | solution.py:293
  82.1 60.6 %all-to-all-start.2 = ((bf16[32,16,16,128]{3,2,1,0:T(8,128)(2,1)}), bf16[32,16,16,128]{3,2,1,0:T(8,128)(2,1)S(1)}, u32[]{:S(2)}, u32[]{:S(2)}) async-start(bf16[32,16,16,128]{3,2,1,0:T(8,128)(2,1)} %copy-done.2), calls=%async_computation.2 | async-start | bytes 4194304 | tf_op jit(solution)/shard_map/all_to_all | solution.py:461
  89.6 15.6 %collective-permute-start.10 = (bf16[4,8,4,16,128]{4,3,2,1,0:T(8,128)(2,1)S(1)}, bf16[4,8,4,16,128]{4,3,2,1,0:T(8,128)(2,1)S(1)}, u32[]{:S(2)}, u32[]{:S(2)}) collective-permute-start(bf16[4,8,4,16,128]{4,3,2,1,0:T(8,128)(2,1)S(1)} %get-tuple-element.74.rest_0_), channel_id=1, source_target_pairs={{0,7},{1,0},{2,1},{3,2},{4,3},{5,4},{6,5},{7,6},{8,15},{9,8},{10,9... | collective-permute-start | bytes 1572872 | tf_op jit(solution)/shard_map/ppermute | solution.py:294
  92.8 16.0 %collective-permute-start.8 = (bf16[4,8,4,16,128]{4,3,2,1,0:T(8,128)(2,1)S(1)}, bf16[4,8,4,16,128]{4,3,2,1,0:T(8,128)(2,1)S(1)}, u32[]{:S(2)}, u32[]{:S(2)}) collective-permute-start(bf16[4,8,4,16,128]{4,3,2,1,0:T(8,128)(2,1)S(1)} %get-tuple-element.74.rest_0_), channel_id=1, source_target_pairs={{0,1},{1,2},{2,3},{3,4},{4,5},{5,6},{6,7},{7,0},{8,9},{9,10},{10,1... | collective-permute-start | bytes 1572872 | tf_op jit(solution)/shard_map/ppermute | solution.py:293
  92.8 23.6 %collective-permute-start.15 = (bf16[4,8,4,16,128]{4,3,2,1,0:T(8,128)(2,1)}, bf16[4,8,4,16,128]{4,3,2,1,0:T(8,128)(2,1)S(1)}, u32[]{:S(2)}, u32[]{:S(2)}) collective-permute-start(bf16[4,8,4,16,128]{4,3,2,1,0:T(8,128)(2,1)} %collective-permute-done.13.rest_2_), channel_id=1, source_target_pairs={{0,7},{1,0},{2,1},{3,2},{4,3},{5,4},{6,5},{7,6},{8,15},{9,8},{10,9... | collective-permute-start | bytes 1572872 | tf_op jit(solution)/shard_map/ppermute | solution.py:294
  96.1 24.0 %collective-permute-start.14 = (bf16[4,8,4,16,128]{4,3,2,1,0:T(8,128)(2,1)}, bf16[4,8,4,16,128]{4,3,2,1,0:T(8,128)(2,1)S(1)}, u32[]{:S(2)}, u32[]{:S(2)}) collective-permute-start(bf16[4,8,4,16,128]{4,3,2,1,0:T(8,128)(2,1)} %collective-permute-done.12.rest_1_), channel_id=1, source_target_pairs={{0,1},{1,2},{2,3},{3,4},{4,5},{5,6},{6,7},{7,0},{8,9},{9,10},{10,1... | collective-permute-start | bytes 1572872 | tf_op jit(solution)/shard_map/ppermute | solution.py:293
  105.1 22.5 %collective-permute-start.11 = (bf16[4,8,4,16,128]{4,3,2,1,0:T(8,128)(2,1)S(1)}, bf16[4,8,4,16,128]{4,3,2,1,0:T(8,128)(2,1)}, u32[]{:S(2)}, u32[]{:S(2)}) collective-permute-start(bf16[4,8,4,16,128]{4,3,2,1,0:T(8,128)(2,1)S(1)} %collective-permute-done.10.rest_2_), channel_id=1, source_target_pairs={{0,7},{1,0},{2,1},{3,2},{4,3},{5,4},{6,5},{7,6},{8,15},{9,8},{10,9... | collective-permute-start | bytes 1572872 | tf_op jit(solution)/shard_map/ppermute | solution.py:294
  108.9 22.6 %collective-permute-start.9 = (bf16[4,8,4,16,128]{4,3,2,1,0:T(8,128)(2,1)S(1)}, bf16[4,8,4,16,128]{4,3,2,1,0:T(8,128)(2,1)}, u32[]{:S(2)}, u32[]{:S(2)}) collective-permute-start(bf16[4,8,4,16,128]{4,3,2,1,0:T(8,128)(2,1)S(1)} %collective-permute-done.8.rest_1_), channel_id=1, source_target_pairs={{0,1},{1,2},{2,3},{3,4},{4,5},{5,6},{6,7},{7,0},{8,9},{9,10},{10,1... | collective-permute-start | bytes 1572872 | tf_op jit(solution)/shard_map/ppermute | solution.py:293
  116.5 23.9 %collective-permute-start.19 = (bf16[4,8,4,16,128]{4,3,2,1,0:T(8,128)(2,1)S(1)}, bf16[4,8,4,16,128]{4,3,2,1,0:T(8,128)(2,1)S(1)}, u32[]{:S(2)}, u32[]{:S(2)}) collective-permute-start(bf16[4,8,4,16,128]{4,3,2,1,0:T(8,128)(2,1)S(1)} %collective-permute-done.15.rest_4_), channel_id=1, source_target_pairs={{0,7},{1,0},{2,1},{3,2},{4,3},{5,4},{6,5},{7,6},{8,15},{9,8},{10,9... | collective-permute-start | bytes 1572872 | tf_op jit(solution)/shard_map/ppermute | solution.py:294
  120.1 22.6 %collective-permute-start.18 = (bf16[4,8,4,16,128]{4,3,2,1,0:T(8,128)(2,1)S(1)}, bf16[4,8,4,16,128]{4,3,2,1,0:T(8,128)(2,1)}, u32[]{:S(2)}, u32[]{:S(2)}) collective-permute-start(bf16[4,8,4,16,128]{4,3,2,1,0:T(8,128)(2,1)S(1)} %collective-permute-done.14.rest_3_), channel_id=1, source_target_pairs={{0,1},{1,2},{2,3},{3,4},{4,5},{5,6},{6,7},{7,0},{8,9},{9,10},{10,1... | collective-permute-start | bytes 1572872 | tf_op jit(solution)/shard_map/ppermute | solution.py:293
  131.4 22.4 %collective-permute-start.16 = (bf16[4,8,4,16,128]{4,3,2,1,0:T(8,128)(2,1)}, bf16[4,8,4,16,128]{4,3,2,1,0:T(8,128)(2,1)S(1)}, u32[]{:S(2)}, u32[]{:S(2)}) collective-permute-start(bf16[4,8,4,16,128]{4,3,2,1,0:T(8,128)(2,1)} %collective-permute-done.9.rest_3_), channel_id=1, source_target_pairs={{0,1},{1,2},{2,3},{3,4},{4,5},{5,6},{6,7},{7,0},{8,9},{9,10},{10,1... | collective-permute-start | bytes 1572872 | tf_op jit(solution)/shard_map/ppermute | solution.py:293
  131.4 22.4 %collective-permute-start.17 = (bf16[4,8,4,16,128]{4,3,2,1,0:T(8,128)(2,1)}, bf16[4,8,4,16,128]{4,3,2,1,0:T(8,128)(2,1)}, u32[]{:S(2)}, u32[]{:S(2)}) collective-permute-start(bf16[4,8,4,16,128]{4,3,2,1,0:T(8,128)(2,1)} %collective-permute-done.11.rest_4_), channel_id=1, source_target_pairs={{0,7},{1,0},{2,1},{3,2},{4,3},{5,4},{6,5},{7,6},{8,15},{9,8},{10,9... | collective-permute-start | bytes 1572872 | tf_op jit(solution)/shard_map/ppermute | solution.py:294
  144.6 14.8 %collective-permute-start.20 = (bf16[2,8,4,16,128]{4,3,2,1,0:T(8,128)(2,1)S(1)}, bf16[2,8,4,16,128]{4,3,2,1,0:T(8,128)(2,1)S(1)}, u32[]{:S(2)}, u32[]{:S(2)}) collective-permute-start(bf16[2,8,4,16,128]{4,3,2,1,0:T(8,128)(2,1)S(1)} %slice.46), channel_id=1, source_target_pairs={{0,1},{1,2},{2,3},{3,4},{4,5},{5,6},{6,7},{7,0},{8,9},{9,10},{10,1... | collective-permute-start | bytes 786440 | tf_op jit(solution)/shard_map/ppermute | solution.py:293
  144.7 14.7 %collective-permute-start.21 = (bf16[2,8,4,16,128]{4,3,2,1,0:T(8,128)(2,1)S(1)}, bf16[2,8,4,16,128]{4,3,2,1,0:T(8,128)(2,1)S(1)}, u32[]{:S(2)}, u32[]{:S(2)}) collective-permute-start(bf16[2,8,4,16,128]{4,3,2,1,0:T(8,128)(2,1)S(1)} %slice.47), channel_id=1, source_target_pairs={{0,7},{1,0},{2,1},{3,2},{4,3},{5,4},{6,5},{7,6},{8,15},{9,8},{10,9... | collective-permute-start | bytes 786440 | tf_op jit(solution)/shard_map/ppermute | solution.py:294
  (30 other events, 213.1 us)
